TPU v7x, 32 devices: a whole 2x2x4 slice. The times are simulated.
32 devices in a mesh: dp: 4 (over x, core), head: 8 (over z, y).
Axes of the slice: x: 2, y: 2, z: 4, core: 2. Of those that a mesh axis runs over, the one named last changes fastest.
Arguments:
- hidden: bfloat16 [2048, 1536], P('dp'), may hold values from -6 to 6
- token_prompt: int32 [2048], replicated, may hold values from 0 to 7, never falling along the last dimension, each value on 1 to 512 neighbouring positions
- request_prompt: int32 [16], P('dp'), may hold values from 0 to 7
- in_gain: float32 [1536], replicated, may hold values from 0.1 to 1.9
- w_zx: float32 [1536, 2, 3072], P('dp', None, 'head'), may hold values from -0.15625 to 0.15625
- w_bc: float32 [1536, 256], P('dp'), may hold values from -0.0390625 to 0.0390625
- w_dt: float32 [1536, 48], P('dp', 'head'), may hold values from -0.15625 to 0.15625
- dt_bias: float32 [48], P('head'), may hold values from -3 to -0.5
- a_log: float32 [48], P('head'), may hold values from -9.5 to -1.6
- conv_x: float32 [4, 3072], P(None, 'head'), may hold values from -3 to 3
- conv_bc: float32 [4, 256], replicated, may hold values from -3 to 3
- skip_gain: float32 [48], P('head'), may hold values from 0.5 to 2
- out_gain: float32 [3072], P('head'), may hold values from 0.1 to 1.9
- w_out: bfloat16 [3072, 1536], P('head'), may hold values from -0.109375 to 0.109375
Outputs:
- layer_out: bfloat16 [2048, 1536], P(('dp', 'head'))
- request_states: float32 [16, 48, 64, 128], P('dp', 'head')
Inputs may be any that keep to these rules, and one draw needn't show every extreme that they name: `token_prompt`: prompt ids never fall along the tokens; each of the 8 prompts has at least one token.
All inputs are finite; a program needn't handle non-finite values.
Results may differ from a plain program's by a relative error of at most 0.012.
Values may be sent and summed in bfloat16 or wider, within the bound.
No kernel may reach another device: no remote copies, remote signals or barrier semaphores. Data moves between devices by JAX's collectives and lax.ppermute only.
A program may use at most 64 MiB of HBM per device.

v0:
```python
import jax
import jax.numpy as jnp
from jax import lax
from jax.sharding import PartitionSpec as P

BLOCK = 256
PROMPTS = 8


EPSILON = 1e-05


def from_behind(shard, axis, by):
    peers = lax.axis_size(axis)
    pairs = [(i, i + by) for i in range(peers) if 0 <= i + by < peers]
    return lax.ppermute(shard, axis, pairs)


def carried_in(shard, axis, combine, identity):
    peers, position = (lax.axis_size(axis), lax.axis_index(axis))
    everything = jax.tree.map(lambda part: lax.all_gather(part, axis), shard)
    start = jax.tree.map(
        lambda part, zero: jnp.broadcast_to(jnp.asarray(zero, part.dtype), part.shape),
        shard,
        identity,
    )

    def step(k, before):
        reached = k < position
        new = combine(before, jax.tree.map(lambda part: part[k], everything))
        return jax.tree.map(lambda a, b: jnp.where(reached, a, b), new, before)

    return lax.fori_loop(0, peers, step, start)


def rms_scale(values):
    return lax.rsqrt(jnp.mean(values * values, axis=-1, keepdims=True) + EPSILON)


def conv_core(extended, extended_ids, token_ids, weights):
    length = token_ids.shape[0]
    total = jnp.zeros((length, extended.shape[1]), jnp.float32)
    for offset in range(weights.shape[0]):
        same = (extended_ids[offset : offset + length] == token_ids)[:, None]
        total = total + jnp.where(
            same, weights[offset] * extended[offset : offset + length].astype(jnp.float32), 0.0
        )
    return jax.nn.silu(total).astype(jnp.bfloat16)


def block_local(x_blk, b_blk, c_blk, step_blk, rate_blk, ids_blk, before_id):
    length = ids_blk.shape[0]
    position = jnp.arange(length, dtype=jnp.int32)
    prefix = jnp.cumsum(rate_blk, axis=0)
    prefix_t = prefix.T
    same = (ids_blk[:, None] == ids_blk[None, :]) & (position[None, :] <= position[:, None])
    gaps = prefix_t[:, :, None] - prefix_t[:, None, :]
    decay = jnp.where(same[None], jnp.exp(jnp.where(same[None], gaps, 0.0)), 0.0)
    scores = jnp.dot(c_blk, b_blk.T, preferred_element_type=jnp.float32)
    mixing = (scores[None] * decay * step_blk.T[:, None, :]).astype(jnp.bfloat16)
    y_intra = jnp.einsum("hts,shp->thp", mixing, x_blk, preferred_element_type=jnp.float32)
    end_id = ids_blk[-1]
    alive = ids_blk == end_id
    weight_end = (
        jnp.where(
            alive[None, :],
            jnp.exp(jnp.where(alive[None, :], prefix_t[:, -1:] - prefix_t, 0.0)),
            0.0,
        )
        * step_blk.T
    )
    b_weighted = (weight_end[:, :, None] * b_blk[None]).astype(jnp.bfloat16)
    local_state = jnp.einsum("hsn,shp->hpn", b_weighted, x_blk, preferred_element_type=jnp.float32)
    carry_gain = jnp.where(end_id == before_id, jnp.exp(prefix_t[:, -1]), 0.0)
    return (y_intra, local_state, carry_gain, prefix)


def block_inter(c_blk, prefix, ids_blk, before_id, state_in):
    entering = ids_blk == before_id
    inter_scale = jnp.where(entering[:, None], jnp.exp(prefix), 0.0)
    return inter_scale[:, :, None] * jnp.einsum(
        "tn,hpn->thp", c_blk.astype(jnp.float32), state_in, precision=lax.Precision.HIGHEST
    )


def block_last(
    last_index, table, x_blk, b_blk, step_blk, prefix, ids_blk, before_id, state_in, start
):
    length = ids_blk.shape[0]
    position = jnp.arange(length, dtype=jnp.int32)
    prompt_ids = jnp.arange(last_index.shape[0], dtype=jnp.int32)
    local_last = last_index - start
    ends_here = (local_last >= 0) & (local_last < length)
    clipped = jnp.clip(local_last, 0, length - 1)

    def with_ends():
        prefix_t = prefix.T
        prefix_last = prefix[clipped]
        pick = (
            ends_here[:, None]
            & (ids_blk[None, :] == prompt_ids[:, None])
            & (position[None, :] <= clipped[:, None])
        )
        spans = prefix_last[:, :, None] - prefix_t[None]
        weight_last = (
            jnp.where(pick[:, None, :], jnp.exp(jnp.where(pick[:, None, :], spans, 0.0)), 0.0)
            * step_blk.T[None]
        )
        b_last = (weight_last[..., None] * b_blk[None, None]).astype(jnp.bfloat16)
        last_local = jnp.einsum("ghsn,shp->ghpn", b_last, x_blk, preferred_element_type=jnp.float32)
        last_gain = jnp.where(
            (ends_here & (prompt_ids == before_id))[:, None], jnp.exp(prefix_last), 0.0
        )
        return table + last_local + last_gain[:, :, None, None] * state_in[None]

    def without_ends():
        return table

    return lax.cond(jnp.any(ends_here), with_ends, without_ends)


def join_states(earlier, later):
    return (earlier[0] * later[0], later[0][:, None, None] * earlier[1] + later[1])


def on_device(
    hidden,
    token_prompt,
    request_prompt,
    in_gain,
    w_zx,
    w_bc,
    w_dt,
    dt_bias,
    a_log,
    conv_x,
    conv_bc,
    skip_gain,
    out_gain,
    w_out,
):
    tok_dev = hidden.shape[0]
    inner_dev = w_zx.shape[2]
    heads_dev = w_dt.shape[1]
    head_dim = inner_dev // heads_dev
    state_width = w_bc.shape[1] // 2
    taps = conv_x.shape[0]
    dp_index = lax.axis_index("dp")
    head_index = lax.axis_index("head")
    head_count = lax.axis_size("head")
    hidden_f = hidden.astype(jnp.float32)
    normed = (hidden_f * rms_scale(hidden_f) * in_gain).astype(jnp.bfloat16)
    pieces = (
        lax.all_gather(w_zx.astype(jnp.bfloat16), "dp", axis=0, tiled=True),
        lax.all_gather(w_dt.astype(jnp.bfloat16), "dp", axis=0, tiled=True),
        lax.all_gather(w_bc.astype(jnp.bfloat16), "dp", axis=0, tiled=True),
    )
    acc_zx, acc_step, acc_bc = tuple(
        (
            jnp.dot(normed, piece.reshape(piece.shape[0], -1), preferred_element_type=jnp.float32)
            for piece in pieces
        )
    )
    proj_bc = acc_bc.astype(jnp.bfloat16)
    proj_zx = acc_zx.astype(jnp.bfloat16)
    gate_z = proj_zx[:, :inner_dev]
    inner_x = proj_zx[:, inner_dev:]
    proj_dt = acc_step.astype(jnp.bfloat16)
    step_size = jax.nn.softplus(proj_dt.astype(jnp.float32) + dt_bias)
    rate = step_size * -jnp.exp(a_log)
    ids_own = lax.dynamic_slice_in_dim(token_prompt, dp_index * tok_dev, tok_dev)
    rim_start = jnp.maximum(dp_index * tok_dev - (taps - 1), 0)
    rim_ids = lax.dynamic_slice_in_dim(token_prompt, rim_start, taps - 1)
    tail_rows = jnp.concatenate(
        [inner_x[tok_dev - taps + 1 :], proj_bc[tok_dev - taps + 1 :]], axis=1
    )
    rim_rows = from_behind(tail_rows, "dp", 1)
    ext_ids = jnp.concatenate([rim_ids, ids_own])
    conv_inner = conv_core(
        jnp.concatenate([rim_rows[:, :inner_dev], inner_x], axis=0), ext_ids, ids_own, conv_x
    )
    conv_bc_out = conv_core(
        jnp.concatenate([rim_rows[:, inner_dev:], proj_bc], axis=0), ext_ids, ids_own, conv_bc
    )
    blocks = tok_dev // BLOCK
    x_heads = conv_inner.reshape(blocks, BLOCK, heads_dev, head_dim)
    b_conv = conv_bc_out[:, :state_width].reshape(blocks, BLOCK, state_width)
    c_conv = conv_bc_out[:, state_width:].reshape(blocks, BLOCK, state_width)
    step_blocks = step_size.reshape(blocks, BLOCK, heads_dev)
    rate_blocks = rate.reshape(blocks, BLOCK, heads_dev)
    id_blocks = ids_own.reshape(blocks, BLOCK)
    prev_last = jnp.where(dp_index > 0, token_prompt[jnp.maximum(dp_index * tok_dev - 1, 0)], -1)
    before_ids = jnp.concatenate([prev_last[None], id_blocks[:-1, -1]])
    y_intra, local_state, carry_gain, prefix = jax.vmap(block_local)(
        x_heads, b_conv, c_conv, step_blocks, rate_blocks, id_blocks, before_ids
    )

    def advance(carry, item):
        gain_acc, state_acc = carry
        gain, block_state = item
        return (
            (gain_acc * gain, gain[:, None, None] * state_acc + block_state),
            (gain_acc, state_acc),
        )

    unit_gain = jnp.ones((heads_dev,), jnp.float32)
    zero_state = jnp.zeros((heads_dev, head_dim, state_width), jnp.float32)
    (dev_gain, dev_state), (prior_gain, prior_state) = lax.scan(
        advance, (unit_gain, zero_state), (carry_gain, local_state)
    )
    scanned = carried_in((dev_gain, dev_state), "dp", join_states, (unit_gain, zero_state))
    incoming = scanned[1]
    block_in = prior_state + prior_gain[:, :, None, None] * incoming[None]
    prompt_ids = jnp.arange(PROMPTS, dtype=jnp.int32)
    last_index = (
        jnp.sum((token_prompt[None, :] <= prompt_ids[:, None]).astype(jnp.int32), axis=1) - 1
    )
    start_pos = (dp_index * blocks + jnp.arange(blocks, dtype=jnp.int32)) * BLOCK
    y_inter = jax.vmap(block_inter)(c_conv, prefix, id_blocks, before_ids, block_in)

    def collect(table, item):
        xb, bb, sb, pb, ib, fb, stb, ob = item
        return (block_last(last_index, table, xb, bb, sb, pb, ib, fb, stb, ob), None)

    empty_table = jnp.zeros((PROMPTS, heads_dev, head_dim, state_width), jnp.float32)
    local_table, unused = lax.scan(
        collect,
        empty_table,
        (x_heads, b_conv, step_blocks, prefix, id_blocks, before_ids, block_in, start_pos),
    )
    ssd_out = (y_intra + y_inter).reshape(tok_dev, heads_dev, head_dim) + skip_gain[
        None, :, None
    ] * conv_inner.astype(jnp.float32).reshape(tok_dev, heads_dev, head_dim)
    gated = ssd_out.reshape(tok_dev, inner_dev) * jax.nn.silu(gate_z.astype(jnp.float32))
    square_sum = lax.psum(jnp.sum(gated * gated, axis=1), "head")
    scale = lax.rsqrt(square_sum / (inner_dev * head_count) + EPSILON)
    normed_out = (gated * scale[:, None] * out_gain).astype(jnp.bfloat16)
    out_rows = tok_dev // head_count
    own_rows = lax.dynamic_slice_in_dim(hidden_f, head_index * out_rows, out_rows, 0)
    mixed = lax.psum_scatter(
        jnp.dot(normed_out, w_out, preferred_element_type=jnp.float32),
        "head",
        scatter_dimension=0,
        tiled=True,
    )
    layer_out = (own_rows + mixed).astype(jnp.bfloat16)
    table = lax.psum(local_table, "dp")
    one_hot = (request_prompt[:, None] == prompt_ids[None, :]).astype(jnp.float32)
    request_states = jnp.einsum("rg,ghpn->rhpn", one_hot, table, precision=lax.Precision.HIGHEST)
    return (layer_out, request_states)


def solution(mesh):
    in_specs = (
        P("dp", None),
        P(),
        P("dp"),
        P(),
        P("dp", None, "head"),
        P("dp", None),
        P("dp", "head"),
        P("head"),
        P("head"),
        P(None, "head"),
        P(),
        P("head"),
        P("head"),
        P("head", None),
    )
    out_specs = (P(("dp", "head"), None), P("dp", "head", None, None))
    return jax.shard_map(
        on_device, mesh=mesh, in_specs=in_specs, out_specs=out_specs, check_vma=False
    )
```

profile of v0, /device:TPU:0, one launch (start us, length us, event | category | flops | bytes accessed | tf_op | source)
XLA Modules:
  0.0 247.6 jit_solution(8383490786278509442)
XLA Ops:
  7.3 2.6 %convert_element_type.107 = bf16[384,2,384]{2,1,0:T(2,128)(2,1)} convert(f32[384,2,384]{2,1,0:T(2,128)} %param.26) | non-fusion elementwise | flops 294912 | bytes 1769472 | tf_op jit(solution)/shard_map/convert_element_type | solution.py:154
  10.5 6.2 %all_gather.23 = bf16[1536,6]{0,1:T(8,128)(2,1)S(1)} all-gather(bf16[384,6]{0,1:T(8,128)(2,1)S(1)} %convert_element_type.121), channel_id=1, replica_groups=mesh['dp'=4,'head'=8] {'dp'}, dimensions={0}, use_global_device_ids=true | all-gather | bytes 23040 | tf_op jit(solution)/shard_map/all_gather | solution.py:155
  17.4 3.6 %reduce-window.6 = f32[2,6,2,128]{3,2,1,0:T(2,128)S(1)} reduce-window(f32[2,6,2,128]{3,2,1,0:T(2,128)S(1)} %copy.88, f32[]{:T(128)} %constant.142.clone.1), window={size=1x1x1x128 pad=0_0x0_0x0_0x127_0}, to_apply=%region_1.2 | reduce-window | flops 390144 | bytes 24580 | tf_op jit(solution)/shard_map/reduce-window
  21.5 13.6 %all_gather.22 = bf16[1536,256]{1,0:T(8,128)(2,1)S(1)} all-gather(bf16[384,256]{1,0:T(8,128)(2,1)S(1)} %convert_element_type.109), channel_id=1, replica_groups=mesh['dp'=4,'head'=8] {'dp'}, dimensions={0}, use_global_device_ids=true | all-gather | bytes 983040 | tf_op jit(solution)/shard_map/all_gather | solution.py:156
  44.9 2.2 copy.111
  47.1 1.5 convolution_convert_fusion
  48.7 2.2 collective-permute-start
  52.1 1.3 copy.94
  53.4 1.3 copy.99
  54.7 1.3 copy.96
  58.3 1.2 dynamic-slice
  60.3 1.9 multiply_convert_fusion.13
  62.9 1.6 convert_element_type.125
  67.9 1.8 fusion.27
  69.7 1.7 while.48
  71.7 7.1 %all-reduce = f32[24]{0:T(128)S(1)} all-reduce(f32[24]{0:T(128)S(1)} %dynamic-update-slice), channel_id=2, replica_groups=mesh['dp'=4,'head'=8] {'dp'}, use_global_device_ids=true, to_apply=%add | all-reduce | flops 24 | bytes 192
  78.8 8.9 %all-gather.1 = f32[24,64,128]{2,1,0:T(8,128)S(1)} all-gather(f32[6,64,128]{2,1,0:T(8,128)S(1)} %get-tuple-element.342), channel_id=3, replica_groups=mesh['dp'=4,'head'=8] {'dp'}, dimensions={0}, use_global_device_ids=true | all-gather | bytes 983040 | tf_op jit(solution)/shard_map/all_gather | solution.py:21
  89.4 2.1 fusion.19
  94.1 13.3 %while.47 = (s32[]{:T(128)}, f32[8,6,64,128]{3,2,0,1:T(8,128)S(1)}, s32[2]{0:T(128)S(1)}, s32[8]{0:T(128)S(1)}, s32[2,256]{1,0:T(2,128)S(1)}, /*index=5*/f32[2,2...) while((s32[]{:T(128)}, f32[8,6,64,128]{3,2,0,1:T(8,128)S(1)}, ...), condition=%wide.region_15.16_spmd.clone, body=%wide.region_11.15_spmd.sunk.clone | while | flops 205743264 | bytes 4429979 | solution.py:226
  96.7 8.0 %conditional.3 = (f32[8,6,64,128]{3,2,0,1:T(8,128)S(1)}) conditional(s32[]{:T(128)} %convert_element_type.201, f32[8,6,64,128]{3,2,0,1:T(8,128)S(1)} %get-tuple-element.774, (pred[8]{0:T(512)(128)(4,1)S(1)}, s32[2,256]{1,0:T(2,128)S(1)}, s32[]{:T(128)}, s32[8]{0:T(128)S(1)}, s32[256]{0:T(256)S(1)}, /*index=5*/s32[8]{0:T(128)S(1)}, ...), branch_computations={%region_13.13_spmd, %region_14.14_spmd} | conditional | flops 205743200 | bytes 4428524 | solution.py:119
  96.8 1.5 bitcast_convert_fusion
  101.6 3.2 %fusion.3 = f32[8,6,64,128]{3,2,0,1:T(8,128)S(1)} fusion(f32[8,6,64,128]{3,2,0,1:T(8,128)S(1)} %get-tuple-element.304, f32[256,128]{1,0:T(8,128)} %bitcast_convert_fusion, f32[8,6,256]{2,0,1:T(8,128)S(1)} %select_multiply_fusion, f32[6,64,128]{2,1,0:T(8,128)S(1)} %dynamic-slice_bitcast_fusion, f32[8,6]{0,1:T(8,128)S(1)} %copy.86, ...), kind=kOutput, calls=%fused_computation.6 | convolution fusion | flops 205651968 | bytes 3719872 | tf_op jit(solution)/shard_map/while/body/eval_jaxpr/cond/branch_1_fun/ghsn,shp->ghpn/dot_general | solution.py:110
  107.5 2.2 copy.106
  110.9 1.4 multiply_reduce_fusion.1
  112.3 21.7 %psum.14 = f32[512]{0:T(512)S(1)} all-reduce(f32[512]{0:T(512)S(1)} %get-tuple-element.495), channel_id=1, replica_groups=mesh['dp'=4,'head'=8] {'head'}, use_global_device_ids=true, to_apply=%region_8.9 | all-reduce | flops 512 | bytes 4096 | tf_op jit(solution)/shard_map/psum | solution.py:235
  134.0 2.7 %fusion.32 = f32[512,1536]{1,0:T(8,128)} fusion(bf16[384,1536]{1,0:T(8,128)(2,1)S(1)} %copy-done, f32[512,384]{1,0:T(8,128)S(1)} %get-tuple-element.496, f32[384]{0:T(512)S(1)} %copy-done.20, f32[512]{0:T(512)S(1)} %add_rsqrt_fusion), kind=kOutput, calls=%fused_computation.73 | convolution fusion | flops 604569600 | bytes 5115392 | tf_op jit(solution)/shard_map/dot_general | solution.py:241
  136.7 1.4 copy-done.2
  138.1 2.1 convert_element_type.105
  140.2 20.9 %all-reduce.3.cloned.1.call-done = f32[8,6,64,128]{3,0,2,1:T(8,128)} async-done(((f32[8,6,64,128]{3,0,2,1:T(8,128)}), f32[8,6,64,128]{3,0,2,1:T(8,128)}) %all-reduce.3.cloned.1.call-update) | async-done | bytes 1572880 | tf_op jit(solution)/shard_map/psum | solution.py:247
  161.0 2.3 fusion.38
  164.3 75.0 %reduce-scatter.2.cloned.1.call-done = f32[64,1536]{1,0:T(8,128)} async-done(((f32[512,1536]{1,0:T(8,128)}), f32[64,1536]{1,0:T(8,128)}) %reduce-scatter.2.cloned.1.call-update) | async-done | bytes 393232 | tf_op jit(solution)/shard_map/reduce_scatter | solution.py:240
  239.3 1.8 add_convert_fusion
  (212 shorter events, 34.3 us)
Async XLA Ops:
  7.2 126.8 %copy-start = (bf16[384,1536]{1,0:T(8,128)(2,1)S(1)}, bf16[384,1536]{1,0:T(8,128)(2,1)}, u32[]{:S(2)}) copy-start(bf16[384,1536]{1,0:T(8,128)(2,1)} %param.35) | copy-start | bytes 3538948
  7.2 2.8 %copy-start.1 = (bf16[512,1536]{1,0:T(8,128)(2,1)S(1)}, bf16[512,1536]{1,0:T(8,128)(2,1)}, u32[]{:S(2)}) copy-start(bf16[512,1536]{1,0:T(8,128)(2,1)} %param.22) | copy-start | bytes 4718596
  7.2 3.2 %copy-start.40 = (f32[6]{0:T(128)S(1)}, f32[6]{0:T(128)}, u32[]{:S(2)}) copy-start(f32[6]{0:T(128)} %param.30) | copy-start | bytes 76
  7.2 3.2 %copy-start.19 = (f32[384,6]{0,1:T(8,128)S(1)}, f32[384,6]{0,1:T(8,128)}, u32[]{:S(2)}) copy-start(f32[384,6]{0,1:T(8,128)} %param.28) | copy-start | bytes 27652
  7.2 9.4 %copy-start.38 = (f32[1536]{0:T(1024)S(1)}, f32[1536]{0:T(1024)}, u32[]{:S(2)}) copy-start(f32[1536]{0:T(1024)} %param.25) | copy-start | bytes 18436
  7.2 9.4 %copy-start.41 = (f32[6]{0:T(128)S(1)}, f32[6]{0:T(128)}, u32[]{:S(2)}) copy-start(f32[6]{0:T(128)} %param.29) | copy-start | bytes 76
  7.2 37.7 %all-gather.4.cloned.1.call-start = ((), (), s32[]{:S(2)}) async-start(), calls=%async_computation.1 | async-start | bytes 2949120 | tf_op jit(solution)/shard_map/all_gather | solution.py:154
  9.9 151.1 %all-reduce.3.cloned.1.call-start = ((), (), s32[]{:S(2)}) async-start(), calls=%async_computation.3 | async-start | bytes 3145728 | tf_op jit(solution)/shard_map/psum | solution.py:247
  10.4 24.7 %copy-start.34 = (f32[512]{0:T(512)}, f32[512]{0:T(512)S(1)}, u32[]{:S(2)}) copy-start(f32[512]{0:T(512)S(1)} %add_rsqrt_fusion.1) | copy-start | bytes 6148
  16.7 4.8 %copy-start.7 = (f32[384,256]{1,0:T(8,128)S(1)}, f32[384,256]{1,0:T(8,128)}, u32[]{:S(2)}) copy-start(f32[384,256]{1,0:T(8,128)} %param.27) | copy-start | bytes 1179652
  17.3 18.4 %copy-start.9 = (f32[512,6]{0,1:T(8,128)}, f32[512,6]{0,1:T(8,128)S(1)}, u32[]{:S(2)}) copy-start(f32[512,6]{0,1:T(8,128)S(1)} %get-tuple-element.514) | copy-start | bytes 36868
  17.3 26.1 %copy-start.12 = (f32[2,256,6]{1,0,2:T(2,128)}, f32[2,256,6]{1,0,2:T(2,128)S(1)}, u32[]{:S(2)}) copy-start(f32[2,256,6]{1,0,2:T(2,128)S(1)} %reshape.252) | copy-start | bytes 36868
  35.1 4.0 %copy-start.27 = (f32[4,384]{1,0:T(4,128)S(1)}, f32[4,384]{1,0:T(4,128)}, u32[]{:S(2)}) copy-start(f32[4,384]{1,0:T(4,128)} %param.31) | copy-start | bytes 18436
  35.1 7.2 %copy-start.31 = (f32[4,256]{1,0:T(4,128)S(1)}, f32[4,256]{1,0:T(4,128)}, u32[]{:S(2)}) copy-start(f32[4,256]{1,0:T(4,128)} %param.32) | copy-start | bytes 12292
  35.7 11.4 %copy-start.8 = (bf16[512,256]{1,0:T(8,128)(2,1)}, bf16[512,256]{1,0:T(8,128)(2,1)S(1)}, u32[]{:S(2)}) copy-start(bf16[512,256]{1,0:T(8,128)(2,1)S(1)} %convolution_convert_fusion.1) | copy-start | bytes 786436
  40.9 6.2 %copy-start.32 = (s32[2]{0:T(128)}, s32[2]{0:T(128)S(1)}, u32[]{:S(2)}) copy-start(s32[2]{0:T(128)S(1)} %get-tuple-element.771) | copy-start | bytes 28
  48.6 11.7 %copy-start.6 = (bf16[512,768]{1,0:T(8,128)(2,1)}, bf16[512,768]{1,0:T(8,128)(2,1)S(1)}, u32[]{:S(2)}) copy-start(bf16[512,768]{1,0:T(8,128)(2,1)S(1)} %convolution_convert_fusion) | copy-start | bytes 2359300
  48.7 11.6 %collective-permute-start = (bf16[3,640]{1,0:T(4,128)(2,1)S(1)}, bf16[3,640]{1,0:T(4,128)(2,1)S(1)}, u32[]{:S(2)}, u32[]{:S(2)}) collective-permute-start(bf16[3,640]{1,0:T(4,128)(2,1)S(1)} %pad_maximum_fusion.2), channel_id=1, source_target_pairs={{0,8},{8,16},{16,24},{1,9},{9,17},{17,25},{2,10},{10,18},{18,26},{... | collective-permute-start | bytes 11528 | tf_op jit(solution)/shard_map/ppermute | solution.py:16
  58.3 7.4 %copy-start.22 = (f32[384]{0:T(512)S(1)}, f32[384]{0:T(512)}, u32[]{:S(2)}) copy-start(f32[384]{0:T(512)} %get-tuple-element.439) | copy-start | bytes 4612
  58.3 7.4 %copy-start.23 = (f32[384]{0:T(512)S(1)}, f32[384]{0:T(512)}, u32[]{:S(2)}) copy-start(f32[384]{0:T(512)} %get-tuple-element.440) | copy-start | bytes 4612
  58.3 7.4 %copy-start.24 = (f32[384]{0:T(512)S(1)}, f32[384]{0:T(512)}, u32[]{:S(2)}) copy-start(f32[384]{0:T(512)} %get-tuple-element.441) | copy-start | bytes 4612
  58.3 7.4 %copy-start.25 = (f32[384]{0:T(512)S(1)}, f32[384]{0:T(512)}, u32[]{:S(2)}) copy-start(f32[384]{0:T(512)} %get-tuple-element.442) | copy-start | bytes 4612
  58.3 7.4 %copy-start.28 = (pred[512]{0:T(512)(128)(4,1)S(1)}, pred[512]{0:T(512)(128)(4,1)}, u32[]{:S(2)}) copy-start(pred[512]{0:T(512)(128)(4,1)} %get-tuple-element.504) | copy-start | bytes 1540
  58.3 7.4 %copy-start.29 = (pred[512]{0:T(512)(128)(4,1)S(1)}, pred[512]{0:T(512)(128)(4,1)}, u32[]{:S(2)}) copy-start(pred[512]{0:T(512)(128)(4,1)} %get-tuple-element.505) | copy-start | bytes 1540
  58.3 7.4 %copy-start.30 = (pred[512]{0:T(512)(128)(4,1)S(1)}, pred[512]{0:T(512)(128)(4,1)}, u32[]{:S(2)}) copy-start(pred[512]{0:T(512)(128)(4,1)} %get-tuple-element.506) | copy-start | bytes 1540
  66.7 2.9 %copy-start.3 = (bf16[512,384]{1,0:T(8,128)(2,1)}, bf16[512,384]{1,0:T(8,128)(2,1)S(1)}, u32[]{:S(2)}) copy-start(bf16[512,384]{1,0:T(8,128)(2,1)S(1)} %multiply_convert_fusion.12) | copy-start | bytes 1179652
  66.7 2.9 %copy-start.16 = (f32[6]{0:T(128)S(1)}, f32[6]{0:T(128)}, u32[]{:S(2)}) copy-start(f32[6]{0:T(128)} %custom-call) | copy-start | bytes 76
  66.7 2.9 %copy-start.18 = (f32[2,6]{1,0:T(2,128)S(1)}, f32[2,6]{1,0:T(2,128)}, u32[]{:S(2)}) copy-start(f32[2,6]{1,0:T(2,128)} %exponential_select_fusion.2) | copy-start | bytes 148
  66.8 2.9 %copy-start.36 = (f32[2,6]{1,0:T(2,128)S(1)}, f32[2,6]{1,0:T(2,128)}, u32[]{:S(2)}) copy-start(f32[2,6]{1,0:T(2,128)} %custom-call.6) | copy-start | bytes 148
  109.7 24.3 %copy-start.20 = (f32[384]{0:T(512)S(1)}, f32[384]{0:T(512)}, u32[]{:S(2)}) copy-start(f32[384]{0:T(512)} %param.34) | copy-start | bytes 4612
  109.7 129.6 %reduce-scatter.2.cloned.1.call-start = ((), (), s32[]{:S(2)}) async-start(), calls=%async_computation.2 | async-start | bytes 3538944 | tf_op jit(solution)/shard_map/reduce_scatter | solution.py:240
  138.1 22.9 %copy-start.37 = (s32[4]{0:T(128)S(1)}, s32[4]{0:T(128)}, u32[]{:S(2)}) copy-start(s32[4]{0:T(128)} %param.24) | copy-start | bytes 52
  (15 other events, 23.5 us)
Sparse Core Ops, SparseCore 0:
  10.2 30.9 all-gather.3
  109.8 51.2 all-reduce.2
  164.6 74.5 reduce-scatter.1
where the time goes:
time: 248 us
  waiting for transfers between devices  95.9 us (39%)
  blocking collectives  57.4 us (23%)
  other arithmetic  30.1 us (12%)
  local copies, waits for them, and re-layouts  28 us (11%)
  matrix products  16.4 us (7%)
  between operations  15.8 us (6%)
    reduce_scatter x1, waiting for transfers between devices, on_device(): lax.psum_scatter(jnp.dot(normed_out, w_out, preferred_element_type=jnp.fl...  75 us
    psum x1, blocking collectives, on_device(): square_sum = lax.psum(jnp.sum(gated * gated, axis=1), 'head')  21.7 us
    psum x1, waiting for transfers between devices, on_device(): table = lax.psum(local_table, 'dp')  20.9 us
    all_gather x1, blocking collectives, on_device(): lax.all_gather(w_bc.astype(jnp.bfloat16), 'dp', axis=0, tiled=True)  13.6 us
    all_gather x1, blocking collectives, carried_in(): everything = jax.tree.map(lambda part: lax.all_gather(part, axis), shard)  8.9 us
    unnamed x92, local copies, waits for them, and re-layouts  7.42 us
    unnamed x1, blocking collectives  7.07 us
    all_gather x1, blocking collectives, on_device(): lax.all_gather(w_dt.astype(jnp.bfloat16), 'dp', axis=0, tiled=True)  6.19 us
  transfers between devices with their start and end apart: 4, of which 2 were waited for; matrix products, arithmetic and copies ran while one was open for 13% of the time, Pallas kernels for 0%

commit v1 on v0

--- a/solution.py
+++ b/solution.py
@@ -1,6 +1,10 @@
+import functools
+
 import jax
 import jax.numpy as jnp
 from jax import lax
+from jax.experimental import pallas as pl
+from jax.experimental.pallas import tpu as pltpu
 from jax.sharding import PartitionSpec as P
 
 BLOCK = 256
@@ -250,6 +254,594 @@
     return (layer_out, request_states)
 
 
+LANES = 128
+TILE_ROWS = 16
+NEVER = -1e30
+MESH_KERNEL_BYTES = 48 * 1024 * 1024
+
+
+def kernel_params():
+    return pltpu.CompilerParams(vmem_limit_bytes=MESH_KERNEL_BYTES)
+
+
+def in_vmem(count):
+    return [pl.BlockSpec(memory_space=pltpu.VMEM)] * count
+
+
+def exchange(values, axis, bits):
+    return lax.ppermute(values, axis, [(i, i ^ bits) for i in range(lax.axis_size(axis))])
+
+
+def dot32(a, b, a_dim=1, b_dim=0):
+    return lax.dot_general(
+        a, b, (((a_dim,), (b_dim,)), ((), ())), preferred_element_type=jnp.float32
+    )
+
+
+def silu_tanh(values):
+    half = 0.5 * values
+    return half + half * jnp.tanh(half)
+
+
+def widen(columns, pair, head_dim):
+    rows = columns.shape[0]
+    lane = lax.broadcasted_iota(jnp.int32, (rows, LANES), 1)
+    first = jnp.broadcast_to(columns[:, 2 * pair : 2 * pair + 1], (rows, LANES))
+    second = jnp.broadcast_to(columns[:, 2 * pair + 1 : 2 * pair + 2], (rows, LANES))
+    return jnp.where(lane < head_dim, first, second)
+
+
+def pack_kernel(req_ref, wzx_ref, wbc_ref, wdt_ref, tail_ref, front_ref, gate_ref, pad_ref):
+    rows, bc_width = wbc_ref.shape
+    inner = gate_ref.shape[1]
+    tiles = inner // LANES
+    for j in range(tiles):
+        own = slice(j * LANES, (j + 1) * LANES)
+        front_ref[0:rows, own] = wzx_ref[pl.ds(2 * j + 1, rows, stride=2 * tiles), :].astype(
+            jnp.bfloat16
+        )
+        gate_ref[:, own] = wzx_ref[pl.ds(2 * j, rows, stride=2 * tiles), :].astype(jnp.bfloat16)
+    front_ref[0:rows, inner:] = wbc_ref[...].astype(jnp.bfloat16)
+    front_ref[rows:, :] = jnp.zeros((front_ref.shape[0] - rows, inner + bc_width), jnp.bfloat16)
+    pad_ref[...] = jnp.zeros_like(pad_ref)
+    pad_ref[0 : wdt_ref.shape[0], 0:rows] = wdt_ref[...]
+    lane = lax.broadcasted_iota(jnp.int32, (TILE_ROWS, LANES), 1)
+    wanted = jnp.zeros((TILE_ROWS, LANES), jnp.float32)
+    for r in range(req_ref.shape[0]):
+        wanted = jnp.where(lane == r, req_ref[r].astype(jnp.float32), wanted)
+    pad_ref[:, rows : rows + LANES] = wanted
+    front_ref[rows : rows + TILE_ROWS, 0 : rows + LANES] = pad_ref[...].astype(jnp.bfloat16)
+    piece = rows + LANES
+    for i in range(tail_ref.shape[1] // piece):
+        at = rows + TILE_ROWS * (i + 1)
+        front_ref[at : at + TILE_ROWS, 0:piece] = tail_ref[:, i * piece : (i + 1) * piece]
+
+
+def front_kernel(
+    place_ref,
+    normed_ref,
+    own_ref,
+    near_ref,
+    far_ref,
+    last_ref,
+    gain_ref,
+    taps_x_ref,
+    taps_bc_ref,
+    meta_ref,
+    order_ref,
+    head_ref,
+    conv_ref,
+    stepx_ref,
+    faded_ref,
+    prefix_ref,
+    leaving_ref,
+    middle_ref,
+    w_ref,
+    extra_ref,
+    dtw_ref,
+    ext_ref,
+    sems,
+):
+    position = place_ref[0]
+    model = normed_ref.shape[1]
+    tok = normed_ref.shape[0]
+    rows = model // extra_ref.shape[0]
+    inner = taps_x_ref.shape[1]
+    width = conv_ref.shape[1]
+    state_width = (width - inner) // 2
+    head_dim = LANES // 2
+    pairs = inner // LANES
+    copies = []
+    for j, buffer in enumerate((own_ref, near_ref, far_ref, last_ref)):
+        source = jnp.bitwise_xor(position, j)
+        at = pl.multiple_of(source * rows, rows)
+        copies.append(
+            pltpu.make_async_copy(buffer.at[0:rows], w_ref.at[pl.ds(at, rows)], sems.at[2 * j])
+        )
+        copies.append(
+            pltpu.make_async_copy(
+                buffer.at[rows : rows + extra_ref.shape[1]],
+                extra_ref.at[source],
+                sems.at[2 * j + 1],
+            )
+        )
+    for copy in copies:
+        copy.start()
+    dtw_ref[...] = jnp.zeros_like(dtw_ref)
+    for copy in copies:
+        copy.wait()
+    for s in range(extra_ref.shape[0]):
+        dtw_ref[0:TILE_ROWS, s * rows : (s + 1) * rows] = extra_ref[s, 0:TILE_ROWS, 0:rows]
+    behind = jnp.maximum(position - 1, 0)
+    piece = rows + LANES
+    halo = jnp.concatenate(
+        [
+            extra_ref[behind, TILE_ROWS * (i + 1) : TILE_ROWS * (i + 2), 0:piece]
+            for i in range(model // piece)
+        ],
+        axis=1,
+    ).astype(jnp.float32)
+    halo = halo * rms_scale(halo) * gain_ref[...]
+    ext_ref[0:TILE_ROWS, :] = dot32(halo.astype(jnp.bfloat16), w_ref[...])
+    normed = normed_ref[...]
+    for at in range(0, width, 2 * LANES):
+        stop = min(at + 2 * LANES, width)
+        ext_ref[TILE_ROWS:, at:stop] = dot32(normed, w_ref[:, at:stop])
+    raw = dot32(normed, dtw_ref[...], 1, 1) + head_ref[0:1, :]
+    step = jnp.maximum(raw, 0.0) + jnp.log1p(jnp.exp(-jnp.abs(raw)))
+    lane = lax.broadcasted_iota(jnp.int32, (tok, LANES), 1)
+    rate = jnp.where(lane < TILE_ROWS, -step * jnp.exp(head_ref[1:2, :]), 0.0)
+    high = rate.astype(jnp.bfloat16).astype(jnp.float32)
+    rest = rate - high
+    mid = rest.astype(jnp.bfloat16).astype(jnp.float32)
+    low = rest - mid
+    packed = high + pltpu.roll(mid, TILE_ROWS, 1) + pltpu.roll(low, 2 * TILE_ROWS, 1)
+    sums = dot32(order_ref[...], packed.astype(jnp.bfloat16))
+    sums = (
+        sums
+        + pltpu.roll(sums, LANES - TILE_ROWS, 1)
+        + pltpu.roll(sums, LANES - 2 * TILE_ROWS, 1)
+    )
+    prefix = sums[0:tok]
+    fade = jnp.exp(sums[tok : 2 * tok])
+    prefix_ref[...] = prefix
+    fade_middle = jnp.exp(prefix[BLOCK - 1 : BLOCK, :] - prefix[0:BLOCK])
+    same = [
+        jnp.broadcast_to(meta_ref[:, k : k + 1], (tok, LANES)) for k in range(3)
+    ]
+    for j in range(width // LANES):
+        own = slice(j * LANES, (j + 1) * LANES)
+        if j < pairs:
+            taps = taps_x_ref[:, own]
+        else:
+            taps = taps_bc_ref[:, j * LANES - inner : (j + 1) * LANES - inner]
+        total = ext_ref[TILE_ROWS : TILE_ROWS + tok, own] * taps[3:4]
+        for k in range(1, 4):
+            total = total + same[k - 1] * (
+                ext_ref[TILE_ROWS - k : TILE_ROWS - k + tok, own] * taps[3 - k : 4 - k]
+            )
+        conv_ref[:, own] = silu_tanh(total).astype(jnp.bfloat16)
+    b_all = conv_ref[:, inner : inner + state_width].astype(jnp.float32)
+    b_leaving = (b_all * meta_ref[:, 7:8]).astype(jnp.bfloat16)
+    b_middle = (b_all * meta_ref[:, 5:6])[0:BLOCK].astype(jnp.bfloat16)
+    for q in range(pairs):
+        own = slice(q * LANES, (q + 1) * LANES)
+        scaled = conv_ref[:, own].astype(jnp.float32) * widen(step, q, head_dim)
+        stepx_ref[:, own] = scaled.astype(jnp.bfloat16)
+        faded = (scaled * widen(fade, q, head_dim)).astype(jnp.bfloat16).T
+        faded_ref[own, :] = faded
+        leaving_ref[own, :] = dot32(faded, b_leaving).astype(jnp.bfloat16)
+        to_middle = (scaled[0:BLOCK] * widen(fade_middle, q, head_dim)).astype(jnp.bfloat16).T
+        middle_ref[own, :] = dot32(to_middle, b_middle).astype(jnp.bfloat16)
+
+
+def local_kernel(
+    place_ref,
+    normed_ref,
+    own_ref,
+    near_ref,
+    far_ref,
+    last_ref,
+    conv_ref,
+    stepx_ref,
+    faded_ref,
+    prefix_ref,
+    middle_ref,
+    meta_ref,
+    pen_ref,
+    skip_ref,
+    y_ref,
+    gate_ref,
+    table_ref,
+    w_ref,
+    sems,
+):
+    position = place_ref[0]
+    inner = y_ref.shape[1]
+    rows = own_ref.shape[0]
+    state_width = middle_ref.shape[1]
+    head_dim = LANES // 2
+    tok = y_ref.shape[0]
+    copies = []
+    for j, buffer in enumerate((own_ref, near_ref, far_ref, last_ref)):
+        at = pl.multiple_of(jnp.bitwise_xor(position, j) * rows, rows)
+        copies.append(pltpu.make_async_copy(buffer, w_ref.at[pl.ds(at, rows)], sems.at[j]))
+    for copy in copies:
+        copy.start()
+    lane = lax.broadcasted_iota(jnp.int32, (BLOCK, LANES), 1)
+    for b in range(tok // BLOCK):
+        own_rows = slice(b * BLOCK, (b + 1) * BLOCK)
+        b_blk = conv_ref[own_rows, inner : inner + state_width]
+        c_blk = conv_ref[own_rows, inner + state_width :]
+        scores = dot32(c_blk, b_blk, 1, 1)
+        pen = pen_ref[b]
+        prefix = prefix_ref[own_rows, :]
+        across = prefix.T
+        if b > 0:
+            carried = jnp.exp(prefix - prefix_ref[b * BLOCK - 1 : b * BLOCK, :])
+            carried = carried * meta_ref[own_rows, 4:5]
+            from_middle = dot32(c_blk, middle_ref[...], 1, 1)
+        for q in range(inner // LANES):
+            own = slice(q * LANES, (q + 1) * LANES)
+            x_pair = conv_ref[own_rows, own].astype(jnp.float32)
+            out = x_pair * skip_ref[:, own]
+            if b > 0:
+                out = out + widen(carried, q, head_dim) * from_middle[:, own]
+            sx = stepx_ref[own_rows, own].astype(jnp.float32)
+            for side in range(2):
+                h = 2 * q + side
+                gaps = prefix[:, h : h + 1] - across[h : h + 1, :] + pen
+                mixing = (scores * jnp.exp(gaps)).astype(jnp.bfloat16)
+                kept = (lane < head_dim) if side == 0 else (lane >= head_dim)
+                out = out + dot32(mixing, jnp.where(kept, sx, 0.0).astype(jnp.bfloat16))
+            y_ref[own_rows, own] = out
+    b_all = conv_ref[:, inner : inner + state_width].astype(jnp.float32)
+    faded = faded_ref[...]
+    for g in range(table_ref.shape[0]):
+        ended = jnp.where(meta_ref[:, 6:7] == g, meta_ref[:, 8:9], 0.0)
+        table_ref[g] = dot32(faded, (b_all * ended).astype(jnp.bfloat16)).astype(jnp.bfloat16)
+    for copy in copies:
+        copy.wait()
+    normed = normed_ref[...]
+    gate_ref[...] = silu_tanh(dot32(normed, w_ref[...]))
+
+
+def gate_kernel(place_ref, enter_ref, conv_ref, prefix_ref, meta_ref, y_ref, z_ref, *outs):
+    scratch = outs[-1]
+    outs = outs[:-1]
+    inner = y_ref.shape[1]
+    state_width = enter_ref.shape[1]
+    head_dim = LANES // 2
+    c_all = conv_ref[:, inner + state_width :]
+    inter = dot32(c_all, enter_ref[...], 1, 1)
+    carried = jnp.exp(prefix_ref[...]) * meta_ref[:, 3:4]
+    for q in range(inner // LANES):
+        own = slice(q * LANES, (q + 1) * LANES)
+        value = y_ref[:, own] + widen(carried, q, head_dim) * inter[:, own]
+        scratch[:, own] = (value * z_ref[:, own]).astype(jnp.bfloat16)
+    members = len(outs)
+    part = y_ref.shape[0] // (2 * members)
+    half = place_ref[5]
+    for j, out in enumerate(outs):
+        member = jnp.bitwise_xor(place_ref[4], j)
+        for k, side in enumerate((1 - half, half)):
+            at = pl.multiple_of((side * members + member) * part, part)
+            out[k * part : (k + 1) * part, :] = scratch[pl.ds(at, part), :]
+
+
+def ends_kernel(place_ref, table_ref, enter_ref, prefix_ref, out_ref):
+    out_ref[...] = table_ref[...]
+    head_dim = LANES // 2
+
+    @pl.when(place_ref[2] == 1)
+    def add():
+        prompt = place_ref[1]
+        gain = jnp.exp(prefix_ref[pl.ds(place_ref[3], 1), :])
+        for h in range(out_ref.shape[1] // head_dim):
+            own = slice(h * head_dim, (h + 1) * head_dim)
+            term = gain[:, h : h + 1] * enter_ref[own, :].astype(jnp.float32)
+            old = table_ref[prompt, own, :].astype(jnp.float32)
+            out_ref[prompt, own, :] = (old + term).astype(jnp.bfloat16)
+
+
+def pick_kernel(wanted_ref, table_ref, other_ref, keep_ref, send_ref):
+    count = keep_ref.shape[0]
+    for k, out in enumerate((keep_ref, send_ref)):
+        for r in range(count):
+            g = wanted_ref[k * count + r]
+            total = table_ref[g].astype(jnp.float32) + other_ref[g].astype(jnp.float32)
+            out[r] = total.astype(jnp.bfloat16)
+
+
+def out_kernel(place_ref, *refs):
+    members = 4
+    gated, own_w = refs[:members], refs[members]
+    near, swapped = refs[members + 1 : 2 * members], refs[2 * members : 3 * members - 1]
+    send_ref, keep_ref = refs[3 * members - 1 :]
+    core = place_ref[6]
+    half = near[0].shape[1]
+    part = send_ref.shape[0]
+    values = [g[...] for g in gated]
+    for others, side in ((near, core), (swapped, 1 - core)):
+        at = pl.multiple_of(side * half, half)
+        total = dot32(values[0], own_w[:, pl.ds(at, half)])
+        for value, weights in zip(values[1:], others):
+            total = total + dot32(value, weights[...])
+        send_ref[:, pl.ds(at, half)] = total[0:part].astype(jnp.bfloat16)
+        keep_ref[:, pl.ds(at, half)] = total[part:]
+    squares = jnp.zeros((2 * part, 1), jnp.float32)
+    for value in values:
+        wide = value.astype(jnp.float32)
+        squares = squares + jnp.sum(wide * wide, axis=1, keepdims=True)
+    model = 2 * half
+    lane = lax.broadcasted_iota(jnp.int32, (part, LANES), 1)
+    high = squares[0:part].astype(jnp.bfloat16).astype(jnp.float32)
+    low = squares[0:part] - high
+    send_ref[:, model:] = jnp.where(lane == 0, high, low).astype(jnp.bfloat16)
+    keep_ref[:, model:] = jnp.broadcast_to(squares[part:], (part, LANES))
+
+
+def finish_kernel(inner_total, hidden_ref, keep_ref, got_ref, out_ref):
+    model = hidden_ref.shape[1]
+    squares = keep_ref[:, model : model + 1]
+    squares = squares + got_ref[:, model : model + 1].astype(jnp.float32)
+    squares = squares + got_ref[:, model + 1 : model + 2].astype(jnp.float32)
+    scale = lax.rsqrt(squares / inner_total + EPSILON)
+    total = keep_ref[:, 0:model] + got_ref[:, 0:model].astype(jnp.float32)
+    out_ref[...] = (hidden_ref[...].astype(jnp.float32) + scale * total).astype(jnp.bfloat16)
+
+
+def fused_on_device(
+    hidden,
+    token_prompt,
+    request_prompt,
+    in_gain,
+    w_zx,
+    w_bc,
+    w_dt,
+    dt_bias,
+    a_log,
+    conv_x,
+    conv_bc,
+    skip_gain,
+    out_gain,
+    w_out,
+):
+    tok, model = hidden.shape
+    rows = w_zx.shape[0]
+    inner = w_zx.shape[2]
+    heads = w_dt.shape[1]
+    state_width = w_bc.shape[1] // 2
+    width = inner + 2 * state_width
+    peers = lax.axis_size("dp")
+    head_count = lax.axis_size("head")
+    position = lax.axis_index("dp")
+    head_index = lax.axis_index("head")
+    bf16, f32 = jnp.bfloat16, jnp.float32
+    shape = jax.ShapeDtypeStruct
+    smem = pl.BlockSpec(memory_space=pltpu.SMEM)
+    anywhere = pl.BlockSpec(memory_space=pl.ANY)
+
+    tiles = inner // LANES
+    flat = w_zx.reshape(rows, 2, tiles, LANES).transpose(0, 2, 1, 3).reshape(-1, LANES)
+    extra = TILE_ROWS * (1 + model // (rows + LANES))
+    front_own, gate_own = pl.pallas_call(
+        pack_kernel,
+        name="pack_weights",
+        grid=(1,),
+        out_shape=(shape((rows + extra, width), bf16), shape((rows, inner), bf16)),
+        in_specs=[
+            smem,
+            pl.BlockSpec(flat.shape, lambda i: (0, 0)),
+            pl.BlockSpec(w_bc.shape, lambda i: (0, 0)),
+            pl.BlockSpec((heads, rows), lambda i: (0, 0)),
+            pl.BlockSpec((TILE_ROWS, model), lambda i: (tok // TILE_ROWS - 1, 0)),
+        ],
+        out_specs=(
+            pl.BlockSpec((rows + extra, width), lambda i: (0, 0)),
+            pl.BlockSpec((rows, inner), lambda i: (0, 0)),
+        ),
+        scratch_shapes=[pltpu.VMEM((TILE_ROWS, rows + LANES), f32)],
+        compiler_params=kernel_params(),
+    )(request_prompt, flat, w_bc, w_dt.T, hidden)
+    front_far = exchange(front_own, "dp", 2)
+    front_near = exchange(front_own, "dp", 1)
+    gate_far = exchange(gate_own, "dp", 2)
+    gate_near = exchange(gate_own, "dp", 1)
+    front_last = exchange(front_far, "dp", 1)
+    gate_last = exchange(gate_far, "dp", 1)
+
+    core = position % 2
+    scaled_out = (w_out.astype(f32) * out_gain[:, None]).astype(bf16)
+    half_width = model // 2
+    half_out = lax.dynamic_slice_in_dim(scaled_out, core * half_width, half_width, 1)
+    near_out = [exchange(half_out, "head", bits) for bits in (1, 2, 3)]
+    swapped_out = [exchange(part, "dp", 1) for part in near_out]
+
+    ids_long = jnp.concatenate([jnp.full((3,), -1, jnp.int32), token_prompt, jnp.full((1,), -1, jnp.int32)])
+    window = lax.dynamic_slice_in_dim(ids_long, position * tok, tok + 4)
+    ids = window[3 : 3 + tok]
+    before, after = window[2], window[3 + tok]
+    end_id, middle_id = ids[tok - 1], ids[BLOCK - 1]
+    index = jnp.arange(tok, dtype=jnp.int32)
+    facts = [ids == window[3 - k : 3 - k + tok] for k in (1, 2, 3)]
+    facts += [
+        ids == before,
+        (ids == middle_id) & (index >= BLOCK),
+        (ids == middle_id) & (index < BLOCK),
+        ids,
+        ids == end_id,
+        (ids != end_id) | (after != end_id),
+    ]
+    meta = jnp.stack([fact.astype(f32) for fact in facts], axis=1)
+    meta = jnp.pad(meta, ((0, 0), (0, LANES - meta.shape[1])))
+    entered = jnp.sum((ids == before).astype(jnp.int32))
+    applies = (entered > 0) & ((before != end_id) | (after != end_id))
+    place = jnp.stack(
+        [
+            position,
+            jnp.maximum(before, 0),
+            applies.astype(jnp.int32),
+            jnp.maximum(entered - 1, 0),
+            head_index % 4,
+            head_index // 4,
+            core,
+            0,
+        ]
+    ).astype(jnp.int32)
+    same = ids[:, None] == ids[None, :]
+    order = jnp.concatenate(
+        [index[None, :] <= index[:, None], (index[None, :] > index[:, None]) & same]
+    ).astype(bf16)
+    blocks = tok // BLOCK
+    pen = jnp.where(same & (index[None, :] <= index[:, None]), 0.0, NEVER).astype(f32)
+    pen = jnp.stack(
+        [pen[b * BLOCK : (b + 1) * BLOCK, b * BLOCK : (b + 1) * BLOCK] for b in range(blocks)]
+    )
+    head_rows = jnp.pad(jnp.stack([dt_bias, a_log]), ((0, 0), (0, LANES - heads)))
+    skip_row = jnp.repeat(skip_gain, inner // heads)[None, :]
+
+    hidden_f = hidden.astype(f32)
+    normed = (hidden_f * rms_scale(hidden_f) * in_gain).astype(bf16)
+
+    conv, stepx, faded, prefix, leaving, middle = pl.pallas_call(
+        front_kernel,
+        name="project_and_convolve",
+        out_shape=(
+            shape((tok, width), bf16),
+            shape((tok, inner), bf16),
+            shape((inner, tok), bf16),
+            shape((tok, LANES), f32),
+            shape((inner, state_width), bf16),
+            shape((inner, state_width), bf16),
+        ),
+        in_specs=[smem] + in_vmem(1) + [anywhere] * 4 + in_vmem(6),
+        out_specs=tuple(in_vmem(6)),
+        scratch_shapes=[
+            pltpu.VMEM((model, width), bf16),
+            pltpu.VMEM((peers, extra, width), bf16),
+            pltpu.VMEM((LANES, model), bf16),
+            pltpu.VMEM((TILE_ROWS + tok, width), f32),
+            pltpu.SemaphoreType.DMA((2 * peers,)),
+        ],
+        compiler_params=kernel_params(),
+        cost_estimate=pl.CostEstimate(
+            flops=2 * tok * model * width, bytes_accessed=8_000_000, transcendentals=500_000
+        ),
+    )(
+        place,
+        normed,
+        front_own,
+        front_near,
+        front_far,
+        front_last,
+        in_gain[None, :],
+        conv_x,
+        conv_bc,
+        meta,
+        order,
+        head_rows,
+    )
+
+    entering = lax.ppermute(leaving, "dp", [(i, i + 1) for i in range(peers - 1)])
+
+    y_local, gate, table = pl.pallas_call(
+        local_kernel,
+        name="mix_within_blocks",
+        out_shape=(
+            shape((tok, inner), f32),
+            shape((tok, inner), f32),
+            shape((PROMPTS, inner, state_width), bf16),
+        ),
+        in_specs=[smem] + in_vmem(1) + [anywhere] * 4 + in_vmem(8),
+        out_specs=tuple(in_vmem(3)),
+        scratch_shapes=[pltpu.VMEM((model, inner), bf16), pltpu.SemaphoreType.DMA((peers,))],
+        compiler_params=kernel_params(),
+        cost_estimate=pl.CostEstimate(
+            flops=2 * tok * model * inner, bytes_accessed=8_000_000, transcendentals=1_000_000
+        ),
+    )(
+        place,
+        normed,
+        gate_own,
+        gate_near,
+        gate_far,
+        gate_last,
+        conv,
+        stepx,
+        faded,
+        prefix,
+        middle,
+        meta,
+        pen,
+        skip_row,
+    )
+
+    out_rows = tok // head_count
+    gated = pl.pallas_call(
+        gate_kernel,
+        name="add_entering_and_gate",
+        out_shape=tuple(shape((2 * out_rows, inner), bf16) for _ in range(4)),
+        in_specs=[smem] + in_vmem(6),
+        out_specs=tuple(in_vmem(4)),
+        scratch_shapes=[pltpu.VMEM((tok, inner), bf16)],
+        compiler_params=kernel_params(),
+    )(place, entering, conv, prefix, meta, y_local, gate)
+    gated_in = [gated[0]] + [exchange(gated[bits], "head", bits) for bits in (1, 2, 3)]
+
+    table = pl.pallas_call(
+        ends_kernel,
+        name="add_entering_to_ends",
+        out_shape=shape(table.shape, bf16),
+        in_specs=[smem] + in_vmem(3),
+        out_specs=in_vmem(1)[0],
+        compiler_params=kernel_params(),
+    )(place, table, entering, prefix)
+    table_near = exchange(table, "dp", 1)
+    requests = request_prompt.shape[0]
+    other_wants = front_far[rows, rows : rows + requests].astype(jnp.int32)
+    keep, send = pl.pallas_call(
+        pick_kernel,
+        name="pick_request_states",
+        out_shape=(shape((requests, inner, state_width), bf16),) * 2,
+        in_specs=[smem] + in_vmem(2),
+        out_specs=tuple(in_vmem(2)),
+        compiler_params=kernel_params(),
+    )(jnp.concatenate([request_prompt, other_wants]), table, table_near)
+    far = exchange(send, "dp", 2)
+
+    sums_send, sums_keep = pl.pallas_call(
+        out_kernel,
+        name="project_out",
+        out_shape=(
+            shape((out_rows, model + LANES), bf16),
+            shape((out_rows, model + LANES), f32),
+        ),
+        in_specs=[smem] + in_vmem(11),
+        out_specs=tuple(in_vmem(2)),
+        compiler_params=kernel_params(),
+    )(place, *gated_in, scaled_out, *near_out, *swapped_out)
+    sums_in = exchange(sums_send, "head", 4)
+    own_hidden = lax.dynamic_slice_in_dim(hidden, head_index * out_rows, out_rows, 0)
+    layer_out = pl.pallas_call(
+        functools.partial(finish_kernel, inner * head_count),
+        name="scale_and_add_hidden",
+        out_shape=shape((out_rows, model), bf16),
+        in_specs=in_vmem(3),
+        out_specs=in_vmem(1)[0],
+        compiler_params=kernel_params(),
+    )(own_hidden, sums_keep, sums_in)
+    request_states = keep.astype(f32) + far.astype(f32)
+    return (
+        layer_out,
+        request_states.reshape(requests, heads, inner // heads, state_width),
+    )
+
+
+def fits_fused(mesh):
+    return dict(mesh.shape) == {"dp": 4, "head": 8}
+
+
 def solution(mesh):
     in_specs = (
         P("dp", None),
@@ -268,6 +860,7 @@
         P("head", None),
     )
     out_specs = (P(("dp", "head"), None), P("dp", "head", None, None))
+    program = fused_on_device if fits_fused(mesh) else on_device
     return jax.shard_map(
-        on_device, mesh=mesh, in_specs=in_specs, out_specs=out_specs, check_vma=False
-    )
+        program, mesh=mesh, in_specs=in_specs, out_specs=out_specs, check_vma=False
+    )

time: 248 us -> 103 us (0.42)
  waiting for transfers between devices: 95.9 us -> 15.3 us
  blocking collectives: 57.4 us -> 0 us
  Pallas kernels: 0 us -> 24.3 us
  starting transfers between devices: 2.37 us -> 19.5 us
  matrix products: 16.4 us -> 0 us
  other arithmetic: 30.1 us -> 14.2 us
  between operations: 15.8 us -> 5.35 us
  local copies, waits for them, and re-layouts: 28 us -> 23.7 us
    reduce_scatter x1 -> x0, waiting for transfers between devices: 75 us -> none  [on_device(): lax.psum_scatter(jnp.dot(normed_out, w_out, preferred_element_type=jnp.fl...]
    all_gather x3 -> x0, blocking collectives: 28.6 us -> none  [the longest x1 13.6 us: on_device(): lax.all_gather(w_bc.astype(jnp.bfloat16), 'dp', axis=0, tiled=True)]
    pallas_call x0 -> x8, Pallas kernels: none -> 24.3 us  [the longest x1 9.21 us: fused_on_device(): pl.pallas_call(front_kernel, name='project_and_convolve', out_shape=(shap...]
    psum x1 -> x0, blocking collectives: 21.7 us -> none  [on_device(): square_sum = lax.psum(jnp.sum(gated * gated, axis=1), 'head')]
    psum x1 -> x0, waiting for transfers between devices: 20.9 us -> none  [on_device(): table = lax.psum(local_table, 'dp')]
    ppermute x1 -> x19, starting transfers between devices: 2.25 us -> 19.5 us  [the longest x18 17.4 us: exchange(): lax.ppermute(values, axis, [(i, i ^ bits) for i in range(lax.axis_size(ax...]
    dot_general x10 -> x0, matrix products: 16.4 us -> none  [the longest x1 3.2 us: with_ends(): jnp.einsum('ghsn,shp->ghpn', b_last, x_blk, preferred_element_type=jnp.fl...]
    ppermute x1 -> x19, waiting for transfers between devices: 0.01 us -> 15.3 us  [the longest x18 15.3 us: exchange(): lax.ppermute(values, axis, [(i, i ^ bits) for i in range(lax.axis_size(ax...]
  transfers between devices with their start and end apart: 4 -> 19, of which waited for: 2 -> 5; matrix products, arithmetic and copies ran while one was open for 13% -> 16% of each run, Pallas kernels for 0% -> 22%
where the time goes in v1:
time: 103 us; the launch traced here: 102 us
  Pallas kernels  24.3 us (24%)
  local copies, waits for them, and re-layouts  23.7 us (23%)
  starting transfers between devices  19.5 us (19%)
  waiting for transfers between devices  15.3 us (15%)
  other arithmetic  14.2 us (14%)
  between operations  5.35 us (5%)
    ppermute x18, starting transfers between devices, exchange(): lax.ppermute(values, axis, [(i, i ^ bits) for i in range(lax.axis_size(ax...  17.4 us
    unnamed x63, local copies, waits for them, and re-layouts  17 us
    ppermute x18, waiting for transfers between devices, exchange(): lax.ppermute(values, axis, [(i, i ^ bits) for i in range(lax.axis_size(ax...  15.3 us
    pallas_call x1, Pallas kernels, fused_on_device(): pl.pallas_call(front_kernel, name='project_and_convolve', out_shape=(shap...  9.21 us
    pallas_call x1, Pallas kernels, fused_on_device(): pl.pallas_call(local_kernel, name='mix_within_blocks', out_shape=(shape((...  6.15 us
    transpose x1, local copies, waits for them, and re-layouts, fused_on_device(): w_zx.reshape(rows, 2, tiles, LANES).transpose(0, 2, 1, 3).reshape(-1, LANES)  2.65 us
    pallas_call x1, Pallas kernels, fused_on_device(): pl.pallas_call(out_kernel, name='project_out', out_shape=(shape((out_rows...  2.59 us
    convert_element_type x1, other arithmetic, fused_on_device(): order = jnp.concatenate([index[None, :] <= index[:, None], (index[None, :...  2.2 us
  transfers between devices with their start and end apart: 19, of which 5 were waited for; matrix products, arithmetic and copies ran while one was open for 16% of the time, Pallas kernels for 22%

profile of v1, /device:TPU:0, one launch (start us, length us, event | category | flops | bytes accessed | tf_op | source)
XLA Modules:
  0.0 102.2 jit_solution(11269006470430054943)
XLA Ops:
  0.6 3.4 %copy.28 = f32[384,2,384]{0,2,1:T(8,128)} copy(f32[384,2,384]{2,1,0:T(2,128)} %param.18) | data formatting | bytes 2359296 | tf_op args[4]
  4.0 2.6 %copy.29 = f32[384,3,2,128]{3,2,1,0:T(2,128)S(1)} copy(f32[384,3,2,128]{0,3,1,2:T(8,128)} %bitcast.39) | data formatting | bytes 2359296 | tf_op jit(solution)/shard_map/transpose | solution.py:626
  7.7 1.4 %pack_weights.1 = (bf16[448,640]{1,0:T(8,128)(2,1)S(1)}, bf16[384,384]{1,0:T(8,128)(2,1)}) custom-call(s32[4]{0:T(128)S(1)} %copy-done.22, f32[2304,128]{1,0:T(8,128)S(1)} %bitcast.37, f32[384,256]{1,0:T(8,128)S(1)} %copy-done.18, f32[6,384]{1,0:T(8,128)S(1)} %bitcast.38, bf16[512,1536]{1,0:T(8,128)(2,1)S(1)} %copy-done), custom_call_target="tpu_custom_call" | custom-call | tf_op jit(solution)/shard_map/pack_weights/pallas_call | solution.py:628
  9.1 2.9 %collective-permute-start.1 = (bf16[448,640]{1,0:T(8,128)(2,1)S(1)}, bf16[448,640]{1,0:T(8,128)(2,1)}, u32[]{:S(2)}, u32[]{:S(2)}) collective-permute-start(bf16[448,640]{1,0:T(8,128)(2,1)S(1)} %get-tuple-element.21.own_ref), channel_id=1, source_target_pairs={{0,16},{8,24},{16,0},{24,8},{1,17},{9,25},{17,1},{25,9},{2,18},{10... | collective-permute-start | bytes 1720328 | tf_op jit(solution)/shard_map/ppermute | solution.py:272
  12.6 1.5 %multiply_convert_fusion.refs_4_ = bf16[384,1536]{1,0:T(8,128)(2,1)S(1)} fusion(bf16[384,1536]{1,0:T(8,128)(2,1)} %param.27, f32[384]{0:T(512)S(1)} %copy-done.27), kind=kLoop, calls=%fused_computation.5 | loop fusion | flops 1769472 | bytes 2360832 | tf_op jit(solution)/shard_map/convert_element_type | solution.py:655
  15.0 1.8 %collective-permute-start.10 = (bf16[384,768]{1,0:T(8,128)(2,1)}, bf16[384,768]{1,0:T(8,128)(2,1)}, u32[]{:S(2)}, u32[]{:S(2)}) collective-permute-start(bf16[384,768]{1,0:T(8,128)(2,1)} %constant_dynamic-slice_fusion), channel_id=1, source_target_pairs={{0,1},{1,0},{2,3},{3,2},{4,5},{5,4},{6,7},{7,6},{8,9},{9,8},{10,11... | collective-permute-start | bytes 1769480 | tf_op jit(solution)/shard_map/ppermute | solution.py:272
  17.4 1.1 %compare_and_fusion.1 = (pred[512,512]{1,0:T(8,128)(4,1)}, pred[512,512]{1,0:T(8,128)(4,1)}) fusion(s32[512]{0:T(512)S(1)} %get-tuple-element.46), kind=kLoop, calls=%fused_computation.8 | loop fusion | flops 1048576 | bytes 526336 | tf_op jit(solution)/shard_map/and | solution.py:694
  18.5 1.2 %fusion.3 = f32[512,512]{1,0:T(8,128)} fusion(s32[512]{0:T(512)S(1)} %get-tuple-element.46), kind=kLoop, calls=%fused_computation.11 | loop fusion | flops 1048576 | bytes 1050624 | tf_op jit(solution)/shard_map/jit(_where)/select_n | solution.py:697
  19.7 1.6 %fusion.2.normed_ref = bf16[512,1536]{1,0:T(8,128)(2,1)} fusion(bf16[512,1536]{1,0:T(8,128)(2,1)S(1)} %copy-done, f32[1536]{0:T(1024)S(1)} %copy-done.25, f32[512]{0:T(512)S(1)} %add_rsqrt_fusion), kind=kLoop, calls=%fused_computation.4 | loop fusion | flops 3145728 | bytes 3153920 | tf_op jit(solution)/shard_map/convert_element_type | solution.py:705
  23.1 1.9 %slice_bitcast_fusion.1 = (f32[1,256,256]{2,1,0:T(8,128)}, f32[1,256,256]{2,1,0:T(8,128)}) fusion(f32[512,512]{1,0:T(8,128)} %fusion.3), kind=kLoop, calls=%fused_computation.15 | loop fusion | bytes 1048576 | tf_op jit(solution)/shard_map/stack | solution.py:698
  25.0 1.8 %fusion.10 = (f32[512]{0:T(512)S(1)}, pred[512]{0:T(512)(128)(4,1)S(1)}, f32[512]{0:T(512)S(1)}, f32[512]{0:T(512)S(1)}, f32[512]{0:T(512)S(1)}, /*index=5*/pred...) fusion(s32[]{:T(128)} %bitcast.18, s32[516]{0:T(1024)S(1)} %dynamic_slice.10, s32[]{:T(128)} %bitcast.3, ...), kind=kLoop, calls=%fused_computation.29 | loop fusion | flops 8704 | bytes 23565 | tf_op jit(solution)/shard_map/stack | solution.py:676
  26.9 2.2 %add_convert_fusion.order_ref = bf16[1024,512]{1,0:T(8,128)(2,1)} fusion(pred[512,512]{1,0:T(8,128)(4,1)} %get-tuple-element.61, pred[512,512]{1,0:T(8,128)(4,1)} %get-tuple-element.62), kind=kLoop, calls=%fused_computation.6 | loop fusion | flops 1048576 | bytes 1572864 | tf_op jit(solution)/shard_map/convert_element_type | solution.py:695
  29.8 1.6 %collective-permute-done.5.far_ref = bf16[384,384]{1,0:T(8,128)(2,1)} collective-permute-done((bf16[384,384]{1,0:T(8,128)(2,1)}, bf16[384,384]{1,0:T(8,128)(2,1)}, u32[]{:S(2)}, u32[]{:S(2)}) %collective-permute-start.5) | collective-permute-done | bytes 294944 | tf_op jit(solution)/shard_map/ppermute | solution.py:272
  31.5 1.8 %collective-permute-start.11 = (bf16[384,768]{1,0:T(8,128)(2,1)}, bf16[384,768]{1,0:T(8,128)(2,1)}, u32[]{:S(2)}, u32[]{:S(2)}) collective-permute-start(bf16[384,768]{1,0:T(8,128)(2,1)} %constant_dynamic-slice_fusion), channel_id=1, source_target_pairs={{0,2},{1,3},{2,0},{3,1},{4,6},{5,7},{6,4},{7,5},{8,10},{9,11},{10,... | collective-permute-start | bytes 1769480 | tf_op jit(solution)/shard_map/ppermute | solution.py:272
  36.9 1.5 %collective-permute-start.12 = (bf16[384,768]{1,0:T(8,128)(2,1)}, bf16[384,768]{1,0:T(8,128)(2,1)}, u32[]{:S(2)}, u32[]{:S(2)}) collective-permute-start(bf16[384,768]{1,0:T(8,128)(2,1)} %constant_dynamic-slice_fusion), channel_id=1, source_target_pairs={{0,3},{1,2},{2,1},{3,0},{4,7},{5,6},{6,5},{7,4},{8,11},{9,10},{10,... | collective-permute-start | bytes 1769480 | tf_op jit(solution)/shard_map/ppermute | solution.py:272
  38.4 1.2 %copy-done.1 = bf16[1024,512]{1,0:T(8,128)(2,1)S(1)} copy-done((bf16[1024,512]{1,0:T(8,128)(2,1)S(1)}, bf16[1024,512]{1,0:T(8,128)(2,1)}, u32[]{:S(2)}) %copy-start.1) | copy-done | bytes 1048600
  40.7 9.2 %project_and_convolve.1 = (bf16[512,640]{1,0:T(8,128)(2,1)S(1)}, bf16[512,384]{1,0:T(8,128)(2,1)S(1)}, bf16[384,512]{1,0:T(8,128)(2,1)S(1)}, f32[512,128]{1,0:T(...) custom-call(s32[8]{0:T(128)S(1)} %stack.107.place_ref, bf16[512,1536]{1,0:T(8,128)(2,1)} %fusion.2.normed_ref, ...), custom_call_target="tpu_custom_call" | custom-call | flops 1006632960 | bytes 8000000 | tf_op jit(solution)/shard_map/project_and_convolve/pallas_call | solution.py:707
  52.3 2.1 %collective-permute-start.3 = (bf16[384,128]{1,0:T(8,128)(2,1)}, bf16[384,128]{1,0:T(8,128)(2,1)S(1)}, u32[]{:S(2)}, u32[]{:S(2)}) collective-permute-start(bf16[384,128]{1,0:T(8,128)(2,1)} %get-tuple-element.22), channel_id=1, source_target_pairs={{0,8},{8,16},{16,24},{1,9},{9,17},{17,25},{2,10},{10,18},{18,26},{... | collective-permute-start | bytes 294920 | tf_op jit(solution)/shard_map/ppermute | solution.py:746
  55.4 1.1 %copy-done.3 = bf16[512,640]{1,0:T(8,128)(2,1)S(1)} copy-done((bf16[512,640]{1,0:T(8,128)(2,1)S(1)}, bf16[512,640]{1,0:T(8,128)(2,1)}, u32[]{:S(2)}) %copy-start.3) | copy-done | bytes 655384
  59.5 6.1 %mix_within_blocks.1 = (f32[512,384]{1,0:T(8,128)S(1)}, f32[512,384]{1,0:T(8,128)S(1)}, bf16[8,384,128]{2,1,0:T(8,128)(2,1)S(1)}) custom-call(s32[8]{0:T(128)S(1)} %stack.107.place_ref, bf16[512,1536]{1,0:T(8,128)(2,1)} %fusion.2.normed_ref, bf16[384,384]{1,0:T(8,128)(2,1)} %get-tuple-element.25.own_ref, bf16[384,384]{1,0:T(8,128)(2,1)} %collective-permute-done.4.near_ref, ...), custom_call_target="tpu_custom_call" | custom-call | flops 603979776 | bytes 8000000 | tf_op jit(solution)/shard_map/mix_within_blocks/pallas_call | solution.py:748
  66.5 1.6 %collective-permute-start.17 = (bf16[8,384,128]{2,1,0:T(8,128)(2,1)S(1)}, bf16[8,384,128]{2,1,0:T(8,128)(2,1)S(1)}, u32[]{:S(2)}, u32[]{:S(2)}) collective-permute-start(bf16[8,384,128]{2,1,0:T(8,128)(2,1)S(1)} %add_entering_to_ends.1.table_ref), channel_id=1, source_target_pairs={{0,8},{8,0},{16,24},{24,16},{1,9},{9,1},{17,25},{25,17},{2,10},{10... | collective-permute-start | bytes 2359304 | tf_op jit(solution)/shard_map/ppermute | solution.py:272
  70.2 1.4 %pick_request_states.1 = (bf16[4,384,128]{2,1,0:T(8,128)(2,1)S(1)}, bf16[4,384,128]{2,1,0:T(8,128)(2,1)}) custom-call(s32[8]{0:T(128)S(1)} %pad_add_fusion.wanted_ref, bf16[8,384,128]{2,1,0:T(8,128)(2,1)S(1)} %add_entering_to_ends.1.table_ref, bf16[8,384,128]{2,1,0:T(8,128)(2,1)S(1)} %collective-permute-done.17.other_ref), custom_call_target="tpu_custom_call" | custom-call | tf_op jit(solution)/shard_map/pick_request_states/pallas_call | solution.py:803
  72.1 1.9 %add_entering_and_gate.1 = (bf16[128,384]{1,0:T(8,128)(2,1)S(1)}, bf16[128,384]{1,0:T(8,128)(2,1)}, bf16[128,384]{1,0:T(8,128)(2,1)}, bf16[128,384]{1,0:T(8,128)(2,1)}) custom-call(s32[8]{0:T(128)S(1)} %stack.107.place_ref, bf16[384,128]{1,0:T(8,128)(2,1)S(1)} %collective-permute-done.3.enter_ref, bf16[512,640]{1,0:T(8,128)(2,1)S(1)} %copy-done.4, ...), custom_call_target="tpu_custom_call" | custom-call | tf_op jit(solution)/shard_map/add_entering_and_gate/pallas_call | solution.py:781
  75.3 1.6 %collective-permute-start.8 = (bf16[128,384]{1,0:T(8,128)(2,1)}, bf16[128,384]{1,0:T(8,128)(2,1)S(1)}, u32[]{:S(2)}, u32[]{:S(2)}) collective-permute-start(bf16[128,384]{1,0:T(8,128)(2,1)} %get-tuple-element.33), channel_id=1, source_target_pairs={{0,2},{1,3},{2,0},{3,1},{4,6},{5,7},{6,4},{7,5},{8,10},{9,11},{10,... | collective-permute-start | bytes 294920 | tf_op jit(solution)/shard_map/ppermute | solution.py:272
  77.7 1.4 %collective-permute-start.9 = (bf16[128,384]{1,0:T(8,128)(2,1)}, bf16[128,384]{1,0:T(8,128)(2,1)S(1)}, u32[]{:S(2)}, u32[]{:S(2)}) collective-permute-start(bf16[128,384]{1,0:T(8,128)(2,1)} %get-tuple-element.34), channel_id=1, source_target_pairs={{0,3},{1,2},{2,1},{3,0},{4,7},{5,6},{6,5},{7,4},{8,11},{9,10},{10,... | collective-permute-start | bytes 294920 | tf_op jit(solution)/shard_map/ppermute | solution.py:272
  80.1 3.3 %collective-permute-done.9.refs_3_ = bf16[128,384]{1,0:T(8,128)(2,1)S(1)} collective-permute-done((bf16[128,384]{1,0:T(8,128)(2,1)}, bf16[128,384]{1,0:T(8,128)(2,1)S(1)}, u32[]{:S(2)}, u32[]{:S(2)}) %collective-permute-start.9) | collective-permute-done | bytes 98336 | tf_op jit(solution)/shard_map/ppermute | solution.py:272
  83.4 1.1 %copy-done.7 = bf16[384,768]{1,0:T(8,128)(2,1)S(1)} copy-done((bf16[384,768]{1,0:T(8,128)(2,1)S(1)}, bf16[384,768]{1,0:T(8,128)(2,1)}, u32[]{:S(2)}) %copy-start.7) | copy-done | bytes 589848
  84.5 1.1 %copy-done.9 = bf16[384,768]{1,0:T(8,128)(2,1)S(1)} copy-done((bf16[384,768]{1,0:T(8,128)(2,1)S(1)}, bf16[384,768]{1,0:T(8,128)(2,1)}, u32[]{:S(2)}) %copy-start.9) | copy-done | bytes 589848
  85.6 2.6 %project_out.1 = (bf16[64,1664]{1,0:T(8,128)(2,1)S(1)}, f32[64,1664]{1,0:T(8,128)S(1)}) custom-call(s32[8]{0:T(128)S(1)} %stack.107.place_ref, bf16[128,384]{1,0:T(8,128)(2,1)S(1)} %get-tuple-element.31.refs_0_, bf16[128,384]{1,0:T(8,128)(2,1)S(1)} %collective-permute-done.7.refs_1_, bf16[128,384]{1,0:T(8,128)(2,1)S(1)} %collective-permute-done.8.refs_2_, ...), custom_call_target="tpu_custom_call" | custom-call | tf_op jit(solution)/shard_map/project_out/pallas_call | solution.py:813
  88.2 2.7 %collective-permute-start.16 = (bf16[64,1664]{1,0:T(8,128)(2,1)S(1)}, bf16[64,1664]{1,0:T(8,128)(2,1)S(1)}, u32[]{:S(2)}, u32[]{:S(2)}) collective-permute-start(bf16[64,1664]{1,0:T(8,128)(2,1)S(1)} %get-tuple-element.36), channel_id=1, source_target_pairs={{0,4},{1,5},{2,6},{3,7},{4,0},{5,1},{6,2},{7,3},{8,12},{9,13},{10,... | collective-permute-start | bytes 638984 | tf_op jit(solution)/shard_map/ppermute | solution.py:272
  90.9 8.5 %collective-permute-done.16.got_ref = bf16[64,1664]{1,0:T(8,128)(2,1)S(1)} collective-permute-done((bf16[64,1664]{1,0:T(8,128)(2,1)S(1)}, bf16[64,1664]{1,0:T(8,128)(2,1)S(1)}, u32[]{:S(2)}, u32[]{:S(2)}) %collective-permute-start.16) | collective-permute-done | bytes 213024 | tf_op jit(solution)/shard_map/ppermute | solution.py:272
  100.3 2.0 %convert_add_fusion = f32[4,384,128]{2,1,0:T(8,128)} fusion(bf16[4,384,128]{2,1,0:T(8,128)(2,1)} %collective-permute-done.18, bf16[4,384,128]{2,1,0:T(8,128)(2,1)S(1)} %copy-done.17), kind=kLoop, calls=%fused_computation.12 | loop fusion | flops 589824 | bytes 1572864 | tf_op jit(solution)/shard_map/add | solution.py:834
  (108 shorter events, 19.6 us)
Async XLA Ops:
  7.7 4.8 %copy-start.27 = (f32[384]{0:T(512)S(1)}, f32[384]{0:T(512)}, u32[]{:S(2)}) copy-start(f32[384]{0:T(512)} %param.26) | copy-start | bytes 4612
  9.1 5.9 %copy-start.10 = (bf16[448,640]{1,0:T(8,128)(2,1)}, bf16[448,640]{1,0:T(8,128)(2,1)S(1)}, u32[]{:S(2)}) copy-start(bf16[448,640]{1,0:T(8,128)(2,1)S(1)} %get-tuple-element.21.own_ref) | copy-start | bytes 1720324
  9.1 17.7 %collective-permute-start.1 = (bf16[448,640]{1,0:T(8,128)(2,1)S(1)}, bf16[448,640]{1,0:T(8,128)(2,1)}, u32[]{:S(2)}, u32[]{:S(2)}) collective-permute-start(bf16[448,640]{1,0:T(8,128)(2,1)S(1)} %get-tuple-element.21.own_ref), channel_id=1, source_target_pairs={{0,16},{8,24},{16,0},{24,8},{1,17},{9,25},{17,1},{25,9},{2,18},{10... | collective-permute-start | bytes 1720328 | tf_op jit(solution)/shard_map/ppermute | solution.py:272
  12.1 21.2 %collective-permute-start = (bf16[448,640]{1,0:T(8,128)(2,1)S(1)}, bf16[448,640]{1,0:T(8,128)(2,1)}, u32[]{:S(2)}, u32[]{:S(2)}) collective-permute-start(bf16[448,640]{1,0:T(8,128)(2,1)S(1)} %get-tuple-element.21.own_ref), channel_id=1, source_target_pairs={{0,8},{8,0},{16,24},{24,16},{1,9},{9,1},{17,25},{25,17},{2,10},{10... | collective-permute-start | bytes 1720328 | tf_op jit(solution)/shard_map/ppermute | solution.py:272
  12.1 19.4 %collective-permute-start.5 = (bf16[384,384]{1,0:T(8,128)(2,1)}, bf16[384,384]{1,0:T(8,128)(2,1)}, u32[]{:S(2)}, u32[]{:S(2)}) collective-permute-start(bf16[384,384]{1,0:T(8,128)(2,1)} %get-tuple-element.25.own_ref), channel_id=1, source_target_pairs={{0,16},{8,24},{16,0},{24,8},{1,17},{9,25},{17,1},{25,9},{2,18},{10... | collective-permute-start | bytes 884744 | tf_op jit(solution)/shard_map/ppermute | solution.py:272
  12.1 40.2 %collective-permute-start.4 = (bf16[384,384]{1,0:T(8,128)(2,1)}, bf16[384,384]{1,0:T(8,128)(2,1)}, u32[]{:S(2)}, u32[]{:S(2)}) collective-permute-start(bf16[384,384]{1,0:T(8,128)(2,1)} %get-tuple-element.25.own_ref), channel_id=1, source_target_pairs={{0,8},{8,0},{16,24},{24,16},{1,9},{9,1},{17,25},{25,17},{2,10},{10... | collective-permute-start | bytes 884744 | tf_op jit(solution)/shard_map/ppermute | solution.py:272
  15.0 4.7 %copy-start.25 = (f32[1536]{0:T(1024)S(1)}, f32[1536]{0:T(1024)}, u32[]{:S(2)}) copy-start(f32[1536]{0:T(1024)} %param.17) | copy-start | bytes 18436
  15.0 53.1 %collective-permute-start.10 = (bf16[384,768]{1,0:T(8,128)(2,1)}, bf16[384,768]{1,0:T(8,128)(2,1)}, u32[]{:S(2)}, u32[]{:S(2)}) collective-permute-start(bf16[384,768]{1,0:T(8,128)(2,1)} %constant_dynamic-slice_fusion), channel_id=1, source_target_pairs={{0,1},{1,0},{2,3},{3,2},{4,5},{5,4},{6,7},{7,6},{8,9},{9,8},{10,11... | collective-permute-start | bytes 1769480 | tf_op jit(solution)/shard_map/ppermute | solution.py:272
  21.3 12.0 %copy-start.29 = (f32[6]{0:T(128)S(1)}, f32[6]{0:T(128)}, u32[]{:S(2)}) copy-start(f32[6]{0:T(128)} %param.22) | copy-start | bytes 76
  21.3 12.0 %copy-start.30 = (f32[6]{0:T(128)S(1)}, f32[6]{0:T(128)}, u32[]{:S(2)}) copy-start(f32[6]{0:T(128)} %param.21) | copy-start | bytes 76
  23.1 15.3 %copy-start.20 = (f32[4,384]{1,0:T(4,128)S(1)}, f32[4,384]{1,0:T(4,128)}, u32[]{:S(2)}) copy-start(f32[4,384]{1,0:T(4,128)} %taps_x_ref.1) | copy-start | bytes 18436
  23.1 15.3 %copy-start.21 = (f32[4,256]{1,0:T(4,128)S(1)}, f32[4,256]{1,0:T(4,128)}, u32[]{:S(2)}) copy-start(f32[4,256]{1,0:T(4,128)} %taps_bc_ref.1) | copy-start | bytes 12292
  26.9 10.1 %collective-permute-start.2 = (bf16[448,640]{1,0:T(8,128)(2,1)}, bf16[448,640]{1,0:T(8,128)(2,1)}, u32[]{:S(2)}, u32[]{:S(2)}) collective-permute-start(bf16[448,640]{1,0:T(8,128)(2,1)} %collective-permute-done.1.far_ref), channel_id=1, source_target_pairs={{0,8},{8,0},{16,24},{24,16},{1,9},{9,1},{17,25},{25,17},{2,10},{10... | collective-permute-start | bytes 1720328 | tf_op jit(solution)/shard_map/ppermute | solution.py:272
  31.5 36.7 %collective-permute-start.11 = (bf16[384,768]{1,0:T(8,128)(2,1)}, bf16[384,768]{1,0:T(8,128)(2,1)}, u32[]{:S(2)}, u32[]{:S(2)}) collective-permute-start(bf16[384,768]{1,0:T(8,128)(2,1)} %constant_dynamic-slice_fusion), channel_id=1, source_target_pairs={{0,2},{1,3},{2,0},{3,1},{4,6},{5,7},{6,4},{7,5},{8,10},{9,11},{10,... | collective-permute-start | bytes 1769480 | tf_op jit(solution)/shard_map/ppermute | solution.py:272
  33.3 22.1 %collective-permute-start.6 = (bf16[384,384]{1,0:T(8,128)(2,1)}, bf16[384,384]{1,0:T(8,128)(2,1)}, u32[]{:S(2)}, u32[]{:S(2)}) collective-permute-start(bf16[384,384]{1,0:T(8,128)(2,1)} %collective-permute-done.5.far_ref), channel_id=1, source_target_pairs={{0,8},{8,0},{16,24},{24,16},{1,9},{9,1},{17,25},{25,17},{2,10},{10... | collective-permute-start | bytes 884744 | tf_op jit(solution)/shard_map/ppermute | solution.py:272
  36.8 18.4 %copy-start.28 = (f32[6]{0:T(128)S(1)}, f32[6]{0:T(128)}, u32[]{:S(2)}) copy-start(f32[6]{0:T(128)} %param.25) | copy-start | bytes 76
  36.9 31.7 %collective-permute-start.12 = (bf16[384,768]{1,0:T(8,128)(2,1)}, bf16[384,768]{1,0:T(8,128)(2,1)}, u32[]{:S(2)}, u32[]{:S(2)}) collective-permute-start(bf16[384,768]{1,0:T(8,128)(2,1)} %constant_dynamic-slice_fusion), channel_id=1, source_target_pairs={{0,3},{1,2},{2,1},{3,0},{4,7},{5,6},{6,5},{7,4},{8,11},{9,10},{10,... | collective-permute-start | bytes 1769480 | tf_op jit(solution)/shard_map/ppermute | solution.py:272
  40.7 13.7 %copy-start.23 = (f32[1,256,256]{2,1,0:T(8,128)S(1)}, f32[1,256,256]{2,1,0:T(8,128)}, u32[]{:S(2)}) copy-start(f32[1,256,256]{2,1,0:T(8,128)} %get-tuple-element.44) | copy-start | bytes 786436
  40.7 13.7 %copy-start.24 = (f32[1,256,256]{2,1,0:T(8,128)S(1)}, f32[1,256,256]{2,1,0:T(8,128)}, u32[]{:S(2)}) copy-start(f32[1,256,256]{2,1,0:T(8,128)} %get-tuple-element.45) | copy-start | bytes 786436
  52.3 13.4 %collective-permute-start.3 = (bf16[384,128]{1,0:T(8,128)(2,1)}, bf16[384,128]{1,0:T(8,128)(2,1)S(1)}, u32[]{:S(2)}, u32[]{:S(2)}) collective-permute-start(bf16[384,128]{1,0:T(8,128)(2,1)} %get-tuple-element.22), channel_id=1, source_target_pairs={{0,8},{8,16},{16,24},{1,9},{9,17},{17,25},{2,10},{10,18},{18,26},{... | collective-permute-start | bytes 294920 | tf_op jit(solution)/shard_map/ppermute | solution.py:746
  65.7 6.4 %copy-start.4 = (bf16[512,640]{1,0:T(8,128)(2,1)S(1)}, bf16[512,640]{1,0:T(8,128)(2,1)}, u32[]{:S(2)}) copy-start(bf16[512,640]{1,0:T(8,128)(2,1)} %copy-done.2) | copy-start | bytes 1966084
  66.5 3.7 %collective-permute-start.17 = (bf16[8,384,128]{2,1,0:T(8,128)(2,1)S(1)}, bf16[8,384,128]{2,1,0:T(8,128)(2,1)S(1)}, u32[]{:S(2)}, u32[]{:S(2)}) collective-permute-start(bf16[8,384,128]{2,1,0:T(8,128)(2,1)S(1)} %add_entering_to_ends.1.table_ref), channel_id=1, source_target_pairs={{0,8},{8,0},{16,24},{24,16},{1,9},{9,1},{17,25},{25,17},{2,10},{10... | collective-permute-start | bytes 2359304 | tf_op jit(solution)/shard_map/ppermute | solution.py:272
  68.1 6.4 %collective-permute-start.13 = (bf16[384,768]{1,0:T(8,128)(2,1)}, bf16[384,768]{1,0:T(8,128)(2,1)S(1)}, u32[]{:S(2)}, u32[]{:S(2)}) collective-permute-start(bf16[384,768]{1,0:T(8,128)(2,1)} %collective-permute-done.10.refs_5_), channel_id=1, source_target_pairs={{0,8},{8,0},{16,24},{24,16},{1,9},{9,1},{17,25},{25,17},{2,10},{10... | collective-permute-start | bytes 1769480 | tf_op jit(solution)/shard_map/ppermute | solution.py:272
  68.2 8.7 %collective-permute-start.14 = (bf16[384,768]{1,0:T(8,128)(2,1)}, bf16[384,768]{1,0:T(8,128)(2,1)S(1)}, u32[]{:S(2)}, u32[]{:S(2)}) collective-permute-start(bf16[384,768]{1,0:T(8,128)(2,1)} %collective-permute-done.11.refs_6_), channel_id=1, source_target_pairs={{0,8},{8,0},{16,24},{24,16},{1,9},{9,1},{17,25},{25,17},{2,10},{10... | collective-permute-start | bytes 1769480 | tf_op jit(solution)/shard_map/ppermute | solution.py:272
  68.6 10.5 %collective-permute-start.15 = (bf16[384,768]{1,0:T(8,128)(2,1)}, bf16[384,768]{1,0:T(8,128)(2,1)}, u32[]{:S(2)}, u32[]{:S(2)}) collective-permute-start(bf16[384,768]{1,0:T(8,128)(2,1)} %collective-permute-done.12.refs_7_), channel_id=1, source_target_pairs={{0,8},{8,0},{16,24},{24,16},{1,9},{9,1},{17,25},{25,17},{2,10},{10... | collective-permute-start | bytes 1769480 | tf_op jit(solution)/shard_map/ppermute | solution.py:272
  71.6 5.3 %copy-start.16 = (bf16[4,384,128]{2,1,0:T(8,128)(2,1)}, bf16[4,384,128]{2,1,0:T(8,128)(2,1)S(1)}, u32[]{:S(2)}) copy-start(bf16[4,384,128]{2,1,0:T(8,128)(2,1)S(1)} %get-tuple-element.38) | copy-start | bytes 1179652
  71.6 28.7 %collective-permute-start.18 = (bf16[4,384,128]{2,1,0:T(8,128)(2,1)}, bf16[4,384,128]{2,1,0:T(8,128)(2,1)}, u32[]{:S(2)}, u32[]{:S(2)}) collective-permute-start(bf16[4,384,128]{2,1,0:T(8,128)(2,1)} %get-tuple-element.39), channel_id=1, source_target_pairs={{0,16},{8,24},{16,0},{24,8},{1,17},{9,25},{17,1},{25,9},{2,18},{10... | collective-permute-start | bytes 1179656 | tf_op jit(solution)/shard_map/ppermute | solution.py:272
  74.0 5.2 %collective-permute-start.7 = (bf16[128,384]{1,0:T(8,128)(2,1)}, bf16[128,384]{1,0:T(8,128)(2,1)S(1)}, u32[]{:S(2)}, u32[]{:S(2)}) collective-permute-start(bf16[128,384]{1,0:T(8,128)(2,1)} %get-tuple-element.32), channel_id=1, source_target_pairs={{0,1},{1,0},{2,3},{3,2},{4,5},{5,4},{6,7},{7,6},{8,9},{9,8},{10,11... | collective-permute-start | bytes 294920 | tf_op jit(solution)/shard_map/ppermute | solution.py:272
  75.3 4.8 %collective-permute-start.8 = (bf16[128,384]{1,0:T(8,128)(2,1)}, bf16[128,384]{1,0:T(8,128)(2,1)S(1)}, u32[]{:S(2)}, u32[]{:S(2)}) collective-permute-start(bf16[128,384]{1,0:T(8,128)(2,1)} %get-tuple-element.33), channel_id=1, source_target_pairs={{0,2},{1,3},{2,0},{3,1},{4,6},{5,7},{6,4},{7,5},{8,10},{9,11},{10,... | collective-permute-start | bytes 294920 | tf_op jit(solution)/shard_map/ppermute | solution.py:272
  77.7 5.7 %collective-permute-start.9 = (bf16[128,384]{1,0:T(8,128)(2,1)}, bf16[128,384]{1,0:T(8,128)(2,1)S(1)}, u32[]{:S(2)}, u32[]{:S(2)}) collective-permute-start(bf16[128,384]{1,0:T(8,128)(2,1)} %get-tuple-element.34), channel_id=1, source_target_pairs={{0,3},{1,2},{2,1},{3,0},{4,7},{5,6},{6,5},{7,4},{8,11},{9,10},{10,... | collective-permute-start | bytes 294920 | tf_op jit(solution)/shard_map/ppermute | solution.py:272
  88.2 12.1 %copy-start.17 = (bf16[4,384,128]{2,1,0:T(8,128)(2,1)S(1)}, bf16[4,384,128]{2,1,0:T(8,128)(2,1)}, u32[]{:S(2)}) copy-start(bf16[4,384,128]{2,1,0:T(8,128)(2,1)} %copy-done.16) | copy-start | bytes 1179652
  88.2 11.2 %collective-permute-start.16 = (bf16[64,1664]{1,0:T(8,128)(2,1)S(1)}, bf16[64,1664]{1,0:T(8,128)(2,1)S(1)}, u32[]{:S(2)}, u32[]{:S(2)}) collective-permute-start(bf16[64,1664]{1,0:T(8,128)(2,1)S(1)} %get-tuple-element.36), channel_id=1, source_target_pairs={{0,4},{1,5},{2,6},{3,7},{4,0},{5,1},{6,2},{7,3},{8,12},{9,13},{10,... | collective-permute-start | bytes 638984 | tf_op jit(solution)/shard_map/ppermute | solution.py:272
  (18 other events, 24.6 us)

commit v2 on v1

--- a/solution.py
+++ b/solution.py
@@ -257,11 +257,10 @@
 LANES = 128
 TILE_ROWS = 16
 NEVER = -1e30
-MESH_KERNEL_BYTES = 48 * 1024 * 1024
-
-
-def kernel_params():
-    return pltpu.CompilerParams(vmem_limit_bytes=MESH_KERNEL_BYTES)
+
+
+def kernel_params(mebibytes):
+    return pltpu.CompilerParams(vmem_limit_bytes=mebibytes << 20)
 
 
 def in_vmem(count):
@@ -291,34 +290,139 @@
     return jnp.where(lane < head_dim, first, second)
 
 
-def pack_kernel(req_ref, wzx_ref, wbc_ref, wdt_ref, tail_ref, front_ref, gate_ref, pad_ref):
-    rows, bc_width = wbc_ref.shape
-    inner = gate_ref.shape[1]
+def pack_kernel(
+    req_ref,
+    wzx_ref,
+    wbc_ref,
+    wdt_ref,
+    hidden_ref,
+    front_ref,
+    gate_ref,
+    tiles_ref,
+    bc_ref,
+    dt_ref,
+    tail_ref,
+    front_v,
+    gate_v,
+    pad_ref,
+    sems,
+):
+    rows, bc_width = bc_ref.shape
+    tok = hidden_ref.shape[0]
+    inner = gate_v.shape[1]
     tiles = inner // LANES
+    pieces = [(wdt_ref, dt_ref), (hidden_ref.at[tok - TILE_ROWS : tok], tail_ref), (wbc_ref, bc_ref)]
     for j in range(tiles):
-        own = slice(j * LANES, (j + 1) * LANES)
-        front_ref[0:rows, own] = wzx_ref[pl.ds(2 * j + 1, rows, stride=2 * tiles), :].astype(
-            jnp.bfloat16
-        )
-        gate_ref[:, own] = wzx_ref[pl.ds(2 * j, rows, stride=2 * tiles), :].astype(jnp.bfloat16)
-    front_ref[0:rows, inner:] = wbc_ref[...].astype(jnp.bfloat16)
-    front_ref[rows:, :] = jnp.zeros((front_ref.shape[0] - rows, inner + bc_width), jnp.bfloat16)
+        pieces.append((wzx_ref.at[:, :, j * LANES : (j + 1) * LANES], tiles_ref.at[j]))
+    arrivals = [
+        pltpu.make_async_copy(source, target, sems.at[k])
+        for k, (source, target) in enumerate(pieces)
+    ]
+    for copy in arrivals:
+        copy.start()
+    front_v[rows:, :] = jnp.zeros((front_v.shape[0] - rows, inner + bc_width), jnp.bfloat16)
     pad_ref[...] = jnp.zeros_like(pad_ref)
-    pad_ref[0 : wdt_ref.shape[0], 0:rows] = wdt_ref[...]
     lane = lax.broadcasted_iota(jnp.int32, (TILE_ROWS, LANES), 1)
     wanted = jnp.zeros((TILE_ROWS, LANES), jnp.float32)
     for r in range(req_ref.shape[0]):
         wanted = jnp.where(lane == r, req_ref[r].astype(jnp.float32), wanted)
     pad_ref[:, rows : rows + LANES] = wanted
-    front_ref[rows : rows + TILE_ROWS, 0 : rows + LANES] = pad_ref[...].astype(jnp.bfloat16)
+    arrivals[0].wait()
+    pad_ref[0 : dt_ref.shape[0], 0:rows] = dt_ref[...]
+    front_v[rows : rows + TILE_ROWS, 0 : rows + LANES] = pad_ref[...].astype(jnp.bfloat16)
+    arrivals[1].wait()
     piece = rows + LANES
     for i in range(tail_ref.shape[1] // piece):
         at = rows + TILE_ROWS * (i + 1)
-        front_ref[at : at + TILE_ROWS, 0:piece] = tail_ref[:, i * piece : (i + 1) * piece]
+        front_v[at : at + TILE_ROWS, 0:piece] = tail_ref[:, i * piece : (i + 1) * piece]
+    arrivals[2].wait()
+    front_v[0:rows, inner:] = bc_ref[...].astype(jnp.bfloat16)
+    for j in range(tiles):
+        arrivals[3 + j].wait()
+        pair = tiles_ref.at[j].reshape(2 * rows, LANES)
+        front_v[0:rows, j * LANES : (j + 1) * LANES] = pair[pl.ds(1, rows, stride=2), :].astype(
+            jnp.bfloat16
+        )
+    front_out = pltpu.make_async_copy(front_v, front_ref, sems.at[3 + tiles])
+    front_out.start()
+    for j in range(tiles):
+        pair = tiles_ref.at[j].reshape(2 * rows, LANES)
+        gate_v[:, j * LANES : (j + 1) * LANES] = pair[pl.ds(0, rows, stride=2), :].astype(
+            jnp.bfloat16
+        )
+    gate_out = pltpu.make_async_copy(gate_v, gate_ref, sems.at[4 + tiles])
+    gate_out.start()
+    front_out.wait()
+    gate_out.wait()
+
+
+def facts_kernel(
+    ids_ref,
+    hidden_hbm,
+    gain_ref,
+    normed_ref,
+    meta_ref,
+    order_ref,
+    pen_ref,
+    hidden_ref,
+    sem,
+):
+    tok = hidden_ref.shape[0]
+    arrival = pltpu.make_async_copy(hidden_hbm, hidden_ref, sem)
+    arrival.start()
+    position = lax.axis_index("dp")
+    start = pl.multiple_of(position * tok, tok)
+    ids_i = ids_ref[:, pl.ds(start, tok)]
+    behind = pl.multiple_of(jnp.maximum(start - LANES, 0), LANES)
+    edge = ids_ref[:, pl.ds(behind, LANES)]
+    edge = jnp.where(position > 0, edge, -1)
+    ahead = pl.multiple_of(jnp.minimum(start + tok, ids_ref.shape[1] - LANES), LANES)
+    after = jnp.where(start + tok < ids_ref.shape[1], ids_ref[:, pl.ds(ahead, LANES)], -1)
+    after = after[:, 0:1].astype(jnp.float32)
+    long = jnp.concatenate([edge, ids_i], axis=1).astype(jnp.float32)
+    ids = ids_i.astype(jnp.float32)
+    index = lax.broadcasted_iota(jnp.int32, (1, tok), 1)
+    before, last = long[:, LANES - 1 : LANES], ids[:, tok - 1 : tok]
+    middle = ids[:, BLOCK - 1 : BLOCK]
+    one, zero = jnp.ones((1, tok), jnp.float32), jnp.zeros((1, tok), jnp.float32)
+    flag = lambda what: jnp.where(what, one, zero)
+    rows = [flag(ids == pltpu.roll(long, k, 1)[:, LANES:]) for k in (1, 2, 3)]
+    rows.append(flag(ids == before))
+    rows.append(flag((ids == middle) & (index >= BLOCK)))
+    rows.append(flag((ids == middle) & (index < BLOCK)))
+    rows.append(ids)
+    rows.append(flag(ids == last))
+    rows.append(flag((ids != last) | (after != last)))
+    rows = jnp.concatenate(rows + [jnp.zeros((LANES - len(rows), tok), jnp.float32)], axis=0)
+    facts = rows.T
+    meta_ref[...] = facts
+    column = facts[:, 6:7]
+    here = lax.broadcasted_iota(jnp.int32, (tok, tok), 0)
+    there = lax.broadcasted_iota(jnp.int32, (tok, tok), 1)
+    same = column == ids
+    order_ref[0:tok, :] = jnp.where(there <= here, 1.0, 0.0).astype(jnp.bfloat16)
+    order_ref[tok:, :] = jnp.where((there > here) & same, 1.0, 0.0).astype(jnp.bfloat16)
+    pen = jnp.where((there <= here) & same, 0.0, NEVER)
+    for b in range(tok // BLOCK):
+        own = slice(b * BLOCK, (b + 1) * BLOCK)
+        pen_ref[b] = pen[own, own]
+    arrival.wait()
+    hidden = hidden_ref[...].astype(jnp.float32)
+    normed_ref[...] = (hidden * rms_scale(hidden) * gain_ref[...]).astype(jnp.bfloat16)
+
+
+def scale_kernel(w_ref, gain_ref, whole_ref, half_ref):
+    rows, model = w_ref.shape
+    half = half_ref.shape[1]
+    gain = jnp.broadcast_to(gain_ref[...], (LANES, rows)).T
+    for j in range(model // LANES):
+        own = slice(j * LANES, (j + 1) * LANES)
+        whole_ref[:, own] = (w_ref[:, own].astype(jnp.float32) * gain).astype(jnp.bfloat16)
+    at = pl.multiple_of((lax.axis_index("dp") % 2) * half, half)
+    half_ref[...] = whole_ref[:, pl.ds(at, half)]
 
 
 def front_kernel(
-    place_ref,
     normed_ref,
     own_ref,
     near_ref,
@@ -329,7 +433,8 @@
     taps_bc_ref,
     meta_ref,
     order_ref,
-    head_ref,
+    bias_ref,
+    decay_ref,
     conv_ref,
     stepx_ref,
     faded_ref,
@@ -342,7 +447,7 @@
     ext_ref,
     sems,
 ):
-    position = place_ref[0]
+    position = lax.axis_index("dp")
     model = normed_ref.shape[1]
     tok = normed_ref.shape[0]
     rows = model // extra_ref.shape[0]
@@ -387,10 +492,16 @@
     for at in range(0, width, 2 * LANES):
         stop = min(at + 2 * LANES, width)
         ext_ref[TILE_ROWS:, at:stop] = dot32(normed, w_ref[:, at:stop])
-    raw = dot32(normed, dtw_ref[...], 1, 1) + head_ref[0:1, :]
+    head_lane = lax.broadcasted_iota(jnp.int32, (1, LANES), 1)
+    bias = jnp.zeros((1, LANES), jnp.float32)
+    decay = jnp.zeros((1, LANES), jnp.float32)
+    for h in range(bias_ref.shape[0]):
+        bias = jnp.where(head_lane == h, bias_ref[h], bias)
+        decay = jnp.where(head_lane == h, decay_ref[h], decay)
+    raw = dot32(normed, dtw_ref[...], 1, 1) + bias
     step = jnp.maximum(raw, 0.0) + jnp.log1p(jnp.exp(-jnp.abs(raw)))
     lane = lax.broadcasted_iota(jnp.int32, (tok, LANES), 1)
-    rate = jnp.where(lane < TILE_ROWS, -step * jnp.exp(head_ref[1:2, :]), 0.0)
+    rate = jnp.where(lane < TILE_ROWS, -step * jnp.exp(decay), 0.0)
     high = rate.astype(jnp.bfloat16).astype(jnp.float32)
     rest = rate - high
     mid = rest.astype(jnp.bfloat16).astype(jnp.float32)
@@ -435,8 +546,17 @@
         middle_ref[own, :] = dot32(to_middle, b_middle).astype(jnp.bfloat16)
 
 
+def table_kernel(conv_ref, faded_ref, meta_ref, table_ref):
+    inner = faded_ref.shape[0]
+    state_width = table_ref.shape[2]
+    b_all = conv_ref[:, inner : inner + state_width].astype(jnp.float32)
+    faded = faded_ref[...]
+    for g in range(table_ref.shape[0]):
+        ended = jnp.where(meta_ref[:, 6:7] == g, meta_ref[:, 8:9], 0.0)
+        table_ref[g] = dot32(faded, (b_all * ended).astype(jnp.bfloat16)).astype(jnp.bfloat16)
+
+
 def local_kernel(
-    place_ref,
     normed_ref,
     own_ref,
     near_ref,
@@ -444,7 +564,6 @@
     last_ref,
     conv_ref,
     stepx_ref,
-    faded_ref,
     prefix_ref,
     middle_ref,
     meta_ref,
@@ -452,11 +571,10 @@
     skip_ref,
     y_ref,
     gate_ref,
-    table_ref,
     w_ref,
     sems,
 ):
-    position = place_ref[0]
+    position = lax.axis_index("dp")
     inner = y_ref.shape[1]
     rows = own_ref.shape[0]
     state_width = middle_ref.shape[1]
@@ -484,7 +602,7 @@
         for q in range(inner // LANES):
             own = slice(q * LANES, (q + 1) * LANES)
             x_pair = conv_ref[own_rows, own].astype(jnp.float32)
-            out = x_pair * skip_ref[:, own]
+            out = x_pair * jnp.where(lane < head_dim, skip_ref[2 * q], skip_ref[2 * q + 1])
             if b > 0:
                 out = out + widen(carried, q, head_dim) * from_middle[:, own]
             sx = stepx_ref[own_rows, own].astype(jnp.float32)
@@ -495,80 +613,107 @@
                 kept = (lane < head_dim) if side == 0 else (lane >= head_dim)
                 out = out + dot32(mixing, jnp.where(kept, sx, 0.0).astype(jnp.bfloat16))
             y_ref[own_rows, own] = out
-    b_all = conv_ref[:, inner : inner + state_width].astype(jnp.float32)
-    faded = faded_ref[...]
-    for g in range(table_ref.shape[0]):
-        ended = jnp.where(meta_ref[:, 6:7] == g, meta_ref[:, 8:9], 0.0)
-        table_ref[g] = dot32(faded, (b_all * ended).astype(jnp.bfloat16)).astype(jnp.bfloat16)
     for copy in copies:
         copy.wait()
     normed = normed_ref[...]
     gate_ref[...] = silu_tanh(dot32(normed, w_ref[...]))
 
 
-def gate_kernel(place_ref, enter_ref, conv_ref, prefix_ref, meta_ref, y_ref, z_ref, *outs):
-    scratch = outs[-1]
-    outs = outs[:-1]
+def before_device(ids_ref, position, tok):
+    return jnp.where(position > 0, ids_ref[jnp.maximum(position * tok - 1, 0)], -1)
+
+
+def gate_kernel(ids_ref, enter_ref, conv_ref, prefix_ref, meta_ref, y_ref, z_ref, *outs):
+    scratch, add_ref = outs[-1], outs[-2]
+    outs = outs[:-2]
     inner = y_ref.shape[1]
     state_width = enter_ref.shape[1]
     head_dim = LANES // 2
+    tok = y_ref.shape[0]
     c_all = conv_ref[:, inner + state_width :]
     inter = dot32(c_all, enter_ref[...], 1, 1)
-    carried = jnp.exp(prefix_ref[...]) * meta_ref[:, 3:4]
+    prefix = prefix_ref[...]
+    carried = jnp.exp(prefix) * meta_ref[:, 3:4]
     for q in range(inner // LANES):
         own = slice(q * LANES, (q + 1) * LANES)
         value = y_ref[:, own] + widen(carried, q, head_dim) * inter[:, own]
         scratch[:, own] = (value * z_ref[:, own]).astype(jnp.bfloat16)
+    position = lax.axis_index("dp")
+    before = before_device(ids_ref, position, tok)
+    stop = (position + 1) * tok
+    after = ids_ref[jnp.minimum(stop, ids_ref.shape[0] - 1)]
+    goes_on = (after == before) & (stop < ids_ref.shape[0])
+    ended = (ids_ref[position * tok] == before) & ((ids_ref[stop - 1] != before) | ~goes_on)
+    inside = jnp.where(meta_ref[:, 3:4] > 0.0, prefix, 0.0)
+    gain = jnp.exp(jnp.min(inside, axis=0, keepdims=True)) * jnp.where(ended, 1.0, 0.0)
+    for h in range(inner // head_dim):
+        own = slice(h * head_dim, (h + 1) * head_dim)
+        term = gain[:, h : h + 1] * enter_ref[own, :].astype(jnp.float32)
+        add_ref[own, :] = term.astype(jnp.bfloat16)
     members = len(outs)
     part = y_ref.shape[0] // (2 * members)
-    half = place_ref[5]
+    half = lax.axis_index("head") // 4
     for j, out in enumerate(outs):
-        member = jnp.bitwise_xor(place_ref[4], j)
+        member = jnp.bitwise_xor(lax.axis_index("head") % 4, j)
         for k, side in enumerate((1 - half, half)):
             at = pl.multiple_of((side * members + member) * part, part)
             out[k * part : (k + 1) * part, :] = scratch[pl.ds(at, part), :]
 
 
-def ends_kernel(place_ref, table_ref, enter_ref, prefix_ref, out_ref):
-    out_ref[...] = table_ref[...]
-    head_dim = LANES // 2
-
-    @pl.when(place_ref[2] == 1)
-    def add():
-        prompt = place_ref[1]
-        gain = jnp.exp(prefix_ref[pl.ds(place_ref[3], 1), :])
-        for h in range(out_ref.shape[1] // head_dim):
-            own = slice(h * head_dim, (h + 1) * head_dim)
-            term = gain[:, h : h + 1] * enter_ref[own, :].astype(jnp.float32)
-            old = table_ref[prompt, own, :].astype(jnp.float32)
-            out_ref[prompt, own, :] = (old + term).astype(jnp.bfloat16)
-
-
-def pick_kernel(wanted_ref, table_ref, other_ref, keep_ref, send_ref):
+def pick_kernel(
+    ids_ref,
+    own_ref,
+    far_ref,
+    table_ref,
+    other_ref,
+    add_ref,
+    other_add_ref,
+    keep_ref,
+    send_ref,
+    far_v,
+    sem,
+):
     count = keep_ref.shape[0]
-    for k, out in enumerate((keep_ref, send_ref)):
-        for r in range(count):
-            g = wanted_ref[k * count + r]
-            total = table_ref[g].astype(jnp.float32) + other_ref[g].astype(jnp.float32)
-            out[r] = total.astype(jnp.bfloat16)
-
-
-def out_kernel(place_ref, *refs):
+    rows = far_ref.shape[0] - 4 * TILE_ROWS
+    arrival = pltpu.make_async_copy(
+        far_ref.at[rows : rows + TILE_ROWS, rows : rows + LANES], far_v, sem
+    )
+    arrival.start()
+    position = lax.axis_index("dp")
+    tok = ids_ref.shape[0] // lax.axis_size("dp")
+    before = before_device(ids_ref, position, tok)
+    other_before = before_device(ids_ref, jnp.bitwise_xor(position, 1), tok)
+    add = add_ref[...].astype(jnp.float32)
+    other_add = other_add_ref[...].astype(jnp.float32)
+
+    def pick(g):
+        total = table_ref[g].astype(jnp.float32) + other_ref[g].astype(jnp.float32)
+        total = total + jnp.where(g == before, 1.0, 0.0) * add
+        return total + jnp.where(g == other_before, 1.0, 0.0) * other_add
+
+    arrival.wait()
+    wanted = far_v[...].astype(jnp.float32)[0:1, :]
+    lane = lax.broadcasted_iota(jnp.int32, (1, LANES), 1)
+    for r in range(count):
+        other = jnp.sum(jnp.where(lane == r, wanted, 0.0)).astype(jnp.int32)
+        send_ref[r] = pick(other).astype(jnp.bfloat16)
+    for r in range(count):
+        keep_ref[r] = pick(own_ref[r]).astype(jnp.bfloat16)
+
+
+def out_kernel(*refs):
     members = 4
-    gated, own_w = refs[:members], refs[members]
-    near, swapped = refs[members + 1 : 2 * members], refs[2 * members : 3 * members - 1]
-    send_ref, keep_ref = refs[3 * members - 1 :]
-    core = place_ref[6]
-    half = near[0].shape[1]
+    gated, buffers = refs[:members], refs[members : 3 * members - 1]
+    send_ref, keep_ref, own_ref, part_ref, sems = refs[3 * members - 1 :]
+    core = lax.axis_index("dp") % 2
+    half = part_ref.shape[2]
     part = send_ref.shape[0]
+    copies = [pltpu.make_async_copy(buffers[0], own_ref, sems.at[0])]
+    for k, buffer in enumerate(buffers[1:]):
+        copies.append(pltpu.make_async_copy(buffer, part_ref.at[k], sems.at[k + 1]))
+    for copy in copies:
+        copy.start()
     values = [g[...] for g in gated]
-    for others, side in ((near, core), (swapped, 1 - core)):
-        at = pl.multiple_of(side * half, half)
-        total = dot32(values[0], own_w[:, pl.ds(at, half)])
-        for value, weights in zip(values[1:], others):
-            total = total + dot32(value, weights[...])
-        send_ref[:, pl.ds(at, half)] = total[0:part].astype(jnp.bfloat16)
-        keep_ref[:, pl.ds(at, half)] = total[part:]
     squares = jnp.zeros((2 * part, 1), jnp.float32)
     for value in values:
         wide = value.astype(jnp.float32)
@@ -579,16 +724,34 @@
     low = squares[0:part] - high
     send_ref[:, model:] = jnp.where(lane == 0, high, low).astype(jnp.bfloat16)
     keep_ref[:, model:] = jnp.broadcast_to(squares[part:], (part, LANES))
-
-
-def finish_kernel(inner_total, hidden_ref, keep_ref, got_ref, out_ref):
-    model = hidden_ref.shape[1]
+    copies[0].wait()
+    for k, side in enumerate((core, 1 - core)):
+        at = pl.multiple_of(side * half, half)
+        total = dot32(values[0], own_ref[:, pl.ds(at, half)])
+        for j in range(1, members):
+            slot = k * (members - 1) + j - 1
+            copies[slot + 1].wait()
+            total = total + dot32(values[j], part_ref[slot])
+        send_ref[:, pl.ds(at, half)] = total[0:part].astype(jnp.bfloat16)
+        keep_ref[:, pl.ds(at, half)] = total[part:]
+
+
+def finish_kernel(inner_total, hidden_all, keep_ref, got_ref, out_ref, hidden_ref, sem):
+    part, model = hidden_ref.shape
+    at = pl.multiple_of(lax.axis_index("head") * part, part)
+    arrival = pltpu.make_async_copy(hidden_all.at[pl.ds(at, part)], hidden_ref, sem)
+    arrival.start()
     squares = keep_ref[:, model : model + 1]
     squares = squares + got_ref[:, model : model + 1].astype(jnp.float32)
     squares = squares + got_ref[:, model + 1 : model + 2].astype(jnp.float32)
     scale = lax.rsqrt(squares / inner_total + EPSILON)
     total = keep_ref[:, 0:model] + got_ref[:, 0:model].astype(jnp.float32)
+    arrival.wait()
     out_ref[...] = (hidden_ref[...].astype(jnp.float32) + scale * total).astype(jnp.bfloat16)
+
+
+def join_kernel(keep_ref, far_ref, out_ref):
+    out_ref[...] = keep_ref[...].astype(jnp.float32) + far_ref[...].astype(jnp.float32)
 
 
 def fused_on_device(
@@ -615,94 +778,97 @@
     width = inner + 2 * state_width
     peers = lax.axis_size("dp")
     head_count = lax.axis_size("head")
-    position = lax.axis_index("dp")
-    head_index = lax.axis_index("head")
     bf16, f32 = jnp.bfloat16, jnp.float32
     shape = jax.ShapeDtypeStruct
     smem = pl.BlockSpec(memory_space=pltpu.SMEM)
-    anywhere = pl.BlockSpec(memory_space=pl.ANY)
-
-    tiles = inner // LANES
-    flat = w_zx.reshape(rows, 2, tiles, LANES).transpose(0, 2, 1, 3).reshape(-1, LANES)
+    in_hbm = pl.BlockSpec(memory_space=pltpu.HBM)
+
     extra = TILE_ROWS * (1 + model // (rows + LANES))
     front_own, gate_own = pl.pallas_call(
         pack_kernel,
         name="pack_weights",
-        grid=(1,),
         out_shape=(shape((rows + extra, width), bf16), shape((rows, inner), bf16)),
-        in_specs=[
-            smem,
-            pl.BlockSpec(flat.shape, lambda i: (0, 0)),
-            pl.BlockSpec(w_bc.shape, lambda i: (0, 0)),
-            pl.BlockSpec((heads, rows), lambda i: (0, 0)),
-            pl.BlockSpec((TILE_ROWS, model), lambda i: (tok // TILE_ROWS - 1, 0)),
+        in_specs=[smem] + [in_hbm] * 4,
+        out_specs=(in_hbm, in_hbm),
+        scratch_shapes=[
+            pltpu.VMEM((inner // LANES, rows, 2, LANES), f32),
+            pltpu.VMEM(w_bc.shape, f32),
+            pltpu.VMEM((heads, rows), f32),
+            pltpu.VMEM((TILE_ROWS, model), bf16),
+            pltpu.VMEM((rows + extra, width), bf16),
+            pltpu.VMEM((rows, inner), bf16),
+            pltpu.VMEM((TILE_ROWS, rows + LANES), f32),
+            pltpu.SemaphoreType.DMA((5 + inner // LANES,)),
         ],
-        out_specs=(
-            pl.BlockSpec((rows + extra, width), lambda i: (0, 0)),
-            pl.BlockSpec((rows, inner), lambda i: (0, 0)),
+        compiler_params=kernel_params(60),
+    )(request_prompt, w_zx, w_bc, w_dt.T, hidden)
+    blocks = tok // BLOCK
+    normed, meta, order, pen = pl.pallas_call(
+        facts_kernel,
+        name="norm_and_token_facts",
+        out_shape=(
+            shape((tok, model), bf16),
+            shape((tok, LANES), f32),
+            shape((2 * tok, tok), bf16),
+            shape((blocks, BLOCK, BLOCK), f32),
         ),
-        scratch_shapes=[pltpu.VMEM((TILE_ROWS, rows + LANES), f32)],
-        compiler_params=kernel_params(),
-    )(request_prompt, flat, w_bc, w_dt.T, hidden)
+        in_specs=in_vmem(1) + [in_hbm] + in_vmem(1),
+        out_specs=tuple(in_vmem(4)),
+        scratch_shapes=[pltpu.VMEM((tok, model), bf16), pltpu.SemaphoreType.DMA],
+        compiler_params=kernel_params(16),
+        cost_estimate=pl.CostEstimate(
+            flops=10 * tok * model, bytes_accessed=8_000_000, transcendentals=tok
+        ),
+    )(token_prompt[None, :], hidden, in_gain[None, :])
+    half_width = model // 2
+    scaled_out, half_out = pl.pallas_call(
+        scale_kernel,
+        name="scale_out_rows",
+        out_shape=(shape(w_out.shape, bf16), shape((inner, half_width), bf16)),
+        in_specs=in_vmem(2),
+        out_specs=tuple(in_vmem(2)),
+        compiler_params=kernel_params(8),
+    )(w_out, out_gain[None, :])
+    near_out = [exchange(half_out, "head", bits) for bits in (1, 2)]
+
     front_far = exchange(front_own, "dp", 2)
     front_near = exchange(front_own, "dp", 1)
+    front_far, gate_own, normed, meta, order, pen = lax.optimization_barrier(
+        (front_far, gate_own, normed, meta, order, pen)
+    )
+    front_last = exchange(front_far, "dp", 1)
     gate_far = exchange(gate_own, "dp", 2)
     gate_near = exchange(gate_own, "dp", 1)
+    gate_last = exchange(gate_far, "dp", 1)
+    half_out, *near_out, front_last = lax.optimization_barrier((half_out, *near_out, front_last))
+    near_out.append(exchange(half_out, "head", 3))
+    swapped_out = [exchange(part, "dp", 1) for part in near_out]
+
+    half_width = model // 2
+    scaled_out, half_out = pl.pallas_call(
+        scale_kernel,
+        name="scale_out_rows",
+        out_shape=(shape(w_out.shape, bf16), shape((inner, half_width), bf16)),
+        in_specs=in_vmem(2),
+        out_specs=tuple(in_vmem(2)),
+        compiler_params=kernel_params(8),
+    )(w_out, out_gain[None, :])
+    near_out = [exchange(half_out, "head", bits) for bits in (1, 2)]
+
+    front_far = exchange(front_own, "dp", 2)
+    front_near = exchange(front_own, "dp", 1)
+    front_far, gate_own, normed, meta, order, pen = lax.optimization_barrier(
+        (front_far, gate_own, normed, meta, order, pen)
+    )
     front_last = exchange(front_far, "dp", 1)
+    gate_far = exchange(gate_own, "dp", 2)
+    gate_near = exchange(gate_own, "dp", 1)
     gate_last = exchange(gate_far, "dp", 1)
-
-    core = position % 2
-    scaled_out = (w_out.astype(f32) * out_gain[:, None]).astype(bf16)
-    half_width = model // 2
-    half_out = lax.dynamic_slice_in_dim(scaled_out, core * half_width, half_width, 1)
-    near_out = [exchange(half_out, "head", bits) for bits in (1, 2, 3)]
+    half_out, *near_out, front_last = lax.optimization_barrier((half_out, *near_out, front_last))
+    near_out.append(exchange(half_out, "head", 3))
     swapped_out = [exchange(part, "dp", 1) for part in near_out]
 
-    ids_long = jnp.concatenate([jnp.full((3,), -1, jnp.int32), token_prompt, jnp.full((1,), -1, jnp.int32)])
-    window = lax.dynamic_slice_in_dim(ids_long, position * tok, tok + 4)
-    ids = window[3 : 3 + tok]
-    before, after = window[2], window[3 + tok]
-    end_id, middle_id = ids[tok - 1], ids[BLOCK - 1]
-    index = jnp.arange(tok, dtype=jnp.int32)
-    facts = [ids == window[3 - k : 3 - k + tok] for k in (1, 2, 3)]
-    facts += [
-        ids == before,
-        (ids == middle_id) & (index >= BLOCK),
-        (ids == middle_id) & (index < BLOCK),
-        ids,
-        ids == end_id,
-        (ids != end_id) | (after != end_id),
-    ]
-    meta = jnp.stack([fact.astype(f32) for fact in facts], axis=1)
-    meta = jnp.pad(meta, ((0, 0), (0, LANES - meta.shape[1])))
-    entered = jnp.sum((ids == before).astype(jnp.int32))
-    applies = (entered > 0) & ((before != end_id) | (after != end_id))
-    place = jnp.stack(
-        [
-            position,
-            jnp.maximum(before, 0),
-            applies.astype(jnp.int32),
-            jnp.maximum(entered - 1, 0),
-            head_index % 4,
-            head_index // 4,
-            core,
-            0,
-        ]
-    ).astype(jnp.int32)
-    same = ids[:, None] == ids[None, :]
-    order = jnp.concatenate(
-        [index[None, :] <= index[:, None], (index[None, :] > index[:, None]) & same]
-    ).astype(bf16)
-    blocks = tok // BLOCK
-    pen = jnp.where(same & (index[None, :] <= index[:, None]), 0.0, NEVER).astype(f32)
-    pen = jnp.stack(
-        [pen[b * BLOCK : (b + 1) * BLOCK, b * BLOCK : (b + 1) * BLOCK] for b in range(blocks)]
-    )
     head_rows = jnp.pad(jnp.stack([dt_bias, a_log]), ((0, 0), (0, LANES - heads)))
-    skip_row = jnp.repeat(skip_gain, inner // heads)[None, :]
-
-    hidden_f = hidden.astype(f32)
-    normed = (hidden_f * rms_scale(hidden_f) * in_gain).astype(bf16)
 
     conv, stepx, faded, prefix, leaving, middle = pl.pallas_call(
         front_kernel,
@@ -715,7 +881,7 @@
             shape((inner, state_width), bf16),
             shape((inner, state_width), bf16),
         ),
-        in_specs=[smem] + in_vmem(1) + [anywhere] * 4 + in_vmem(6),
+        in_specs=in_vmem(1) + [in_hbm] * 4 + in_vmem(5) + [smem] * 2,
         out_specs=tuple(in_vmem(6)),
         scratch_shapes=[
             pltpu.VMEM((model, width), bf16),
@@ -724,12 +890,11 @@
             pltpu.VMEM((TILE_ROWS + tok, width), f32),
             pltpu.SemaphoreType.DMA((2 * peers,)),
         ],
-        compiler_params=kernel_params(),
+        compiler_params=kernel_params(24),
         cost_estimate=pl.CostEstimate(
             flops=2 * tok * model * width, bytes_accessed=8_000_000, transcendentals=500_000
         ),
     )(
-        place,
         normed,
         front_own,
         front_near,
@@ -740,28 +905,40 @@
         conv_bc,
         meta,
         order,
-        head_rows,
+        dt_bias,
+        a_log,
     )
 
     entering = lax.ppermute(leaving, "dp", [(i, i + 1) for i in range(peers - 1)])
 
-    y_local, gate, table = pl.pallas_call(
+    table = pl.pallas_call(
+        table_kernel,
+        name="sum_ended_states",
+        out_shape=shape((PROMPTS, inner, state_width), bf16),
+        in_specs=in_vmem(3),
+        out_specs=in_vmem(1)[0],
+        compiler_params=kernel_params(8),
+        cost_estimate=pl.CostEstimate(
+            flops=2 * tok * inner * state_width * PROMPTS, bytes_accessed=2_000_000, transcendentals=0
+        ),
+    )(conv, faded, meta)
+    table_near = exchange(table, "dp", 1)
+
+    y_local, gate = pl.pallas_call(
         local_kernel,
         name="mix_within_blocks",
         out_shape=(
             shape((tok, inner), f32),
             shape((tok, inner), f32),
-            shape((PROMPTS, inner, state_width), bf16),
         ),
-        in_specs=[smem] + in_vmem(1) + [anywhere] * 4 + in_vmem(8),
-        out_specs=tuple(in_vmem(3)),
+        in_specs=in_vmem(1) + [in_hbm] * 4 + in_vmem(6) + [smem],
+        out_specs=tuple(in_vmem(2)),
         scratch_shapes=[pltpu.VMEM((model, inner), bf16), pltpu.SemaphoreType.DMA((peers,))],
-        compiler_params=kernel_params(),
+        compiler_params=kernel_params(24),
         cost_estimate=pl.CostEstimate(
             flops=2 * tok * model * inner, bytes_accessed=8_000_000, transcendentals=1_000_000
         ),
     )(
-        place,
         normed,
         gate_own,
         gate_near,
@@ -769,45 +946,37 @@
         gate_last,
         conv,
         stepx,
-        faded,
         prefix,
         middle,
         meta,
         pen,
-        skip_row,
+        skip_gain,
     )
 
     out_rows = tok // head_count
-    gated = pl.pallas_call(
+    *gated, add = pl.pallas_call(
         gate_kernel,
         name="add_entering_and_gate",
-        out_shape=tuple(shape((2 * out_rows, inner), bf16) for _ in range(4)),
+        out_shape=tuple(shape((2 * out_rows, inner), bf16) for _ in range(4))
+        + (shape((inner, state_width), bf16),),
         in_specs=[smem] + in_vmem(6),
-        out_specs=tuple(in_vmem(4)),
+        out_specs=tuple(in_vmem(5)),
         scratch_shapes=[pltpu.VMEM((tok, inner), bf16)],
-        compiler_params=kernel_params(),
-    )(place, entering, conv, prefix, meta, y_local, gate)
+        compiler_params=kernel_params(8),
+    )(token_prompt, entering, conv, prefix, meta, y_local, gate)
     gated_in = [gated[0]] + [exchange(gated[bits], "head", bits) for bits in (1, 2, 3)]
 
-    table = pl.pallas_call(
-        ends_kernel,
-        name="add_entering_to_ends",
-        out_shape=shape(table.shape, bf16),
-        in_specs=[smem] + in_vmem(3),
-        out_specs=in_vmem(1)[0],
-        compiler_params=kernel_params(),
-    )(place, table, entering, prefix)
-    table_near = exchange(table, "dp", 1)
+    near_add = exchange(add, "dp", 1)
     requests = request_prompt.shape[0]
-    other_wants = front_far[rows, rows : rows + requests].astype(jnp.int32)
     keep, send = pl.pallas_call(
         pick_kernel,
         name="pick_request_states",
         out_shape=(shape((requests, inner, state_width), bf16),) * 2,
-        in_specs=[smem] + in_vmem(2),
+        in_specs=[smem, smem, in_hbm] + in_vmem(4),
         out_specs=tuple(in_vmem(2)),
-        compiler_params=kernel_params(),
-    )(jnp.concatenate([request_prompt, other_wants]), table, table_near)
+        scratch_shapes=[pltpu.VMEM((TILE_ROWS, LANES), bf16), pltpu.SemaphoreType.DMA],
+        compiler_params=kernel_params(8),
+    )(token_prompt, request_prompt, front_far, table, table_near, add, near_add)
     far = exchange(send, "dp", 2)
 
     sums_send, sums_keep = pl.pallas_call(
@@ -817,21 +986,36 @@
             shape((out_rows, model + LANES), bf16),
             shape((out_rows, model + LANES), f32),
         ),
-        in_specs=[smem] + in_vmem(11),
+        in_specs=in_vmem(4) + [in_hbm] * 7,
         out_specs=tuple(in_vmem(2)),
-        compiler_params=kernel_params(),
-    )(place, *gated_in, scaled_out, *near_out, *swapped_out)
+        scratch_shapes=[
+            pltpu.VMEM((inner, model), bf16),
+            pltpu.VMEM((6, inner, half_width), bf16),
+            pltpu.SemaphoreType.DMA((7,)),
+        ],
+        compiler_params=kernel_params(20),
+        cost_estimate=pl.CostEstimate(
+            flops=16 * out_rows * inner * model, bytes_accessed=6_000_000, transcendentals=0
+        ),
+    )(*gated_in, scaled_out, *near_out, *swapped_out)
     sums_in = exchange(sums_send, "head", 4)
-    own_hidden = lax.dynamic_slice_in_dim(hidden, head_index * out_rows, out_rows, 0)
     layer_out = pl.pallas_call(
         functools.partial(finish_kernel, inner * head_count),
         name="scale_and_add_hidden",
         out_shape=shape((out_rows, model), bf16),
-        in_specs=in_vmem(3),
+        in_specs=[in_hbm] + in_vmem(2),
         out_specs=in_vmem(1)[0],
-        compiler_params=kernel_params(),
-    )(own_hidden, sums_keep, sums_in)
-    request_states = keep.astype(f32) + far.astype(f32)
+        scratch_shapes=[pltpu.VMEM((out_rows, model), bf16), pltpu.SemaphoreType.DMA],
+        compiler_params=kernel_params(4),
+    )(hidden, sums_keep, sums_in)
+    request_states = pl.pallas_call(
+        join_kernel,
+        name="join_request_states",
+        out_shape=shape(keep.shape, f32),
+        in_specs=in_vmem(2),
+        out_specs=in_vmem(1)[0],
+        compiler_params=kernel_params(4),
+    )(keep, far)
     return (
         layer_out,
         request_states.reshape(requests, heads, inner // heads, state_width),

time: 103 us -> 75.3 us (0.73)
  local copies, waits for them, and re-layouts: 23.7 us -> 0.08 us
  other arithmetic: 14.2 us -> 0 us
  waiting for transfers between devices: 15.3 us -> 25.6 us
  between operations: 5.35 us -> 1.06 us
  starting transfers between devices: 19.5 us -> 23 us
    unnamed x63 -> x26, local copies, waits for them, and re-layouts: 17 us -> 0.07 us
    ppermute x18 -> x19, waiting for transfers between devices: 15.3 us -> 25.6 us  [exchange(): lax.ppermute(values, axis, [(i, i ^ bits) for i in range(lax.axis_size(ax...]
    convert_element_type x4 -> x0, other arithmetic: 6.02 us -> none  [the longest x1 2.2 us: fused_on_device(): order = jnp.concatenate([index[None, :] <= index[:, None], (index[None, :...]
    pallas_call x2 -> x5, Pallas kernels: 2.15 us -> 7.36 us  [the longest x1 3.21 us: fused_on_device(): pl.pallas_call(pack_kernel, name='pack_weights', out_shape=(shape((rows +...]
    ppermute x18 -> x19, starting transfers between devices: 17.4 us -> 20.8 us  [exchange(): lax.ppermute(values, axis, [(i, i ^ bits) for i in range(lax.axis_size(ax...]
    pallas_call x1, Pallas kernels: 6.15 us -> 3.13 us  [fused_on_device(): pl.pallas_call(local_kernel, name='mix_within_blocks', out_shape=(shape((...]
    another operation x4 -> x0, other arithmetic: 2.65 us -> none  [the longest x2 1.82 us: fused_on_device(): meta = jnp.stack([fact.astype(f32) for fact in facts], axis=1)]
    transpose x1 -> x0, local copies, waits for them, and re-layouts: 2.65 us -> none  [fused_on_device(): w_zx.reshape(rows, 2, tiles, LANES).transpose(0, 2, 1, 3).reshape(-1, LANES)]
  transfers between devices with their start and end apart: 19 -> 20, of which waited for: 5 -> 9; matrix products, arithmetic and copies ran while one was open for 16% -> 0% of each run, Pallas kernels for 22% -> 28%
where the time goes in v2:
time: 75.3 us; the launch traced here: 75.1 us
  waiting for transfers between devices  25.6 us (34%)
  Pallas kernels  25.3 us (34%)
  starting transfers between devices  23 us (31%)
  between operations  1.06 us (1%)
    ppermute x19, waiting for transfers between devices, exchange(): lax.ppermute(values, axis, [(i, i ^ bits) for i in range(lax.axis_size(ax...  25.6 us
    ppermute x19, starting transfers between devices, exchange(): lax.ppermute(values, axis, [(i, i ^ bits) for i in range(lax.axis_size(ax...  20.8 us
    pallas_call x1, Pallas kernels, fused_on_device(): pl.pallas_call(front_kernel, name='project_and_convolve', out_shape=(shap...  7.69 us
    pallas_call x1, Pallas kernels, fused_on_device(): pl.pallas_call(out_kernel, name='project_out', out_shape=(shape((out_rows...  3.27 us
    pallas_call x1, Pallas kernels, fused_on_device(): pl.pallas_call(pack_kernel, name='pack_weights', out_shape=(shape((rows +...  3.21 us
    pallas_call x1, Pallas kernels, fused_on_device(): pl.pallas_call(local_kernel, name='mix_within_blocks', out_shape=(shape((...  3.13 us
    ppermute x1, starting transfers between devices, fused_on_device(): lax.ppermute(leaving, 'dp', [(i, i + 1) for i in range(peers - 1)])  2.22 us
    pallas_call x1, Pallas kernels, fused_on_device(): pl.pallas_call(table_kernel, name='sum_ended_states', out_shape=shape((PR...  1.51 us
  transfers between devices with their start and end apart: 20, of which 9 were waited for; matrix products, arithmetic and copies ran while one was open for 0% of the time, Pallas kernels for 28%

profile of v2, /device:TPU:0, one launch (start us, length us, event | category | flops | bytes accessed | tf_op | source)
XLA Modules:
  0.0 75.1 jit_solution(18129750409863157566)
XLA Ops:
  0.7 3.2 %pack_weights.1 = (bf16[448,640]{1,0:T(8,128)(2,1)}, bf16[384,384]{1,0:T(8,128)(2,1)}) custom-call(s32[4]{0:T(128)} %own_ref.1, f32[384,2,384]{2,1,0:T(2,128)} %wzx_ref.1, f32[384,256]{1,0:T(8,128)} %wbc_ref.1, f32[6,384]{1,0:T(8,128)} %bitcast.5, bf16[512,1536]{1,0:T(8,128)(2,1)} %hidden_all.1), custom_call_target="tpu_custom_call" | custom-call | tf_op jit(solution)/shard_map/pack_weights/pallas_call | solution.py:787
  3.9 3.0 %collective-permute-start = (bf16[448,640]{1,0:T(8,128)(2,1)}, bf16[448,640]{1,0:T(8,128)(2,1)S(1)}, u32[]{:S(2)}, u32[]{:S(2)}) collective-permute-start(bf16[448,640]{1,0:T(8,128)(2,1)} %get-tuple-element.42.own_ref), channel_id=1, source_target_pairs={{0,16},{8,24},{16,0},{24,8},{1,17},{9,25},{17,1},{25,9},{2,18},{10... | collective-permute-start | bytes 1720328 | tf_op jit(solution)/shard_map/ppermute | solution.py:271
  7.4 1.6 %collective-permute-start.2 = (bf16[384,768]{1,0:T(8,128)(2,1)S(1)}, bf16[384,768]{1,0:T(8,128)(2,1)S(1)}, u32[]{:S(2)}, u32[]{:S(2)}) collective-permute-start(bf16[384,768]{1,0:T(8,128)(2,1)S(1)} %get-tuple-element.75), channel_id=1, source_target_pairs={{0,1},{1,0},{2,3},{3,2},{4,5},{5,4},{6,7},{7,6},{8,9},{9,8},{10,11... | collective-permute-start | bytes 1769480 | tf_op jit(solution)/shard_map/ppermute | solution.py:271
  9.0 1.6 %collective-permute-start.3 = (bf16[384,768]{1,0:T(8,128)(2,1)S(1)}, bf16[384,768]{1,0:T(8,128)(2,1)S(1)}, u32[]{:S(2)}, u32[]{:S(2)}) collective-permute-start(bf16[384,768]{1,0:T(8,128)(2,1)S(1)} %get-tuple-element.75), channel_id=1, source_target_pairs={{0,2},{1,3},{2,0},{3,1},{4,6},{5,7},{6,4},{7,5},{8,10},{9,11},{10,... | collective-permute-start | bytes 1769480 | tf_op jit(solution)/shard_map/ppermute | solution.py:271
  10.6 1.2 %norm_and_token_facts.1 = (bf16[512,1536]{1,0:T(8,128)(2,1)S(1)}, f32[512,128]{1,0:T(8,128)S(1)}, bf16[1024,512]{1,0:T(8,128)(2,1)S(1)}, f32[2,256,256]{2,1,0:T(8,128)S(1)}) custom-call(s32[1,2048]{1,0:T(1,128)S(1)} %bitcast.3, bf16[512,1536]{1,0:T(8,128)(2,1)S(1)} %copy-done, f32[1,1536]{1,0:T(1,128)S(1)} %broadcast_in_dim.11.gain_ref), custom_call_target="tpu_custom_call" | custom-call | flops 7864320 | bytes 8000000 | tf_op jit(solution)/shard_map/norm_and_token_facts/pallas_call | solution.py:806
  11.9 8.2 %collective-permute-done.far_ref = bf16[448,640]{1,0:T(8,128)(2,1)S(1)} collective-permute-done((bf16[448,640]{1,0:T(8,128)(2,1)}, bf16[448,640]{1,0:T(8,128)(2,1)S(1)}, u32[]{:S(2)}, u32[]{:S(2)}) %collective-permute-start) | collective-permute-done | bytes 573472 | tf_op jit(solution)/shard_map/ppermute | solution.py:271
  20.1 0.5 collective-permute-start.1
  20.6 1.7 %collective-permute-done.2.refs_5_ = bf16[384,768]{1,0:T(8,128)(2,1)S(1)} collective-permute-done((bf16[384,768]{1,0:T(8,128)(2,1)S(1)}, bf16[384,768]{1,0:T(8,128)(2,1)S(1)}, u32[]{:S(2)}, u32[]{:S(2)}) %collective-permute-start.2) | collective-permute-done | bytes 589856 | tf_op jit(solution)/shard_map/ppermute | solution.py:271
  22.3 1.2 %collective-permute-done.3.refs_6_ = bf16[384,768]{1,0:T(8,128)(2,1)S(1)} collective-permute-done((bf16[384,768]{1,0:T(8,128)(2,1)S(1)}, bf16[384,768]{1,0:T(8,128)(2,1)S(1)}, u32[]{:S(2)}, u32[]{:S(2)}) %collective-permute-start.3) | collective-permute-done | bytes 589856 | tf_op jit(solution)/shard_map/ppermute | solution.py:271
  23.5 1.5 %collective-permute-start.12 = (bf16[384,768]{1,0:T(8,128)(2,1)S(1)}, bf16[384,768]{1,0:T(8,128)(2,1)S(1)}, u32[]{:S(2)}, u32[]{:S(2)}) collective-permute-start(bf16[384,768]{1,0:T(8,128)(2,1)S(1)} %get-tuple-element.75), channel_id=1, source_target_pairs={{0,3},{1,2},{2,1},{3,0},{4,7},{5,6},{6,5},{7,4},{8,11},{9,10},{10,... | collective-permute-start | bytes 1769480 | tf_op jit(solution)/shard_map/ppermute | solution.py:271
  25.1 1.3 %collective-permute-start.7 = (bf16[384,384]{1,0:T(8,128)(2,1)S(1)}, bf16[384,384]{1,0:T(8,128)(2,1)S(1)}, u32[]{:S(2)}, u32[]{:S(2)}) collective-permute-start(bf16[384,384]{1,0:T(8,128)(2,1)S(1)} %copy-done.3), channel_id=1, source_target_pairs={{0,16},{8,24},{16,0},{24,8},{1,17},{9,25},{17,1},{25,9},{2,18},{10... | collective-permute-start | bytes 884744 | tf_op jit(solution)/shard_map/ppermute | solution.py:271
  26.4 7.7 %project_and_convolve.1 = (bf16[512,640]{1,0:T(8,128)(2,1)S(1)}, bf16[512,384]{1,0:T(8,128)(2,1)S(1)}, bf16[384,512]{1,0:T(8,128)(2,1)S(1)}, f32[512,128]{1,0:T(...) custom-call(bf16[512,1536]{1,0:T(8,128)(2,1)S(1)} %get-tuple-element.53.normed_ref, ...), custom_call_target="tpu_custom_call" | custom-call | flops 1006632960 | bytes 8000000 | tf_op jit(solution)/shard_map/project_and_convolve/pallas_call | solution.py:873
  34.1 1.5 %sum_ended_states.1.table_ref = bf16[8,384,128]{2,1,0:T(8,128)(2,1)S(1)} custom-call(bf16[512,640]{1,0:T(8,128)(2,1)S(1)} %get-tuple-element.60.conv_ref, bf16[384,512]{1,0:T(8,128)(2,1)S(1)} %get-tuple-element.78.faded_ref, f32[512,128]{1,0:T(8,128)S(1)} %get-tuple-element.57.meta_ref), custom_call_target="tpu_custom_call" | custom-call | flops 402653184 | bytes 2000000 | tf_op jit(solution)/shard_map/sum_ended_states/pallas_call | solution.py:914
  36.7 1.7 %collective-permute-done.6.near_ref = bf16[384,384]{1,0:T(8,128)(2,1)S(1)} collective-permute-done((bf16[384,384]{1,0:T(8,128)(2,1)S(1)}, bf16[384,384]{1,0:T(8,128)(2,1)S(1)}, u32[]{:S(2)}, u32[]{:S(2)}) %collective-permute-start.6) | collective-permute-done | bytes 294944 | tf_op jit(solution)/shard_map/ppermute | solution.py:271
  38.9 2.2 %collective-permute-start.5 = (bf16[384,128]{1,0:T(8,128)(2,1)S(1)}, bf16[384,128]{1,0:T(8,128)(2,1)S(1)}, u32[]{:S(2)}, u32[]{:S(2)}) collective-permute-start(bf16[384,128]{1,0:T(8,128)(2,1)S(1)} %get-tuple-element.59), channel_id=1, source_target_pairs={{0,8},{8,16},{16,24},{1,9},{9,17},{17,25},{2,10},{10,18},{18,26},{... | collective-permute-start | bytes 294920 | tf_op jit(solution)/shard_map/ppermute | solution.py:912
  41.1 3.1 %mix_within_blocks.1 = (f32[512,384]{1,0:T(8,128)S(1)}, f32[512,384]{1,0:T(8,128)S(1)}) custom-call(bf16[512,1536]{1,0:T(8,128)(2,1)S(1)} %get-tuple-element.53.normed_ref, bf16[384,384]{1,0:T(8,128)(2,1)S(1)} %copy-done.3, bf16[384,384]{1,0:T(8,128)(2,1)S(1)} %collective-permute-done.6.near_ref, bf16[384,384]{1,0:T(8,128)(2,1)S(1)} %collective-permute-done.7.far_ref, ...), custom_call_target="tpu_custom_call" | custom-call | flops 603979776 | bytes 8000000 | tf_op jit(solution)/shard_map/mix_within_blocks/pallas_call | solution.py:927
  44.3 1.5 %add_entering_and_gate.1 = (bf16[128,384]{1,0:T(8,128)(2,1)S(1)}, bf16[128,384]{1,0:T(8,128)(2,1)S(1)}, bf16[128,384]{1,0:T(8,128)(2,1)S(1)}, bf16[128,384]{1,0:T(8,128)(2,1)S(1)}, bf16[384,128]{1,0:T(8,128)(2,1)S(1)}) custom-call(s32[2048]{0:T(1024)S(1)} %copy-done.4, bf16[384,128]{1,0:T(8,128)(2,1)S(1)} %collective-permute-done.5.enter_ref, ...), custom_call_target="tpu_custom_call" | custom-call | tf_op jit(solution)/shard_map/add_entering_and_gate/pallas_call | solution.py:957
  45.8 1.2 %collective-permute-start.18 = (bf16[384,128]{1,0:T(8,128)(2,1)S(1)}, bf16[384,128]{1,0:T(8,128)(2,1)S(1)}, u32[]{:S(2)}, u32[]{:S(2)}) collective-permute-start(bf16[384,128]{1,0:T(8,128)(2,1)S(1)} %get-tuple-element.79.add_ref), channel_id=1, source_target_pairs={{0,8},{8,0},{16,24},{24,16},{1,9},{9,1},{17,25},{25,17},{2,10},{10... | collective-permute-start | bytes 294920 | tf_op jit(solution)/shard_map/ppermute | solution.py:271
  47.0 0.9 %collective-permute-done.18.other_add_ref = bf16[384,128]{1,0:T(8,128)(2,1)S(1)} collective-permute-done((bf16[384,128]{1,0:T(8,128)(2,1)S(1)}, bf16[384,128]{1,0:T(8,128)(2,1)S(1)}, u32[]{:S(2)}, u32[]{:S(2)}) %collective-permute-start.18) | collective-permute-done | bytes 98336 | tf_op jit(solution)/shard_map/ppermute | solution.py:271
  47.9 1.5 %collective-permute-start.9 = (bf16[128,384]{1,0:T(8,128)(2,1)S(1)}, bf16[128,384]{1,0:T(8,128)(2,1)S(1)}, u32[]{:S(2)}, u32[]{:S(2)}) collective-permute-start(bf16[128,384]{1,0:T(8,128)(2,1)S(1)} %get-tuple-element.69), channel_id=1, source_target_pairs={{0,1},{1,0},{2,3},{3,2},{4,5},{5,4},{6,7},{7,6},{8,9},{9,8},{10,11... | collective-permute-start | bytes 294920 | tf_op jit(solution)/shard_map/ppermute | solution.py:271
  49.5 1.6 %collective-permute-start.10 = (bf16[128,384]{1,0:T(8,128)(2,1)S(1)}, bf16[128,384]{1,0:T(8,128)(2,1)S(1)}, u32[]{:S(2)}, u32[]{:S(2)}) collective-permute-start(bf16[128,384]{1,0:T(8,128)(2,1)S(1)} %get-tuple-element.70), channel_id=1, source_target_pairs={{0,2},{1,3},{2,0},{3,1},{4,6},{5,7},{6,4},{7,5},{8,10},{9,11},{10,... | collective-permute-start | bytes 294920 | tf_op jit(solution)/shard_map/ppermute | solution.py:271
  51.1 1.3 %pick_request_states.1 = (bf16[4,384,128]{2,1,0:T(8,128)(2,1)S(1)}, bf16[4,384,128]{2,1,0:T(8,128)(2,1)S(1)}) custom-call(s32[2048]{0:T(1024)S(1)} %copy-done.4, s32[4]{0:T(128)S(1)} %copy-done.7, bf16[448,640]{1,0:T(8,128)(2,1)S(1)} %collective-permute-done.far_ref, bf16[8,384,128]{2,1,0:T(8,128)(2,1)S(1)} %sum_ended_states.1.table_ref, ...), custom_call_target="tpu_custom_call" | custom-call | tf_op jit(solution)/shard_map/pick_request_states/pallas_call | solution.py:971
  52.4 0.6 collective-permute-done.9.refs_1_
  53.0 0.7 collective-permute-start.19
  53.7 0.5 collective-permute-done.10.refs_2_
  54.2 2.0 %collective-permute-start.11 = (bf16[128,384]{1,0:T(8,128)(2,1)S(1)}, bf16[128,384]{1,0:T(8,128)(2,1)S(1)}, u32[]{:S(2)}, u32[]{:S(2)}) collective-permute-start(bf16[128,384]{1,0:T(8,128)(2,1)S(1)} %get-tuple-element.71), channel_id=1, source_target_pairs={{0,3},{1,2},{2,1},{3,0},{4,7},{5,6},{6,5},{7,4},{8,11},{9,10},{10,... | collective-permute-start | bytes 294920 | tf_op jit(solution)/shard_map/ppermute | solution.py:271
  56.3 3.5 %collective-permute-done.11.refs_3_ = bf16[128,384]{1,0:T(8,128)(2,1)S(1)} collective-permute-done((bf16[128,384]{1,0:T(8,128)(2,1)S(1)}, bf16[128,384]{1,0:T(8,128)(2,1)S(1)}, u32[]{:S(2)}, u32[]{:S(2)}) %collective-permute-start.11) | collective-permute-done | bytes 98336 | tf_op jit(solution)/shard_map/ppermute | solution.py:271
  59.8 3.3 %project_out.1 = (bf16[64,1664]{1,0:T(8,128)(2,1)S(1)}, f32[64,1664]{1,0:T(8,128)S(1)}) custom-call(bf16[128,384]{1,0:T(8,128)(2,1)S(1)} %get-tuple-element.68.refs_0_, bf16[128,384]{1,0:T(8,128)(2,1)S(1)} %collective-permute-done.9.refs_1_, bf16[128,384]{1,0:T(8,128)(2,1)S(1)} %collective-permute-done.10.refs_2_, ...), custom_call_target="tpu_custom_call" | custom-call | flops 603979776 | bytes 6000000 | tf_op jit(solution)/shard_map/project_out/pallas_call | solution.py:982
  63.1 2.7 %collective-permute-start.16 = (bf16[64,1664]{1,0:T(8,128)(2,1)S(1)}, bf16[64,1664]{1,0:T(8,128)(2,1)S(1)}, u32[]{:S(2)}, u32[]{:S(2)}) collective-permute-start(bf16[64,1664]{1,0:T(8,128)(2,1)S(1)} %get-tuple-element.77), channel_id=1, source_target_pairs={{0,4},{1,5},{2,6},{3,7},{4,0},{5,1},{6,2},{7,3},{8,12},{9,13},{10,... | collective-permute-start | bytes 638984 | tf_op jit(solution)/shard_map/ppermute | solution.py:271
  65.7 1.0 %join_request_states.1 = f32[4,384,128]{2,1,0:T(8,128)} custom-call(bf16[4,384,128]{2,1,0:T(8,128)(2,1)S(1)} %get-tuple-element.80.keep_ref, bf16[4,384,128]{2,1,0:T(8,128)(2,1)S(1)} %collective-permute-done.19.far_ref), custom_call_target="tpu_custom_call" | custom-call | tf_op jit(solution)/shard_map/join_request_states/pallas_call | solution.py:1011
  66.7 7.1 %collective-permute-done.16.got_ref = bf16[64,1664]{1,0:T(8,128)(2,1)S(1)} collective-permute-done((bf16[64,1664]{1,0:T(8,128)(2,1)S(1)}, bf16[64,1664]{1,0:T(8,128)(2,1)S(1)}, u32[]{:S(2)}, u32[]{:S(2)}) %collective-permute-start.16) | collective-permute-done | bytes 213024 | tf_op jit(solution)/shard_map/ppermute | solution.py:271
  73.8 1.1 %scale_and_add_hidden.1 = bf16[64,1536]{1,0:T(8,128)(2,1)} custom-call(bf16[512,1536]{1,0:T(8,128)(2,1)S(1)} %copy-done, f32[64,1664]{1,0:T(8,128)S(1)} %get-tuple-element.76.keep_ref, bf16[64,1664]{1,0:T(8,128)(2,1)S(1)} %collective-permute-done.16.got_ref), custom_call_target="tpu_custom_call" | custom-call | tf_op jit(solution)/shard_map/scale_and_add_hidden/pallas_call | solution.py:1002
  (47 shorter events, 2.2 us)
Async XLA Ops:
  0.6 6.3 %copy-start.12 = (f32[384]{0:T(512)S(1)}, f32[384]{0:T(512)}, u32[]{:S(2)}) copy-start(f32[384]{0:T(512)} %param.26) | copy-start | bytes 4612
  0.7 10.0 %copy-start = (bf16[512,1536]{1,0:T(8,128)(2,1)S(1)}, bf16[512,1536]{1,0:T(8,128)(2,1)}, u32[]{:S(2)}) copy-start(bf16[512,1536]{1,0:T(8,128)(2,1)} %hidden_all.1) | copy-start | bytes 4718596
  3.9 6.7 %copy-start.11 = (f32[1536]{0:T(1024)S(1)}, f32[1536]{0:T(1024)}, u32[]{:S(2)}) copy-start(f32[1536]{0:T(1024)} %param.17) | copy-start | bytes 18436
  3.9 6.7 %copy-start.4 = (s32[2048]{0:T(1024)S(1)}, s32[2048]{0:T(1024)}, u32[]{:S(2)}) copy-start(s32[2048]{0:T(1024)} %ids_ref.3) | copy-start | bytes 24580
  3.9 16.2 %collective-permute-start = (bf16[448,640]{1,0:T(8,128)(2,1)}, bf16[448,640]{1,0:T(8,128)(2,1)S(1)}, u32[]{:S(2)}, u32[]{:S(2)}) collective-permute-start(bf16[448,640]{1,0:T(8,128)(2,1)} %get-tuple-element.42.own_ref), channel_id=1, source_target_pairs={{0,16},{8,24},{16,0},{24,8},{1,17},{9,25},{17,1},{25,9},{2,18},{10... | collective-permute-start | bytes 1720328 | tf_op jit(solution)/shard_map/ppermute | solution.py:271
  6.9 13.2 %copy-start.2 = (bf16[448,640]{1,0:T(8,128)(2,1)S(1)}, bf16[448,640]{1,0:T(8,128)(2,1)}, u32[]{:S(2)}) copy-start(bf16[448,640]{1,0:T(8,128)(2,1)} %get-tuple-element.42.own_ref) | copy-start | bytes 1720324
  6.9 18.1 %copy-start.3 = (bf16[384,384]{1,0:T(8,128)(2,1)S(1)}, bf16[384,384]{1,0:T(8,128)(2,1)}, u32[]{:S(2)}) copy-start(bf16[384,384]{1,0:T(8,128)(2,1)} %get-tuple-element.62.own_ref) | copy-start | bytes 884740
  6.9 19.4 %copy-start.5 = (f32[4,384]{1,0:T(4,128)S(1)}, f32[4,384]{1,0:T(4,128)}, u32[]{:S(2)}) copy-start(f32[4,384]{1,0:T(4,128)} %taps_x_ref.1) | copy-start | bytes 18436
  6.9 19.4 %copy-start.6 = (f32[4,256]{1,0:T(4,128)S(1)}, f32[4,256]{1,0:T(4,128)}, u32[]{:S(2)}) copy-start(f32[4,256]{1,0:T(4,128)} %taps_bc_ref.1) | copy-start | bytes 12292
  7.0 19.4 %copy-start.8 = (f32[6]{0:T(128)S(1)}, f32[6]{0:T(128)}, u32[]{:S(2)}) copy-start(f32[6]{0:T(128)} %bias_ref.1) | copy-start | bytes 76
  7.0 19.4 %copy-start.9 = (f32[6]{0:T(128)S(1)}, f32[6]{0:T(128)}, u32[]{:S(2)}) copy-start(f32[6]{0:T(128)} %decay_ref.1) | copy-start | bytes 76
  7.4 14.9 %collective-permute-start.2 = (bf16[384,768]{1,0:T(8,128)(2,1)S(1)}, bf16[384,768]{1,0:T(8,128)(2,1)S(1)}, u32[]{:S(2)}, u32[]{:S(2)}) collective-permute-start(bf16[384,768]{1,0:T(8,128)(2,1)S(1)} %get-tuple-element.75), channel_id=1, source_target_pairs={{0,1},{1,0},{2,3},{3,2},{4,5},{5,4},{6,7},{7,6},{8,9},{9,8},{10,11... | collective-permute-start | bytes 1769480 | tf_op jit(solution)/shard_map/ppermute | solution.py:271
  9.0 14.5 %collective-permute-start.3 = (bf16[384,768]{1,0:T(8,128)(2,1)S(1)}, bf16[384,768]{1,0:T(8,128)(2,1)S(1)}, u32[]{:S(2)}, u32[]{:S(2)}) collective-permute-start(bf16[384,768]{1,0:T(8,128)(2,1)S(1)} %get-tuple-element.75), channel_id=1, source_target_pairs={{0,2},{1,3},{2,0},{3,1},{4,6},{5,7},{6,4},{7,5},{8,10},{9,11},{10,... | collective-permute-start | bytes 1769480 | tf_op jit(solution)/shard_map/ppermute | solution.py:271
  20.1 3.4 %collective-permute-start.4 = (bf16[448,640]{1,0:T(8,128)(2,1)S(1)}, bf16[448,640]{1,0:T(8,128)(2,1)S(1)}, u32[]{:S(2)}, u32[]{:S(2)}) collective-permute-start(bf16[448,640]{1,0:T(8,128)(2,1)S(1)} %collective-permute-done.far_ref), channel_id=1, source_target_pairs={{0,8},{8,0},{16,24},{24,16},{1,9},{9,1},{17,25},{25,17},{2,10},{10... | collective-permute-start | bytes 1720328 | tf_op jit(solution)/shard_map/ppermute | solution.py:271
  20.1 6.3 %collective-permute-start.1 = (bf16[448,640]{1,0:T(8,128)(2,1)S(1)}, bf16[448,640]{1,0:T(8,128)(2,1)S(1)}, u32[]{:S(2)}, u32[]{:S(2)}) collective-permute-start(bf16[448,640]{1,0:T(8,128)(2,1)S(1)} %copy-done.2), channel_id=1, source_target_pairs={{0,8},{8,0},{16,24},{24,16},{1,9},{9,1},{17,25},{25,17},{2,10},{10... | collective-permute-start | bytes 1720328 | tf_op jit(solution)/shard_map/ppermute | solution.py:271
  23.5 15.0 %collective-permute-start.12 = (bf16[384,768]{1,0:T(8,128)(2,1)S(1)}, bf16[384,768]{1,0:T(8,128)(2,1)S(1)}, u32[]{:S(2)}, u32[]{:S(2)}) collective-permute-start(bf16[384,768]{1,0:T(8,128)(2,1)S(1)} %get-tuple-element.75), channel_id=1, source_target_pairs={{0,3},{1,2},{2,1},{3,0},{4,7},{5,6},{6,5},{7,4},{8,11},{9,10},{10,... | collective-permute-start | bytes 1769480 | tf_op jit(solution)/shard_map/ppermute | solution.py:271
  25.1 11.1 %collective-permute-start.7 = (bf16[384,384]{1,0:T(8,128)(2,1)S(1)}, bf16[384,384]{1,0:T(8,128)(2,1)S(1)}, u32[]{:S(2)}, u32[]{:S(2)}) collective-permute-start(bf16[384,384]{1,0:T(8,128)(2,1)S(1)} %copy-done.3), channel_id=1, source_target_pairs={{0,16},{8,24},{16,0},{24,8},{1,17},{9,25},{17,1},{25,9},{2,18},{10... | collective-permute-start | bytes 884744 | tf_op jit(solution)/shard_map/ppermute | solution.py:271
  34.1 7.0 %copy-start.10 = (f32[6]{0:T(128)S(1)}, f32[6]{0:T(128)}, u32[]{:S(2)}) copy-start(f32[6]{0:T(128)} %skip_ref.1) | copy-start | bytes 76
  35.6 13.9 %collective-permute-start.17 = (bf16[8,384,128]{2,1,0:T(8,128)(2,1)S(1)}, bf16[8,384,128]{2,1,0:T(8,128)(2,1)S(1)}, u32[]{:S(2)}, u32[]{:S(2)}) collective-permute-start(bf16[8,384,128]{2,1,0:T(8,128)(2,1)S(1)} %sum_ended_states.1.table_ref), channel_id=1, source_target_pairs={{0,8},{8,0},{16,24},{24,16},{1,9},{9,1},{17,25},{25,17},{2,10},{10... | collective-permute-start | bytes 2359304 | tf_op jit(solution)/shard_map/ppermute | solution.py:271
  35.7 2.7 %collective-permute-start.6 = (bf16[384,384]{1,0:T(8,128)(2,1)S(1)}, bf16[384,384]{1,0:T(8,128)(2,1)S(1)}, u32[]{:S(2)}, u32[]{:S(2)}) collective-permute-start(bf16[384,384]{1,0:T(8,128)(2,1)S(1)} %copy-done.3), channel_id=1, source_target_pairs={{0,8},{8,0},{16,24},{24,16},{1,9},{9,1},{17,25},{25,17},{2,10},{10... | collective-permute-start | bytes 884744 | tf_op jit(solution)/shard_map/ppermute | solution.py:271
  36.2 2.7 %collective-permute-start.8 = (bf16[384,384]{1,0:T(8,128)(2,1)S(1)}, bf16[384,384]{1,0:T(8,128)(2,1)S(1)}, u32[]{:S(2)}, u32[]{:S(2)}) collective-permute-start(bf16[384,384]{1,0:T(8,128)(2,1)S(1)} %collective-permute-done.7.far_ref), channel_id=1, source_target_pairs={{0,8},{8,0},{16,24},{24,16},{1,9},{9,1},{17,25},{25,17},{2,10},{10... | collective-permute-start | bytes 884744 | tf_op jit(solution)/shard_map/ppermute | solution.py:271
  36.3 23.5 %collective-permute-start.13 = (bf16[384,768]{1,0:T(8,128)(2,1)S(1)}, bf16[384,768]{1,0:T(8,128)(2,1)S(1)}, u32[]{:S(2)}, u32[]{:S(2)}) collective-permute-start(bf16[384,768]{1,0:T(8,128)(2,1)S(1)} %collective-permute-done.2.refs_5_), channel_id=1, source_target_pairs={{0,8},{8,0},{16,24},{24,16},{1,9},{9,1},{17,25},{25,17},{2,10},{10... | collective-permute-start | bytes 1769480 | tf_op jit(solution)/shard_map/ppermute | solution.py:271
  38.4 21.4 %collective-permute-start.14 = (bf16[384,768]{1,0:T(8,128)(2,1)S(1)}, bf16[384,768]{1,0:T(8,128)(2,1)S(1)}, u32[]{:S(2)}, u32[]{:S(2)}) collective-permute-start(bf16[384,768]{1,0:T(8,128)(2,1)S(1)} %collective-permute-done.3.refs_6_), channel_id=1, source_target_pairs={{0,8},{8,0},{16,24},{24,16},{1,9},{9,1},{17,25},{25,17},{2,10},{10... | collective-permute-start | bytes 1769480 | tf_op jit(solution)/shard_map/ppermute | solution.py:271
  38.5 21.3 %collective-permute-start.15 = (bf16[384,768]{1,0:T(8,128)(2,1)S(1)}, bf16[384,768]{1,0:T(8,128)(2,1)S(1)}, u32[]{:S(2)}, u32[]{:S(2)}) collective-permute-start(bf16[384,768]{1,0:T(8,128)(2,1)S(1)} %collective-permute-done.12.refs_7_), channel_id=1, source_target_pairs={{0,8},{8,0},{16,24},{24,16},{1,9},{9,1},{17,25},{25,17},{2,10},{10... | collective-permute-start | bytes 1769480 | tf_op jit(solution)/shard_map/ppermute | solution.py:271
  38.9 5.4 %collective-permute-start.5 = (bf16[384,128]{1,0:T(8,128)(2,1)S(1)}, bf16[384,128]{1,0:T(8,128)(2,1)S(1)}, u32[]{:S(2)}, u32[]{:S(2)}) collective-permute-start(bf16[384,128]{1,0:T(8,128)(2,1)S(1)} %get-tuple-element.59), channel_id=1, source_target_pairs={{0,8},{8,16},{16,24},{1,9},{9,17},{17,25},{2,10},{10,18},{18,26},{... | collective-permute-start | bytes 294920 | tf_op jit(solution)/shard_map/ppermute | solution.py:912
  44.3 6.8 %copy-start.7 = (s32[4]{0:T(128)S(1)}, s32[4]{0:T(128)}, u32[]{:S(2)}) copy-start(s32[4]{0:T(128)} %own_ref.1) | copy-start | bytes 52
  45.8 2.2 %collective-permute-start.18 = (bf16[384,128]{1,0:T(8,128)(2,1)S(1)}, bf16[384,128]{1,0:T(8,128)(2,1)S(1)}, u32[]{:S(2)}, u32[]{:S(2)}) collective-permute-start(bf16[384,128]{1,0:T(8,128)(2,1)S(1)} %get-tuple-element.79.add_ref), channel_id=1, source_target_pairs={{0,8},{8,0},{16,24},{24,16},{1,9},{9,1},{17,25},{25,17},{2,10},{10... | collective-permute-start | bytes 294920 | tf_op jit(solution)/shard_map/ppermute | solution.py:271
  47.9 5.1 %collective-permute-start.9 = (bf16[128,384]{1,0:T(8,128)(2,1)S(1)}, bf16[128,384]{1,0:T(8,128)(2,1)S(1)}, u32[]{:S(2)}, u32[]{:S(2)}) collective-permute-start(bf16[128,384]{1,0:T(8,128)(2,1)S(1)} %get-tuple-element.69), channel_id=1, source_target_pairs={{0,1},{1,0},{2,3},{3,2},{4,5},{5,4},{6,7},{7,6},{8,9},{9,8},{10,11... | collective-permute-start | bytes 294920 | tf_op jit(solution)/shard_map/ppermute | solution.py:271
  49.5 4.8 %collective-permute-start.10 = (bf16[128,384]{1,0:T(8,128)(2,1)S(1)}, bf16[128,384]{1,0:T(8,128)(2,1)S(1)}, u32[]{:S(2)}, u32[]{:S(2)}) collective-permute-start(bf16[128,384]{1,0:T(8,128)(2,1)S(1)} %get-tuple-element.70), channel_id=1, source_target_pairs={{0,2},{1,3},{2,0},{3,1},{4,6},{5,7},{6,4},{7,5},{8,10},{9,11},{10,... | collective-permute-start | bytes 294920 | tf_op jit(solution)/shard_map/ppermute | solution.py:271
  53.0 12.7 %collective-permute-start.19 = (bf16[4,384,128]{2,1,0:T(8,128)(2,1)S(1)}, bf16[4,384,128]{2,1,0:T(8,128)(2,1)S(1)}, u32[]{:S(2)}, u32[]{:S(2)}) collective-permute-start(bf16[4,384,128]{2,1,0:T(8,128)(2,1)S(1)} %get-tuple-element.81), channel_id=1, source_target_pairs={{0,16},{8,24},{16,0},{24,8},{1,17},{9,25},{17,1},{25,9},{2,18},{10... | collective-permute-start | bytes 1179656 | tf_op jit(solution)/shard_map/ppermute | solution.py:271
  54.2 5.5 %collective-permute-start.11 = (bf16[128,384]{1,0:T(8,128)(2,1)S(1)}, bf16[128,384]{1,0:T(8,128)(2,1)S(1)}, u32[]{:S(2)}, u32[]{:S(2)}) collective-permute-start(bf16[128,384]{1,0:T(8,128)(2,1)S(1)} %get-tuple-element.71), channel_id=1, source_target_pairs={{0,3},{1,2},{2,1},{3,0},{4,7},{5,6},{6,5},{7,4},{8,11},{9,10},{10,... | collective-permute-start | bytes 294920 | tf_op jit(solution)/shard_map/ppermute | solution.py:271
  63.1 10.8 %collective-permute-start.16 = (bf16[64,1664]{1,0:T(8,128)(2,1)S(1)}, bf16[64,1664]{1,0:T(8,128)(2,1)S(1)}, u32[]{:S(2)}, u32[]{:S(2)}) collective-permute-start(bf16[64,1664]{1,0:T(8,128)(2,1)S(1)} %get-tuple-element.77), channel_id=1, source_target_pairs={{0,4},{1,5},{2,6},{3,7},{4,0},{5,1},{6,2},{7,3},{8,12},{9,13},{10,... | collective-permute-start | bytes 638984 | tf_op jit(solution)/shard_map/ppermute | solution.py:271
  (1 other events, 6.3 us)

commit v3 on v2

v3 whole, which is shorter than its diff:
```python
import functools

import jax
import jax.numpy as jnp
from jax import lax
from jax.experimental import pallas as pl
from jax.experimental.pallas import tpu as pltpu
from jax.sharding import PartitionSpec as P

BLOCK = 256
PROMPTS = 8


EPSILON = 1e-05


def from_behind(shard, axis, by):
    peers = lax.axis_size(axis)
    pairs = [(i, i + by) for i in range(peers) if 0 <= i + by < peers]
    return lax.ppermute(shard, axis, pairs)


def carried_in(shard, axis, combine, identity):
    peers, position = (lax.axis_size(axis), lax.axis_index(axis))
    everything = jax.tree.map(lambda part: lax.all_gather(part, axis), shard)
    start = jax.tree.map(
        lambda part, zero: jnp.broadcast_to(jnp.asarray(zero, part.dtype), part.shape),
        shard,
        identity,
    )

    def step(k, before):
        reached = k < position
        new = combine(before, jax.tree.map(lambda part: part[k], everything))
        return jax.tree.map(lambda a, b: jnp.where(reached, a, b), new, before)

    return lax.fori_loop(0, peers, step, start)


def rms_scale(values):
    return lax.rsqrt(jnp.mean(values * values, axis=-1, keepdims=True) + EPSILON)


def conv_core(extended, extended_ids, token_ids, weights):
    length = token_ids.shape[0]
    total = jnp.zeros((length, extended.shape[1]), jnp.float32)
    for offset in range(weights.shape[0]):
        same = (extended_ids[offset : offset + length] == token_ids)[:, None]
        total = total + jnp.where(
            same, weights[offset] * extended[offset : offset + length].astype(jnp.float32), 0.0
        )
    return jax.nn.silu(total).astype(jnp.bfloat16)


def block_local(x_blk, b_blk, c_blk, step_blk, rate_blk, ids_blk, before_id):
    length = ids_blk.shape[0]
    position = jnp.arange(length, dtype=jnp.int32)
    prefix = jnp.cumsum(rate_blk, axis=0)
    prefix_t = prefix.T
    same = (ids_blk[:, None] == ids_blk[None, :]) & (position[None, :] <= position[:, None])
    gaps = prefix_t[:, :, None] - prefix_t[:, None, :]
    decay = jnp.where(same[None], jnp.exp(jnp.where(same[None], gaps, 0.0)), 0.0)
    scores = jnp.dot(c_blk, b_blk.T, preferred_element_type=jnp.float32)
    mixing = (scores[None] * decay * step_blk.T[:, None, :]).astype(jnp.bfloat16)
    y_intra = jnp.einsum("hts,shp->thp", mixing, x_blk, preferred_element_type=jnp.float32)
    end_id = ids_blk[-1]
    alive = ids_blk == end_id
    weight_end = (
        jnp.where(
            alive[None, :],
            jnp.exp(jnp.where(alive[None, :], prefix_t[:, -1:] - prefix_t, 0.0)),
            0.0,
        )
        * step_blk.T
    )
    b_weighted = (weight_end[:, :, None] * b_blk[None]).astype(jnp.bfloat16)
    local_state = jnp.einsum("hsn,shp->hpn", b_weighted, x_blk, preferred_element_type=jnp.float32)
    carry_gain = jnp.where(end_id == before_id, jnp.exp(prefix_t[:, -1]), 0.0)
    return (y_intra, local_state, carry_gain, prefix)


def block_inter(c_blk, prefix, ids_blk, before_id, state_in):
    entering = ids_blk == before_id
    inter_scale = jnp.where(entering[:, None], jnp.exp(prefix), 0.0)
    return inter_scale[:, :, None] * jnp.einsum(
        "tn,hpn->thp", c_blk.astype(jnp.float32), state_in, precision=lax.Precision.HIGHEST
    )


def block_last(
    last_index, table, x_blk, b_blk, step_blk, prefix, ids_blk, before_id, state_in, start
):
    length = ids_blk.shape[0]
    position = jnp.arange(length, dtype=jnp.int32)
    prompt_ids = jnp.arange(last_index.shape[0], dtype=jnp.int32)
    local_last = last_index - start
    ends_here = (local_last >= 0) & (local_last < length)
    clipped = jnp.clip(local_last, 0, length - 1)

    def with_ends():
        prefix_t = prefix.T
        prefix_last = prefix[clipped]
        pick = (
            ends_here[:, None]
            & (ids_blk[None, :] == prompt_ids[:, None])
            & (position[None, :] <= clipped[:, None])
        )
        spans = prefix_last[:, :, None] - prefix_t[None]
        weight_last = (
            jnp.where(pick[:, None, :], jnp.exp(jnp.where(pick[:, None, :], spans, 0.0)), 0.0)
            * step_blk.T[None]
        )
        b_last = (weight_last[..., None] * b_blk[None, None]).astype(jnp.bfloat16)
        last_local = jnp.einsum("ghsn,shp->ghpn", b_last, x_blk, preferred_element_type=jnp.float32)
        last_gain = jnp.where(
            (ends_here & (prompt_ids == before_id))[:, None], jnp.exp(prefix_last), 0.0
        )
        return table + last_local + last_gain[:, :, None, None] * state_in[None]

    def without_ends():
        return table

    return lax.cond(jnp.any(ends_here), with_ends, without_ends)


def join_states(earlier, later):
    return (earlier[0] * later[0], later[0][:, None, None] * earlier[1] + later[1])


def on_device(
    hidden,
    token_prompt,
    request_prompt,
    in_gain,
    w_zx,
    w_bc,
    w_dt,
    dt_bias,
    a_log,
    conv_x,
    conv_bc,
    skip_gain,
    out_gain,
    w_out,
):
    tok_dev = hidden.shape[0]
    inner_dev = w_zx.shape[2]
    heads_dev = w_dt.shape[1]
    head_dim = inner_dev // heads_dev
    state_width = w_bc.shape[1] // 2
    taps = conv_x.shape[0]
    dp_index = lax.axis_index("dp")
    head_index = lax.axis_index("head")
    head_count = lax.axis_size("head")
    hidden_f = hidden.astype(jnp.float32)
    normed = (hidden_f * rms_scale(hidden_f) * in_gain).astype(jnp.bfloat16)
    pieces = (
        lax.all_gather(w_zx.astype(jnp.bfloat16), "dp", axis=0, tiled=True),
        lax.all_gather(w_dt.astype(jnp.bfloat16), "dp", axis=0, tiled=True),
        lax.all_gather(w_bc.astype(jnp.bfloat16), "dp", axis=0, tiled=True),
    )
    acc_zx, acc_step, acc_bc = tuple(
        (
            jnp.dot(normed, piece.reshape(piece.shape[0], -1), preferred_element_type=jnp.float32)
            for piece in pieces
        )
    )
    proj_bc = acc_bc.astype(jnp.bfloat16)
    proj_zx = acc_zx.astype(jnp.bfloat16)
    gate_z = proj_zx[:, :inner_dev]
    inner_x = proj_zx[:, inner_dev:]
    proj_dt = acc_step.astype(jnp.bfloat16)
    step_size = jax.nn.softplus(proj_dt.astype(jnp.float32) + dt_bias)
    rate = step_size * -jnp.exp(a_log)
    ids_own = lax.dynamic_slice_in_dim(token_prompt, dp_index * tok_dev, tok_dev)
    rim_start = jnp.maximum(dp_index * tok_dev - (taps - 1), 0)
    rim_ids = lax.dynamic_slice_in_dim(token_prompt, rim_start, taps - 1)
    tail_rows = jnp.concatenate(
        [inner_x[tok_dev - taps + 1 :], proj_bc[tok_dev - taps + 1 :]], axis=1
    )
    rim_rows = from_behind(tail_rows, "dp", 1)
    ext_ids = jnp.concatenate([rim_ids, ids_own])
    conv_inner = conv_core(
        jnp.concatenate([rim_rows[:, :inner_dev], inner_x], axis=0), ext_ids, ids_own, conv_x
    )
    conv_bc_out = conv_core(
        jnp.concatenate([rim_rows[:, inner_dev:], proj_bc], axis=0), ext_ids, ids_own, conv_bc
    )
    blocks = tok_dev // BLOCK
    x_heads = conv_inner.reshape(blocks, BLOCK, heads_dev, head_dim)
    b_conv = conv_bc_out[:, :state_width].reshape(blocks, BLOCK, state_width)
    c_conv = conv_bc_out[:, state_width:].reshape(blocks, BLOCK, state_width)
    step_blocks = step_size.reshape(blocks, BLOCK, heads_dev)
    rate_blocks = rate.reshape(blocks, BLOCK, heads_dev)
    id_blocks = ids_own.reshape(blocks, BLOCK)
    prev_last = jnp.where(dp_index > 0, token_prompt[jnp.maximum(dp_index * tok_dev - 1, 0)], -1)
    before_ids = jnp.concatenate([prev_last[None], id_blocks[:-1, -1]])
    y_intra, local_state, carry_gain, prefix = jax.vmap(block_local)(
        x_heads, b_conv, c_conv, step_blocks, rate_blocks, id_blocks, before_ids
    )

    def advance(carry, item):
        gain_acc, state_acc = carry
        gain, block_state = item
        return (
            (gain_acc * gain, gain[:, None, None] * state_acc + block_state),
            (gain_acc, state_acc),
        )

    unit_gain = jnp.ones((heads_dev,), jnp.float32)
    zero_state = jnp.zeros((heads_dev, head_dim, state_width), jnp.float32)
    (dev_gain, dev_state), (prior_gain, prior_state) = lax.scan(
        advance, (unit_gain, zero_state), (carry_gain, local_state)
    )
    scanned = carried_in((dev_gain, dev_state), "dp", join_states, (unit_gain, zero_state))
    incoming = scanned[1]
    block_in = prior_state + prior_gain[:, :, None, None] * incoming[None]
    prompt_ids = jnp.arange(PROMPTS, dtype=jnp.int32)
    last_index = (
        jnp.sum((token_prompt[None, :] <= prompt_ids[:, None]).astype(jnp.int32), axis=1) - 1
    )
    start_pos = (dp_index * blocks + jnp.arange(blocks, dtype=jnp.int32)) * BLOCK
    y_inter = jax.vmap(block_inter)(c_conv, prefix, id_blocks, before_ids, block_in)

    def collect(table, item):
        xb, bb, sb, pb, ib, fb, stb, ob = item
        return (block_last(last_index, table, xb, bb, sb, pb, ib, fb, stb, ob), None)

    empty_table = jnp.zeros((PROMPTS, heads_dev, head_dim, state_width), jnp.float32)
    local_table, unused = lax.scan(
        collect,
        empty_table,
        (x_heads, b_conv, step_blocks, prefix, id_blocks, before_ids, block_in, start_pos),
    )
    ssd_out = (y_intra + y_inter).reshape(tok_dev, heads_dev, head_dim) + skip_gain[
        None, :, None
    ] * conv_inner.astype(jnp.float32).reshape(tok_dev, heads_dev, head_dim)
    gated = ssd_out.reshape(tok_dev, inner_dev) * jax.nn.silu(gate_z.astype(jnp.float32))
    square_sum = lax.psum(jnp.sum(gated * gated, axis=1), "head")
    scale = lax.rsqrt(square_sum / (inner_dev * head_count) + EPSILON)
    normed_out = (gated * scale[:, None] * out_gain).astype(jnp.bfloat16)
    out_rows = tok_dev // head_count
    own_rows = lax.dynamic_slice_in_dim(hidden_f, head_index * out_rows, out_rows, 0)
    mixed = lax.psum_scatter(
        jnp.dot(normed_out, w_out, preferred_element_type=jnp.float32),
        "head",
        scatter_dimension=0,
        tiled=True,
    )
    layer_out = (own_rows + mixed).astype(jnp.bfloat16)
    table = lax.psum(local_table, "dp")
    one_hot = (request_prompt[:, None] == prompt_ids[None, :]).astype(jnp.float32)
    request_states = jnp.einsum("rg,ghpn->rhpn", one_hot, table, precision=lax.Precision.HIGHEST)
    return (layer_out, request_states)


LANES = 128
TILE_ROWS = 16
NEVER = -1e30
Y_NEAR, Z_NEAR, Z_FAR = 1, 2, 4
RELATED = (0, Y_NEAR, Z_FAR, Y_NEAR | Z_FAR)
LITTLE = pl.CostEstimate(flops=1000, bytes_accessed=1000, transcendentals=0)


def kernel_params(mebibytes):
    return pltpu.CompilerParams(vmem_limit_bytes=mebibytes << 20)


def in_vmem(count):
    return [pl.BlockSpec(memory_space=pltpu.VMEM)] * count


def exchange(values, axis, bits):
    return lax.ppermute(values, axis, [(i, i ^ bits) for i in range(lax.axis_size(axis))])


def dot32(a, b, a_dim=1, b_dim=0):
    return lax.dot_general(
        a, b, (((a_dim,), (b_dim,)), ((), ())), preferred_element_type=jnp.float32
    )


def silu_tanh(values):
    half = 0.5 * values
    return half + half * jnp.tanh(half)


def widen(columns, pair, head_dim):
    rows = columns.shape[0]
    lane = lax.broadcasted_iota(jnp.int32, (rows, LANES), 1)
    first = jnp.broadcast_to(columns[:, 2 * pair : 2 * pair + 1], (rows, LANES))
    second = jnp.broadcast_to(columns[:, 2 * pair + 1 : 2 * pair + 2], (rows, LANES))
    return jnp.where(lane < head_dim, first, second)


def pack_first_kernel(
    req_ref, wbc_ref, wdt_ref, hidden_ref, first_ref, bc_v, dt_v, tail_v, dt_wide, sems
):
    rows, width = bc_v.shape
    tok, model = hidden_ref.shape
    arrivals = [
        pltpu.make_async_copy(source, target, sems.at[k])
        for k, (source, target) in enumerate(
            (
                (wdt_ref, dt_v),
                (hidden_ref.at[tok - TILE_ROWS : tok], tail_v),
                (wbc_ref, bc_v),
            )
        )
    ]
    for copy in arrivals:
        copy.start()
    dt_wide[...] = jnp.zeros_like(dt_wide)
    lane = lax.broadcasted_iota(jnp.int32, (1, LANES), 1)
    wanted = jnp.zeros((1, LANES), jnp.float32)
    for r in range(req_ref.shape[0]):
        wanted = jnp.where(lane == r, req_ref[r].astype(jnp.float32), wanted)
    dt_wide[0:1, rows : rows + LANES] = wanted
    arrivals[0].wait()
    dt_wide[0 : dt_v.shape[0], 0:rows] = dt_v[...]
    arrivals[1].wait()
    upper = lax.broadcasted_iota(jnp.int32, (TILE_ROWS, model), 0) < TILE_ROWS // 2
    below = jnp.where(upper, dt_wide[...], tail_v[...].astype(jnp.float32)).astype(jnp.bfloat16)
    for i in range(model // width):
        at = rows + TILE_ROWS * i
        first_ref[at : at + TILE_ROWS, :] = below[:, i * width : (i + 1) * width]
    arrivals[2].wait()
    first_ref[0:rows, :] = bc_v[...].astype(jnp.bfloat16)


def pack_rest_kernel(wzx_ref, x_ref, gate_ref, tiles_ref, sems):
    rows, inner = x_ref.shape
    arrivals = [
        pltpu.make_async_copy(
            wzx_ref.at[:, :, j * LANES : (j + 1) * LANES], tiles_ref.at[j], sems.at[j]
        )
        for j in range(inner // LANES)
    ]
    for copy in arrivals:
        copy.start()
    for j, copy in enumerate(arrivals):
        copy.wait()
        own = slice(j * LANES, (j + 1) * LANES)
        pair = tiles_ref.at[j].reshape(2 * rows, LANES)
        x_ref[:, own] = pair[pl.ds(1, rows, stride=2), :].astype(jnp.bfloat16)
        gate_ref[:, own] = pair[pl.ds(0, rows, stride=2), :].astype(jnp.bfloat16)


def facts_kernel(
    ids_ref,
    hidden_hbm,
    gain_ref,
    normed_ref,
    meta_ref,
    order_ref,
    pen_ref,
    hidden_ref,
    sem,
):
    tok = hidden_ref.shape[0]
    arrival = pltpu.make_async_copy(hidden_hbm, hidden_ref, sem)
    arrival.start()
    position = lax.axis_index("dp")
    start = pl.multiple_of(position * tok, tok)
    ids_i = ids_ref[:, pl.ds(start, tok)]
    behind = pl.multiple_of(jnp.maximum(start - LANES, 0), LANES)
    edge = ids_ref[:, pl.ds(behind, LANES)]
    edge = jnp.where(position > 0, edge, -1)
    ahead = pl.multiple_of(jnp.minimum(start + tok, ids_ref.shape[1] - LANES), LANES)
    after = jnp.where(start + tok < ids_ref.shape[1], ids_ref[:, pl.ds(ahead, LANES)], -1)
    after = after[:, 0:1].astype(jnp.float32)
    long = jnp.concatenate([edge, ids_i], axis=1).astype(jnp.float32)
    ids = ids_i.astype(jnp.float32)
    index = lax.broadcasted_iota(jnp.int32, (1, tok), 1)
    before, last = long[:, LANES - 1 : LANES], ids[:, tok - 1 : tok]
    middle = ids[:, BLOCK - 1 : BLOCK]
    one, zero = jnp.ones((1, tok), jnp.float32), jnp.zeros((1, tok), jnp.float32)
    flag = lambda what: jnp.where(what, one, zero)
    rows = [flag(ids == pltpu.roll(long, k, 1)[:, LANES:]) for k in (1, 2, 3)]
    rows.append(flag(ids == before))
    rows.append(flag((ids == middle) & (index >= BLOCK)))
    rows.append(flag((ids == middle) & (index < BLOCK)))
    rows.append(ids)
    rows.append(flag(ids == last))
    rows.append(flag((ids != last) | (after != last)))
    rows = jnp.concatenate(rows + [jnp.zeros((LANES - len(rows), tok), jnp.float32)], axis=0)
    facts = rows.T
    meta_ref[...] = facts
    column = facts[:, 6:7]
    here = lax.broadcasted_iota(jnp.int32, (tok, tok), 0)
    there = lax.broadcasted_iota(jnp.int32, (tok, tok), 1)
    same = column == ids
    order_ref[0:tok, :] = jnp.where(there <= here, 1.0, 0.0).astype(jnp.bfloat16)
    order_ref[tok:, :] = jnp.where((there > here) & same, 1.0, 0.0).astype(jnp.bfloat16)
    pen = jnp.where((there <= here) & same, 0.0, NEVER)
    for b in range(tok // BLOCK):
        own = slice(b * BLOCK, (b + 1) * BLOCK)
        pen_ref[b] = pen[own, own]
    arrival.wait()
    hidden = hidden_ref[...].astype(jnp.float32)
    normed_ref[...] = (hidden * rms_scale(hidden) * gain_ref[...]).astype(jnp.bfloat16)


def scale_kernel(w_ref, gain_ref, whole_ref, part_ref):
    rows, model = w_ref.shape
    width = part_ref.shape[1]
    gain = jnp.broadcast_to(gain_ref[...], (LANES, rows)).T
    for j in range(model // LANES):
        own = slice(j * LANES, (j + 1) * LANES)
        whole_ref[:, own] = (w_ref[:, own].astype(jnp.float32) * gain).astype(jnp.bfloat16)
    at = pl.multiple_of((lax.axis_index("dp") % 2) * width, LANES)
    part_ref[...] = whole_ref[:, pl.ds(at, width)]


def gather_rows(position, buffers, rows, w_ref, sems):
    copies = []
    for j, buffer in enumerate(buffers):
        at = pl.multiple_of(jnp.bitwise_xor(position, j) * rows, rows)
        copies.append(
            pltpu.make_async_copy(buffer.at[0:rows], w_ref.at[pl.ds(at, rows)], sems.at[j])
        )
    return copies


def project_rows(normed, halo, w, ext_ref, at, stop):
    ext_ref[0:TILE_ROWS, at:stop] = dot32(halo, w)
    ext_ref[TILE_ROWS:, at:stop] = dot32(normed, w)


def convolve(ext_ref, own, taps, same):
    tok = same[0].shape[0]
    total = ext_ref[TILE_ROWS : TILE_ROWS + tok, own] * taps[3:4]
    for k in range(1, 4):
        total = total + same[k - 1] * (
            ext_ref[TILE_ROWS - k : TILE_ROWS - k + tok, own] * taps[3 - k : 4 - k]
        )
    return silu_tanh(total)


def first_kernel(
    normed_ref,
    own_ref,
    near_ref,
    far_ref,
    last_ref,
    gain_ref,
    taps_ref,
    meta_ref,
    order_ref,
    bias_ref,
    decay_ref,
    bc_ref,
    step_ref,
    prefix_ref,
    fade_ref,
    halo_ref,
    w_ref,
    extra_ref,
    dtw_ref,
    ext_ref,
    sems,
):
    position = lax.axis_index("dp")
    tok, model = normed_ref.shape
    peers, extra, width = extra_ref.shape
    rows = model // peers
    buffers = (own_ref, near_ref, far_ref, last_ref)
    copies = gather_rows(position, buffers, rows, w_ref, sems)
    for j, buffer in enumerate(buffers):
        copies.append(
            pltpu.make_async_copy(
                buffer.at[rows : rows + extra],
                extra_ref.at[jnp.bitwise_xor(position, j)],
                sems.at[peers + j],
            )
        )
    for copy in copies:
        copy.start()
    dtw_ref[...] = jnp.zeros_like(dtw_ref)
    for copy in copies:
        copy.wait()
    pieces = model // width
    for s in range(peers):
        below = jnp.concatenate(
            [extra_ref[s, i * TILE_ROWS : (i + 1) * TILE_ROWS, :] for i in range(pieces)], axis=1
        )
        row = lax.broadcasted_iota(jnp.int32, (TILE_ROWS, rows), 0)
        steps = jnp.where(row < bias_ref.shape[0], below[:, 0:rows].astype(jnp.float32), 0.0)
        dtw_ref[0:TILE_ROWS, s * rows : (s + 1) * rows] = steps.astype(jnp.bfloat16)
    behind = jnp.maximum(position - 1, 0)
    halo = jnp.concatenate(
        [extra_ref[behind, i * TILE_ROWS : (i + 1) * TILE_ROWS, :] for i in range(pieces)], axis=1
    ).astype(jnp.float32)
    halo = (halo * rms_scale(halo) * gain_ref[...]).astype(jnp.bfloat16)
    halo_ref[...] = halo
    normed = normed_ref[...]
    head_lane = lax.broadcasted_iota(jnp.int32, (1, LANES), 1)
    bias = jnp.zeros((1, LANES), jnp.float32)
    decay = jnp.zeros((1, LANES), jnp.float32)
    for h in range(bias_ref.shape[0]):
        bias = jnp.where(head_lane == h, bias_ref[h], bias)
        decay = jnp.where(head_lane == h, decay_ref[h], decay)
    raw = dot32(normed, dtw_ref[...], 1, 1) + bias
    step = jnp.maximum(raw, 0.0) + jnp.log1p(jnp.exp(-jnp.abs(raw)))
    step_ref[...] = step
    lane = lax.broadcasted_iota(jnp.int32, (tok, LANES), 1)
    rate = jnp.where(lane < TILE_ROWS, -step * jnp.exp(decay), 0.0)
    high = rate.astype(jnp.bfloat16).astype(jnp.float32)
    rest = rate - high
    mid = rest.astype(jnp.bfloat16).astype(jnp.float32)
    low = rest - mid
    packed = high + pltpu.roll(mid, TILE_ROWS, 1) + pltpu.roll(low, 2 * TILE_ROWS, 1)
    sums = dot32(order_ref[...], packed.astype(jnp.bfloat16))
    sums = (
        sums
        + pltpu.roll(sums, LANES - TILE_ROWS, 1)
        + pltpu.roll(sums, LANES - 2 * TILE_ROWS, 1)
    )
    prefix_ref[...] = sums[0:tok]
    fade_ref[...] = jnp.exp(sums[tok : 2 * tok])
    project_rows(normed, halo, w_ref[...], ext_ref, 0, width)
    same = [jnp.broadcast_to(meta_ref[:, k : k + 1], (tok, LANES)) for k in range(3)]
    for j in range(width // LANES):
        own = slice(j * LANES, (j + 1) * LANES)
        bc_ref[:, own] = convolve(ext_ref, own, taps_ref[:, own], same).astype(jnp.bfloat16)


def inner_kernel(
    normed_ref,
    own_ref,
    near_ref,
    far_ref,
    last_ref,
    halo_ref,
    taps_ref,
    meta_ref,
    bc_ref,
    step_ref,
    prefix_ref,
    fade_ref,
    x_ref,
    stepx_ref,
    faded_ref,
    leaving_ref,
    middle_ref,
    w_ref,
    ext_ref,
    sems,
):
    position = lax.axis_index("dp")
    tok = normed_ref.shape[0]
    inner = x_ref.shape[1]
    rows = own_ref.shape[0]
    head_dim = LANES // 2
    copies = gather_rows(position, (own_ref, near_ref, far_ref, last_ref), rows, w_ref, sems)
    for copy in copies:
        copy.start()
    state_width = leaving_ref.shape[1]
    step = step_ref[...]
    fade = fade_ref[...]
    fade_middle = jnp.exp(prefix_ref[BLOCK - 1 : BLOCK, :] - prefix_ref[0:BLOCK, :])
    b_all = bc_ref[:, 0:state_width].astype(jnp.float32)
    b_leaving = (b_all * meta_ref[:, 7:8]).astype(jnp.bfloat16)
    b_middle = (b_all * meta_ref[:, 5:6])[0:BLOCK].astype(jnp.bfloat16)
    same = [jnp.broadcast_to(meta_ref[:, k : k + 1], (tok, LANES)) for k in range(3)]
    for copy in copies:
        copy.wait()
    project_rows(normed_ref[...], halo_ref[...], w_ref[...], ext_ref, 0, inner)
    for q in range(inner // LANES):
        own = slice(q * LANES, (q + 1) * LANES)
        rounded = convolve(ext_ref, own, taps_ref[:, own], same).astype(jnp.bfloat16)
        x_ref[:, own] = rounded
        scaled = rounded.astype(jnp.float32) * widen(step, q, head_dim)
        stepx_ref[:, own] = scaled.astype(jnp.bfloat16)
        faded = (scaled * widen(fade, q, head_dim)).astype(jnp.bfloat16).T
        faded_ref[own, :] = faded
        leaving_ref[own, :] = dot32(faded, b_leaving).astype(jnp.bfloat16)
        to_middle = (scaled[0:BLOCK] * widen(fade_middle, q, head_dim)).astype(jnp.bfloat16).T
        middle_ref[own, :] = dot32(to_middle, b_middle).astype(jnp.bfloat16)


def table_kernel(bc_ref, faded_ref, meta_ref, *table_refs):
    rows, state_width = table_refs[0].shape[1:]
    b_all = bc_ref[:, 0:state_width].astype(jnp.float32)
    for g in range(table_refs[0].shape[0]):
        ended = jnp.where(meta_ref[:, 6:7] == g, meta_ref[:, 8:9], 0.0)
        b_ended = (b_all * ended).astype(jnp.bfloat16)
        for k, table_ref in enumerate(table_refs):
            faded = faded_ref[k * rows : (k + 1) * rows, :]
            table_ref[g] = dot32(faded, b_ended).astype(jnp.bfloat16)


def local_kernel(
    x_ref,
    bc_ref,
    stepx_ref,
    prefix_ref,
    middle_ref,
    meta_ref,
    pen_ref,
    skip_ref,
    y_ref,
):
    inner = y_ref.shape[1]
    state_width = middle_ref.shape[1]
    head_dim = LANES // 2
    tok = y_ref.shape[0]
    lane = lax.broadcasted_iota(jnp.int32, (BLOCK, LANES), 1)
    for b in range(tok // BLOCK):
        own_rows = slice(b * BLOCK, (b + 1) * BLOCK)
        b_blk = bc_ref[own_rows, 0:state_width]
        c_blk = bc_ref[own_rows, state_width:]
        scores = dot32(c_blk, b_blk, 1, 1)
        pen = pen_ref[b]
        prefix = prefix_ref[own_rows, :]
        across = prefix.T
        if b > 0:
            carried = jnp.exp(prefix - prefix_ref[b * BLOCK - 1 : b * BLOCK, :])
            carried = carried * meta_ref[own_rows, 4:5]
            from_middle = dot32(c_blk, middle_ref[...], 1, 1)
        for q in range(inner // LANES):
            own = slice(q * LANES, (q + 1) * LANES)
            x_pair = x_ref[own_rows, own].astype(jnp.float32)
            out = x_pair * jnp.where(lane < head_dim, skip_ref[2 * q], skip_ref[2 * q + 1])
            if b > 0:
                out = out + widen(carried, q, head_dim) * from_middle[:, own]
            sx = stepx_ref[own_rows, own].astype(jnp.float32)
            for side in range(2):
                h = 2 * q + side
                gaps = prefix[:, h : h + 1] - across[h : h + 1, :] + pen
                mixing = (scores * jnp.exp(gaps)).astype(jnp.bfloat16)
                kept = (lane < head_dim) if side == 0 else (lane >= head_dim)
                out = out + dot32(mixing, jnp.where(kept, sx, 0.0).astype(jnp.bfloat16))
            y_ref[own_rows, own] = out


def z_kernel(normed_ref, own_ref, near_ref, far_ref, last_ref, gate_ref, w_ref, sems):
    rows = own_ref.shape[0]
    position = lax.axis_index("dp")
    copies = gather_rows(position, (own_ref, near_ref, far_ref, last_ref), rows, w_ref, sems)
    for copy in copies:
        copy.start()
    for copy in copies:
        copy.wait()
    gate_ref[...] = silu_tanh(dot32(normed_ref[...], w_ref[...]))


def before_device(ids_ref, position, tok):
    return jnp.where(position > 0, ids_ref[jnp.maximum(position * tok - 1, 0)], -1)


def gate_kernel(
    ids_ref, enter_ref, bc_ref, prefix_ref, meta_ref, y_ref, z_ref, arrived_ref, *outs
):
    scratch, add_ref = outs[-1], outs[-2]
    outs = outs[:-2]
    inner = y_ref.shape[1]
    state_width = enter_ref.shape[1]
    head_dim = LANES // 2
    tok = y_ref.shape[0]
    c_all = bc_ref[:, state_width:]
    inter = dot32(c_all, enter_ref[...], 1, 1)
    prefix = prefix_ref[...]
    carried = jnp.exp(prefix) * meta_ref[:, 3:4]
    for q in range(inner // LANES):
        own = slice(q * LANES, (q + 1) * LANES)
        value = y_ref[:, own] + widen(carried, q, head_dim) * inter[:, own]
        scratch[:, own] = (value * z_ref[:, own]).astype(jnp.bfloat16)
    position = lax.axis_index("dp")
    before = before_device(ids_ref, position, tok)
    stop = (position + 1) * tok
    after = ids_ref[jnp.minimum(stop, ids_ref.shape[0] - 1)]
    goes_on = (after == before) & (stop < ids_ref.shape[0])
    ended = (ids_ref[position * tok] == before) & ((ids_ref[stop - 1] != before) | ~goes_on)
    inside = jnp.where(meta_ref[:, 3:4] > 0.0, prefix, 0.0)
    gain = jnp.exp(jnp.min(inside, axis=0, keepdims=True)) * jnp.where(ended, 1.0, 0.0)
    for h in range(inner // head_dim):
        own = slice(h * head_dim, (h + 1) * head_dim)
        term = gain[:, h : h + 1] * enter_ref[own, :].astype(jnp.float32)
        add_ref[own, :] = term.astype(jnp.bfloat16)
    head = lax.axis_index("head")
    part = outs[0].shape[0] // len(RELATED)
    for out, owner in zip(outs, (head, jnp.bitwise_xor(head, Z_NEAR))):
        for k, bits in enumerate(RELATED):
            at = pl.multiple_of(jnp.bitwise_xor(owner, bits) * part, part)
            out[k * part : (k + 1) * part, :] = scratch[pl.ds(at, part), :]


def pick_kernel(own_ref, far_ref, *refs):
    tables, others, (keep_ref, send_ref, far_v, sem) = refs[:2], refs[2:4], refs[4:]
    count = keep_ref.shape[0]
    rows = far_ref.shape[0] - 6 * TILE_ROWS
    width = far_ref.shape[1]
    model_rows = rows // width
    at = rows + TILE_ROWS * model_rows
    lanes = rows - model_rows * width
    arrival = pltpu.make_async_copy(
        far_ref.at[at : at + TILE_ROWS, lanes : lanes + LANES], far_v, sem
    )
    arrival.start()

    def pick(out_ref, r, g):
        half = tables[0].shape[1]
        for k, (table_ref, other_ref) in enumerate(zip(tables, others)):
            total = table_ref[g].astype(jnp.float32) + other_ref[g].astype(jnp.float32)
            out_ref[r, k * half : (k + 1) * half] = total.astype(jnp.bfloat16)

    for r in range(count):
        pick(keep_ref, r, own_ref[r])
    arrival.wait()
    wanted = far_v[...].astype(jnp.float32)[0:1, :]
    lane = lax.broadcasted_iota(jnp.int32, (1, LANES), 1)
    for r in range(count):
        pick(send_ref, r, jnp.sum(jnp.where(lane == r, wanted, 0.0)).astype(jnp.int32))


def split_squares(squares):
    lane = lax.broadcasted_iota(jnp.int32, (squares.shape[0], LANES), 1)
    high = squares.astype(jnp.bfloat16).astype(jnp.float32)
    return jnp.where(lane == 0, high, squares - high).astype(jnp.bfloat16)


def joined_squares(ref, model):
    high = ref[:, model : model + 1].astype(jnp.float32)
    return high + ref[:, model + 1 : model + 2].astype(jnp.float32)


def out_kernel(
    kept_ref,
    got_ref,
    own_hbm,
    part_ref,
    near_ref,
    keep_ref,
    near_out,
    pass_ref,
    cross_out,
    own_ref,
    other_ref,
    sums_ref,
    sems,
):
    core = lax.axis_index("dp") % 2
    width = part_ref.shape[1]
    rows, model = sums_ref.shape
    part = keep_ref.shape[0]
    copies = [pltpu.make_async_copy(own_hbm, own_ref, sems.at[2])]
    for j, buffer in enumerate((part_ref, near_ref)):
        at = pl.multiple_of(jnp.bitwise_xor(core, j) * width, LANES)
        copies.append(
            pltpu.make_async_copy(buffer, other_ref.at[:, pl.ds(at, width)], sems.at[j])
        )
    for copy in copies:
        copy.start()
    kept, got = kept_ref[...], got_ref[...]
    squares = jnp.zeros((rows, 1), jnp.float32)
    for value in (kept, got):
        wide = value.astype(jnp.float32)
        squares = squares + jnp.sum(wide * wide, axis=1, keepdims=True)
    copies[0].wait()
    sums_ref[...] = dot32(kept, own_ref[...])
    for copy in copies[1:]:
        copy.wait()
    sums_ref[...] += dot32(got, other_ref[...])
    for k, out in enumerate((keep_ref, near_out, pass_ref, cross_out)):
        own = slice(k * part, (k + 1) * part)
        out[:, 0:model] = sums_ref[own, :].astype(out.dtype)
        if out.dtype == jnp.bfloat16:
            out[:, model:] = split_squares(squares[own])
        else:
            out[:, model:] = jnp.broadcast_to(squares[own], (part, LANES))


def pass_kernel(pass_ref, cross_ref, out_ref):
    model = out_ref.shape[1] - LANES
    total = pass_ref[:, 0:model] + cross_ref[:, 0:model].astype(jnp.float32)
    out_ref[:, 0:model] = total.astype(jnp.bfloat16)
    squares = pass_ref[:, model : model + 1] + joined_squares(cross_ref, model)
    out_ref[:, model:] = split_squares(squares)


def finish_kernel(inner_total, hidden_all, joined_ref, keep_ref, *refs):
    got, (out_ref, hidden_ref, sem) = refs[:-3], refs[-3:]
    part, model = hidden_ref.shape
    at = pl.multiple_of(lax.axis_index("head") * part, part)
    arrival = pltpu.make_async_copy(hidden_all.at[pl.ds(at, part)], hidden_ref, sem)
    arrival.start()
    squares = keep_ref[:, model : model + 1]
    total = keep_ref[:, 0:model]
    for ref in got:
        squares = squares + joined_squares(ref, model)
        total = total + ref[:, 0:model].astype(jnp.float32)
    scale = lax.rsqrt(squares / inner_total + EPSILON)
    arrival.wait()
    out_ref[...] = (hidden_ref[...].astype(jnp.float32) + scale * total).astype(jnp.bfloat16)


def join_kernel(ids_ref, own_ref, keep_ref, far_ref, *refs):
    adds, (out_ref, done_ref) = refs[:4], refs[-2:]
    done_ref[...] = jnp.zeros_like(done_ref)
    position = lax.axis_index("dp")
    tok = ids_ref.shape[0] // lax.axis_size("dp")
    befores = [
        before_device(ids_ref, jnp.bitwise_xor(position, j), tok) for j in range(len(adds))
    ]
    for r in range(keep_ref.shape[0]):
        total = keep_ref[r].astype(jnp.float32) + far_ref[r].astype(jnp.float32)
        out_ref[r] = total
        for add_ref, before in zip(adds, befores):

            @pl.when(own_ref[r] == before)
            def _():
                out_ref[r] = out_ref[r] + add_ref[...].astype(jnp.float32)


def fused_on_device(
    hidden,
    token_prompt,
    request_prompt,
    in_gain,
    w_zx,
    w_bc,
    w_dt,
    dt_bias,
    a_log,
    conv_x,
    conv_bc,
    skip_gain,
    out_gain,
    w_out,
):
    tok, model = hidden.shape
    rows = w_zx.shape[0]
    inner = w_zx.shape[2]
    heads = w_dt.shape[1]
    state_width = w_bc.shape[1] // 2
    width = inner + 2 * state_width
    peers = lax.axis_size("dp")
    head_count = lax.axis_size("head")
    bf16, f32 = jnp.bfloat16, jnp.float32
    shape = jax.ShapeDtypeStruct
    smem = pl.BlockSpec(memory_space=pltpu.SMEM)
    anywhere = pl.BlockSpec(memory_space=pl.ANY)
    in_hbm = pl.BlockSpec(memory_space=pltpu.HBM)

    extra = TILE_ROWS * (model // (2 * state_width))
    first_own = pl.pallas_call(
        pack_first_kernel,
        name="pack_first_weights",
        out_shape=shape((rows + extra, 2 * state_width), bf16),
        in_specs=[smem] + [in_hbm] * 3,
        out_specs=in_vmem(1)[0],
        scratch_shapes=[
            pltpu.VMEM(w_bc.shape, f32),
            pltpu.VMEM((heads, rows), f32),
            pltpu.VMEM((TILE_ROWS, model), bf16),
            pltpu.VMEM((TILE_ROWS, model), f32),
            pltpu.SemaphoreType.DMA((3,)),
        ],
        compiler_params=kernel_params(60),
        cost_estimate=LITTLE,
    )(request_prompt, w_bc, w_dt.T, hidden)
    first_far = exchange(first_own, "dp", 2)
    first_near = exchange(first_own, "dp", 1)
    x_own, gate_own = pl.pallas_call(
        pack_rest_kernel,
        name="pack_x_and_gate_weights",
        out_shape=(shape((rows, inner), bf16), shape((rows, inner), bf16)),
        in_specs=[in_hbm],
        out_specs=tuple(in_vmem(2)),
        scratch_shapes=[
            pltpu.VMEM((inner // LANES, rows, 2, LANES), f32),
            pltpu.SemaphoreType.DMA((inner // LANES,)),
        ],
        compiler_params=kernel_params(8),
        cost_estimate=LITTLE,
    )(w_zx)

    blocks = tok // BLOCK
    normed, meta, order, pen = pl.pallas_call(
        facts_kernel,
        name="norm_and_token_facts",
        out_shape=(
            shape((tok, model), bf16),
            shape((tok, LANES), f32),
            shape((2 * tok, tok), bf16),
            shape((blocks, BLOCK, BLOCK), f32),
        ),
        in_specs=in_vmem(1) + [in_hbm] + in_vmem(1),
        out_specs=tuple(in_vmem(4)),
        scratch_shapes=[pltpu.VMEM((tok, model), bf16), pltpu.SemaphoreType.DMA],
        compiler_params=kernel_params(16),
        cost_estimate=LITTLE,
    )(token_prompt[None, :], hidden, in_gain[None, :])
    scaled_out, half_out = pl.pallas_call(
        scale_kernel,
        name="scale_out_rows",
        out_shape=(shape(w_out.shape, bf16), shape((inner, model // 2), bf16)),
        in_specs=in_vmem(2),
        out_specs=tuple(in_vmem(2)),
        compiler_params=kernel_params(8),
        cost_estimate=LITTLE,
    )(w_out, out_gain[None, :])
    out_part = exchange(half_out, "head", Z_NEAR)
    out_near = exchange(out_part, "dp", 1)

    first_far, x_own, normed, meta, order, pen = lax.optimization_barrier(
        (first_far, x_own, normed, meta, order, pen)
    )
    x_far = exchange(x_own, "dp", 2)
    first_last = exchange(first_far, "dp", 1)
    x_near = exchange(x_own, "dp", 1)
    bc, step, prefix, fade, halo = pl.pallas_call(
        first_kernel,
        name="project_b_c_and_steps",
        out_shape=(
            shape((tok, 2 * state_width), bf16),
            shape((tok, LANES), f32),
            shape((tok, LANES), f32),
            shape((tok, LANES), f32),
            shape((TILE_ROWS, model), bf16),
        ),
        in_specs=in_vmem(1) + [anywhere] * 4 + in_vmem(4) + [smem] * 2,
        out_specs=tuple(in_vmem(5)),
        scratch_shapes=[
            pltpu.VMEM((model, 2 * state_width), bf16),
            pltpu.VMEM((peers, extra, 2 * state_width), bf16),
            pltpu.VMEM((LANES, model), bf16),
            pltpu.VMEM((TILE_ROWS + tok, 2 * state_width), f32),
            pltpu.SemaphoreType.DMA((2 * peers,)),
        ],
        compiler_params=kernel_params(14),
        cost_estimate=LITTLE,
    )(
        normed,
        first_own,
        first_near,
        first_far,
        first_last,
        in_gain[None, :],
        conv_bc,
        meta,
        order,
        dt_bias,
        a_log,
    )
    x_far, gate_own, bc, step, prefix, fade, halo = lax.optimization_barrier(
        (x_far, gate_own, bc, step, prefix, fade, halo)
    )
    x_last = exchange(x_far, "dp", 1)
    gate_far = exchange(gate_own, "dp", 2)
    gate_near = exchange(gate_own, "dp", 1)
    x, stepx, faded, leaving, middle = pl.pallas_call(
        inner_kernel,
        name="project_and_convolve_x",
        out_shape=(
            shape((tok, inner), bf16),
            shape((tok, inner), bf16),
            shape((inner, tok), bf16),
            shape((inner, state_width), bf16),
            shape((inner, state_width), bf16),
        ),
        in_specs=in_vmem(1) + [anywhere] * 4 + in_vmem(7),
        out_specs=tuple(in_vmem(5)),
        scratch_shapes=[
            pltpu.VMEM((model, inner), bf16),
            pltpu.VMEM((TILE_ROWS + tok, inner), f32),
            pltpu.SemaphoreType.DMA((peers,)),
        ],
        compiler_params=kernel_params(14),
        cost_estimate=LITTLE,
    )(
        normed,
        x_own,
        x_near,
        x_far,
        x_last,
        halo,
        conv_x,
        meta,
        bc,
        step,
        prefix,
        fade,
    )

    entering = lax.ppermute(leaving, "dp", [(i, i + 1) for i in range(peers - 1)])
    gate_far, entering = lax.optimization_barrier((gate_far, entering))
    gate_last = exchange(gate_far, "dp", 1)

    y_local = pl.pallas_call(
        local_kernel,
        name="mix_within_blocks",
        out_shape=shape((tok, inner), f32),
        in_specs=in_vmem(7) + [smem],
        out_specs=in_vmem(1)[0],
        compiler_params=kernel_params(14),
        cost_estimate=LITTLE,
    )(x, bc, stepx, prefix, middle, meta, pen, skip_gain)
    tables = pl.pallas_call(
        table_kernel,
        name="sum_ended_states",
        out_shape=(shape((PROMPTS, inner // 2, state_width), bf16),) * 2,
        in_specs=in_vmem(3),
        out_specs=tuple(in_vmem(2)),
        compiler_params=kernel_params(8),
        cost_estimate=LITTLE,
    )(bc, faded, meta)
    tables_near = [exchange(table, "dp", 1) for table in tables]

    gate = pl.pallas_call(
        z_kernel,
        name="project_gate",
        out_shape=shape((tok, inner), f32),
        in_specs=in_vmem(1) + [anywhere] * 4,
        out_specs=in_vmem(1)[0],
        scratch_shapes=[pltpu.VMEM((model, inner), bf16), pltpu.SemaphoreType.DMA((peers,))],
        compiler_params=kernel_params(8),
        cost_estimate=LITTLE,
    )(normed, gate_own, gate_near, gate_far, gate_last)

    out_rows = tok // head_count
    gated_kept, gated_sent, add = pl.pallas_call(
        gate_kernel,
        name="add_entering_and_gate",
        out_shape=(shape((tok // 2, inner), bf16),) * 2 + (shape((inner, state_width), bf16),),
        in_specs=[smem] + in_vmem(6) + [anywhere],
        out_specs=tuple(in_vmem(3)),
        scratch_shapes=[pltpu.VMEM((tok, inner), bf16)],
        compiler_params=kernel_params(8),
        cost_estimate=LITTLE,
    )(token_prompt, entering, bc, prefix, meta, y_local, gate, out_near)
    gated_got = exchange(gated_sent, "head", Z_NEAR)

    requests = request_prompt.shape[0]
    keep, send = pl.pallas_call(
        pick_kernel,
        name="pick_request_states",
        out_shape=(shape((requests, inner, state_width), bf16),) * 2,
        in_specs=[smem, anywhere] + in_vmem(4),
        out_specs=tuple(in_vmem(2)),
        scratch_shapes=[pltpu.VMEM((TILE_ROWS, LANES), bf16), pltpu.SemaphoreType.DMA],
        compiler_params=kernel_params(8),
        cost_estimate=LITTLE,
    )(request_prompt, first_far, *tables, *tables_near)
    far = exchange(send, "dp", 2)
    adds = [add, exchange(add, "dp", 1), exchange(add, "dp", 2)]
    adds.append(exchange(adds[2], "dp", 1))

    sums_shape = (out_rows, model + LANES)
    sums_keep, sums_near, sums_pass, sums_cross = pl.pallas_call(
        out_kernel,
        name="project_out",
        out_shape=tuple(shape(sums_shape, kind) for kind in (f32, bf16, f32, bf16)),
        in_specs=in_vmem(2) + [anywhere] * 3,
        out_specs=tuple(in_vmem(4)),
        scratch_shapes=[
            pltpu.VMEM((inner, model), bf16),
            pltpu.VMEM((inner, model), bf16),
            pltpu.VMEM((tok // 2, model), f32),
            pltpu.SemaphoreType.DMA((3,)),
        ],
        compiler_params=kernel_params(14),
        cost_estimate=LITTLE,
    )(gated_kept, gated_got, scaled_out, out_part, out_near)
    cross = exchange(sums_cross, "head", Y_NEAR)
    cross, sums_near = lax.optimization_barrier((cross, sums_near))
    sums_near = exchange(sums_near, "head", Y_NEAR)
    passed = pl.pallas_call(
        pass_kernel,
        name="add_sums_to_pass_on",
        out_shape=shape(sums_shape, bf16),
        in_specs=in_vmem(2),
        out_specs=in_vmem(1)[0],
        compiler_params=kernel_params(4),
        cost_estimate=LITTLE,
    )(sums_pass, cross)
    passed = exchange(passed, "head", Z_FAR)
    request_states, joined = pl.pallas_call(
        join_kernel,
        name="join_request_states",
        out_shape=(shape(keep.shape, f32), shape((8, LANES), f32)),
        in_specs=[smem] * 2 + in_vmem(6) + [anywhere],
        out_specs=tuple(in_vmem(2)),
        compiler_params=kernel_params(6),
        cost_estimate=LITTLE,
    )(token_prompt, request_prompt, keep, far, *adds, sums_keep)
    layer_out = pl.pallas_call(
        functools.partial(finish_kernel, inner * head_count),
        name="scale_and_add_hidden",
        out_shape=shape((out_rows, model), bf16),
        in_specs=[in_hbm, anywhere] + in_vmem(3),
        out_specs=in_vmem(1)[0],
        scratch_shapes=[pltpu.VMEM((out_rows, model), bf16), pltpu.SemaphoreType.DMA],
        compiler_params=kernel_params(4),
        cost_estimate=LITTLE,
    )(hidden, joined, sums_keep, sums_near, passed)
    return (
        layer_out,
        request_states.reshape(requests, heads, inner // heads, state_width),
    )


def fits_fused(mesh):
    return dict(mesh.shape) == {"dp": 4, "head": 8}


def solution(mesh):
    in_specs = (
        P("dp", None),
        P(),
        P("dp"),
        P(),
        P("dp", None, "head"),
        P("dp", None),
        P("dp", "head"),
        P("head"),
        P("head"),
        P(None, "head"),
        P(),
        P("head"),
        P("head"),
        P("head", None),
    )
    out_specs = (P(("dp", "head"), None), P("dp", "head", None, None))
    program = fused_on_device if fits_fused(mesh) else on_device
    return jax.shard_map(
        program, mesh=mesh, in_specs=in_specs, out_specs=out_specs, check_vma=False
    )
```

time: 75.3 us -> 66.6 us (0.88)
  waiting for transfers between devices: 25.6 us -> 16.6 us
  starting transfers between devices: 23 us -> 24.9 us
  Pallas kernels: 25.3 us -> 23.7 us
    ppermute x19 -> x21, waiting for transfers between devices: 25.6 us -> 16.6 us  [exchange(): lax.ppermute(values, axis, [(i, i ^ bits) for i in range(lax.axis_size(ax...]
    ppermute x19 -> x21, starting transfers between devices: 20.8 us -> 22.6 us  [exchange(): lax.ppermute(values, axis, [(i, i ^ bits) for i in range(lax.axis_size(ax...]
    pallas_call x7 -> x11, Pallas kernels: 21.2 us -> 20 us  [the longest x1 4.59 us: fused_on_device(): pl.pallas_call(first_kernel, name='project_b_c_and_steps', out_shape=(sha...]
  transfers between devices with their start and end apart: 20 -> 22, of which waited for: 9 -> 8; matrix products, arithmetic and copies ran while one was open for 0% -> 0% of each run, Pallas kernels for 28% -> 30%
where the time goes in v3:
time: 66.6 us; the launch traced here: 66.3 us
  starting transfers between devices  24.9 us (37%)
  Pallas kernels  23.7 us (36%)
  waiting for transfers between devices  16.6 us (25%)
  between operations  1.07 us (2%)
    ppermute x21, starting transfers between devices, exchange(): lax.ppermute(values, axis, [(i, i ^ bits) for i in range(lax.axis_size(ax...  22.6 us
    ppermute x21, waiting for transfers between devices, exchange(): lax.ppermute(values, axis, [(i, i ^ bits) for i in range(lax.axis_size(ax...  16.6 us
    pallas_call x1, Pallas kernels, fused_on_device(): pl.pallas_call(first_kernel, name='project_b_c_and_steps', out_shape=(sha...  4.59 us
    pallas_call x1, Pallas kernels, fused_on_device(): pl.pallas_call(inner_kernel, name='project_and_convolve_x', out_shape=(sh...  2.79 us
    pallas_call x1, Pallas kernels, fused_on_device(): pl.pallas_call(pack_first_kernel, name='pack_first_weights', out_shape=sh...  2.58 us
    ppermute x1, starting transfers between devices, fused_on_device(): lax.ppermute(leaving, 'dp', [(i, i + 1) for i in range(peers - 1)])  2.37 us
    pallas_call x1, Pallas kernels, fused_on_device(): pl.pallas_call(local_kernel, name='mix_within_blocks', out_shape=shape((t...  1.81 us
    pallas_call x1, Pallas kernels, fused_on_device(): pl.pallas_call(join_kernel, name='join_request_states', out_shape=(shape(...  1.74 us
  transfers between devices with their start and end apart: 22, of which 8 were waited for; matrix products, arithmetic and copies ran while one was open for 0% of the time, Pallas kernels for 30%

profile of v3, /device:TPU:0, one launch (start us, length us, event | category | flops | bytes accessed | tf_op | source)
XLA Modules:
  0.0 66.3 jit_solution(4789359455450735079)
XLA Ops:
  0.7 2.6 %pack_first_weights.1.own_ref = bf16[480,256]{1,0:T(8,128)(2,1)} custom-call(s32[4]{0:T(128)} %own_ref.3, f32[384,256]{1,0:T(8,128)} %wbc_ref.1, f32[6,384]{1,0:T(8,128)} %bitcast.4, bf16[512,1536]{1,0:T(8,128)(2,1)} %hidden_all.1), custom_call_target="tpu_custom_call" | custom-call | flops 1000 | bytes 1000 | tf_op jit(solution)/shard_map/pack_first_weights/pallas_call | solution.py:847
  3.2 3.0 %collective-permute-start = (bf16[480,256]{1,0:T(8,128)(2,1)}, bf16[480,256]{1,0:T(8,128)(2,1)S(1)}, u32[]{:S(2)}, u32[]{:S(2)}) collective-permute-start(bf16[480,256]{1,0:T(8,128)(2,1)} %pack_first_weights.1.own_ref), channel_id=1, source_target_pairs={{0,16},{8,24},{16,0},{24,8},{1,17},{9,25},{17,1},{25,9},{2,18},{10... | collective-permute-start | bytes 737288 | tf_op jit(solution)/shard_map/ppermute | solution.py:274
  6.8 1.6 %collective-permute-start.13 = (bf16[384,768]{1,0:T(8,128)(2,1)S(1)}, bf16[384,768]{1,0:T(8,128)(2,1)S(1)}, u32[]{:S(2)}, u32[]{:S(2)}) collective-permute-start(bf16[384,768]{1,0:T(8,128)(2,1)S(1)} %get-tuple-element.85), channel_id=1, source_target_pairs={{0,2},{1,3},{2,0},{3,1},{4,6},{5,7},{6,4},{7,5},{8,10},{9,11},{10,... | collective-permute-start | bytes 1769480 | tf_op jit(solution)/shard_map/ppermute | solution.py:274
  9.0 1.2 %norm_and_token_facts.1 = (bf16[512,1536]{1,0:T(8,128)(2,1)S(1)}, f32[512,128]{1,0:T(8,128)S(1)}, bf16[1024,512]{1,0:T(8,128)(2,1)S(1)}, f32[2,256,256]{2,1,0:T(8,128)S(1)}) custom-call(s32[1,2048]{1,0:T(1,128)S(1)} %bitcast.3, bf16[512,1536]{1,0:T(8,128)(2,1)S(1)} %copy-done, f32[1,1536]{1,0:T(1,128)S(1)} %broadcast_in_dim.11.gain_ref), custom_call_target="tpu_custom_call" | custom-call | flops 1000 | bytes 1000 | tf_op jit(solution)/shard_map/norm_and_token_facts/pallas_call | solution.py:880
  10.3 2.1 %collective-permute-done.far_ref = bf16[480,256]{1,0:T(8,128)(2,1)S(1)} collective-permute-done((bf16[480,256]{1,0:T(8,128)(2,1)}, bf16[480,256]{1,0:T(8,128)(2,1)S(1)}, u32[]{:S(2)}, u32[]{:S(2)}) %collective-permute-start) | collective-permute-done | bytes 245792 | tf_op jit(solution)/shard_map/ppermute | solution.py:274
  12.4 1.7 %collective-permute-start.1 = (bf16[384,384]{1,0:T(8,128)(2,1)S(1)}, bf16[384,384]{1,0:T(8,128)(2,1)S(1)}, u32[]{:S(2)}, u32[]{:S(2)}) collective-permute-start(bf16[384,384]{1,0:T(8,128)(2,1)S(1)} %get-tuple-element.56.own_ref), channel_id=1, source_target_pairs={{0,16},{8,24},{16,0},{24,8},{1,17},{9,25},{17,1},{25,9},{2,18},{10... | collective-permute-start | bytes 884744 | tf_op jit(solution)/shard_map/ppermute | solution.py:274
  14.7 1.0 %collective-permute-done.2.near_ref = bf16[480,256]{1,0:T(8,128)(2,1)S(1)} collective-permute-done((bf16[480,256]{1,0:T(8,128)(2,1)S(1)}, bf16[480,256]{1,0:T(8,128)(2,1)S(1)}, u32[]{:S(2)}, u32[]{:S(2)}) %collective-permute-start.2) | collective-permute-done | bytes 245792 | tf_op jit(solution)/shard_map/ppermute | solution.py:274
  16.0 4.6 %project_b_c_and_steps.1 = (bf16[512,256]{1,0:T(8,128)(2,1)S(1)}, f32[512,128]{1,0:T(8,128)S(1)}, f32[512,128]{1,0:T(8,128)S(1)}, f32[512,128]{1,0:T(8,128)S(1)}, bf16[16,1536]{1,0:T(8,128)(2,1)S(1)}) custom-call(bf16[512,1536]{1,0:T(8,128)(2,1)S(1)} %get-tuple-element.58.normed_ref, bf16[480,256]{1,0:T(8,128)(2,1)S(1)} %copy-done.3, ...), custom_call_target="tpu_custom_call" | custom-call | flops 1000 | bytes 1000 | tf_op jit(solution)/shard_map/project_b_c_and_steps/pallas_call | solution.py:913
  20.9 1.2 %collective-permute-start.9 = (bf16[384,384]{1,0:T(8,128)(2,1)S(1)}, bf16[384,384]{1,0:T(8,128)(2,1)S(1)}, u32[]{:S(2)}, u32[]{:S(2)}) collective-permute-start(bf16[384,384]{1,0:T(8,128)(2,1)S(1)} %get-tuple-element.77.own_ref), channel_id=1, source_target_pairs={{0,16},{8,24},{16,0},{24,8},{1,17},{9,25},{17,1},{25,9},{2,18},{10... | collective-permute-start | bytes 884744 | tf_op jit(solution)/shard_map/ppermute | solution.py:274
  22.3 2.8 %project_and_convolve_x.1 = (bf16[512,384]{1,0:T(8,128)(2,1)S(1)}, bf16[512,384]{1,0:T(8,128)(2,1)S(1)}, bf16[384,512]{1,0:T(8,128)(2,1)S(1)}, bf16[384,128]{1,0:T(8,128)(2,1)S(1)}, bf16[384,128]{1,0:T(8,128)(2,1)S(1)}) custom-call(bf16[512,1536]{1,0:T(8,128)(2,1)S(1)} %get-tuple-element.58.normed_ref, bf16[384,384]{1,0:T(8,128)(2,1)S(1)} %get-tuple-element.56.own_ref, ...), custom_call_target="tpu_custom_call" | custom-call | flops 1000 | bytes 1000 | tf_op jit(solution)/shard_map/project_and_convolve_x/pallas_call | solution.py:953
  25.1 2.4 %collective-permute-start.10 = (bf16[384,128]{1,0:T(8,128)(2,1)S(1)}, bf16[384,128]{1,0:T(8,128)(2,1)S(1)}, u32[]{:S(2)}, u32[]{:S(2)}) collective-permute-start(bf16[384,128]{1,0:T(8,128)(2,1)S(1)} %get-tuple-element.78), channel_id=1, source_target_pairs={{0,8},{8,16},{16,24},{1,9},{9,17},{17,25},{2,10},{10,18},{18,26},{... | collective-permute-start | bytes 294920 | tf_op jit(solution)/shard_map/ppermute | solution.py:987
  27.5 1.2 %collective-permute-start.11 = (bf16[384,384]{1,0:T(8,128)(2,1)S(1)}, bf16[384,384]{1,0:T(8,128)(2,1)S(1)}, u32[]{:S(2)}, u32[]{:S(2)}) collective-permute-start(bf16[384,384]{1,0:T(8,128)(2,1)S(1)} %get-tuple-element.77.own_ref), channel_id=1, source_target_pairs={{0,8},{8,0},{16,24},{24,16},{1,9},{9,1},{17,25},{25,17},{2,10},{10... | collective-permute-start | bytes 884744 | tf_op jit(solution)/shard_map/ppermute | solution.py:274
  28.7 1.4 %collective-permute-done.9.far_ref = bf16[384,384]{1,0:T(8,128)(2,1)S(1)} collective-permute-done((bf16[384,384]{1,0:T(8,128)(2,1)S(1)}, bf16[384,384]{1,0:T(8,128)(2,1)S(1)}, u32[]{:S(2)}, u32[]{:S(2)}) %collective-permute-start.9) | collective-permute-done | bytes 294944 | tf_op jit(solution)/shard_map/ppermute | solution.py:274
  30.2 1.5 %sum_ended_states.1 = (bf16[8,192,128]{2,1,0:T(8,128)(2,1)S(1)}, bf16[8,192,128]{2,1,0:T(8,128)(2,1)S(1)}) custom-call(bf16[512,256]{1,0:T(8,128)(2,1)S(1)} %get-tuple-element.66.bc_ref, bf16[384,512]{1,0:T(8,128)(2,1)S(1)} %get-tuple-element.72.faded_ref, f32[512,128]{1,0:T(8,128)S(1)} %get-tuple-element.59.meta_ref), custom_call_target="tpu_custom_call" | custom-call | flops 1000 | bytes 1000 | tf_op jit(solution)/shard_map/sum_ended_states/pallas_call | solution.py:1000
  31.7 0.6 collective-permute-start.6
  32.3 1.8 %mix_within_blocks.1.y_ref = f32[512,384]{1,0:T(8,128)S(1)} custom-call(bf16[512,384]{1,0:T(8,128)(2,1)S(1)} %get-tuple-element.80.x_ref, bf16[512,256]{1,0:T(8,128)(2,1)S(1)} %get-tuple-element.66.bc_ref, bf16[512,384]{1,0:T(8,128)(2,1)S(1)} %get-tuple-element.81.stepx_ref, f32[512,128]{1,0:T(8,128)S(1)} %get-tuple-element.70.prefix_ref, ...), custom_call_target="tpu_custom_call" | custom-call | flops 1000 | bytes 1000 | tf_op jit(solution)/shard_map/mix_within_blocks/pallas_call | solution.py:991
  34.1 1.3 %project_gate.1.z_ref = f32[512,384]{1,0:T(8,128)S(1)} custom-call(bf16[512,1536]{1,0:T(8,128)(2,1)S(1)} %get-tuple-element.58.normed_ref, bf16[384,384]{1,0:T(8,128)(2,1)S(1)} %get-tuple-element.77.own_ref, bf16[384,384]{1,0:T(8,128)(2,1)S(1)} %collective-permute-done.11.near_ref, bf16[384,384]{1,0:T(8,128)(2,1)S(1)} %collective-permute-done.9.far_ref, ...), custom_call_target="tpu_custom_call" | custom-call | flops 1000 | bytes 1000 | tf_op jit(solution)/shard_map/project_gate/pallas_call | solution.py:1011
  35.5 1.5 %add_entering_and_gate.1 = (bf16[256,384]{1,0:T(8,128)(2,1)S(1)}, bf16[256,384]{1,0:T(8,128)(2,1)S(1)}, bf16[384,128]{1,0:T(8,128)(2,1)S(1)}) custom-call(s32[2048]{0:T(1024)S(1)} %copy-done.4, bf16[384,128]{1,0:T(8,128)(2,1)S(1)} %collective-permute-done.10.enter_ref, bf16[512,256]{1,0:T(8,128)(2,1)S(1)} %get-tuple-element.66.bc_ref, ...), custom_call_target="tpu_custom_call" | custom-call | flops 1000 | bytes 1000 | tf_op jit(solution)/shard_map/add_entering_and_gate/pallas_call | solution.py:1023
  36.9 1.6 %collective-permute-start.18 = (bf16[256,384]{1,0:T(8,128)(2,1)S(1)}, bf16[256,384]{1,0:T(8,128)(2,1)S(1)}, u32[]{:S(2)}, u32[]{:S(2)}) collective-permute-start(bf16[256,384]{1,0:T(8,128)(2,1)S(1)} %get-tuple-element.88), channel_id=1, source_target_pairs={{0,2},{1,3},{2,0},{3,1},{4,6},{5,7},{6,4},{7,5},{8,10},{9,11},{10,... | collective-permute-start | bytes 589832 | tf_op jit(solution)/shard_map/ppermute | solution.py:274
  38.6 5.7 %collective-permute-done.18.got_ref = bf16[256,384]{1,0:T(8,128)(2,1)S(1)} collective-permute-done((bf16[256,384]{1,0:T(8,128)(2,1)S(1)}, bf16[256,384]{1,0:T(8,128)(2,1)S(1)}, u32[]{:S(2)}, u32[]{:S(2)}) %collective-permute-start.18) | collective-permute-done | bytes 196640 | tf_op jit(solution)/shard_map/ppermute | solution.py:274
  44.2 1.5 %project_out.1 = (f32[64,1664]{1,0:T(8,128)S(1)}, bf16[64,1664]{1,0:T(8,128)(2,1)S(1)}, f32[64,1664]{1,0:T(8,128)S(1)}, bf16[64,1664]{1,0:T(8,128)(2,1)S(1)}) custom-call(bf16[256,384]{1,0:T(8,128)(2,1)S(1)} %get-tuple-element.87.kept_ref, bf16[256,384]{1,0:T(8,128)(2,1)S(1)} %collective-permute-done.18.got_ref, ...), custom_call_target="tpu_custom_call" | custom-call | flops 1000 | bytes 1000 | tf_op jit(solution)/shard_map/project_out/pallas_call | solution.py:1051
  45.8 1.6 %collective-permute-start.19 = (bf16[64,1664]{1,0:T(8,128)(2,1)S(1)}, bf16[64,1664]{1,0:T(8,128)(2,1)S(1)}, u32[]{:S(2)}, u32[]{:S(2)}) collective-permute-start(bf16[64,1664]{1,0:T(8,128)(2,1)S(1)} %get-tuple-element.92), channel_id=1, source_target_pairs={{0,1},{1,0},{2,3},{3,2},{4,5},{5,4},{6,7},{7,6},{8,9},{9,8},{10,11... | collective-permute-start | bytes 638984 | tf_op jit(solution)/shard_map/ppermute | solution.py:274
  47.4 0.9 %pick_request_states.1 = (bf16[4,384,128]{2,1,0:T(8,128)(2,1)S(1)}, bf16[4,384,128]{2,1,0:T(8,128)(2,1)S(1)}) custom-call(s32[4]{0:T(128)S(1)} %copy-done.6, bf16[480,256]{1,0:T(8,128)(2,1)S(1)} %collective-permute-done.far_ref, bf16[8,192,128]{2,1,0:T(8,128)(2,1)S(1)} %get-tuple-element.73.refs_0_, bf16[8,192,128]{2,1,0:T(8,128)(2,1)S(1)} %get-tuple-element.74.refs_1_, ...), custom_call_target="tpu_custom_call" | custom-call | flops 1000 | bytes 1000 | tf_op jit(solution)/shard_map/pick_request_states/pallas_call | solution.py:1036
  48.2 2.4 %collective-permute-start.8 = (bf16[4,384,128]{2,1,0:T(8,128)(2,1)S(1)}, bf16[4,384,128]{2,1,0:T(8,128)(2,1)S(1)}, u32[]{:S(2)}, u32[]{:S(2)}) collective-permute-start(bf16[4,384,128]{2,1,0:T(8,128)(2,1)S(1)} %get-tuple-element.76), channel_id=1, source_target_pairs={{0,16},{8,24},{16,0},{24,8},{1,17},{9,25},{17,1},{25,9},{2,18},{10... | collective-permute-start | bytes 1179656 | tf_op jit(solution)/shard_map/ppermute | solution.py:274
  50.7 2.0 %collective-permute-done.19.cross_ref = bf16[64,1664]{1,0:T(8,128)(2,1)S(1)} collective-permute-done((bf16[64,1664]{1,0:T(8,128)(2,1)S(1)}, bf16[64,1664]{1,0:T(8,128)(2,1)S(1)}, u32[]{:S(2)}, u32[]{:S(2)}) %collective-permute-start.19) | collective-permute-done | bytes 213024 | tf_op jit(solution)/shard_map/ppermute | solution.py:274
  52.8 2.7 %collective-permute-start.21 = (bf16[64,1664]{1,0:T(8,128)(2,1)S(1)}, bf16[64,1664]{1,0:T(8,128)(2,1)S(1)}, u32[]{:S(2)}, u32[]{:S(2)}) collective-permute-start(bf16[64,1664]{1,0:T(8,128)(2,1)S(1)} %add_sums_to_pass_on.1), channel_id=1, source_target_pairs={{0,4},{1,5},{2,6},{3,7},{4,0},{5,1},{6,2},{7,3},{8,12},{9,13},{10,... | collective-permute-start | bytes 638984 | tf_op jit(solution)/shard_map/ppermute | solution.py:274
  55.5 1.5 %collective-permute-start.20 = (bf16[64,1664]{1,0:T(8,128)(2,1)S(1)}, bf16[64,1664]{1,0:T(8,128)(2,1)S(1)}, u32[]{:S(2)}, u32[]{:S(2)}) collective-permute-start(bf16[64,1664]{1,0:T(8,128)(2,1)S(1)} %get-tuple-element.94), channel_id=1, source_target_pairs={{0,1},{1,0},{2,3},{3,2},{4,5},{5,4},{6,7},{7,6},{8,9},{9,8},{10,11... | collective-permute-start | bytes 638984 | tf_op jit(solution)/shard_map/ppermute | solution.py:274
  57.0 2.4 %collective-permute-start.16 = (bf16[384,128]{1,0:T(8,128)(2,1)S(1)}, bf16[384,128]{1,0:T(8,128)(2,1)S(1)}, u32[]{:S(2)}, u32[]{:S(2)}) collective-permute-start(bf16[384,128]{1,0:T(8,128)(2,1)S(1)} %get-tuple-element.86.refs_0_), channel_id=1, source_target_pairs={{0,16},{8,24},{16,0},{24,8},{1,17},{9,25},{17,1},{25,9},{2,18},{10... | collective-permute-start | bytes 294920 | tf_op jit(solution)/shard_map/ppermute | solution.py:274
  59.4 2.6 %collective-permute-done.16.refs_2_ = bf16[384,128]{1,0:T(8,128)(2,1)S(1)} collective-permute-done((bf16[384,128]{1,0:T(8,128)(2,1)S(1)}, bf16[384,128]{1,0:T(8,128)(2,1)S(1)}, u32[]{:S(2)}, u32[]{:S(2)}) %collective-permute-start.16) | collective-permute-done | bytes 98336 | tf_op jit(solution)/shard_map/ppermute | solution.py:274
  62.0 1.3 %collective-permute-done.17.refs_3_ = bf16[384,128]{1,0:T(8,128)(2,1)S(1)} collective-permute-done((bf16[384,128]{1,0:T(8,128)(2,1)S(1)}, bf16[384,128]{1,0:T(8,128)(2,1)S(1)}, u32[]{:S(2)}, u32[]{:S(2)}) %collective-permute-start.17) | collective-permute-done | bytes 98336 | tf_op jit(solution)/shard_map/ppermute | solution.py:274
  63.3 1.7 %join_request_states.1 = (f32[4,384,128]{2,1,0:T(8,128)}, f32[8,128]{1,0:T(8,128)S(1)}) custom-call(s32[2048]{0:T(1024)S(1)} %copy-done.4, s32[4]{0:T(128)S(1)} %copy-done.6, bf16[4,384,128]{2,1,0:T(8,128)(2,1)S(1)} %get-tuple-element.75.keep_ref, bf16[4,384,128]{2,1,0:T(8,128)(2,1)S(1)} %collective-permute-done.8.far_ref, ...), custom_call_target="tpu_custom_call" | custom-call | flops 1000 | bytes 1000 | tf_op jit(solution)/shard_map/join_request_states/pallas_call | solution.py:1079
  65.0 1.1 %scale_and_add_hidden.1 = bf16[64,1536]{1,0:T(8,128)(2,1)} custom-call(bf16[512,1536]{1,0:T(8,128)(2,1)S(1)} %copy-done, f32[8,128]{1,0:T(8,128)S(1)} %get-tuple-element.91.joined_ref, f32[64,1664]{1,0:T(8,128)S(1)} %get-tuple-element.90.refs_4_.keep_ref, bf16[64,1664]{1,0:T(8,128)(2,1)S(1)} %collective-permute-done.20.refs_0_, ...), custom_call_target="tpu_custom_call" | custom-call | flops 1000 | bytes 1000 | tf_op jit(solution)/shard_map/scale_and_add_hidden/pallas_call | solution.py:1088
  (55 shorter events, 2.7 us)
Async XLA Ops:
  0.6 5.6 %copy-start.12 = (f32[384]{0:T(512)S(1)}, f32[384]{0:T(512)}, u32[]{:S(2)}) copy-start(f32[384]{0:T(512)} %param.26) | copy-start | bytes 4612
  0.6 5.6 %copy-start.1 = (bf16[384,1536]{1,0:T(8,128)(2,1)S(1)}, bf16[384,1536]{1,0:T(8,128)(2,1)}, u32[]{:S(2)}) copy-start(bf16[384,1536]{1,0:T(8,128)(2,1)} %w_ref.1) | copy-start | bytes 3538948
  0.7 7.8 %copy-start.2 = (f32[384,2,384]{2,1,0:T(2,128)S(1)}, f32[384,2,384]{2,1,0:T(2,128)}, u32[]{:S(2)}) copy-start(f32[384,2,384]{2,1,0:T(2,128)} %wzx_ref.1) | copy-start | bytes 3538948
  3.2 9.2 %collective-permute-start = (bf16[480,256]{1,0:T(8,128)(2,1)}, bf16[480,256]{1,0:T(8,128)(2,1)S(1)}, u32[]{:S(2)}, u32[]{:S(2)}) collective-permute-start(bf16[480,256]{1,0:T(8,128)(2,1)} %pack_first_weights.1.own_ref), channel_id=1, source_target_pairs={{0,16},{8,24},{16,0},{24,8},{1,17},{9,25},{17,1},{25,9},{2,18},{10... | collective-permute-start | bytes 737288 | tf_op jit(solution)/shard_map/ppermute | solution.py:274
  6.7 7.4 %copy-start.3 = (bf16[480,256]{1,0:T(8,128)(2,1)S(1)}, bf16[480,256]{1,0:T(8,128)(2,1)}, u32[]{:S(2)}) copy-start(bf16[480,256]{1,0:T(8,128)(2,1)} %pack_first_weights.1.own_ref) | copy-start | bytes 737284
  6.8 9.3 %copy-start.7 = (f32[4,256]{1,0:T(4,128)S(1)}, f32[4,256]{1,0:T(4,128)}, u32[]{:S(2)}) copy-start(f32[4,256]{1,0:T(4,128)} %taps_ref.2) | copy-start | bytes 12292
  6.8 9.3 %copy-start.8 = (f32[6]{0:T(128)S(1)}, f32[6]{0:T(128)}, u32[]{:S(2)}) copy-start(f32[6]{0:T(128)} %bias_ref.1) | copy-start | bytes 76
  6.8 9.2 %copy-start.9 = (f32[6]{0:T(128)S(1)}, f32[6]{0:T(128)}, u32[]{:S(2)}) copy-start(f32[6]{0:T(128)} %decay_ref.1) | copy-start | bytes 76
  6.8 15.2 %collective-permute-start.13 = (bf16[384,768]{1,0:T(8,128)(2,1)S(1)}, bf16[384,768]{1,0:T(8,128)(2,1)S(1)}, u32[]{:S(2)}, u32[]{:S(2)}) collective-permute-start(bf16[384,768]{1,0:T(8,128)(2,1)S(1)} %get-tuple-element.85), channel_id=1, source_target_pairs={{0,2},{1,3},{2,0},{3,1},{4,6},{5,7},{6,4},{7,5},{8,10},{9,11},{10,... | collective-permute-start | bytes 1769480 | tf_op jit(solution)/shard_map/ppermute | solution.py:274
  12.4 9.9 %copy-start.5 = (f32[4,384]{1,0:T(4,128)S(1)}, f32[4,384]{1,0:T(4,128)}, u32[]{:S(2)}) copy-start(f32[4,384]{1,0:T(4,128)} %taps_ref.3) | copy-start | bytes 18436
  12.4 8.2 %collective-permute-start.1 = (bf16[384,384]{1,0:T(8,128)(2,1)S(1)}, bf16[384,384]{1,0:T(8,128)(2,1)S(1)}, u32[]{:S(2)}, u32[]{:S(2)}) collective-permute-start(bf16[384,384]{1,0:T(8,128)(2,1)S(1)} %get-tuple-element.56.own_ref), channel_id=1, source_target_pairs={{0,16},{8,24},{16,0},{24,8},{1,17},{9,25},{17,1},{25,9},{2,18},{10... | collective-permute-start | bytes 884744 | tf_op jit(solution)/shard_map/ppermute | solution.py:274
  14.2 1.5 %collective-permute-start.2 = (bf16[480,256]{1,0:T(8,128)(2,1)S(1)}, bf16[480,256]{1,0:T(8,128)(2,1)S(1)}, u32[]{:S(2)}, u32[]{:S(2)}) collective-permute-start(bf16[480,256]{1,0:T(8,128)(2,1)S(1)} %copy-done.3), channel_id=1, source_target_pairs={{0,8},{8,0},{16,24},{24,16},{1,9},{9,1},{17,25},{25,17},{2,10},{10... | collective-permute-start | bytes 737288 | tf_op jit(solution)/shard_map/ppermute | solution.py:274
  14.2 1.9 %collective-permute-start.3 = (bf16[480,256]{1,0:T(8,128)(2,1)S(1)}, bf16[480,256]{1,0:T(8,128)(2,1)S(1)}, u32[]{:S(2)}, u32[]{:S(2)}) collective-permute-start(bf16[480,256]{1,0:T(8,128)(2,1)S(1)} %collective-permute-done.far_ref), channel_id=1, source_target_pairs={{0,8},{8,0},{16,24},{24,16},{1,9},{9,1},{17,25},{25,17},{2,10},{10... | collective-permute-start | bytes 737288 | tf_op jit(solution)/shard_map/ppermute | solution.py:274
  14.7 7.6 %collective-permute-start.4 = (bf16[384,384]{1,0:T(8,128)(2,1)S(1)}, bf16[384,384]{1,0:T(8,128)(2,1)S(1)}, u32[]{:S(2)}, u32[]{:S(2)}) collective-permute-start(bf16[384,384]{1,0:T(8,128)(2,1)S(1)} %get-tuple-element.56.own_ref), channel_id=1, source_target_pairs={{0,8},{8,0},{16,24},{24,16},{1,9},{9,1},{17,25},{25,17},{2,10},{10... | collective-permute-start | bytes 884744 | tf_op jit(solution)/shard_map/ppermute | solution.py:274
  20.6 11.7 %copy-start.10 = (f32[6]{0:T(128)S(1)}, f32[6]{0:T(128)}, u32[]{:S(2)}) copy-start(f32[6]{0:T(128)} %skip_ref.1) | copy-start | bytes 76
  20.7 1.6 %collective-permute-start.5 = (bf16[384,384]{1,0:T(8,128)(2,1)S(1)}, bf16[384,384]{1,0:T(8,128)(2,1)S(1)}, u32[]{:S(2)}, u32[]{:S(2)}) collective-permute-start(bf16[384,384]{1,0:T(8,128)(2,1)S(1)} %collective-permute-done.1.far_ref), channel_id=1, source_target_pairs={{0,8},{8,0},{16,24},{24,16},{1,9},{9,1},{17,25},{25,17},{2,10},{10... | collective-permute-start | bytes 884744 | tf_op jit(solution)/shard_map/ppermute | solution.py:274
  20.9 9.3 %collective-permute-start.9 = (bf16[384,384]{1,0:T(8,128)(2,1)S(1)}, bf16[384,384]{1,0:T(8,128)(2,1)S(1)}, u32[]{:S(2)}, u32[]{:S(2)}) collective-permute-start(bf16[384,384]{1,0:T(8,128)(2,1)S(1)} %get-tuple-element.77.own_ref), channel_id=1, source_target_pairs={{0,16},{8,24},{16,0},{24,8},{1,17},{9,25},{17,1},{25,9},{2,18},{10... | collective-permute-start | bytes 884744 | tf_op jit(solution)/shard_map/ppermute | solution.py:274
  22.0 13.4 %collective-permute-start.14 = (bf16[384,768]{1,0:T(8,128)(2,1)S(1)}, bf16[384,768]{1,0:T(8,128)(2,1)S(1)}, u32[]{:S(2)}, u32[]{:S(2)}) collective-permute-start(bf16[384,768]{1,0:T(8,128)(2,1)S(1)} %collective-permute-done.13.part_ref), channel_id=1, source_target_pairs={{0,8},{8,0},{16,24},{24,16},{1,9},{9,1},{17,25},{25,17},{2,10},{10... | collective-permute-start | bytes 1769480 | tf_op jit(solution)/shard_map/ppermute | solution.py:274
  25.1 5.0 %collective-permute-start.10 = (bf16[384,128]{1,0:T(8,128)(2,1)S(1)}, bf16[384,128]{1,0:T(8,128)(2,1)S(1)}, u32[]{:S(2)}, u32[]{:S(2)}) collective-permute-start(bf16[384,128]{1,0:T(8,128)(2,1)S(1)} %get-tuple-element.78), channel_id=1, source_target_pairs={{0,8},{8,16},{16,24},{1,9},{9,17},{17,25},{2,10},{10,18},{18,26},{... | collective-permute-start | bytes 294920 | tf_op jit(solution)/shard_map/ppermute | solution.py:987
  27.5 6.6 %collective-permute-start.11 = (bf16[384,384]{1,0:T(8,128)(2,1)S(1)}, bf16[384,384]{1,0:T(8,128)(2,1)S(1)}, u32[]{:S(2)}, u32[]{:S(2)}) collective-permute-start(bf16[384,384]{1,0:T(8,128)(2,1)S(1)} %get-tuple-element.77.own_ref), channel_id=1, source_target_pairs={{0,8},{8,0},{16,24},{24,16},{1,9},{9,1},{17,25},{25,17},{2,10},{10... | collective-permute-start | bytes 884744 | tf_op jit(solution)/shard_map/ppermute | solution.py:274
  30.1 4.0 %collective-permute-start.12 = (bf16[384,384]{1,0:T(8,128)(2,1)S(1)}, bf16[384,384]{1,0:T(8,128)(2,1)S(1)}, u32[]{:S(2)}, u32[]{:S(2)}) collective-permute-start(bf16[384,384]{1,0:T(8,128)(2,1)S(1)} %collective-permute-done.9.far_ref), channel_id=1, source_target_pairs={{0,8},{8,0},{16,24},{24,16},{1,9},{9,1},{17,25},{25,17},{2,10},{10... | collective-permute-start | bytes 884744 | tf_op jit(solution)/shard_map/ppermute | solution.py:274
  31.7 15.7 %collective-permute-start.6 = (bf16[8,192,128]{2,1,0:T(8,128)(2,1)S(1)}, bf16[8,192,128]{2,1,0:T(8,128)(2,1)S(1)}, u32[]{:S(2)}, u32[]{:S(2)}) collective-permute-start(bf16[8,192,128]{2,1,0:T(8,128)(2,1)S(1)} %get-tuple-element.73.refs_0_), channel_id=1, source_target_pairs={{0,8},{8,0},{16,24},{24,16},{1,9},{9,1},{17,25},{25,17},{2,10},{10... | collective-permute-start | bytes 1179656 | tf_op jit(solution)/shard_map/ppermute | solution.py:274
  32.2 15.1 %collective-permute-start.7 = (bf16[8,192,128]{2,1,0:T(8,128)(2,1)S(1)}, bf16[8,192,128]{2,1,0:T(8,128)(2,1)S(1)}, u32[]{:S(2)}, u32[]{:S(2)}) collective-permute-start(bf16[8,192,128]{2,1,0:T(8,128)(2,1)S(1)} %get-tuple-element.74.refs_1_), channel_id=1, source_target_pairs={{0,8},{8,0},{16,24},{24,16},{1,9},{9,1},{17,25},{25,17},{2,10},{10... | collective-permute-start | bytes 1179656 | tf_op jit(solution)/shard_map/ppermute | solution.py:274
  36.9 7.3 %collective-permute-start.18 = (bf16[256,384]{1,0:T(8,128)(2,1)S(1)}, bf16[256,384]{1,0:T(8,128)(2,1)S(1)}, u32[]{:S(2)}, u32[]{:S(2)}) collective-permute-start(bf16[256,384]{1,0:T(8,128)(2,1)S(1)} %get-tuple-element.88), channel_id=1, source_target_pairs={{0,2},{1,3},{2,0},{3,1},{4,6},{5,7},{6,4},{7,5},{8,10},{9,11},{10,... | collective-permute-start | bytes 589832 | tf_op jit(solution)/shard_map/ppermute | solution.py:274
  44.2 3.1 %copy-start.6 = (s32[4]{0:T(128)S(1)}, s32[4]{0:T(128)}, u32[]{:S(2)}) copy-start(s32[4]{0:T(128)} %own_ref.3) | copy-start | bytes 52
  45.8 6.9 %collective-permute-start.19 = (bf16[64,1664]{1,0:T(8,128)(2,1)S(1)}, bf16[64,1664]{1,0:T(8,128)(2,1)S(1)}, u32[]{:S(2)}, u32[]{:S(2)}) collective-permute-start(bf16[64,1664]{1,0:T(8,128)(2,1)S(1)} %get-tuple-element.92), channel_id=1, source_target_pairs={{0,1},{1,0},{2,3},{3,2},{4,5},{5,4},{6,7},{7,6},{8,9},{9,8},{10,11... | collective-permute-start | bytes 638984 | tf_op jit(solution)/shard_map/ppermute | solution.py:274
  48.2 15.0 %collective-permute-start.8 = (bf16[4,384,128]{2,1,0:T(8,128)(2,1)S(1)}, bf16[4,384,128]{2,1,0:T(8,128)(2,1)S(1)}, u32[]{:S(2)}, u32[]{:S(2)}) collective-permute-start(bf16[4,384,128]{2,1,0:T(8,128)(2,1)S(1)} %get-tuple-element.76), channel_id=1, source_target_pairs={{0,16},{8,24},{16,0},{24,8},{1,17},{9,25},{17,1},{25,9},{2,18},{10... | collective-permute-start | bytes 1179656 | tf_op jit(solution)/shard_map/ppermute | solution.py:274
  52.8 12.2 %collective-permute-start.21 = (bf16[64,1664]{1,0:T(8,128)(2,1)S(1)}, bf16[64,1664]{1,0:T(8,128)(2,1)S(1)}, u32[]{:S(2)}, u32[]{:S(2)}) collective-permute-start(bf16[64,1664]{1,0:T(8,128)(2,1)S(1)} %add_sums_to_pass_on.1), channel_id=1, source_target_pairs={{0,4},{1,5},{2,6},{3,7},{4,0},{5,1},{6,2},{7,3},{8,12},{9,13},{10,... | collective-permute-start | bytes 638984 | tf_op jit(solution)/shard_map/ppermute | solution.py:274
  55.5 9.5 %collective-permute-start.20 = (bf16[64,1664]{1,0:T(8,128)(2,1)S(1)}, bf16[64,1664]{1,0:T(8,128)(2,1)S(1)}, u32[]{:S(2)}, u32[]{:S(2)}) collective-permute-start(bf16[64,1664]{1,0:T(8,128)(2,1)S(1)} %get-tuple-element.94), channel_id=1, source_target_pairs={{0,1},{1,0},{2,3},{3,2},{4,5},{5,4},{6,7},{7,6},{8,9},{9,8},{10,11... | collective-permute-start | bytes 638984 | tf_op jit(solution)/shard_map/ppermute | solution.py:274
  57.0 5.0 %collective-permute-start.16 = (bf16[384,128]{1,0:T(8,128)(2,1)S(1)}, bf16[384,128]{1,0:T(8,128)(2,1)S(1)}, u32[]{:S(2)}, u32[]{:S(2)}) collective-permute-start(bf16[384,128]{1,0:T(8,128)(2,1)S(1)} %get-tuple-element.86.refs_0_), channel_id=1, source_target_pairs={{0,16},{8,24},{16,0},{24,8},{1,17},{9,25},{17,1},{25,9},{2,18},{10... | collective-permute-start | bytes 294920 | tf_op jit(solution)/shard_map/ppermute | solution.py:274
  59.4 2.6 %collective-permute-start.15 = (bf16[384,128]{1,0:T(8,128)(2,1)S(1)}, bf16[384,128]{1,0:T(8,128)(2,1)S(1)}, u32[]{:S(2)}, u32[]{:S(2)}) collective-permute-start(bf16[384,128]{1,0:T(8,128)(2,1)S(1)} %get-tuple-element.86.refs_0_), channel_id=1, source_target_pairs={{0,8},{8,0},{16,24},{24,16},{1,9},{9,1},{17,25},{25,17},{2,10},{10... | collective-permute-start | bytes 294920 | tf_op jit(solution)/shard_map/ppermute | solution.py:274
  62.0 1.3 %collective-permute-start.17 = (bf16[384,128]{1,0:T(8,128)(2,1)S(1)}, bf16[384,128]{1,0:T(8,128)(2,1)S(1)}, u32[]{:S(2)}, u32[]{:S(2)}) collective-permute-start(bf16[384,128]{1,0:T(8,128)(2,1)S(1)} %collective-permute-done.16.refs_2_), channel_id=1, source_target_pairs={{0,8},{8,0},{16,24},{24,16},{1,9},{9,1},{17,25},{25,17},{2,10},{10... | collective-permute-start | bytes 294920 | tf_op jit(solution)/shard_map/ppermute | solution.py:274
  (3 other events, 8.2 us)

commit v4 on v3

--- a/solution.py
+++ b/solution.py
@@ -258,7 +258,8 @@
 TILE_ROWS = 16
 NEVER = -1e30
 Y_NEAR, Z_NEAR, Z_FAR = 1, 2, 4
-RELATED = (0, Y_NEAR, Z_FAR, Y_NEAR | Z_FAR)
+PASSED = (Z_FAR, Y_NEAR | Z_FAR)
+STAYING = (0, Y_NEAR)
 LITTLE = pl.CostEstimate(flops=1000, bytes_accessed=1000, transcendentals=0)
 
 
@@ -294,7 +295,7 @@
 
 
 def pack_first_kernel(
-    req_ref, wbc_ref, wdt_ref, hidden_ref, first_ref, bc_v, dt_v, tail_v, dt_wide, sems
+    req_ref, wbc_ref, wdt_ref, hidden_ref, first_ref, req_v, bc_v, dt_v, tail_v, dt_wide, sems
 ):
     rows, width = bc_v.shape
     tok, model = hidden_ref.shape
@@ -302,6 +303,7 @@
         pltpu.make_async_copy(source, target, sems.at[k])
         for k, (source, target) in enumerate(
             (
+                (req_ref, req_v),
                 (wdt_ref, dt_v),
                 (hidden_ref.at[tok - TILE_ROWS : tok], tail_v),
                 (wbc_ref, bc_v),
@@ -311,20 +313,17 @@
     for copy in arrivals:
         copy.start()
     dt_wide[...] = jnp.zeros_like(dt_wide)
-    lane = lax.broadcasted_iota(jnp.int32, (1, LANES), 1)
-    wanted = jnp.zeros((1, LANES), jnp.float32)
-    for r in range(req_ref.shape[0]):
-        wanted = jnp.where(lane == r, req_ref[r].astype(jnp.float32), wanted)
-    dt_wide[0:1, rows : rows + LANES] = wanted
     arrivals[0].wait()
+    dt_wide[0:1, rows : rows + req_v.shape[1]] = req_v[...].astype(jnp.float32)
+    arrivals[1].wait()
     dt_wide[0 : dt_v.shape[0], 0:rows] = dt_v[...]
-    arrivals[1].wait()
+    arrivals[2].wait()
     upper = lax.broadcasted_iota(jnp.int32, (TILE_ROWS, model), 0) < TILE_ROWS // 2
     below = jnp.where(upper, dt_wide[...], tail_v[...].astype(jnp.float32)).astype(jnp.bfloat16)
     for i in range(model // width):
         at = rows + TILE_ROWS * i
         first_ref[at : at + TILE_ROWS, :] = below[:, i * width : (i + 1) * width]
-    arrivals[2].wait()
+    arrivals[3].wait()
     first_ref[0:rows, :] = bc_v[...].astype(jnp.bfloat16)
 
 
@@ -536,13 +535,11 @@
     meta_ref,
     bc_ref,
     step_ref,
-    prefix_ref,
     fade_ref,
     x_ref,
     stepx_ref,
     faded_ref,
     leaving_ref,
-    middle_ref,
     w_ref,
     ext_ref,
     sems,
@@ -558,10 +555,8 @@
     state_width = leaving_ref.shape[1]
     step = step_ref[...]
     fade = fade_ref[...]
-    fade_middle = jnp.exp(prefix_ref[BLOCK - 1 : BLOCK, :] - prefix_ref[0:BLOCK, :])
     b_all = bc_ref[:, 0:state_width].astype(jnp.float32)
     b_leaving = (b_all * meta_ref[:, 7:8]).astype(jnp.bfloat16)
-    b_middle = (b_all * meta_ref[:, 5:6])[0:BLOCK].astype(jnp.bfloat16)
     same = [jnp.broadcast_to(meta_ref[:, k : k + 1], (tok, LANES)) for k in range(3)]
     for copy in copies:
         copy.wait()
@@ -575,12 +570,16 @@
         faded = (scaled * widen(fade, q, head_dim)).astype(jnp.bfloat16).T
         faded_ref[own, :] = faded
         leaving_ref[own, :] = dot32(faded, b_leaving).astype(jnp.bfloat16)
-        to_middle = (scaled[0:BLOCK] * widen(fade_middle, q, head_dim)).astype(jnp.bfloat16).T
-        middle_ref[own, :] = dot32(to_middle, b_middle).astype(jnp.bfloat16)
-
-
-def table_kernel(bc_ref, faded_ref, meta_ref, *table_refs):
+
+
+def before_device(ids_ref, position, tok):
+    return jnp.where(position > 0, ids_ref[jnp.maximum(position * tok - 1, 0)], -1)
+
+
+def table_kernel(ids_ref, bc_ref, faded_ref, meta_ref, prefix_ref, enter_ref, *table_refs):
     rows, state_width = table_refs[0].shape[1:]
+    head_dim = LANES // 2
+    tok = bc_ref.shape[0]
     b_all = bc_ref[:, 0:state_width].astype(jnp.float32)
     for g in range(table_refs[0].shape[0]):
         ended = jnp.where(meta_ref[:, 6:7] == g, meta_ref[:, 8:9], 0.0)
@@ -588,6 +587,25 @@
         for k, table_ref in enumerate(table_refs):
             faded = faded_ref[k * rows : (k + 1) * rows, :]
             table_ref[g] = dot32(faded, b_ended).astype(jnp.bfloat16)
+    position = lax.axis_index("dp")
+    before = before_device(ids_ref, position, tok)
+    stop = (position + 1) * tok
+    after = ids_ref[jnp.minimum(stop, ids_ref.shape[0] - 1)]
+    goes_on = (after == before) & (stop < ids_ref.shape[0])
+    ended = (ids_ref[position * tok] == before) & ((ids_ref[stop - 1] != before) | ~goes_on)
+
+    @pl.when(ended)
+    def add():
+        inside = jnp.where(meta_ref[:, 3:4] > 0.0, prefix_ref[...], 0.0)
+        gain = jnp.exp(jnp.min(inside, axis=0, keepdims=True))
+        chunk = head_dim // 2
+        for n in range(faded_ref.shape[0] // chunk):
+            table_ref = table_refs[n * chunk // rows]
+            own = slice(n * chunk % rows, n * chunk % rows + chunk)
+            h = n * chunk // head_dim
+            entering = enter_ref[n * chunk : (n + 1) * chunk, :].astype(jnp.float32)
+            old = table_ref[before, own, :].astype(jnp.float32)
+            table_ref[before, own, :] = (old + gain[:, h : h + 1] * entering).astype(jnp.bfloat16)
 
 
 def local_kernel(
@@ -595,14 +613,13 @@
     bc_ref,
     stepx_ref,
     prefix_ref,
-    middle_ref,
     meta_ref,
     pen_ref,
     skip_ref,
     y_ref,
 ):
     inner = y_ref.shape[1]
-    state_width = middle_ref.shape[1]
+    state_width = bc_ref.shape[1] // 2
     head_dim = LANES // 2
     tok = y_ref.shape[0]
     lane = lax.broadcasted_iota(jnp.int32, (BLOCK, LANES), 1)
@@ -617,13 +634,19 @@
         if b > 0:
             carried = jnp.exp(prefix - prefix_ref[b * BLOCK - 1 : b * BLOCK, :])
             carried = carried * meta_ref[own_rows, 4:5]
-            from_middle = dot32(c_blk, middle_ref[...], 1, 1)
+            before_rows = slice((b - 1) * BLOCK, b * BLOCK)
+            before = prefix_ref[before_rows, :]
+            fade = jnp.exp(before[BLOCK - 1 : BLOCK, :] - before)
+            b_before = bc_ref[before_rows, 0:state_width].astype(jnp.float32)
+            b_before = (b_before * meta_ref[before_rows, 5:6]).astype(jnp.bfloat16)
         for q in range(inner // LANES):
             own = slice(q * LANES, (q + 1) * LANES)
             x_pair = x_ref[own_rows, own].astype(jnp.float32)
             out = x_pair * jnp.where(lane < head_dim, skip_ref[2 * q], skip_ref[2 * q + 1])
             if b > 0:
-                out = out + widen(carried, q, head_dim) * from_middle[:, own]
+                faded = stepx_ref[before_rows, own].astype(jnp.float32) * widen(fade, q, head_dim)
+                middle = dot32(faded.astype(jnp.bfloat16).T, b_before).astype(jnp.bfloat16)
+                out = out + widen(carried, q, head_dim) * dot32(c_blk, middle, 1, 1)
             sx = stepx_ref[own_rows, own].astype(jnp.float32)
             for side in range(2):
                 h = 2 * q + side
@@ -634,61 +657,47 @@
             y_ref[own_rows, own] = out
 
 
-def z_kernel(normed_ref, own_ref, near_ref, far_ref, last_ref, gate_ref, w_ref, sems):
+def z_most_kernel(normed_ref, own_ref, near_ref, far_ref, most_ref):
+    position = lax.axis_index("dp")
     rows = own_ref.shape[0]
-    position = lax.axis_index("dp")
-    copies = gather_rows(position, (own_ref, near_ref, far_ref, last_ref), rows, w_ref, sems)
-    for copy in copies:
-        copy.start()
-    for copy in copies:
-        copy.wait()
-    gate_ref[...] = silu_tanh(dot32(normed_ref[...], w_ref[...]))
-
-
-def before_device(ids_ref, position, tok):
-    return jnp.where(position > 0, ids_ref[jnp.maximum(position * tok - 1, 0)], -1)
-
-
-def gate_kernel(
-    ids_ref, enter_ref, bc_ref, prefix_ref, meta_ref, y_ref, z_ref, arrived_ref, *outs
-):
-    scratch, add_ref = outs[-1], outs[-2]
-    outs = outs[:-2]
+    total = 0.0
+    for j, w_ref in enumerate((own_ref, near_ref, far_ref)):
+        at = pl.multiple_of(jnp.bitwise_xor(position, j) * rows, LANES)
+        total = total + dot32(normed_ref[:, pl.ds(at, rows)], w_ref[...])
+    most_ref[...] = total
+
+
+def z_last_kernel(normed_ref, last_ref, most_ref, gate_ref):
+    rows = last_ref.shape[0]
+    at = pl.multiple_of(jnp.bitwise_xor(lax.axis_index("dp"), 3) * rows, LANES)
+    gate_ref[...] = silu_tanh(most_ref[...] + dot32(normed_ref[:, pl.ds(at, rows)], last_ref[...]))
+
+
+def gate_kernel(enter_ref, bc_ref, prefix_ref, meta_ref, y_ref, z_ref, arrived_ref, *outs):
+    scratch = outs[-1]
     inner = y_ref.shape[1]
     state_width = enter_ref.shape[1]
     head_dim = LANES // 2
-    tok = y_ref.shape[0]
     c_all = bc_ref[:, state_width:]
     inter = dot32(c_all, enter_ref[...], 1, 1)
-    prefix = prefix_ref[...]
-    carried = jnp.exp(prefix) * meta_ref[:, 3:4]
+    carried = jnp.exp(prefix_ref[...]) * meta_ref[:, 3:4]
     for q in range(inner // LANES):
         own = slice(q * LANES, (q + 1) * LANES)
         value = y_ref[:, own] + widen(carried, q, head_dim) * inter[:, own]
         scratch[:, own] = (value * z_ref[:, own]).astype(jnp.bfloat16)
-    position = lax.axis_index("dp")
-    before = before_device(ids_ref, position, tok)
-    stop = (position + 1) * tok
-    after = ids_ref[jnp.minimum(stop, ids_ref.shape[0] - 1)]
-    goes_on = (after == before) & (stop < ids_ref.shape[0])
-    ended = (ids_ref[position * tok] == before) & ((ids_ref[stop - 1] != before) | ~goes_on)
-    inside = jnp.where(meta_ref[:, 3:4] > 0.0, prefix, 0.0)
-    gain = jnp.exp(jnp.min(inside, axis=0, keepdims=True)) * jnp.where(ended, 1.0, 0.0)
-    for h in range(inner // head_dim):
-        own = slice(h * head_dim, (h + 1) * head_dim)
-        term = gain[:, h : h + 1] * enter_ref[own, :].astype(jnp.float32)
-        add_ref[own, :] = term.astype(jnp.bfloat16)
     head = lax.axis_index("head")
-    part = outs[0].shape[0] // len(RELATED)
-    for out, owner in zip(outs, (head, jnp.bitwise_xor(head, Z_NEAR))):
-        for k, bits in enumerate(RELATED):
-            at = pl.multiple_of(jnp.bitwise_xor(owner, bits) * part, part)
-            out[k * part : (k + 1) * part, :] = scratch[pl.ds(at, part), :]
+    part = outs[0].shape[0] // 2
+    for n, related in enumerate((PASSED, STAYING)):
+        for out, owner in zip(outs[2 * n : 2 * n + 2], (head, jnp.bitwise_xor(head, Z_NEAR))):
+            for k, bits in enumerate(related):
+                at = pl.multiple_of(jnp.bitwise_xor(owner, bits) * part, part)
+                out[k * part : (k + 1) * part, :] = scratch[pl.ds(at, part), :]
 
 
 def pick_kernel(own_ref, far_ref, *refs):
-    tables, others, (keep_ref, send_ref, far_v, sem) = refs[:2], refs[2:4], refs[4:]
+    tables, others, (keep_ref, send_ref, send_last_ref, far_v, sem) = refs[:4], refs[4:8], refs[8:]
     count = keep_ref.shape[0]
+    part = tables[0].shape[1]
     rows = far_ref.shape[0] - 6 * TILE_ROWS
     width = far_ref.shape[1]
     model_rows = rows // width
@@ -699,19 +708,21 @@
     )
     arrival.start()
 
-    def pick(out_ref, r, g):
-        half = tables[0].shape[1]
-        for k, (table_ref, other_ref) in enumerate(zip(tables, others)):
-            total = table_ref[g].astype(jnp.float32) + other_ref[g].astype(jnp.float32)
-            out_ref[r, k * half : (k + 1) * half] = total.astype(jnp.bfloat16)
+    def pick(k, g):
+        total = tables[k][g].astype(jnp.float32) + others[k][g].astype(jnp.float32)
+        return total.astype(jnp.bfloat16)
 
     for r in range(count):
-        pick(keep_ref, r, own_ref[r])
+        for k in range(len(tables)):
+            keep_ref[r, k * part : (k + 1) * part] = pick(k, own_ref[r])
     arrival.wait()
     wanted = far_v[...].astype(jnp.float32)[0:1, :]
     lane = lax.broadcasted_iota(jnp.int32, (1, LANES), 1)
     for r in range(count):
-        pick(send_ref, r, jnp.sum(jnp.where(lane == r, wanted, 0.0)).astype(jnp.int32))
+        g = jnp.sum(jnp.where(lane == r, wanted, 0.0)).astype(jnp.int32)
+        for k in range(len(tables) - 1):
+            send_ref[r, k * part : (k + 1) * part] = pick(k, g)
+        send_last_ref[r] = pick(len(tables) - 1, g)
 
 
 def split_squares(squares):
@@ -725,50 +736,24 @@
     return high + ref[:, model + 1 : model + 2].astype(jnp.float32)
 
 
-def out_kernel(
-    kept_ref,
-    got_ref,
-    own_hbm,
-    part_ref,
-    near_ref,
-    keep_ref,
-    near_out,
-    pass_ref,
-    cross_out,
-    own_ref,
-    other_ref,
-    sums_ref,
-    sems,
-):
+def out_kernel(kept_ref, got_ref, own_ref, part_ref, near_ref, wide_out, bf16_out, sums_ref):
     core = lax.axis_index("dp") % 2
     width = part_ref.shape[1]
     rows, model = sums_ref.shape
-    part = keep_ref.shape[0]
-    copies = [pltpu.make_async_copy(own_hbm, own_ref, sems.at[2])]
-    for j, buffer in enumerate((part_ref, near_ref)):
-        at = pl.multiple_of(jnp.bitwise_xor(core, j) * width, LANES)
-        copies.append(
-            pltpu.make_async_copy(buffer, other_ref.at[:, pl.ds(at, width)], sems.at[j])
-        )
-    for copy in copies:
-        copy.start()
+    part = wide_out.shape[0]
     kept, got = kept_ref[...], got_ref[...]
     squares = jnp.zeros((rows, 1), jnp.float32)
     for value in (kept, got):
         wide = value.astype(jnp.float32)
         squares = squares + jnp.sum(wide * wide, axis=1, keepdims=True)
-    copies[0].wait()
-    sums_ref[...] = dot32(kept, own_ref[...])
-    for copy in copies[1:]:
-        copy.wait()
-    sums_ref[...] += dot32(got, other_ref[...])
-    for k, out in enumerate((keep_ref, near_out, pass_ref, cross_out)):
-        own = slice(k * part, (k + 1) * part)
-        out[:, 0:model] = sums_ref[own, :].astype(out.dtype)
-        if out.dtype == jnp.bfloat16:
-            out[:, model:] = split_squares(squares[own])
-        else:
-            out[:, model:] = jnp.broadcast_to(squares[own], (part, LANES))
+    for j, other_ref in enumerate((part_ref, near_ref)):
+        at = pl.multiple_of(jnp.bitwise_xor(core, j) * width, LANES)
+        own = dot32(kept, own_ref[:, pl.ds(at, width)])
+        sums_ref[:, pl.ds(at, width)] = own + dot32(got, other_ref[...])
+    wide_out[:, 0:model] = sums_ref[0:part, :]
+    wide_out[:, model:] = jnp.broadcast_to(squares[0:part], (part, LANES))
+    bf16_out[:, 0:model] = sums_ref[part:, :].astype(jnp.bfloat16)
+    bf16_out[:, model:] = split_squares(squares[part:])
 
 
 def pass_kernel(pass_ref, cross_ref, out_ref):
@@ -795,22 +780,14 @@
     out_ref[...] = (hidden_ref[...].astype(jnp.float32) + scale * total).astype(jnp.bfloat16)
 
 
-def join_kernel(ids_ref, own_ref, keep_ref, far_ref, *refs):
-    adds, (out_ref, done_ref) = refs[:4], refs[-2:]
+def join_kernel(keep_ref, *refs):
+    fars, (out_ref, done_ref) = refs[:-2], refs[-2:]
     done_ref[...] = jnp.zeros_like(done_ref)
-    position = lax.axis_index("dp")
-    tok = ids_ref.shape[0] // lax.axis_size("dp")
-    befores = [
-        before_device(ids_ref, jnp.bitwise_xor(position, j), tok) for j in range(len(adds))
-    ]
-    for r in range(keep_ref.shape[0]):
-        total = keep_ref[r].astype(jnp.float32) + far_ref[r].astype(jnp.float32)
-        out_ref[r] = total
-        for add_ref, before in zip(adds, befores):
-
-            @pl.when(own_ref[r] == before)
-            def _():
-                out_ref[r] = out_ref[r] + add_ref[...].astype(jnp.float32)
+    at = 0
+    for far_ref in fars:
+        own = slice(at, at + far_ref.shape[1])
+        out_ref[:, own] = keep_ref[:, own].astype(jnp.float32) + far_ref[...].astype(jnp.float32)
+        at += far_ref.shape[1]
 
 
 def fused_on_device(
@@ -834,7 +811,7 @@
     inner = w_zx.shape[2]
     heads = w_dt.shape[1]
     state_width = w_bc.shape[1] // 2
-    width = inner + 2 * state_width
+    tiles = inner // LANES
     peers = lax.axis_size("dp")
     head_count = lax.axis_size("head")
     bf16, f32 = jnp.bfloat16, jnp.float32
@@ -848,18 +825,19 @@
         pack_first_kernel,
         name="pack_first_weights",
         out_shape=shape((rows + extra, 2 * state_width), bf16),
-        in_specs=[smem] + [in_hbm] * 3,
+        in_specs=[in_hbm] * 4,
         out_specs=in_vmem(1)[0],
         scratch_shapes=[
+            pltpu.VMEM((1, request_prompt.shape[0]), jnp.int32),
             pltpu.VMEM(w_bc.shape, f32),
             pltpu.VMEM((heads, rows), f32),
             pltpu.VMEM((TILE_ROWS, model), bf16),
             pltpu.VMEM((TILE_ROWS, model), f32),
-            pltpu.SemaphoreType.DMA((3,)),
+            pltpu.SemaphoreType.DMA((4,)),
         ],
         compiler_params=kernel_params(60),
         cost_estimate=LITTLE,
-    )(request_prompt, w_bc, w_dt.T, hidden)
+    )(request_prompt[None, :], w_bc, w_dt.T, hidden)
     first_far = exchange(first_own, "dp", 2)
     first_near = exchange(first_own, "dp", 1)
     x_own, gate_own = pl.pallas_call(
@@ -904,12 +882,13 @@
     out_part = exchange(half_out, "head", Z_NEAR)
     out_near = exchange(out_part, "dp", 1)
 
-    first_far, x_own, normed, meta, order, pen = lax.optimization_barrier(
-        (first_far, x_own, normed, meta, order, pen)
-    )
     x_far = exchange(x_own, "dp", 2)
+    first_far, first_near, normed, meta, order, pen, x_own, gate_own = lax.optimization_barrier(
+        (first_far, first_near, normed, meta, order, pen, x_own, gate_own)
+    )
+    x_near = exchange(x_own, "dp", 1)
+    gate_near = exchange(gate_own, "dp", 1)
     first_last = exchange(first_far, "dp", 1)
-    x_near = exchange(x_own, "dp", 1)
     bc, step, prefix, fade, halo = pl.pallas_call(
         first_kernel,
         name="project_b_c_and_steps",
@@ -949,8 +928,7 @@
     )
     x_last = exchange(x_far, "dp", 1)
     gate_far = exchange(gate_own, "dp", 2)
-    gate_near = exchange(gate_own, "dp", 1)
-    x, stepx, faded, leaving, middle = pl.pallas_call(
+    x, stepx, faded, leaving = pl.pallas_call(
         inner_kernel,
         name="project_and_convolve_x",
         out_shape=(
@@ -958,10 +936,9 @@
             shape((tok, inner), bf16),
             shape((inner, tok), bf16),
             shape((inner, state_width), bf16),
-            shape((inner, state_width), bf16),
         ),
-        in_specs=in_vmem(1) + [anywhere] * 4 + in_vmem(7),
-        out_specs=tuple(in_vmem(5)),
+        in_specs=in_vmem(1) + [anywhere] * 4 + in_vmem(6),
+        out_specs=tuple(in_vmem(4)),
         scratch_shapes=[
             pltpu.VMEM((model, inner), bf16),
             pltpu.VMEM((TILE_ROWS + tok, inner), f32),
@@ -980,89 +957,97 @@
         meta,
         bc,
         step,
-        prefix,
         fade,
     )
 
     entering = lax.ppermute(leaving, "dp", [(i, i + 1) for i in range(peers - 1)])
-    gate_far, entering = lax.optimization_barrier((gate_far, entering))
-    gate_last = exchange(gate_far, "dp", 1)
 
     y_local = pl.pallas_call(
         local_kernel,
         name="mix_within_blocks",
         out_shape=shape((tok, inner), f32),
-        in_specs=in_vmem(7) + [smem],
+        in_specs=in_vmem(6) + [smem],
         out_specs=in_vmem(1)[0],
         compiler_params=kernel_params(14),
         cost_estimate=LITTLE,
-    )(x, bc, stepx, prefix, middle, meta, pen, skip_gain)
+    )(x, bc, stepx, prefix, meta, pen, skip_gain)
+    gate_far, gate_near, entering, y_local = lax.optimization_barrier(
+        (gate_far, gate_near, entering, y_local)
+    )
+    gate_last = exchange(gate_far, "dp", 1)
     tables = pl.pallas_call(
         table_kernel,
         name="sum_ended_states",
-        out_shape=(shape((PROMPTS, inner // 2, state_width), bf16),) * 2,
+        out_shape=(shape((PROMPTS, inner // 4, state_width), bf16),) * 4,
+        in_specs=[smem] + in_vmem(5),
+        out_specs=tuple(in_vmem(4)),
+        compiler_params=kernel_params(8),
+        cost_estimate=LITTLE,
+    )(token_prompt, bc, faded, meta, prefix, entering)
+    tables_near = [exchange(table, "dp", 1) for table in tables]
+
+    gate_most = pl.pallas_call(
+        z_most_kernel,
+        name="project_gate_most",
+        out_shape=shape((tok, inner), f32),
+        in_specs=in_vmem(4),
+        out_specs=in_vmem(1)[0],
+        compiler_params=kernel_params(8),
+        cost_estimate=LITTLE,
+    )(normed, gate_own, gate_near, gate_far)
+    gate = pl.pallas_call(
+        z_last_kernel,
+        name="project_gate_last",
+        out_shape=shape((tok, inner), f32),
         in_specs=in_vmem(3),
-        out_specs=tuple(in_vmem(2)),
+        out_specs=in_vmem(1)[0],
         compiler_params=kernel_params(8),
         cost_estimate=LITTLE,
-    )(bc, faded, meta)
-    tables_near = [exchange(table, "dp", 1) for table in tables]
-
-    gate = pl.pallas_call(
-        z_kernel,
-        name="project_gate",
-        out_shape=shape((tok, inner), f32),
-        in_specs=in_vmem(1) + [anywhere] * 4,
-        out_specs=in_vmem(1)[0],
-        scratch_shapes=[pltpu.VMEM((model, inner), bf16), pltpu.SemaphoreType.DMA((peers,))],
-        compiler_params=kernel_params(8),
-        cost_estimate=LITTLE,
-    )(normed, gate_own, gate_near, gate_far, gate_last)
+    )(normed, gate_last, gate_most)
 
     out_rows = tok // head_count
-    gated_kept, gated_sent, add = pl.pallas_call(
+    kept_first, sent_first, kept_rest, sent_rest = pl.pallas_call(
         gate_kernel,
         name="add_entering_and_gate",
-        out_shape=(shape((tok // 2, inner), bf16),) * 2 + (shape((inner, state_width), bf16),),
-        in_specs=[smem] + in_vmem(6) + [anywhere],
-        out_specs=tuple(in_vmem(3)),
+        out_shape=(shape((2 * out_rows, inner), bf16),) * 4,
+        in_specs=in_vmem(6) + [anywhere],
+        out_specs=tuple(in_vmem(4)),
         scratch_shapes=[pltpu.VMEM((tok, inner), bf16)],
         compiler_params=kernel_params(8),
         cost_estimate=LITTLE,
-    )(token_prompt, entering, bc, prefix, meta, y_local, gate, out_near)
-    gated_got = exchange(gated_sent, "head", Z_NEAR)
+    )(entering, bc, prefix, meta, y_local, gate, out_near)
+    got_first = exchange(sent_first, "head", Z_NEAR)
+    got_rest = exchange(sent_rest, "head", Z_NEAR)
 
     requests = request_prompt.shape[0]
-    keep, send = pl.pallas_call(
+    part = inner // 4
+    keep, *sends = pl.pallas_call(
         pick_kernel,
         name="pick_request_states",
-        out_shape=(shape((requests, inner, state_width), bf16),) * 2,
-        in_specs=[smem, anywhere] + in_vmem(4),
-        out_specs=tuple(in_vmem(2)),
+        out_shape=tuple(
+            shape((requests, size, state_width), bf16) for size in (inner, inner - part, part)
+        ),
+        in_specs=[smem, anywhere] + in_vmem(8),
+        out_specs=tuple(in_vmem(3)),
         scratch_shapes=[pltpu.VMEM((TILE_ROWS, LANES), bf16), pltpu.SemaphoreType.DMA],
         compiler_params=kernel_params(8),
         cost_estimate=LITTLE,
     )(request_prompt, first_far, *tables, *tables_near)
-    far = exchange(send, "dp", 2)
-    adds = [add, exchange(add, "dp", 1), exchange(add, "dp", 2)]
-    adds.append(exchange(adds[2], "dp", 1))
+    fars = [exchange(send, "dp", 2) for send in sends]
 
     sums_shape = (out_rows, model + LANES)
-    sums_keep, sums_near, sums_pass, sums_cross = pl.pallas_call(
+    project = pl.pallas_call(
         out_kernel,
         name="project_out",
-        out_shape=tuple(shape(sums_shape, kind) for kind in (f32, bf16, f32, bf16)),
-        in_specs=in_vmem(2) + [anywhere] * 3,
-        out_specs=tuple(in_vmem(4)),
-        scratch_shapes=[
-            pltpu.VMEM((inner, model), bf16),
-            pltpu.VMEM((inner, model), bf16),
-            pltpu.VMEM((tok // 2, model), f32),
-            pltpu.SemaphoreType.DMA((3,)),
-        ],
-        compiler_params=kernel_params(14),
-        cost_estimate=LITTLE,
-    )(gated_kept, gated_got, scaled_out, out_part, out_near)
+        out_shape=(shape(sums_shape, f32), shape(sums_shape, bf16)),
+        in_specs=in_vmem(5),
+        out_specs=tuple(in_vmem(2)),
+        scratch_shapes=[pltpu.VMEM((2 * out_rows, model), f32)],
+        compiler_params=kernel_params(8),
+        cost_estimate=LITTLE,
+    )
+    sums_pass, sums_cross = project(kept_first, got_first, scaled_out, out_part, out_near)
+    sums_keep, sums_near = project(kept_rest, got_rest, scaled_out, out_part, out_near)
     cross = exchange(sums_cross, "head", Y_NEAR)
     cross, sums_near = lax.optimization_barrier((cross, sums_near))
     sums_near = exchange(sums_near, "head", Y_NEAR)
@@ -1079,12 +1064,12 @@
     request_states, joined = pl.pallas_call(
         join_kernel,
         name="join_request_states",
-        out_shape=(shape(keep.shape, f32), shape((8, LANES), f32)),
-        in_specs=[smem] * 2 + in_vmem(6) + [anywhere],
+        out_shape=(shape((requests, inner, state_width), f32), shape((8, LANES), f32)),
+        in_specs=in_vmem(3),
         out_specs=tuple(in_vmem(2)),
         compiler_params=kernel_params(6),
         cost_estimate=LITTLE,
-    )(token_prompt, request_prompt, keep, far, *adds, sums_keep)
+    )(keep, *fars)
     layer_out = pl.pallas_call(
         functools.partial(finish_kernel, inner * head_count),
         name="scale_and_add_hidden",

time: 66.6 us -> 58.3 us (0.88)
  waiting for transfers between devices: 16.6 us -> 9.12 us
  Pallas kernels: 23.7 us -> 22.3 us
    ppermute x21 -> x22, waiting for transfers between devices: 16.6 us -> 9.11 us  [exchange(): lax.ppermute(values, axis, [(i, i ^ bits) for i in range(lax.axis_size(ax...]
    pallas_call x1, Pallas kernels: 1.46 us -> 0.66 us  [fused_on_device(): pl.pallas_call(gate_kernel, name='add_entering_and_gate', out_shape=(shap...]
    pallas_call x1, Pallas kernels: 1.74 us -> 0.96 us  [fused_on_device(): pl.pallas_call(join_kernel, name='join_request_states', out_shape=(shape(...]
    pallas_call x1, Pallas kernels: 1.5 us -> 2.21 us  [fused_on_device(): pl.pallas_call(table_kernel, name='sum_ended_states', out_shape=(shape((P...]
    ppermute x21 -> x22, starting transfers between devices: 22.6 us -> 23 us  [exchange(): lax.ppermute(values, axis, [(i, i ^ bits) for i in range(lax.axis_size(ax...]
    pallas_call x3 -> x5, Pallas kernels: 3.68 us -> 3.46 us  [the longest x1 0.89 us: fused_on_device(): pl.pallas_call(z_most_kernel, name='project_gate_most', out_shape=shape((...]
  transfers between devices with their start and end apart: 22 -> 23, of which waited for: 8 -> 8; matrix products, arithmetic and copies ran while one was open for 0% -> 0% of each run, Pallas kernels for 30% -> 32%
where the time goes in v4:
time: 58.3 us; the launch traced here: 58.1 us
  starting transfers between devices  25.5 us (44%)
  Pallas kernels  22.3 us (38%)
  waiting for transfers between devices  9.12 us (16%)
  between operations  1.13 us (2%)
    ppermute x22, starting transfers between devices, exchange(): lax.ppermute(values, axis, [(i, i ^ bits) for i in range(lax.axis_size(ax...  23 us
    ppermute x22, waiting for transfers between devices, exchange(): lax.ppermute(values, axis, [(i, i ^ bits) for i in range(lax.axis_size(ax...  9.11 us
    pallas_call x1, Pallas kernels, fused_on_device(): pl.pallas_call(first_kernel, name='project_b_c_and_steps', out_shape=(sha...  4.6 us
    pallas_call x1, Pallas kernels, fused_on_device(): pl.pallas_call(inner_kernel, name='project_and_convolve_x', out_shape=(sh...  2.64 us
    ppermute x1, starting transfers between devices, fused_on_device(): lax.ppermute(leaving, 'dp', [(i, i + 1) for i in range(peers - 1)])  2.59 us
    pallas_call x1, Pallas kernels, fused_on_device(): pl.pallas_call(local_kernel, name='mix_within_blocks', out_shape=shape((t...  2.27 us
    pallas_call x1, Pallas kernels, fused_on_device(): pl.pallas_call(table_kernel, name='sum_ended_states', out_shape=(shape((P...  2.21 us
    pallas_call x1, Pallas kernels, fused_on_device(): pl.pallas_call(pack_first_kernel, name='pack_first_weights', out_shape=sh...  1.95 us
  transfers between devices with their start and end apart: 23, of which 8 were waited for; matrix products, arithmetic and copies ran while one was open for 0% of the time, Pallas kernels for 32%

profile of v4, /device:TPU:0, one launch (start us, length us, event | category | flops | bytes accessed | tf_op | source)
XLA Modules:
  0.0 58.1 jit_solution(7431409978199644931)
XLA Ops:
  0.7 2.0 %pack_first_weights.1.own_ref = bf16[480,256]{1,0:T(8,128)(2,1)} custom-call(s32[1,4]{1,0:T(1,128)} %bitcast.5, f32[384,256]{1,0:T(8,128)} %wbc_ref.1, f32[6,384]{1,0:T(8,128)} %bitcast.6, bf16[512,1536]{1,0:T(8,128)(2,1)} %hidden_all.1), custom_call_target="tpu_custom_call" | custom-call | flops 1000 | bytes 1000 | tf_op jit(solution)/shard_map/pack_first_weights/pallas_call | solution.py:824
  2.6 3.0 %collective-permute-start = (bf16[480,256]{1,0:T(8,128)(2,1)}, bf16[480,256]{1,0:T(8,128)(2,1)S(1)}, u32[]{:S(2)}, u32[]{:S(2)}) collective-permute-start(bf16[480,256]{1,0:T(8,128)(2,1)} %pack_first_weights.1.own_ref), channel_id=1, source_target_pairs={{0,16},{8,24},{16,0},{24,8},{1,17},{9,25},{17,1},{25,9},{2,18},{10... | collective-permute-start | bytes 737288 | tf_op jit(solution)/shard_map/ppermute | solution.py:275
  6.2 1.6 %collective-permute-start.16 = (bf16[384,768]{1,0:T(8,128)(2,1)S(1)}, bf16[384,768]{1,0:T(8,128)(2,1)S(1)}, u32[]{:S(2)}, u32[]{:S(2)}) collective-permute-start(bf16[384,768]{1,0:T(8,128)(2,1)S(1)} %get-tuple-element.99), channel_id=1, source_target_pairs={{0,2},{1,3},{2,0},{3,1},{4,6},{5,7},{6,4},{7,5},{8,10},{9,11},{10,... | collective-permute-start | bytes 1769480 | tf_op jit(solution)/shard_map/ppermute | solution.py:275
  7.8 0.5 pack_x_and_gate_weights.1
  8.4 0.6 %collective-permute-start.2 = (bf16[384,384]{1,0:T(8,128)(2,1)S(1)}, bf16[384,384]{1,0:T(8,128)(2,1)S(1)}, u32[]{:S(2)}, u32[]{:S(2)}) collective-permute-start(bf16[384,384]{1,0:T(8,128)(2,1)S(1)} %get-tuple-element.75.own_ref), channel_id=1, source_target_pairs={{0,16},{8,24},{16,0},{24,8},{1,17},{9,25},{17,1},{25,9},{2,18},{10... | collective-permute-start | bytes 884744 | tf_op jit(solution)/shard_map/ppermute | solution.py:275
  9.0 1.2 %norm_and_token_facts.1 = (bf16[512,1536]{1,0:T(8,128)(2,1)S(1)}, f32[512,128]{1,0:T(8,128)S(1)}, bf16[1024,512]{1,0:T(8,128)(2,1)S(1)}, f32[2,256,256]{2,1,0:T(8,128)S(1)}) custom-call(s32[1,2048]{1,0:T(1,128)S(1)} %bitcast.4, bf16[512,1536]{1,0:T(8,128)(2,1)S(1)} %copy-done, f32[1,1536]{1,0:T(1,128)S(1)} %broadcast_in_dim.15.gain_ref), custom_call_target="tpu_custom_call" | custom-call | flops 1000 | bytes 1000 | tf_op jit(solution)/shard_map/norm_and_token_facts/pallas_call | solution.py:858
  10.3 2.0 %collective-permute-done.far_ref = bf16[480,256]{1,0:T(8,128)(2,1)S(1)} collective-permute-done((bf16[480,256]{1,0:T(8,128)(2,1)}, bf16[480,256]{1,0:T(8,128)(2,1)S(1)}, u32[]{:S(2)}, u32[]{:S(2)}) %collective-permute-start) | collective-permute-done | bytes 245792 | tf_op jit(solution)/shard_map/ppermute | solution.py:275
  12.8 1.0 %collective-permute-done.3.last_ref = bf16[480,256]{1,0:T(8,128)(2,1)S(1)} collective-permute-done((bf16[480,256]{1,0:T(8,128)(2,1)S(1)}, bf16[480,256]{1,0:T(8,128)(2,1)S(1)}, u32[]{:S(2)}, u32[]{:S(2)}) %collective-permute-start.3) | collective-permute-done | bytes 245792 | tf_op jit(solution)/shard_map/ppermute | solution.py:275
  13.8 4.6 %project_b_c_and_steps.1 = (bf16[512,256]{1,0:T(8,128)(2,1)S(1)}, f32[512,128]{1,0:T(8,128)S(1)}, f32[512,128]{1,0:T(8,128)S(1)}, f32[512,128]{1,0:T(8,128)S(1)}, bf16[16,1536]{1,0:T(8,128)(2,1)S(1)}) custom-call(bf16[512,1536]{1,0:T(8,128)(2,1)S(1)} %get-tuple-element.65.normed_ref, bf16[480,256]{1,0:T(8,128)(2,1)S(1)} %copy-done.3, ...), custom_call_target="tpu_custom_call" | custom-call | flops 1000 | bytes 1000 | tf_op jit(solution)/shard_map/project_b_c_and_steps/pallas_call | solution.py:892
  19.0 2.4 %collective-permute-start.6 = (bf16[384,384]{1,0:T(8,128)(2,1)S(1)}, bf16[384,384]{1,0:T(8,128)(2,1)S(1)}, u32[]{:S(2)}, u32[]{:S(2)}) collective-permute-start(bf16[384,384]{1,0:T(8,128)(2,1)S(1)} %get-tuple-element.82.own_ref), channel_id=1, source_target_pairs={{0,16},{8,24},{16,0},{24,8},{1,17},{9,25},{17,1},{25,9},{2,18},{10... | collective-permute-start | bytes 884744 | tf_op jit(solution)/shard_map/ppermute | solution.py:275
  21.4 0.6 collective-permute-done.16.part_ref
  22.0 2.6 %project_and_convolve_x.1 = (bf16[512,384]{1,0:T(8,128)(2,1)S(1)}, bf16[512,384]{1,0:T(8,128)(2,1)S(1)}, bf16[384,512]{1,0:T(8,128)(2,1)S(1)}, bf16[384,128]{1,0:T(8,128)(2,1)S(1)}) custom-call(bf16[512,1536]{1,0:T(8,128)(2,1)S(1)} %get-tuple-element.65.normed_ref, bf16[384,384]{1,0:T(8,128)(2,1)S(1)} %get-tuple-element.75.own_ref, ...), custom_call_target="tpu_custom_call" | custom-call | flops 1000 | bytes 1000 | tf_op jit(solution)/shard_map/project_and_convolve_x/pallas_call | solution.py:931
  24.6 2.6 %collective-permute-start.8 = (bf16[384,128]{1,0:T(8,128)(2,1)S(1)}, bf16[384,128]{1,0:T(8,128)(2,1)S(1)}, u32[]{:S(2)}, u32[]{:S(2)}) collective-permute-start(bf16[384,128]{1,0:T(8,128)(2,1)S(1)} %get-tuple-element.83), channel_id=1, source_target_pairs={{0,8},{8,16},{16,24},{1,9},{9,17},{17,25},{2,10},{10,18},{18,26},{... | collective-permute-start | bytes 294920 | tf_op jit(solution)/shard_map/ppermute | solution.py:963
  27.3 2.3 %mix_within_blocks.1.y_ref = f32[512,384]{1,0:T(8,128)S(1)} custom-call(bf16[512,384]{1,0:T(8,128)(2,1)S(1)} %get-tuple-element.84.x_ref, bf16[512,256]{1,0:T(8,128)(2,1)S(1)} %get-tuple-element.74.bc_ref, bf16[512,384]{1,0:T(8,128)(2,1)S(1)} %get-tuple-element.85.stepx_ref, f32[512,128]{1,0:T(8,128)S(1)} %get-tuple-element.81.prefix_ref, ...), custom_call_target="tpu_custom_call" | custom-call | flops 1000 | bytes 1000 | tf_op jit(solution)/shard_map/mix_within_blocks/pallas_call | solution.py:965
  29.7 0.9 %project_gate_most.1.most_ref = f32[512,384]{1,0:T(8,128)S(1)} custom-call(bf16[512,1536]{1,0:T(8,128)(2,1)S(1)} %get-tuple-element.65.normed_ref, bf16[384,384]{1,0:T(8,128)(2,1)S(1)} %get-tuple-element.82.own_ref, bf16[384,384]{1,0:T(8,128)(2,1)S(1)} %collective-permute-done.7.near_ref, bf16[384,384]{1,0:T(8,128)(2,1)S(1)} %collective-permute-done.6.far_ref), custom_call_target="tpu_custom_call" | custom-call | flops 1000 | bytes 1000 | tf_op jit(solution)/shard_map/project_gate_most/pallas_call | solution.py:989
  30.6 0.6 %collective-permute-done.15.last_ref = bf16[384,384]{1,0:T(8,128)(2,1)S(1)} collective-permute-done((bf16[384,384]{1,0:T(8,128)(2,1)S(1)}, bf16[384,384]{1,0:T(8,128)(2,1)S(1)}, u32[]{:S(2)}, u32[]{:S(2)}) %collective-permute-start.15) | collective-permute-done | bytes 294944 | tf_op jit(solution)/shard_map/ppermute | solution.py:275
  31.7 0.7 %add_entering_and_gate.1 = (bf16[128,384]{1,0:T(8,128)(2,1)S(1)}, bf16[128,384]{1,0:T(8,128)(2,1)S(1)}, bf16[128,384]{1,0:T(8,128)(2,1)S(1)}, bf16[128,384]{1,0:T(8,128)(2,1)S(1)}) custom-call(bf16[384,128]{1,0:T(8,128)(2,1)S(1)} %collective-permute-done.8.enter_ref, bf16[512,256]{1,0:T(8,128)(2,1)S(1)} %get-tuple-element.74.bc_ref, ...), custom_call_target="tpu_custom_call" | custom-call | flops 1000 | bytes 1000 | tf_op jit(solution)/shard_map/add_entering_and_gate/pallas_call | solution.py:1009
  32.3 1.6 %collective-permute-start.19 = (bf16[128,384]{1,0:T(8,128)(2,1)S(1)}, bf16[128,384]{1,0:T(8,128)(2,1)S(1)}, u32[]{:S(2)}, u32[]{:S(2)}) collective-permute-start(bf16[128,384]{1,0:T(8,128)(2,1)S(1)} %get-tuple-element.105), channel_id=1, source_target_pairs={{0,2},{1,3},{2,0},{3,1},{4,6},{5,7},{6,4},{7,5},{8,10},{9,11},{10,... | collective-permute-start | bytes 294920 | tf_op jit(solution)/shard_map/ppermute | solution.py:275
  34.0 2.2 %sum_ended_states.1 = (bf16[8,96,128]{2,1,0:T(8,128)(2,1)S(1)}, bf16[8,96,128]{2,1,0:T(8,128)(2,1)S(1)}, bf16[8,96,128]{2,1,0:T(8,128)(2,1)S(1)}, bf16[8,96,128]{2,1,0:T(8,128)(2,1)S(1)}) custom-call(s32[2048]{0:T(1024)S(1)} %copy-done.4, bf16[512,256]{1,0:T(8,128)(2,1)S(1)} %get-tuple-element.74.bc_ref, bf16[384,512]{1,0:T(8,128)(2,1)S(1)} %get-tuple-element.80.faded_ref, ...), custom_call_target="tpu_custom_call" | custom-call | flops 1000 | bytes 1000 | tf_op jit(solution)/shard_map/sum_ended_states/pallas_call | solution.py:978
  37.3 0.6 %project_out.3 = (f32[64,1664]{1,0:T(8,128)S(1)}, bf16[64,1664]{1,0:T(8,128)(2,1)S(1)}) custom-call(bf16[128,384]{1,0:T(8,128)(2,1)S(1)} %get-tuple-element.104.kept_ref, bf16[128,384]{1,0:T(8,128)(2,1)S(1)} %collective-permute-done.19.got_ref, bf16[384,1536]{1,0:T(8,128)(2,1)S(1)} %get-tuple-element.102.own_ref, ...), custom_call_target="tpu_custom_call" | custom-call | flops 1000 | bytes 1000 | tf_op jit(solution)/shard_map/project_out/pallas_call | solution.py:1049
  37.9 1.6 %collective-permute-start.20 = (bf16[64,1664]{1,0:T(8,128)(2,1)S(1)}, bf16[64,1664]{1,0:T(8,128)(2,1)S(1)}, u32[]{:S(2)}, u32[]{:S(2)}) collective-permute-start(bf16[64,1664]{1,0:T(8,128)(2,1)S(1)} %get-tuple-element.106), channel_id=1, source_target_pairs={{0,1},{1,0},{2,3},{3,2},{4,5},{5,4},{6,7},{7,6},{8,9},{9,8},{10,11... | collective-permute-start | bytes 638984 | tf_op jit(solution)/shard_map/ppermute | solution.py:275
  39.5 1.5 %collective-permute-start.18 = (bf16[128,384]{1,0:T(8,128)(2,1)S(1)}, bf16[128,384]{1,0:T(8,128)(2,1)S(1)}, u32[]{:S(2)}, u32[]{:S(2)}) collective-permute-start(bf16[128,384]{1,0:T(8,128)(2,1)S(1)} %get-tuple-element.101), channel_id=1, source_target_pairs={{0,2},{1,3},{2,0},{3,1},{4,6},{5,7},{6,4},{7,5},{8,10},{9,11},{10,... | collective-permute-start | bytes 294920 | tf_op jit(solution)/shard_map/ppermute | solution.py:275
  41.1 0.9 %pick_request_states.1 = (bf16[4,384,128]{2,1,0:T(8,128)(2,1)S(1)}, bf16[4,288,128]{2,1,0:T(8,128)(2,1)S(1)}, bf16[4,96,128]{2,1,0:T(8,128)(2,1)S(1)}) custom-call(s32[4]{0:T(128)S(1)} %copy-done.7, bf16[480,256]{1,0:T(8,128)(2,1)S(1)} %collective-permute-done.far_ref, bf16[8,96,128]{2,1,0:T(8,128)(2,1)S(1)} %get-tuple-element.88.refs_0_, ...), custom_call_target="tpu_custom_call" | custom-call | flops 1000 | bytes 1000 | tf_op jit(solution)/shard_map/pick_request_states/pallas_call | solution.py:1024
  42.0 2.0 %collective-permute-start.13 = (bf16[4,288,128]{2,1,0:T(8,128)(2,1)S(1)}, bf16[4,288,128]{2,1,0:T(8,128)(2,1)S(1)}, u32[]{:S(2)}, u32[]{:S(2)}) collective-permute-start(bf16[4,288,128]{2,1,0:T(8,128)(2,1)S(1)} %get-tuple-element.93), channel_id=1, source_target_pairs={{0,16},{8,24},{16,0},{24,8},{1,17},{9,25},{17,1},{25,9},{2,18},{10... | collective-permute-start | bytes 884744 | tf_op jit(solution)/shard_map/ppermute | solution.py:275
  44.1 0.6 %project_out.2 = (f32[64,1664]{1,0:T(8,128)S(1)}, bf16[64,1664]{1,0:T(8,128)(2,1)S(1)}) custom-call(bf16[128,384]{1,0:T(8,128)(2,1)S(1)} %get-tuple-element.100.kept_ref, bf16[128,384]{1,0:T(8,128)(2,1)S(1)} %collective-permute-done.18.got_ref, bf16[384,1536]{1,0:T(8,128)(2,1)S(1)} %get-tuple-element.102.own_ref, ...), custom_call_target="tpu_custom_call" | custom-call | flops 1000 | bytes 1000 | tf_op jit(solution)/shard_map/project_out/pallas_call | solution.py:1050
  45.4 2.7 %collective-permute-start.22 = (bf16[64,1664]{1,0:T(8,128)(2,1)S(1)}, bf16[64,1664]{1,0:T(8,128)(2,1)S(1)}, u32[]{:S(2)}, u32[]{:S(2)}) collective-permute-start(bf16[64,1664]{1,0:T(8,128)(2,1)S(1)} %add_sums_to_pass_on.1), channel_id=1, source_target_pairs={{0,4},{1,5},{2,6},{3,7},{4,0},{5,1},{6,2},{7,3},{8,12},{9,13},{10,... | collective-permute-start | bytes 638984 | tf_op jit(solution)/shard_map/ppermute | solution.py:275
  48.1 1.5 %collective-permute-start.21 = (bf16[64,1664]{1,0:T(8,128)(2,1)S(1)}, bf16[64,1664]{1,0:T(8,128)(2,1)S(1)}, u32[]{:S(2)}, u32[]{:S(2)}) collective-permute-start(bf16[64,1664]{1,0:T(8,128)(2,1)S(1)} %get-tuple-element.108), channel_id=1, source_target_pairs={{0,1},{1,0},{2,3},{3,2},{4,5},{5,4},{6,7},{7,6},{8,9},{9,8},{10,11... | collective-permute-start | bytes 638984 | tf_op jit(solution)/shard_map/ppermute | solution.py:275
  49.6 2.1 %collective-permute-start.14 = (bf16[4,96,128]{2,1,0:T(8,128)(2,1)S(1)}, bf16[4,96,128]{2,1,0:T(8,128)(2,1)S(1)}, u32[]{:S(2)}, u32[]{:S(2)}) collective-permute-start(bf16[4,96,128]{2,1,0:T(8,128)(2,1)S(1)} %get-tuple-element.94), channel_id=1, source_target_pairs={{0,16},{8,24},{16,0},{24,8},{1,17},{9,25},{17,1},{25,9},{2,18},{10... | collective-permute-start | bytes 294920 | tf_op jit(solution)/shard_map/ppermute | solution.py:275
  51.7 2.6 %collective-permute-done.14.refs_1_ = bf16[4,96,128]{2,1,0:T(8,128)(2,1)S(1)} collective-permute-done((bf16[4,96,128]{2,1,0:T(8,128)(2,1)S(1)}, bf16[4,96,128]{2,1,0:T(8,128)(2,1)S(1)}, u32[]{:S(2)}, u32[]{:S(2)}) %collective-permute-start.14) | collective-permute-done | bytes 98336 | tf_op jit(solution)/shard_map/ppermute | solution.py:275
  54.3 1.0 %join_request_states.1 = (f32[4,384,128]{2,1,0:T(8,128)}, f32[8,128]{1,0:T(8,128)S(1)}) custom-call(bf16[4,384,128]{2,1,0:T(8,128)(2,1)S(1)} %get-tuple-element.92.keep_ref, bf16[4,288,128]{2,1,0:T(8,128)(2,1)S(1)} %collective-permute-done.13.refs_0_, bf16[4,96,128]{2,1,0:T(8,128)(2,1)S(1)} %collective-permute-done.14.refs_1_), custom_call_target="tpu_custom_call" | custom-call | flops 1000 | bytes 1000 | tf_op jit(solution)/shard_map/join_request_states/pallas_call | solution.py:1064
  55.3 1.6 %collective-permute-done.22.refs_1_ = bf16[64,1664]{1,0:T(8,128)(2,1)S(1)} collective-permute-done((bf16[64,1664]{1,0:T(8,128)(2,1)S(1)}, bf16[64,1664]{1,0:T(8,128)(2,1)S(1)}, u32[]{:S(2)}, u32[]{:S(2)}) %collective-permute-start.22) | collective-permute-done | bytes 213024 | tf_op jit(solution)/shard_map/ppermute | solution.py:275
  56.8 1.1 %scale_and_add_hidden.1 = bf16[64,1536]{1,0:T(8,128)(2,1)} custom-call(bf16[512,1536]{1,0:T(8,128)(2,1)S(1)} %copy-done, f32[8,128]{1,0:T(8,128)S(1)} %get-tuple-element.95.joined_ref, f32[64,1664]{1,0:T(8,128)S(1)} %get-tuple-element.103.keep_ref, bf16[64,1664]{1,0:T(8,128)(2,1)S(1)} %collective-permute-done.21.refs_0_, ...), custom_call_target="tpu_custom_call" | custom-call | flops 1000 | bytes 1000 | tf_op jit(solution)/shard_map/scale_and_add_hidden/pallas_call | solution.py:1073
  (59 shorter events, 4.2 us)
Async XLA Ops:
  0.6 5.0 %copy-start.12 = (f32[384]{0:T(512)S(1)}, f32[384]{0:T(512)}, u32[]{:S(2)}) copy-start(f32[384]{0:T(512)} %param.26) | copy-start | bytes 4612
  0.6 5.0 %copy-start.1 = (bf16[384,1536]{1,0:T(8,128)(2,1)S(1)}, bf16[384,1536]{1,0:T(8,128)(2,1)}, u32[]{:S(2)}) copy-start(bf16[384,1536]{1,0:T(8,128)(2,1)} %w_ref.1) | copy-start | bytes 3538948
  0.7 7.2 %copy-start.2 = (f32[384,2,384]{2,1,0:T(2,128)S(1)}, f32[384,2,384]{2,1,0:T(2,128)}, u32[]{:S(2)}) copy-start(f32[384,2,384]{2,1,0:T(2,128)} %wzx_ref.1) | copy-start | bytes 3538948
  2.6 9.7 %collective-permute-start = (bf16[480,256]{1,0:T(8,128)(2,1)}, bf16[480,256]{1,0:T(8,128)(2,1)S(1)}, u32[]{:S(2)}, u32[]{:S(2)}) collective-permute-start(bf16[480,256]{1,0:T(8,128)(2,1)} %pack_first_weights.1.own_ref), channel_id=1, source_target_pairs={{0,16},{8,24},{16,0},{24,8},{1,17},{9,25},{17,1},{25,9},{2,18},{10... | collective-permute-start | bytes 737288 | tf_op jit(solution)/shard_map/ppermute | solution.py:275
  5.6 6.7 %collective-permute-start.1 = (bf16[480,256]{1,0:T(8,128)(2,1)}, bf16[480,256]{1,0:T(8,128)(2,1)S(1)}, u32[]{:S(2)}, u32[]{:S(2)}) collective-permute-start(bf16[480,256]{1,0:T(8,128)(2,1)} %pack_first_weights.1.own_ref), channel_id=1, source_target_pairs={{0,8},{8,0},{16,24},{24,16},{1,9},{9,1},{17,25},{25,17},{2,10},{10... | collective-permute-start | bytes 737288 | tf_op jit(solution)/shard_map/ppermute | solution.py:275
  6.1 7.7 %copy-start.3 = (bf16[480,256]{1,0:T(8,128)(2,1)S(1)}, bf16[480,256]{1,0:T(8,128)(2,1)}, u32[]{:S(2)}) copy-start(bf16[480,256]{1,0:T(8,128)(2,1)} %pack_first_weights.1.own_ref) | copy-start | bytes 737284
  6.2 7.7 %copy-start.6 = (f32[4,256]{1,0:T(4,128)S(1)}, f32[4,256]{1,0:T(4,128)}, u32[]{:S(2)}) copy-start(f32[4,256]{1,0:T(4,128)} %taps_ref.2) | copy-start | bytes 12292
  6.2 7.7 %copy-start.8 = (f32[6]{0:T(128)S(1)}, f32[6]{0:T(128)}, u32[]{:S(2)}) copy-start(f32[6]{0:T(128)} %bias_ref.1) | copy-start | bytes 76
  6.2 7.7 %copy-start.9 = (f32[6]{0:T(128)S(1)}, f32[6]{0:T(128)}, u32[]{:S(2)}) copy-start(f32[6]{0:T(128)} %decay_ref.1) | copy-start | bytes 76
  6.2 15.8 %collective-permute-start.16 = (bf16[384,768]{1,0:T(8,128)(2,1)S(1)}, bf16[384,768]{1,0:T(8,128)(2,1)S(1)}, u32[]{:S(2)}, u32[]{:S(2)}) collective-permute-start(bf16[384,768]{1,0:T(8,128)(2,1)S(1)} %get-tuple-element.99), channel_id=1, source_target_pairs={{0,2},{1,3},{2,0},{3,1},{4,6},{5,7},{6,4},{7,5},{8,10},{9,11},{10,... | collective-permute-start | bytes 1769480 | tf_op jit(solution)/shard_map/ppermute | solution.py:275
  8.4 10.1 %collective-permute-start.2 = (bf16[384,384]{1,0:T(8,128)(2,1)S(1)}, bf16[384,384]{1,0:T(8,128)(2,1)S(1)}, u32[]{:S(2)}, u32[]{:S(2)}) collective-permute-start(bf16[384,384]{1,0:T(8,128)(2,1)S(1)} %get-tuple-element.75.own_ref), channel_id=1, source_target_pairs={{0,16},{8,24},{16,0},{24,8},{1,17},{9,25},{17,1},{25,9},{2,18},{10... | collective-permute-start | bytes 884744 | tf_op jit(solution)/shard_map/ppermute | solution.py:275
  12.3 9.7 %copy-start.5 = (f32[4,384]{1,0:T(4,128)S(1)}, f32[4,384]{1,0:T(4,128)}, u32[]{:S(2)}) copy-start(f32[4,384]{1,0:T(4,128)} %taps_ref.3) | copy-start | bytes 18436
  12.3 1.5 %collective-permute-start.3 = (bf16[480,256]{1,0:T(8,128)(2,1)S(1)}, bf16[480,256]{1,0:T(8,128)(2,1)S(1)}, u32[]{:S(2)}, u32[]{:S(2)}) collective-permute-start(bf16[480,256]{1,0:T(8,128)(2,1)S(1)} %collective-permute-done.far_ref), channel_id=1, source_target_pairs={{0,8},{8,0},{16,24},{24,16},{1,9},{9,1},{17,25},{25,17},{2,10},{10... | collective-permute-start | bytes 737288 | tf_op jit(solution)/shard_map/ppermute | solution.py:275
  12.3 9.7 %collective-permute-start.4 = (bf16[384,384]{1,0:T(8,128)(2,1)S(1)}, bf16[384,384]{1,0:T(8,128)(2,1)S(1)}, u32[]{:S(2)}, u32[]{:S(2)}) collective-permute-start(bf16[384,384]{1,0:T(8,128)(2,1)S(1)} %get-tuple-element.75.own_ref), channel_id=1, source_target_pairs={{0,8},{8,0},{16,24},{24,16},{1,9},{9,1},{17,25},{25,17},{2,10},{10... | collective-permute-start | bytes 884744 | tf_op jit(solution)/shard_map/ppermute | solution.py:275
  18.5 8.8 %copy-start.10 = (f32[6]{0:T(128)S(1)}, f32[6]{0:T(128)}, u32[]{:S(2)}) copy-start(f32[6]{0:T(128)} %skip_ref.1) | copy-start | bytes 76
  18.5 3.5 %collective-permute-start.5 = (bf16[384,384]{1,0:T(8,128)(2,1)S(1)}, bf16[384,384]{1,0:T(8,128)(2,1)S(1)}, u32[]{:S(2)}, u32[]{:S(2)}) collective-permute-start(bf16[384,384]{1,0:T(8,128)(2,1)S(1)} %collective-permute-done.2.far_ref), channel_id=1, source_target_pairs={{0,8},{8,0},{16,24},{24,16},{1,9},{9,1},{17,25},{25,17},{2,10},{10... | collective-permute-start | bytes 884744 | tf_op jit(solution)/shard_map/ppermute | solution.py:275
  18.7 10.9 %collective-permute-start.7 = (bf16[384,384]{1,0:T(8,128)(2,1)S(1)}, bf16[384,384]{1,0:T(8,128)(2,1)S(1)}, u32[]{:S(2)}, u32[]{:S(2)}) collective-permute-start(bf16[384,384]{1,0:T(8,128)(2,1)S(1)} %get-tuple-element.82.own_ref), channel_id=1, source_target_pairs={{0,8},{8,0},{16,24},{24,16},{1,9},{9,1},{17,25},{25,17},{2,10},{10... | collective-permute-start | bytes 884744 | tf_op jit(solution)/shard_map/ppermute | solution.py:275
  19.0 10.5 %collective-permute-start.6 = (bf16[384,384]{1,0:T(8,128)(2,1)S(1)}, bf16[384,384]{1,0:T(8,128)(2,1)S(1)}, u32[]{:S(2)}, u32[]{:S(2)}) collective-permute-start(bf16[384,384]{1,0:T(8,128)(2,1)S(1)} %get-tuple-element.82.own_ref), channel_id=1, source_target_pairs={{0,16},{8,24},{16,0},{24,8},{1,17},{9,25},{17,1},{25,9},{2,18},{10... | collective-permute-start | bytes 884744 | tf_op jit(solution)/shard_map/ppermute | solution.py:275
  22.0 9.7 %collective-permute-start.17 = (bf16[384,768]{1,0:T(8,128)(2,1)S(1)}, bf16[384,768]{1,0:T(8,128)(2,1)S(1)}, u32[]{:S(2)}, u32[]{:S(2)}) collective-permute-start(bf16[384,768]{1,0:T(8,128)(2,1)S(1)} %collective-permute-done.16.part_ref), channel_id=1, source_target_pairs={{0,8},{8,0},{16,24},{24,16},{1,9},{9,1},{17,25},{25,17},{2,10},{10... | collective-permute-start | bytes 1769480 | tf_op jit(solution)/shard_map/ppermute | solution.py:275
  24.6 4.9 %collective-permute-start.8 = (bf16[384,128]{1,0:T(8,128)(2,1)S(1)}, bf16[384,128]{1,0:T(8,128)(2,1)S(1)}, u32[]{:S(2)}, u32[]{:S(2)}) collective-permute-start(bf16[384,128]{1,0:T(8,128)(2,1)S(1)} %get-tuple-element.83), channel_id=1, source_target_pairs={{0,8},{8,16},{16,24},{1,9},{9,17},{17,25},{2,10},{10,18},{18,26},{... | collective-permute-start | bytes 294920 | tf_op jit(solution)/shard_map/ppermute | solution.py:963
  29.6 1.6 %collective-permute-start.15 = (bf16[384,384]{1,0:T(8,128)(2,1)S(1)}, bf16[384,384]{1,0:T(8,128)(2,1)S(1)}, u32[]{:S(2)}, u32[]{:S(2)}) collective-permute-start(bf16[384,384]{1,0:T(8,128)(2,1)S(1)} %collective-permute-done.6.far_ref), channel_id=1, source_target_pairs={{0,8},{8,0},{16,24},{24,16},{1,9},{9,1},{17,25},{25,17},{2,10},{10... | collective-permute-start | bytes 884744 | tf_op jit(solution)/shard_map/ppermute | solution.py:275
  32.3 4.9 %collective-permute-start.19 = (bf16[128,384]{1,0:T(8,128)(2,1)S(1)}, bf16[128,384]{1,0:T(8,128)(2,1)S(1)}, u32[]{:S(2)}, u32[]{:S(2)}) collective-permute-start(bf16[128,384]{1,0:T(8,128)(2,1)S(1)} %get-tuple-element.105), channel_id=1, source_target_pairs={{0,2},{1,3},{2,0},{3,1},{4,6},{5,7},{6,4},{7,5},{8,10},{9,11},{10,... | collective-permute-start | bytes 294920 | tf_op jit(solution)/shard_map/ppermute | solution.py:275
  36.2 3.3 %collective-permute-start.10 = (bf16[8,96,128]{2,1,0:T(8,128)(2,1)S(1)}, bf16[8,96,128]{2,1,0:T(8,128)(2,1)S(1)}, u32[]{:S(2)}, u32[]{:S(2)}) collective-permute-start(bf16[8,96,128]{2,1,0:T(8,128)(2,1)S(1)} %get-tuple-element.89.refs_1_), channel_id=1, source_target_pairs={{0,8},{8,0},{16,24},{24,16},{1,9},{9,1},{17,25},{25,17},{2,10},{10... | collective-permute-start | bytes 589832 | tf_op jit(solution)/shard_map/ppermute | solution.py:275
  36.4 4.7 %collective-permute-start.11 = (bf16[8,96,128]{2,1,0:T(8,128)(2,1)S(1)}, bf16[8,96,128]{2,1,0:T(8,128)(2,1)S(1)}, u32[]{:S(2)}, u32[]{:S(2)}) collective-permute-start(bf16[8,96,128]{2,1,0:T(8,128)(2,1)S(1)} %get-tuple-element.90.refs_2_), channel_id=1, source_target_pairs={{0,8},{8,0},{16,24},{24,16},{1,9},{9,1},{17,25},{25,17},{2,10},{10... | collective-permute-start | bytes 589832 | tf_op jit(solution)/shard_map/ppermute | solution.py:275
  36.8 4.3 %collective-permute-start.12 = (bf16[8,96,128]{2,1,0:T(8,128)(2,1)S(1)}, bf16[8,96,128]{2,1,0:T(8,128)(2,1)S(1)}, u32[]{:S(2)}, u32[]{:S(2)}) collective-permute-start(bf16[8,96,128]{2,1,0:T(8,128)(2,1)S(1)} %get-tuple-element.91.refs_3_), channel_id=1, source_target_pairs={{0,8},{8,0},{16,24},{24,16},{1,9},{9,1},{17,25},{25,17},{2,10},{10... | collective-permute-start | bytes 589832 | tf_op jit(solution)/shard_map/ppermute | solution.py:275
  36.9 4.2 %collective-permute-start.9 = (bf16[8,96,128]{2,1,0:T(8,128)(2,1)S(1)}, bf16[8,96,128]{2,1,0:T(8,128)(2,1)S(1)}, u32[]{:S(2)}, u32[]{:S(2)}) collective-permute-start(bf16[8,96,128]{2,1,0:T(8,128)(2,1)S(1)} %get-tuple-element.88.refs_0_), channel_id=1, source_target_pairs={{0,8},{8,0},{16,24},{24,16},{1,9},{9,1},{17,25},{25,17},{2,10},{10... | collective-permute-start | bytes 589832 | tf_op jit(solution)/shard_map/ppermute | solution.py:275
  37.9 7.3 %collective-permute-start.20 = (bf16[64,1664]{1,0:T(8,128)(2,1)S(1)}, bf16[64,1664]{1,0:T(8,128)(2,1)S(1)}, u32[]{:S(2)}, u32[]{:S(2)}) collective-permute-start(bf16[64,1664]{1,0:T(8,128)(2,1)S(1)} %get-tuple-element.106), channel_id=1, source_target_pairs={{0,1},{1,0},{2,3},{3,2},{4,5},{5,4},{6,7},{7,6},{8,9},{9,8},{10,11... | collective-permute-start | bytes 638984 | tf_op jit(solution)/shard_map/ppermute | solution.py:275
  39.5 4.6 %collective-permute-start.18 = (bf16[128,384]{1,0:T(8,128)(2,1)S(1)}, bf16[128,384]{1,0:T(8,128)(2,1)S(1)}, u32[]{:S(2)}, u32[]{:S(2)}) collective-permute-start(bf16[128,384]{1,0:T(8,128)(2,1)S(1)} %get-tuple-element.101), channel_id=1, source_target_pairs={{0,2},{1,3},{2,0},{3,1},{4,6},{5,7},{6,4},{7,5},{8,10},{9,11},{10,... | collective-permute-start | bytes 294920 | tf_op jit(solution)/shard_map/ppermute | solution.py:275
  42.0 12.4 %collective-permute-start.13 = (bf16[4,288,128]{2,1,0:T(8,128)(2,1)S(1)}, bf16[4,288,128]{2,1,0:T(8,128)(2,1)S(1)}, u32[]{:S(2)}, u32[]{:S(2)}) collective-permute-start(bf16[4,288,128]{2,1,0:T(8,128)(2,1)S(1)} %get-tuple-element.93), channel_id=1, source_target_pairs={{0,16},{8,24},{16,0},{24,8},{1,17},{9,25},{17,1},{25,9},{2,18},{10... | collective-permute-start | bytes 884744 | tf_op jit(solution)/shard_map/ppermute | solution.py:275
  45.4 11.4 %collective-permute-start.22 = (bf16[64,1664]{1,0:T(8,128)(2,1)S(1)}, bf16[64,1664]{1,0:T(8,128)(2,1)S(1)}, u32[]{:S(2)}, u32[]{:S(2)}) collective-permute-start(bf16[64,1664]{1,0:T(8,128)(2,1)S(1)} %add_sums_to_pass_on.1), channel_id=1, source_target_pairs={{0,4},{1,5},{2,6},{3,7},{4,0},{5,1},{6,2},{7,3},{8,12},{9,13},{10,... | collective-permute-start | bytes 638984 | tf_op jit(solution)/shard_map/ppermute | solution.py:275
  48.1 8.7 %collective-permute-start.21 = (bf16[64,1664]{1,0:T(8,128)(2,1)S(1)}, bf16[64,1664]{1,0:T(8,128)(2,1)S(1)}, u32[]{:S(2)}, u32[]{:S(2)}) collective-permute-start(bf16[64,1664]{1,0:T(8,128)(2,1)S(1)} %get-tuple-element.108), channel_id=1, source_target_pairs={{0,1},{1,0},{2,3},{3,2},{4,5},{5,4},{6,7},{7,6},{8,9},{9,8},{10,11... | collective-permute-start | bytes 638984 | tf_op jit(solution)/shard_map/ppermute | solution.py:275
  49.6 4.7 %collective-permute-start.14 = (bf16[4,96,128]{2,1,0:T(8,128)(2,1)S(1)}, bf16[4,96,128]{2,1,0:T(8,128)(2,1)S(1)}, u32[]{:S(2)}, u32[]{:S(2)}) collective-permute-start(bf16[4,96,128]{2,1,0:T(8,128)(2,1)S(1)} %get-tuple-element.94), channel_id=1, source_target_pairs={{0,16},{8,24},{16,0},{24,8},{1,17},{9,25},{17,1},{25,9},{2,18},{10... | collective-permute-start | bytes 294920 | tf_op jit(solution)/shard_map/ppermute | solution.py:275
  (4 other events, 13.8 us)

commit v5 on v4

--- a/solution.py
+++ b/solution.py
@@ -353,6 +353,7 @@
     meta_ref,
     order_ref,
     pen_ref,
+    rows_ref,
     hidden_ref,
     sem,
 ):
@@ -396,6 +397,9 @@
         own = slice(b * BLOCK, (b + 1) * BLOCK)
         pen_ref[b] = pen[own, own]
     arrival.wait()
+    part = rows_ref.shape[0]
+    at = pl.multiple_of(lax.axis_index("head") * part, part)
+    rows_ref[...] = hidden_ref[pl.ds(at, part), :]
     hidden = hidden_ref[...].astype(jnp.float32)
     normed_ref[...] = (hidden * rms_scale(hidden) * gain_ref[...]).astype(jnp.bfloat16)
 
@@ -436,8 +440,35 @@
     return silu_tanh(total)
 
 
+def below_rows(buffer, rows):
+    count = (buffer.shape[0] - rows) // TILE_ROWS
+    return jnp.concatenate(
+        [buffer[rows + i * TILE_ROWS : rows + (i + 1) * TILE_ROWS, :] for i in range(count)], axis=1
+    )
+
+
+def project_shard(normed_ref, buffer, j, steps, dtw_ref):
+    rows = dtw_ref.shape[1]
+    at = pl.multiple_of(jnp.bitwise_xor(lax.axis_index("dp"), j) * rows, LANES)
+    normed = normed_ref[:, pl.ds(at, rows)]
+    row = lax.broadcasted_iota(jnp.int32, (TILE_ROWS, rows), 0)
+    below = below_rows(buffer, rows)[:, 0:rows].astype(jnp.float32)
+    dtw_ref[0:TILE_ROWS, :] = jnp.where(row < steps, below, 0.0).astype(jnp.bfloat16)
+    return dot32(normed, buffer[0:rows, :]), dot32(normed, dtw_ref[...], 1, 1)
+
+
+def first_most_kernel(steps, normed_ref, own_ref, near_ref, most_ref, raw_ref, dtw_ref):
+    dtw_ref[...] = jnp.zeros_like(dtw_ref)
+    most, raw = project_shard(normed_ref, own_ref, 0, steps, dtw_ref)
+    more, more_raw = project_shard(normed_ref, near_ref, 1, steps, dtw_ref)
+    most_ref[...] = most + more
+    raw_ref[...] = raw + more_raw
+
+
 def first_kernel(
     normed_ref,
+    most_ref,
+    most_raw_ref,
     own_ref,
     near_ref,
     far_ref,
@@ -453,53 +484,36 @@
     prefix_ref,
     fade_ref,
     halo_ref,
-    w_ref,
-    extra_ref,
+    halo_rows_ref,
     dtw_ref,
     ext_ref,
-    sems,
 ):
     position = lax.axis_index("dp")
     tok, model = normed_ref.shape
-    peers, extra, width = extra_ref.shape
-    rows = model // peers
+    width = bc_ref.shape[1]
+    rows = dtw_ref.shape[1]
     buffers = (own_ref, near_ref, far_ref, last_ref)
-    copies = gather_rows(position, buffers, rows, w_ref, sems)
     for j, buffer in enumerate(buffers):
-        copies.append(
-            pltpu.make_async_copy(
-                buffer.at[rows : rows + extra],
-                extra_ref.at[jnp.bitwise_xor(position, j)],
-                sems.at[peers + j],
-            )
-        )
-    for copy in copies:
-        copy.start()
+        halo_rows_ref[jnp.bitwise_xor(position, j)] = below_rows(buffer, rows)
+    halo = halo_rows_ref[jnp.maximum(position - 1, 0)].astype(jnp.float32)
+    halo_ref[...] = (halo * rms_scale(halo) * gain_ref[...]).astype(jnp.bfloat16)
+    halo_sum = 0.0
+    for j, buffer in enumerate(buffers):
+        at = pl.multiple_of(jnp.bitwise_xor(position, j) * rows, LANES)
+        halo_sum = halo_sum + dot32(halo_ref[:, pl.ds(at, rows)], buffer[0:rows, :])
+    ext_ref[0:TILE_ROWS, :] = halo_sum
     dtw_ref[...] = jnp.zeros_like(dtw_ref)
-    for copy in copies:
-        copy.wait()
-    pieces = model // width
-    for s in range(peers):
-        below = jnp.concatenate(
-            [extra_ref[s, i * TILE_ROWS : (i + 1) * TILE_ROWS, :] for i in range(pieces)], axis=1
-        )
-        row = lax.broadcasted_iota(jnp.int32, (TILE_ROWS, rows), 0)
-        steps = jnp.where(row < bias_ref.shape[0], below[:, 0:rows].astype(jnp.float32), 0.0)
-        dtw_ref[0:TILE_ROWS, s * rows : (s + 1) * rows] = steps.astype(jnp.bfloat16)
-    behind = jnp.maximum(position - 1, 0)
-    halo = jnp.concatenate(
-        [extra_ref[behind, i * TILE_ROWS : (i + 1) * TILE_ROWS, :] for i in range(pieces)], axis=1
-    ).astype(jnp.float32)
-    halo = (halo * rms_scale(halo) * gain_ref[...]).astype(jnp.bfloat16)
-    halo_ref[...] = halo
-    normed = normed_ref[...]
+    steps = bias_ref.shape[0]
+    most, raw = project_shard(normed_ref, far_ref, 2, steps, dtw_ref)
+    more, more_raw = project_shard(normed_ref, last_ref, 3, steps, dtw_ref)
+    ext_ref[TILE_ROWS:, :] = most_ref[...] + most + more
     head_lane = lax.broadcasted_iota(jnp.int32, (1, LANES), 1)
     bias = jnp.zeros((1, LANES), jnp.float32)
     decay = jnp.zeros((1, LANES), jnp.float32)
-    for h in range(bias_ref.shape[0]):
+    for h in range(steps):
         bias = jnp.where(head_lane == h, bias_ref[h], bias)
         decay = jnp.where(head_lane == h, decay_ref[h], decay)
-    raw = dot32(normed, dtw_ref[...], 1, 1) + bias
+    raw = most_raw_ref[...] + raw + more_raw + bias
     step = jnp.maximum(raw, 0.0) + jnp.log1p(jnp.exp(-jnp.abs(raw)))
     step_ref[...] = step
     lane = lax.broadcasted_iota(jnp.int32, (tok, LANES), 1)
@@ -517,7 +531,6 @@
     )
     prefix_ref[...] = sums[0:tok]
     fade_ref[...] = jnp.exp(sums[tok : 2 * tok])
-    project_rows(normed, halo, w_ref[...], ext_ref, 0, width)
     same = [jnp.broadcast_to(meta_ref[:, k : k + 1], (tok, LANES)) for k in range(3)]
     for j in range(width // LANES):
         own = slice(j * LANES, (j + 1) * LANES)
@@ -581,12 +594,16 @@
     head_dim = LANES // 2
     tok = bc_ref.shape[0]
     b_all = bc_ref[:, 0:state_width].astype(jnp.float32)
-    for g in range(table_refs[0].shape[0]):
-        ended = jnp.where(meta_ref[:, 6:7] == g, meta_ref[:, 8:9], 0.0)
-        b_ended = (b_all * ended).astype(jnp.bfloat16)
-        for k, table_ref in enumerate(table_refs):
-            faded = faded_ref[k * rows : (k + 1) * rows, :]
-            table_ref[g] = dot32(faded, b_ended).astype(jnp.bfloat16)
+    owner = jnp.where(meta_ref[:, 8:9] > 0.0, meta_ref[:, 6:7], -1.0)
+    owner = jnp.broadcast_to(owner, (tok, state_width))
+    for g in range(0, table_refs[0].shape[0], 2):
+        pair = [jnp.where(owner == g + k, b_all, 0.0).astype(jnp.bfloat16) for k in range(2)]
+        sums = dot32(faded_ref[...], jnp.concatenate(pair, axis=1)).astype(jnp.bfloat16)
+        for n, table_ref in enumerate(table_refs):
+            for k in range(2):
+                table_ref[g + k] = sums[
+                    n * rows : (n + 1) * rows, k * state_width : (k + 1) * state_width
+                ]
     position = lax.axis_index("dp")
     before = before_device(ids_ref, position, tok)
     stop = (position + 1) * tok
@@ -623,6 +640,7 @@
     head_dim = LANES // 2
     tok = y_ref.shape[0]
     lane = lax.broadcasted_iota(jnp.int32, (BLOCK, LANES), 1)
+    half = BLOCK // 2
     for b in range(tok // BLOCK):
         own_rows = slice(b * BLOCK, (b + 1) * BLOCK)
         b_blk = bc_ref[own_rows, 0:state_width]
@@ -648,13 +666,16 @@
                 middle = dot32(faded.astype(jnp.bfloat16).T, b_before).astype(jnp.bfloat16)
                 out = out + widen(carried, q, head_dim) * dot32(c_blk, middle, 1, 1)
             sx = stepx_ref[own_rows, own].astype(jnp.float32)
-            for side in range(2):
-                h = 2 * q + side
-                gaps = prefix[:, h : h + 1] - across[h : h + 1, :] + pen
-                mixing = (scores * jnp.exp(gaps)).astype(jnp.bfloat16)
-                kept = (lane < head_dim) if side == 0 else (lane >= head_dim)
-                out = out + dot32(mixing, jnp.where(kept, sx, 0.0).astype(jnp.bfloat16))
-            y_ref[own_rows, own] = out
+            sides = [jnp.where(lane < head_dim, sx, 0.0), jnp.where(lane >= head_dim, sx, 0.0)]
+            sides = [side.astype(jnp.bfloat16) for side in sides]
+            for rows, seen in ((slice(0, half), half), (slice(half, BLOCK), BLOCK)):
+                part = out[rows]
+                for side in range(2):
+                    h = 2 * q + side
+                    gaps = prefix[rows, h : h + 1] - across[h : h + 1, 0:seen] + pen[rows, 0:seen]
+                    mixing = (scores[rows, 0:seen] * jnp.exp(gaps)).astype(jnp.bfloat16)
+                    part = part + dot32(mixing, sides[side][0:seen])
+                y_ref[b * BLOCK + rows.start : b * BLOCK + rows.stop, own] = part
 
 
 def z_most_kernel(normed_ref, own_ref, near_ref, far_ref, most_ref):
@@ -764,19 +785,15 @@
     out_ref[:, model:] = split_squares(squares)
 
 
-def finish_kernel(inner_total, hidden_all, joined_ref, keep_ref, *refs):
-    got, (out_ref, hidden_ref, sem) = refs[:-3], refs[-3:]
-    part, model = hidden_ref.shape
-    at = pl.multiple_of(lax.axis_index("head") * part, part)
-    arrival = pltpu.make_async_copy(hidden_all.at[pl.ds(at, part)], hidden_ref, sem)
-    arrival.start()
+def finish_kernel(inner_total, hidden_ref, joined_ref, keep_ref, *refs):
+    got, out_ref = refs[:-1], refs[-1]
+    model = hidden_ref.shape[1]
     squares = keep_ref[:, model : model + 1]
     total = keep_ref[:, 0:model]
     for ref in got:
         squares = squares + joined_squares(ref, model)
         total = total + ref[:, 0:model].astype(jnp.float32)
     scale = lax.rsqrt(squares / inner_total + EPSILON)
-    arrival.wait()
     out_ref[...] = (hidden_ref[...].astype(jnp.float32) + scale * total).astype(jnp.bfloat16)
 
 
@@ -855,7 +872,7 @@
     )(w_zx)
 
     blocks = tok // BLOCK
-    normed, meta, order, pen = pl.pallas_call(
+    normed, meta, order, pen, own_hidden = pl.pallas_call(
         facts_kernel,
         name="norm_and_token_facts",
         out_shape=(
@@ -863,9 +880,10 @@
             shape((tok, LANES), f32),
             shape((2 * tok, tok), bf16),
             shape((blocks, BLOCK, BLOCK), f32),
+            shape((tok // head_count, model), bf16),
         ),
         in_specs=in_vmem(1) + [in_hbm] + in_vmem(1),
-        out_specs=tuple(in_vmem(4)),
+        out_specs=tuple(in_vmem(5)),
         scratch_shapes=[pltpu.VMEM((tok, model), bf16), pltpu.SemaphoreType.DMA],
         compiler_params=kernel_params(16),
         cost_estimate=LITTLE,
@@ -883,8 +901,18 @@
     out_near = exchange(out_part, "dp", 1)
 
     x_far = exchange(x_own, "dp", 2)
-    first_far, first_near, normed, meta, order, pen, x_own, gate_own = lax.optimization_barrier(
-        (first_far, first_near, normed, meta, order, pen, x_own, gate_own)
+    first_most, first_raw = pl.pallas_call(
+        functools.partial(first_most_kernel, heads),
+        name="project_b_c_and_steps_of_chip",
+        out_shape=(shape((tok, 2 * state_width), f32), shape((tok, LANES), f32)),
+        in_specs=in_vmem(3),
+        out_specs=tuple(in_vmem(2)),
+        scratch_shapes=[pltpu.VMEM((LANES, rows), bf16)],
+        compiler_params=kernel_params(8),
+        cost_estimate=LITTLE,
+    )(normed, first_own, first_near)
+    first_far, first_most, first_raw, meta, order, pen, x_own, gate_own = lax.optimization_barrier(
+        (first_far, first_most, first_raw, meta, order, pen, x_own, gate_own)
     )
     x_near = exchange(x_own, "dp", 1)
     gate_near = exchange(gate_own, "dp", 1)
@@ -899,19 +927,19 @@
             shape((tok, LANES), f32),
             shape((TILE_ROWS, model), bf16),
         ),
-        in_specs=in_vmem(1) + [anywhere] * 4 + in_vmem(4) + [smem] * 2,
+        in_specs=in_vmem(11) + [smem] * 2,
         out_specs=tuple(in_vmem(5)),
         scratch_shapes=[
-            pltpu.VMEM((model, 2 * state_width), bf16),
-            pltpu.VMEM((peers, extra, 2 * state_width), bf16),
-            pltpu.VMEM((LANES, model), bf16),
+            pltpu.VMEM((peers, TILE_ROWS, model), bf16),
+            pltpu.VMEM((LANES, rows), bf16),
             pltpu.VMEM((TILE_ROWS + tok, 2 * state_width), f32),
-            pltpu.SemaphoreType.DMA((2 * peers,)),
         ],
         compiler_params=kernel_params(14),
         cost_estimate=LITTLE,
     )(
         normed,
+        first_most,
+        first_raw,
         first_own,
         first_near,
         first_far,
@@ -1074,12 +1102,11 @@
         functools.partial(finish_kernel, inner * head_count),
         name="scale_and_add_hidden",
         out_shape=shape((out_rows, model), bf16),
-        in_specs=[in_hbm, anywhere] + in_vmem(3),
+        in_specs=in_vmem(1) + [anywhere] + in_vmem(3),
         out_specs=in_vmem(1)[0],
-        scratch_shapes=[pltpu.VMEM((out_rows, model), bf16), pltpu.SemaphoreType.DMA],
         compiler_params=kernel_params(4),
         cost_estimate=LITTLE,
-    )(hidden, joined, sums_keep, sums_near, passed)
+    )(own_hidden, joined, sums_keep, sums_near, passed)
     return (
         layer_out,
         request_states.reshape(requests, heads, inner // heads, state_width),

time: 58.3 us -> 56.4 us (0.967)
  Pallas kernels: 22.3 us -> 19.4 us
  waiting for transfers between devices: 9.12 us -> 11.2 us
  starting transfers between devices: 25.5 us -> 24.6 us
    pallas_call x1, Pallas kernels: 4.6 us -> 2.29 us  [fused_on_device(): pl.pallas_call(first_kernel, name='project_b_c_and_steps', out_shape=(sha...]
    ppermute x22, waiting for transfers between devices: 9.11 us -> 11.2 us  [exchange(): lax.ppermute(values, axis, [(i, i ^ bits) for i in range(lax.axis_size(ax...]
    pallas_call x1, Pallas kernels: 2.21 us -> 1.39 us  [fused_on_device(): pl.pallas_call(table_kernel, name='sum_ended_states', out_shape=(shape((P...]
    ppermute x22, starting transfers between devices: 23 us -> 22.2 us  [exchange(): lax.ppermute(values, axis, [(i, i ^ bits) for i in range(lax.axis_size(ax...]
    pallas_call x0 -> x1, Pallas kernels: none -> 0.63 us  [fused_on_device(): pl.pallas_call(functools.partial(first_most_kernel, heads), name='project...]
  transfers between devices with their start and end apart: 23 -> 23, of which waited for: 8 -> 9; matrix products, arithmetic and copies ran while one was open for 0% -> 0% of each run, Pallas kernels for 32% -> 28%
where the time goes in v5:
time: 56.4 us; the launch traced here: 56.2 us
  starting transfers between devices  24.6 us (44%)
  Pallas kernels  19.4 us (34%)
  waiting for transfers between devices  11.2 us (20%)
  between operations  0.96 us (2%)
    ppermute x22, starting transfers between devices, exchange(): lax.ppermute(values, axis, [(i, i ^ bits) for i in range(lax.axis_size(ax...  22.2 us
    ppermute x22, waiting for transfers between devices, exchange(): lax.ppermute(values, axis, [(i, i ^ bits) for i in range(lax.axis_size(ax...  11.2 us
    pallas_call x1, Pallas kernels, fused_on_device(): pl.pallas_call(inner_kernel, name='project_and_convolve_x', out_shape=(sh...  2.64 us
    ppermute x1, starting transfers between devices, fused_on_device(): lax.ppermute(leaving, 'dp', [(i, i + 1) for i in range(peers - 1)])  2.41 us
    pallas_call x1, Pallas kernels, fused_on_device(): pl.pallas_call(first_kernel, name='project_b_c_and_steps', out_shape=(sha...  2.29 us
    pallas_call x1, Pallas kernels, fused_on_device(): pl.pallas_call(local_kernel, name='mix_within_blocks', out_shape=shape((t...  2.16 us
    pallas_call x1, Pallas kernels, fused_on_device(): pl.pallas_call(pack_first_kernel, name='pack_first_weights', out_shape=sh...  1.95 us
    pallas_call x1, Pallas kernels, fused_on_device(): pl.pallas_call(table_kernel, name='sum_ended_states', out_shape=(shape((P...  1.39 us
  transfers between devices with their start and end apart: 23, of which 9 were waited for; matrix products, arithmetic and copies ran while one was open for 0% of the time, Pallas kernels for 28%

profile of v5, /device:TPU:0, one launch (start us, length us, event | category | flops | bytes accessed | tf_op | source)
XLA Modules:
  0.0 56.2 jit_solution(5896381547124076455)
XLA Ops:
  0.7 2.0 %pack_first_weights.1.own_ref = bf16[480,256]{1,0:T(8,128)(2,1)} custom-call(s32[1,4]{1,0:T(1,128)} %bitcast.5, f32[384,256]{1,0:T(8,128)} %wbc_ref.1, f32[6,384]{1,0:T(8,128)} %bitcast.6, bf16[512,1536]{1,0:T(8,128)(2,1)} %hidden_ref.1), custom_call_target="tpu_custom_call" | custom-call | flops 1000 | bytes 1000 | tf_op jit(solution)/shard_map/pack_first_weights/pallas_call | solution.py:841
  3.1 2.6 %collective-permute-start = (bf16[480,256]{1,0:T(8,128)(2,1)}, bf16[480,256]{1,0:T(8,128)(2,1)S(1)}, u32[]{:S(2)}, u32[]{:S(2)}) collective-permute-start(bf16[480,256]{1,0:T(8,128)(2,1)} %pack_first_weights.1.own_ref), channel_id=1, source_target_pairs={{0,16},{8,24},{16,0},{24,8},{1,17},{9,25},{17,1},{25,9},{2,18},{10... | collective-permute-start | bytes 737288 | tf_op jit(solution)/shard_map/ppermute | solution.py:275
  6.2 1.6 %collective-permute-start.16 = (bf16[384,768]{1,0:T(8,128)(2,1)S(1)}, bf16[384,768]{1,0:T(8,128)(2,1)S(1)}, u32[]{:S(2)}, u32[]{:S(2)}) collective-permute-start(bf16[384,768]{1,0:T(8,128)(2,1)S(1)} %get-tuple-element.105), channel_id=1, source_target_pairs={{0,2},{1,3},{2,0},{3,1},{4,6},{5,7},{6,4},{7,5},{8,10},{9,11},{10,... | collective-permute-start | bytes 1769480 | tf_op jit(solution)/shard_map/ppermute | solution.py:275
  9.0 1.2 %norm_and_token_facts.1 = (bf16[512,1536]{1,0:T(8,128)(2,1)S(1)}, f32[512,128]{1,0:T(8,128)S(1)}, bf16[1024,512]{1,0:T(8,128)(2,1)S(1)}, f32[2,256,256]{2,1,0:T(8,128)S(1)}, bf16[64,1536]{1,0:T(8,128)(2,1)S(1)}) custom-call(s32[1,2048]{1,0:T(1,128)S(1)} %bitcast.4, bf16[512,1536]{1,0:T(8,128)(2,1)S(1)} %copy-done, f32[1,1536]{1,0:T(1,128)S(1)} %broadcast_in_dim.14.gain_ref), custom_call_target="tpu_custom_call" | custom-call | flops 1000 | bytes 1000 | tf_op jit(solution)/shard_map/norm_and_token_facts/pallas_call | solution.py:875
  10.3 0.6 %project_b_c_and_steps_of_chip.1 = (f32[512,256]{1,0:T(8,128)S(1)}, f32[512,128]{1,0:T(8,128)S(1)}) custom-call(bf16[512,1536]{1,0:T(8,128)(2,1)S(1)} %get-tuple-element.61.normed_ref, bf16[480,256]{1,0:T(8,128)(2,1)S(1)} %copy-done.1, bf16[480,256]{1,0:T(8,128)(2,1)S(1)} %collective-permute-done.1.near_ref), custom_call_target="tpu_custom_call" | custom-call | flops 1000 | bytes 1000 | tf_op jit(solution)/shard_map/project_b_c_and_steps_of_chip/pallas_call | solution.py:904
  11.0 1.7 %collective-permute-done.far_ref = bf16[480,256]{1,0:T(8,128)(2,1)S(1)} collective-permute-done((bf16[480,256]{1,0:T(8,128)(2,1)}, bf16[480,256]{1,0:T(8,128)(2,1)S(1)}, u32[]{:S(2)}, u32[]{:S(2)}) %collective-permute-start) | collective-permute-done | bytes 245792 | tf_op jit(solution)/shard_map/ppermute | solution.py:275
  13.2 1.0 %collective-permute-done.3.last_ref = bf16[480,256]{1,0:T(8,128)(2,1)S(1)} collective-permute-done((bf16[480,256]{1,0:T(8,128)(2,1)S(1)}, bf16[480,256]{1,0:T(8,128)(2,1)S(1)}, u32[]{:S(2)}, u32[]{:S(2)}) %collective-permute-start.3) | collective-permute-done | bytes 245792 | tf_op jit(solution)/shard_map/ppermute | solution.py:275
  14.2 2.3 %project_b_c_and_steps.1 = (bf16[512,256]{1,0:T(8,128)(2,1)S(1)}, f32[512,128]{1,0:T(8,128)S(1)}, f32[512,128]{1,0:T(8,128)S(1)}, f32[512,128]{1,0:T(8,128)S(1)}, bf16[16,1536]{1,0:T(8,128)(2,1)S(1)}) custom-call(bf16[512,1536]{1,0:T(8,128)(2,1)S(1)} %get-tuple-element.61.normed_ref, f32[512,256]{1,0:T(8,128)S(1)} %get-tuple-element.71.most_ref, ...), custom_call_target="tpu_custom_call" | custom-call | flops 1000 | bytes 1000 | tf_op jit(solution)/shard_map/project_b_c_and_steps/pallas_call | solution.py:920
  16.5 2.2 %collective-permute-done.2.far_ref = bf16[384,384]{1,0:T(8,128)(2,1)S(1)} collective-permute-done((bf16[384,384]{1,0:T(8,128)(2,1)S(1)}, bf16[384,384]{1,0:T(8,128)(2,1)S(1)}, u32[]{:S(2)}, u32[]{:S(2)}) %collective-permute-start.2) | collective-permute-done | bytes 294944 | tf_op jit(solution)/shard_map/ppermute | solution.py:275
  19.3 1.8 %collective-permute-start.6 = (bf16[384,384]{1,0:T(8,128)(2,1)S(1)}, bf16[384,384]{1,0:T(8,128)(2,1)S(1)}, u32[]{:S(2)}, u32[]{:S(2)}) collective-permute-start(bf16[384,384]{1,0:T(8,128)(2,1)S(1)} %get-tuple-element.88.own_ref), channel_id=1, source_target_pairs={{0,16},{8,24},{16,0},{24,8},{1,17},{9,25},{17,1},{25,9},{2,18},{10... | collective-permute-start | bytes 884744 | tf_op jit(solution)/shard_map/ppermute | solution.py:275
  21.1 0.6 %collective-permute-done.16.part_ref = bf16[384,768]{1,0:T(8,128)(2,1)S(1)} collective-permute-done((bf16[384,768]{1,0:T(8,128)(2,1)S(1)}, bf16[384,768]{1,0:T(8,128)(2,1)S(1)}, u32[]{:S(2)}, u32[]{:S(2)}) %collective-permute-start.16) | collective-permute-done | bytes 589856 | tf_op jit(solution)/shard_map/ppermute | solution.py:275
  21.7 2.6 %project_and_convolve_x.1 = (bf16[512,384]{1,0:T(8,128)(2,1)S(1)}, bf16[512,384]{1,0:T(8,128)(2,1)S(1)}, bf16[384,512]{1,0:T(8,128)(2,1)S(1)}, bf16[384,128]{1,0:T(8,128)(2,1)S(1)}) custom-call(bf16[512,1536]{1,0:T(8,128)(2,1)S(1)} %get-tuple-element.61.normed_ref, bf16[384,384]{1,0:T(8,128)(2,1)S(1)} %get-tuple-element.81.own_ref, ...), custom_call_target="tpu_custom_call" | custom-call | flops 1000 | bytes 1000 | tf_op jit(solution)/shard_map/project_and_convolve_x/pallas_call | solution.py:959
  24.3 2.4 %collective-permute-start.8 = (bf16[384,128]{1,0:T(8,128)(2,1)S(1)}, bf16[384,128]{1,0:T(8,128)(2,1)S(1)}, u32[]{:S(2)}, u32[]{:S(2)}) collective-permute-start(bf16[384,128]{1,0:T(8,128)(2,1)S(1)} %get-tuple-element.89), channel_id=1, source_target_pairs={{0,8},{8,16},{16,24},{1,9},{9,17},{17,25},{2,10},{10,18},{18,26},{... | collective-permute-start | bytes 294920 | tf_op jit(solution)/shard_map/ppermute | solution.py:991
  26.8 2.2 %mix_within_blocks.1.y_ref = f32[512,384]{1,0:T(8,128)S(1)} custom-call(bf16[512,384]{1,0:T(8,128)(2,1)S(1)} %get-tuple-element.90.x_ref, bf16[512,256]{1,0:T(8,128)(2,1)S(1)} %get-tuple-element.80.bc_ref, bf16[512,384]{1,0:T(8,128)(2,1)S(1)} %get-tuple-element.91.stepx_ref, f32[512,128]{1,0:T(8,128)S(1)} %get-tuple-element.87.prefix_ref, ...), custom_call_target="tpu_custom_call" | custom-call | flops 1000 | bytes 1000 | tf_op jit(solution)/shard_map/mix_within_blocks/pallas_call | solution.py:993
  29.1 0.9 %project_gate_most.1.most_ref = f32[512,384]{1,0:T(8,128)S(1)} custom-call(bf16[512,1536]{1,0:T(8,128)(2,1)S(1)} %get-tuple-element.61.normed_ref, bf16[384,384]{1,0:T(8,128)(2,1)S(1)} %get-tuple-element.88.own_ref, bf16[384,384]{1,0:T(8,128)(2,1)S(1)} %collective-permute-done.7.near_ref, bf16[384,384]{1,0:T(8,128)(2,1)S(1)} %collective-permute-done.6.far_ref), custom_call_target="tpu_custom_call" | custom-call | flops 1000 | bytes 1000 | tf_op jit(solution)/shard_map/project_gate_most/pallas_call | solution.py:1017
  29.9 0.7 %collective-permute-done.15.last_ref = bf16[384,384]{1,0:T(8,128)(2,1)S(1)} collective-permute-done((bf16[384,384]{1,0:T(8,128)(2,1)S(1)}, bf16[384,384]{1,0:T(8,128)(2,1)S(1)}, u32[]{:S(2)}, u32[]{:S(2)}) %collective-permute-start.15) | collective-permute-done | bytes 294944 | tf_op jit(solution)/shard_map/ppermute | solution.py:275
  31.7 1.6 %collective-permute-start.19 = (bf16[128,384]{1,0:T(8,128)(2,1)S(1)}, bf16[128,384]{1,0:T(8,128)(2,1)S(1)}, u32[]{:S(2)}, u32[]{:S(2)}) collective-permute-start(bf16[128,384]{1,0:T(8,128)(2,1)S(1)} %get-tuple-element.111), channel_id=1, source_target_pairs={{0,2},{1,3},{2,0},{3,1},{4,6},{5,7},{6,4},{7,5},{8,10},{9,11},{10,... | collective-permute-start | bytes 294920 | tf_op jit(solution)/shard_map/ppermute | solution.py:275
  33.3 1.4 %sum_ended_states.1 = (bf16[8,96,128]{2,1,0:T(8,128)(2,1)S(1)}, bf16[8,96,128]{2,1,0:T(8,128)(2,1)S(1)}, bf16[8,96,128]{2,1,0:T(8,128)(2,1)S(1)}, bf16[8,96,128]{2,1,0:T(8,128)(2,1)S(1)}) custom-call(s32[2048]{0:T(1024)S(1)} %copy-done.4, bf16[512,256]{1,0:T(8,128)(2,1)S(1)} %get-tuple-element.80.bc_ref, bf16[384,512]{1,0:T(8,128)(2,1)S(1)} %get-tuple-element.86.faded_ref, ...), custom_call_target="tpu_custom_call" | custom-call | flops 1000 | bytes 1000 | tf_op jit(solution)/shard_map/sum_ended_states/pallas_call | solution.py:1006
  35.8 0.8 %collective-permute-done.19.got_ref = bf16[128,384]{1,0:T(8,128)(2,1)S(1)} collective-permute-done((bf16[128,384]{1,0:T(8,128)(2,1)S(1)}, bf16[128,384]{1,0:T(8,128)(2,1)S(1)}, u32[]{:S(2)}, u32[]{:S(2)}) %collective-permute-start.19) | collective-permute-done | bytes 98336 | tf_op jit(solution)/shard_map/ppermute | solution.py:275
  36.6 0.6 %project_out.3 = (f32[64,1664]{1,0:T(8,128)S(1)}, bf16[64,1664]{1,0:T(8,128)(2,1)S(1)}) custom-call(bf16[128,384]{1,0:T(8,128)(2,1)S(1)} %get-tuple-element.110.kept_ref, bf16[128,384]{1,0:T(8,128)(2,1)S(1)} %collective-permute-done.19.got_ref, bf16[384,1536]{1,0:T(8,128)(2,1)S(1)} %get-tuple-element.108.own_ref, ...), custom_call_target="tpu_custom_call" | custom-call | flops 1000 | bytes 1000 | tf_op jit(solution)/shard_map/project_out/pallas_call | solution.py:1077
  37.2 1.6 %collective-permute-start.20 = (bf16[64,1664]{1,0:T(8,128)(2,1)S(1)}, bf16[64,1664]{1,0:T(8,128)(2,1)S(1)}, u32[]{:S(2)}, u32[]{:S(2)}) collective-permute-start(bf16[64,1664]{1,0:T(8,128)(2,1)S(1)} %get-tuple-element.112), channel_id=1, source_target_pairs={{0,1},{1,0},{2,3},{3,2},{4,5},{5,4},{6,7},{7,6},{8,9},{9,8},{10,11... | collective-permute-start | bytes 638984 | tf_op jit(solution)/shard_map/ppermute | solution.py:275
  38.8 1.6 %collective-permute-start.18 = (bf16[128,384]{1,0:T(8,128)(2,1)S(1)}, bf16[128,384]{1,0:T(8,128)(2,1)S(1)}, u32[]{:S(2)}, u32[]{:S(2)}) collective-permute-start(bf16[128,384]{1,0:T(8,128)(2,1)S(1)} %get-tuple-element.107), channel_id=1, source_target_pairs={{0,2},{1,3},{2,0},{3,1},{4,6},{5,7},{6,4},{7,5},{8,10},{9,11},{10,... | collective-permute-start | bytes 294920 | tf_op jit(solution)/shard_map/ppermute | solution.py:275
  40.4 0.9 %pick_request_states.1 = (bf16[4,384,128]{2,1,0:T(8,128)(2,1)S(1)}, bf16[4,288,128]{2,1,0:T(8,128)(2,1)S(1)}, bf16[4,96,128]{2,1,0:T(8,128)(2,1)S(1)}) custom-call(s32[4]{0:T(128)S(1)} %copy-done.7, bf16[480,256]{1,0:T(8,128)(2,1)S(1)} %collective-permute-done.far_ref, bf16[8,96,128]{2,1,0:T(8,128)(2,1)S(1)} %get-tuple-element.94.refs_0_, ...), custom_call_target="tpu_custom_call" | custom-call | flops 1000 | bytes 1000 | tf_op jit(solution)/shard_map/pick_request_states/pallas_call | solution.py:1052
  41.3 2.0 %collective-permute-start.13 = (bf16[4,288,128]{2,1,0:T(8,128)(2,1)S(1)}, bf16[4,288,128]{2,1,0:T(8,128)(2,1)S(1)}, u32[]{:S(2)}, u32[]{:S(2)}) collective-permute-start(bf16[4,288,128]{2,1,0:T(8,128)(2,1)S(1)} %get-tuple-element.99), channel_id=1, source_target_pairs={{0,16},{8,24},{16,0},{24,8},{1,17},{9,25},{17,1},{25,9},{2,18},{10... | collective-permute-start | bytes 884744 | tf_op jit(solution)/shard_map/ppermute | solution.py:275
  43.5 0.6 %project_out.2 = (f32[64,1664]{1,0:T(8,128)S(1)}, bf16[64,1664]{1,0:T(8,128)(2,1)S(1)}) custom-call(bf16[128,384]{1,0:T(8,128)(2,1)S(1)} %get-tuple-element.106.kept_ref, bf16[128,384]{1,0:T(8,128)(2,1)S(1)} %collective-permute-done.18.got_ref, bf16[384,1536]{1,0:T(8,128)(2,1)S(1)} %get-tuple-element.108.own_ref, ...), custom_call_target="tpu_custom_call" | custom-call | flops 1000 | bytes 1000 | tf_op jit(solution)/shard_map/project_out/pallas_call | solution.py:1078
  44.3 2.7 %collective-permute-start.22 = (bf16[64,1664]{1,0:T(8,128)(2,1)S(1)}, bf16[64,1664]{1,0:T(8,128)(2,1)S(1)}, u32[]{:S(2)}, u32[]{:S(2)}) collective-permute-start(bf16[64,1664]{1,0:T(8,128)(2,1)S(1)} %add_sums_to_pass_on.1), channel_id=1, source_target_pairs={{0,4},{1,5},{2,6},{3,7},{4,0},{5,1},{6,2},{7,3},{8,12},{9,13},{10,... | collective-permute-start | bytes 638984 | tf_op jit(solution)/shard_map/ppermute | solution.py:275
  46.9 1.2 %collective-permute-start.21 = (bf16[64,1664]{1,0:T(8,128)(2,1)S(1)}, bf16[64,1664]{1,0:T(8,128)(2,1)S(1)}, u32[]{:S(2)}, u32[]{:S(2)}) collective-permute-start(bf16[64,1664]{1,0:T(8,128)(2,1)S(1)} %get-tuple-element.114), channel_id=1, source_target_pairs={{0,1},{1,0},{2,3},{3,2},{4,5},{5,4},{6,7},{7,6},{8,9},{9,8},{10,11... | collective-permute-start | bytes 638984 | tf_op jit(solution)/shard_map/ppermute | solution.py:275
  48.1 2.2 %collective-permute-start.14 = (bf16[4,96,128]{2,1,0:T(8,128)(2,1)S(1)}, bf16[4,96,128]{2,1,0:T(8,128)(2,1)S(1)}, u32[]{:S(2)}, u32[]{:S(2)}) collective-permute-start(bf16[4,96,128]{2,1,0:T(8,128)(2,1)S(1)} %get-tuple-element.100), channel_id=1, source_target_pairs={{0,16},{8,24},{16,0},{24,8},{1,17},{9,25},{17,1},{25,9},{2,18},{10... | collective-permute-start | bytes 294920 | tf_op jit(solution)/shard_map/ppermute | solution.py:275
  50.3 2.6 %collective-permute-done.14.refs_1_ = bf16[4,96,128]{2,1,0:T(8,128)(2,1)S(1)} collective-permute-done((bf16[4,96,128]{2,1,0:T(8,128)(2,1)S(1)}, bf16[4,96,128]{2,1,0:T(8,128)(2,1)S(1)}, u32[]{:S(2)}, u32[]{:S(2)}) %collective-permute-start.14) | collective-permute-done | bytes 98336 | tf_op jit(solution)/shard_map/ppermute | solution.py:275
  52.9 1.0 %join_request_states.1 = (f32[4,384,128]{2,1,0:T(8,128)}, f32[8,128]{1,0:T(8,128)S(1)}) custom-call(bf16[4,384,128]{2,1,0:T(8,128)(2,1)S(1)} %get-tuple-element.98.keep_ref, bf16[4,288,128]{2,1,0:T(8,128)(2,1)S(1)} %collective-permute-done.13.refs_0_, bf16[4,96,128]{2,1,0:T(8,128)(2,1)S(1)} %collective-permute-done.14.refs_1_), custom_call_target="tpu_custom_call" | custom-call | flops 1000 | bytes 1000 | tf_op jit(solution)/shard_map/join_request_states/pallas_call | solution.py:1092
  53.9 1.4 %collective-permute-done.22.refs_1_ = bf16[64,1664]{1,0:T(8,128)(2,1)S(1)} collective-permute-done((bf16[64,1664]{1,0:T(8,128)(2,1)S(1)}, bf16[64,1664]{1,0:T(8,128)(2,1)S(1)}, u32[]{:S(2)}, u32[]{:S(2)}) %collective-permute-start.22) | collective-permute-done | bytes 213024 | tf_op jit(solution)/shard_map/ppermute | solution.py:275
  55.3 0.9 %scale_and_add_hidden.1 = bf16[64,1536]{1,0:T(8,128)(2,1)} custom-call(bf16[64,1536]{1,0:T(8,128)(2,1)S(1)} %get-tuple-element.60.hidden_ref, f32[8,128]{1,0:T(8,128)S(1)} %get-tuple-element.101.joined_ref, f32[64,1664]{1,0:T(8,128)S(1)} %get-tuple-element.109.keep_ref, bf16[64,1664]{1,0:T(8,128)(2,1)S(1)} %collective-permute-done.21.refs_0_, ...), custom_call_target="tpu_custom_call" | custom-call | flops 1000 | bytes 1000 | tf_op jit(solution)/shard_map/scale_and_add_hidden/pallas_call | solution.py:1101
  (60 shorter events, 5.7 us)
Async XLA Ops:
  0.6 5.1 %copy-start.12 = (f32[384]{0:T(512)S(1)}, f32[384]{0:T(512)}, u32[]{:S(2)}) copy-start(f32[384]{0:T(512)} %param.26) | copy-start | bytes 4612
  0.6 5.1 %copy-start.2 = (bf16[384,1536]{1,0:T(8,128)(2,1)S(1)}, bf16[384,1536]{1,0:T(8,128)(2,1)}, u32[]{:S(2)}) copy-start(bf16[384,1536]{1,0:T(8,128)(2,1)} %w_ref.1) | copy-start | bytes 3538948
  0.7 7.2 %copy-start.3 = (f32[384,2,384]{2,1,0:T(2,128)S(1)}, f32[384,2,384]{2,1,0:T(2,128)}, u32[]{:S(2)}) copy-start(f32[384,2,384]{2,1,0:T(2,128)} %wzx_ref.1) | copy-start | bytes 3538948
  2.6 7.7 %collective-permute-start.1 = (bf16[480,256]{1,0:T(8,128)(2,1)}, bf16[480,256]{1,0:T(8,128)(2,1)S(1)}, u32[]{:S(2)}, u32[]{:S(2)}) collective-permute-start(bf16[480,256]{1,0:T(8,128)(2,1)} %pack_first_weights.1.own_ref), channel_id=1, source_target_pairs={{0,8},{8,0},{16,24},{24,16},{1,9},{9,1},{17,25},{25,17},{2,10},{10... | collective-permute-start | bytes 737288 | tf_op jit(solution)/shard_map/ppermute | solution.py:275
  3.1 9.6 %collective-permute-start = (bf16[480,256]{1,0:T(8,128)(2,1)}, bf16[480,256]{1,0:T(8,128)(2,1)S(1)}, u32[]{:S(2)}, u32[]{:S(2)}) collective-permute-start(bf16[480,256]{1,0:T(8,128)(2,1)} %pack_first_weights.1.own_ref), channel_id=1, source_target_pairs={{0,16},{8,24},{16,0},{24,8},{1,17},{9,25},{17,1},{25,9},{2,18},{10... | collective-permute-start | bytes 737288 | tf_op jit(solution)/shard_map/ppermute | solution.py:275
  6.2 4.1 %copy-start.1 = (bf16[480,256]{1,0:T(8,128)(2,1)S(1)}, bf16[480,256]{1,0:T(8,128)(2,1)}, u32[]{:S(2)}) copy-start(bf16[480,256]{1,0:T(8,128)(2,1)} %pack_first_weights.1.own_ref) | copy-start | bytes 737284
  6.2 15.5 %collective-permute-start.16 = (bf16[384,768]{1,0:T(8,128)(2,1)S(1)}, bf16[384,768]{1,0:T(8,128)(2,1)S(1)}, u32[]{:S(2)}, u32[]{:S(2)}) collective-permute-start(bf16[384,768]{1,0:T(8,128)(2,1)S(1)} %get-tuple-element.105), channel_id=1, source_target_pairs={{0,2},{1,3},{2,0},{3,1},{4,6},{5,7},{6,4},{7,5},{8,10},{9,11},{10,... | collective-permute-start | bytes 1769480 | tf_op jit(solution)/shard_map/ppermute | solution.py:275
  8.4 10.4 %collective-permute-start.2 = (bf16[384,384]{1,0:T(8,128)(2,1)S(1)}, bf16[384,384]{1,0:T(8,128)(2,1)S(1)}, u32[]{:S(2)}, u32[]{:S(2)}) collective-permute-start(bf16[384,384]{1,0:T(8,128)(2,1)S(1)} %get-tuple-element.81.own_ref), channel_id=1, source_target_pairs={{0,16},{8,24},{16,0},{24,8},{1,17},{9,25},{17,1},{25,9},{2,18},{10... | collective-permute-start | bytes 884744 | tf_op jit(solution)/shard_map/ppermute | solution.py:275
  10.3 4.0 %copy-start.6 = (f32[4,256]{1,0:T(4,128)S(1)}, f32[4,256]{1,0:T(4,128)}, u32[]{:S(2)}) copy-start(f32[4,256]{1,0:T(4,128)} %taps_ref.2) | copy-start | bytes 12292
  10.3 3.9 %copy-start.8 = (f32[6]{0:T(128)S(1)}, f32[6]{0:T(128)}, u32[]{:S(2)}) copy-start(f32[6]{0:T(128)} %bias_ref.1) | copy-start | bytes 76
  10.3 3.9 %copy-start.9 = (f32[6]{0:T(128)S(1)}, f32[6]{0:T(128)}, u32[]{:S(2)}) copy-start(f32[6]{0:T(128)} %decay_ref.1) | copy-start | bytes 76
  12.7 9.0 %copy-start.5 = (f32[4,384]{1,0:T(4,128)S(1)}, f32[4,384]{1,0:T(4,128)}, u32[]{:S(2)}) copy-start(f32[4,384]{1,0:T(4,128)} %taps_ref.3) | copy-start | bytes 18436
  12.7 1.5 %collective-permute-start.3 = (bf16[480,256]{1,0:T(8,128)(2,1)S(1)}, bf16[480,256]{1,0:T(8,128)(2,1)S(1)}, u32[]{:S(2)}, u32[]{:S(2)}) collective-permute-start(bf16[480,256]{1,0:T(8,128)(2,1)S(1)} %collective-permute-done.far_ref), channel_id=1, source_target_pairs={{0,8},{8,0},{16,24},{24,16},{1,9},{9,1},{17,25},{25,17},{2,10},{10... | collective-permute-start | bytes 737288 | tf_op jit(solution)/shard_map/ppermute | solution.py:275
  12.7 9.0 %collective-permute-start.4 = (bf16[384,384]{1,0:T(8,128)(2,1)S(1)}, bf16[384,384]{1,0:T(8,128)(2,1)S(1)}, u32[]{:S(2)}, u32[]{:S(2)}) collective-permute-start(bf16[384,384]{1,0:T(8,128)(2,1)S(1)} %get-tuple-element.81.own_ref), channel_id=1, source_target_pairs={{0,8},{8,0},{16,24},{24,16},{1,9},{9,1},{17,25},{25,17},{2,10},{10... | collective-permute-start | bytes 884744 | tf_op jit(solution)/shard_map/ppermute | solution.py:275
  18.8 8.0 %copy-start.10 = (f32[6]{0:T(128)S(1)}, f32[6]{0:T(128)}, u32[]{:S(2)}) copy-start(f32[6]{0:T(128)} %skip_ref.1) | copy-start | bytes 76
  18.8 2.9 %collective-permute-start.5 = (bf16[384,384]{1,0:T(8,128)(2,1)S(1)}, bf16[384,384]{1,0:T(8,128)(2,1)S(1)}, u32[]{:S(2)}, u32[]{:S(2)}) collective-permute-start(bf16[384,384]{1,0:T(8,128)(2,1)S(1)} %collective-permute-done.2.far_ref), channel_id=1, source_target_pairs={{0,8},{8,0},{16,24},{24,16},{1,9},{9,1},{17,25},{25,17},{2,10},{10... | collective-permute-start | bytes 884744 | tf_op jit(solution)/shard_map/ppermute | solution.py:275
  18.8 10.1 %collective-permute-start.7 = (bf16[384,384]{1,0:T(8,128)(2,1)S(1)}, bf16[384,384]{1,0:T(8,128)(2,1)S(1)}, u32[]{:S(2)}, u32[]{:S(2)}) collective-permute-start(bf16[384,384]{1,0:T(8,128)(2,1)S(1)} %get-tuple-element.88.own_ref), channel_id=1, source_target_pairs={{0,8},{8,0},{16,24},{24,16},{1,9},{9,1},{17,25},{25,17},{2,10},{10... | collective-permute-start | bytes 884744 | tf_op jit(solution)/shard_map/ppermute | solution.py:275
  19.3 9.7 %collective-permute-start.6 = (bf16[384,384]{1,0:T(8,128)(2,1)S(1)}, bf16[384,384]{1,0:T(8,128)(2,1)S(1)}, u32[]{:S(2)}, u32[]{:S(2)}) collective-permute-start(bf16[384,384]{1,0:T(8,128)(2,1)S(1)} %get-tuple-element.88.own_ref), channel_id=1, source_target_pairs={{0,16},{8,24},{16,0},{24,8},{1,17},{9,25},{17,1},{25,9},{2,18},{10... | collective-permute-start | bytes 884744 | tf_op jit(solution)/shard_map/ppermute | solution.py:275
  21.7 9.4 %collective-permute-start.17 = (bf16[384,768]{1,0:T(8,128)(2,1)S(1)}, bf16[384,768]{1,0:T(8,128)(2,1)S(1)}, u32[]{:S(2)}, u32[]{:S(2)}) collective-permute-start(bf16[384,768]{1,0:T(8,128)(2,1)S(1)} %collective-permute-done.16.part_ref), channel_id=1, source_target_pairs={{0,8},{8,0},{16,24},{24,16},{1,9},{9,1},{17,25},{25,17},{2,10},{10... | collective-permute-start | bytes 1769480 | tf_op jit(solution)/shard_map/ppermute | solution.py:275
  24.3 4.6 %collective-permute-start.8 = (bf16[384,128]{1,0:T(8,128)(2,1)S(1)}, bf16[384,128]{1,0:T(8,128)(2,1)S(1)}, u32[]{:S(2)}, u32[]{:S(2)}) collective-permute-start(bf16[384,128]{1,0:T(8,128)(2,1)S(1)} %get-tuple-element.89), channel_id=1, source_target_pairs={{0,8},{8,16},{16,24},{1,9},{9,17},{17,25},{2,10},{10,18},{18,26},{... | collective-permute-start | bytes 294920 | tf_op jit(solution)/shard_map/ppermute | solution.py:991
  29.0 1.6 %collective-permute-start.15 = (bf16[384,384]{1,0:T(8,128)(2,1)S(1)}, bf16[384,384]{1,0:T(8,128)(2,1)S(1)}, u32[]{:S(2)}, u32[]{:S(2)}) collective-permute-start(bf16[384,384]{1,0:T(8,128)(2,1)S(1)} %collective-permute-done.6.far_ref), channel_id=1, source_target_pairs={{0,8},{8,0},{16,24},{24,16},{1,9},{9,1},{17,25},{25,17},{2,10},{10... | collective-permute-start | bytes 884744 | tf_op jit(solution)/shard_map/ppermute | solution.py:275
  31.7 4.9 %collective-permute-start.19 = (bf16[128,384]{1,0:T(8,128)(2,1)S(1)}, bf16[128,384]{1,0:T(8,128)(2,1)S(1)}, u32[]{:S(2)}, u32[]{:S(2)}) collective-permute-start(bf16[128,384]{1,0:T(8,128)(2,1)S(1)} %get-tuple-element.111), channel_id=1, source_target_pairs={{0,2},{1,3},{2,0},{3,1},{4,6},{5,7},{6,4},{7,5},{8,10},{9,11},{10,... | collective-permute-start | bytes 294920 | tf_op jit(solution)/shard_map/ppermute | solution.py:275
  34.7 4.1 %collective-permute-start.10 = (bf16[8,96,128]{2,1,0:T(8,128)(2,1)S(1)}, bf16[8,96,128]{2,1,0:T(8,128)(2,1)S(1)}, u32[]{:S(2)}, u32[]{:S(2)}) collective-permute-start(bf16[8,96,128]{2,1,0:T(8,128)(2,1)S(1)} %get-tuple-element.95.refs_1_), channel_id=1, source_target_pairs={{0,8},{8,0},{16,24},{24,16},{1,9},{9,1},{17,25},{25,17},{2,10},{10... | collective-permute-start | bytes 589832 | tf_op jit(solution)/shard_map/ppermute | solution.py:275
  34.9 5.5 %collective-permute-start.11 = (bf16[8,96,128]{2,1,0:T(8,128)(2,1)S(1)}, bf16[8,96,128]{2,1,0:T(8,128)(2,1)S(1)}, u32[]{:S(2)}, u32[]{:S(2)}) collective-permute-start(bf16[8,96,128]{2,1,0:T(8,128)(2,1)S(1)} %get-tuple-element.96.refs_2_), channel_id=1, source_target_pairs={{0,8},{8,0},{16,24},{24,16},{1,9},{9,1},{17,25},{25,17},{2,10},{10... | collective-permute-start | bytes 589832 | tf_op jit(solution)/shard_map/ppermute | solution.py:275
  35.3 5.1 %collective-permute-start.12 = (bf16[8,96,128]{2,1,0:T(8,128)(2,1)S(1)}, bf16[8,96,128]{2,1,0:T(8,128)(2,1)S(1)}, u32[]{:S(2)}, u32[]{:S(2)}) collective-permute-start(bf16[8,96,128]{2,1,0:T(8,128)(2,1)S(1)} %get-tuple-element.97.refs_3_), channel_id=1, source_target_pairs={{0,8},{8,0},{16,24},{24,16},{1,9},{9,1},{17,25},{25,17},{2,10},{10... | collective-permute-start | bytes 589832 | tf_op jit(solution)/shard_map/ppermute | solution.py:275
  35.4 5.0 %collective-permute-start.9 = (bf16[8,96,128]{2,1,0:T(8,128)(2,1)S(1)}, bf16[8,96,128]{2,1,0:T(8,128)(2,1)S(1)}, u32[]{:S(2)}, u32[]{:S(2)}) collective-permute-start(bf16[8,96,128]{2,1,0:T(8,128)(2,1)S(1)} %get-tuple-element.94.refs_0_), channel_id=1, source_target_pairs={{0,8},{8,0},{16,24},{24,16},{1,9},{9,1},{17,25},{25,17},{2,10},{10... | collective-permute-start | bytes 589832 | tf_op jit(solution)/shard_map/ppermute | solution.py:275
  37.2 6.8 %collective-permute-start.20 = (bf16[64,1664]{1,0:T(8,128)(2,1)S(1)}, bf16[64,1664]{1,0:T(8,128)(2,1)S(1)}, u32[]{:S(2)}, u32[]{:S(2)}) collective-permute-start(bf16[64,1664]{1,0:T(8,128)(2,1)S(1)} %get-tuple-element.112), channel_id=1, source_target_pairs={{0,1},{1,0},{2,3},{3,2},{4,5},{5,4},{6,7},{7,6},{8,9},{9,8},{10,11... | collective-permute-start | bytes 638984 | tf_op jit(solution)/shard_map/ppermute | solution.py:275
  38.8 4.6 %collective-permute-start.18 = (bf16[128,384]{1,0:T(8,128)(2,1)S(1)}, bf16[128,384]{1,0:T(8,128)(2,1)S(1)}, u32[]{:S(2)}, u32[]{:S(2)}) collective-permute-start(bf16[128,384]{1,0:T(8,128)(2,1)S(1)} %get-tuple-element.107), channel_id=1, source_target_pairs={{0,2},{1,3},{2,0},{3,1},{4,6},{5,7},{6,4},{7,5},{8,10},{9,11},{10,... | collective-permute-start | bytes 294920 | tf_op jit(solution)/shard_map/ppermute | solution.py:275
  41.3 11.6 %collective-permute-start.13 = (bf16[4,288,128]{2,1,0:T(8,128)(2,1)S(1)}, bf16[4,288,128]{2,1,0:T(8,128)(2,1)S(1)}, u32[]{:S(2)}, u32[]{:S(2)}) collective-permute-start(bf16[4,288,128]{2,1,0:T(8,128)(2,1)S(1)} %get-tuple-element.99), channel_id=1, source_target_pairs={{0,16},{8,24},{16,0},{24,8},{1,17},{9,25},{17,1},{25,9},{2,18},{10... | collective-permute-start | bytes 884744 | tf_op jit(solution)/shard_map/ppermute | solution.py:275
  44.3 11.0 %collective-permute-start.22 = (bf16[64,1664]{1,0:T(8,128)(2,1)S(1)}, bf16[64,1664]{1,0:T(8,128)(2,1)S(1)}, u32[]{:S(2)}, u32[]{:S(2)}) collective-permute-start(bf16[64,1664]{1,0:T(8,128)(2,1)S(1)} %add_sums_to_pass_on.1), channel_id=1, source_target_pairs={{0,4},{1,5},{2,6},{3,7},{4,0},{5,1},{6,2},{7,3},{8,12},{9,13},{10,... | collective-permute-start | bytes 638984 | tf_op jit(solution)/shard_map/ppermute | solution.py:275
  46.9 8.4 %collective-permute-start.21 = (bf16[64,1664]{1,0:T(8,128)(2,1)S(1)}, bf16[64,1664]{1,0:T(8,128)(2,1)S(1)}, u32[]{:S(2)}, u32[]{:S(2)}) collective-permute-start(bf16[64,1664]{1,0:T(8,128)(2,1)S(1)} %get-tuple-element.114), channel_id=1, source_target_pairs={{0,1},{1,0},{2,3},{3,2},{4,5},{5,4},{6,7},{7,6},{8,9},{9,8},{10,11... | collective-permute-start | bytes 638984 | tf_op jit(solution)/shard_map/ppermute | solution.py:275
  48.1 4.8 %collective-permute-start.14 = (bf16[4,96,128]{2,1,0:T(8,128)(2,1)S(1)}, bf16[4,96,128]{2,1,0:T(8,128)(2,1)S(1)}, u32[]{:S(2)}, u32[]{:S(2)}) collective-permute-start(bf16[4,96,128]{2,1,0:T(8,128)(2,1)S(1)} %get-tuple-element.100), channel_id=1, source_target_pairs={{0,16},{8,24},{16,0},{24,8},{1,17},{9,25},{17,1},{25,9},{2,18},{10... | collective-permute-start | bytes 294920 | tf_op jit(solution)/shard_map/ppermute | solution.py:275
  (4 other events, 13.7 us)

commit v6 on v5

--- a/solution.py
+++ b/solution.py
@@ -413,21 +413,6 @@
         whole_ref[:, own] = (w_ref[:, own].astype(jnp.float32) * gain).astype(jnp.bfloat16)
     at = pl.multiple_of((lax.axis_index("dp") % 2) * width, LANES)
     part_ref[...] = whole_ref[:, pl.ds(at, width)]
-
-
-def gather_rows(position, buffers, rows, w_ref, sems):
-    copies = []
-    for j, buffer in enumerate(buffers):
-        at = pl.multiple_of(jnp.bitwise_xor(position, j) * rows, rows)
-        copies.append(
-            pltpu.make_async_copy(buffer.at[0:rows], w_ref.at[pl.ds(at, rows)], sems.at[j])
-        )
-    return copies
-
-
-def project_rows(normed, halo, w, ext_ref, at, stop):
-    ext_ref[0:TILE_ROWS, at:stop] = dot32(halo, w)
-    ext_ref[TILE_ROWS:, at:stop] = dot32(normed, w)
 
 
 def convolve(ext_ref, own, taps, same):
@@ -537,12 +522,31 @@
         bc_ref[:, own] = convolve(ext_ref, own, taps_ref[:, own], same).astype(jnp.bfloat16)
 
 
+def shard_product(normed_ref, j, w_ref):
+    rows = w_ref.shape[0]
+    at = pl.multiple_of(jnp.bitwise_xor(lax.axis_index("dp"), j) * rows, LANES)
+    return dot32(normed_ref[:, pl.ds(at, rows)], w_ref[...])
+
+
+def inner_most_kernel(normed_ref, own_ref, near_ref, most_ref):
+    most_ref[...] = shard_product(normed_ref, 0, own_ref) + shard_product(normed_ref, 1, near_ref)
+
+
+def inner_far_kernel(normed_ref, most_ref, far_ref, sum_ref, first_ref, second_ref):
+    half = first_ref.shape[0]
+    first_ref[...] = far_ref[0:half, :]
+    second_ref[...] = far_ref[half:, :]
+    sum_ref[...] = most_ref[...] + shard_product(normed_ref, 2, far_ref)
+
+
 def inner_kernel(
     normed_ref,
+    most_ref,
     own_ref,
     near_ref,
     far_ref,
-    last_ref,
+    last_first_ref,
+    last_second_ref,
     halo_ref,
     taps_ref,
     meta_ref,
@@ -553,27 +557,24 @@
     stepx_ref,
     faded_ref,
     leaving_ref,
-    w_ref,
     ext_ref,
-    sems,
 ):
-    position = lax.axis_index("dp")
     tok = normed_ref.shape[0]
     inner = x_ref.shape[1]
-    rows = own_ref.shape[0]
     head_dim = LANES // 2
-    copies = gather_rows(position, (own_ref, near_ref, far_ref, last_ref), rows, w_ref, sems)
-    for copy in copies:
-        copy.start()
+    rows = far_ref.shape[0]
+    at = pl.multiple_of(jnp.bitwise_xor(lax.axis_index("dp"), 3) * rows, LANES)
+    last = jnp.concatenate([last_first_ref[...], last_second_ref[...]], axis=0)
+    ext_ref[0:TILE_ROWS, :] = sum(
+        shard_product(halo_ref, j, w_ref) for j, w_ref in enumerate((own_ref, near_ref, far_ref))
+    ) + dot32(halo_ref[:, pl.ds(at, rows)], last)
+    ext_ref[TILE_ROWS:, :] = most_ref[...] + dot32(normed_ref[:, pl.ds(at, rows)], last)
     state_width = leaving_ref.shape[1]
     step = step_ref[...]
     fade = fade_ref[...]
     b_all = bc_ref[:, 0:state_width].astype(jnp.float32)
     b_leaving = (b_all * meta_ref[:, 7:8]).astype(jnp.bfloat16)
     same = [jnp.broadcast_to(meta_ref[:, k : k + 1], (tok, LANES)) for k in range(3)]
-    for copy in copies:
-        copy.wait()
-    project_rows(normed_ref[...], halo_ref[...], w_ref[...], ext_ref, 0, inner)
     for q in range(inner // LANES):
         own = slice(q * LANES, (q + 1) * LANES)
         rounded = convolve(ext_ref, own, taps_ref[:, own], same).astype(jnp.bfloat16)
@@ -589,7 +590,8 @@
     return jnp.where(position > 0, ids_ref[jnp.maximum(position * tok - 1, 0)], -1)
 
 
-def table_kernel(ids_ref, bc_ref, faded_ref, meta_ref, prefix_ref, enter_ref, *table_refs):
+def table_kernel(ids_ref, bc_ref, faded_ref, meta_ref, prefix_ref, enter_ref, *refs):
+    table_refs = refs[2:]
     rows, state_width = table_refs[0].shape[1:]
     head_dim = LANES // 2
     tok = bc_ref.shape[0]
@@ -625,35 +627,38 @@
             table_ref[before, own, :] = (old + gain[:, h : h + 1] * entering).astype(jnp.bfloat16)
 
 
-def local_kernel(
-    x_ref,
-    bc_ref,
-    stepx_ref,
-    prefix_ref,
-    meta_ref,
-    pen_ref,
-    skip_ref,
-    y_ref,
-):
+def mixing_kernel(bc_ref, prefix_ref, pen_ref, mixing_ref):
+    blocks, heads = mixing_ref.shape[0:2]
+    state_width = bc_ref.shape[1] // 2
+    half = BLOCK // 2
+    for b in range(blocks):
+        own_rows = slice(b * BLOCK, (b + 1) * BLOCK)
+        scores = dot32(bc_ref[own_rows, state_width:], bc_ref[own_rows, 0:state_width], 1, 1)
+        prefix = prefix_ref[own_rows, :]
+        across = prefix.T
+        for h in range(heads):
+            for rows, seen in ((slice(0, half), half), (slice(half, BLOCK), BLOCK)):
+                gaps = prefix[rows, h : h + 1] - across[h : h + 1, 0:seen] + pen_ref[b, rows, 0:seen]
+                mixing_ref[b, h, rows, 0:seen] = (scores[rows, 0:seen] * jnp.exp(gaps)).astype(
+                    jnp.bfloat16
+                )
+
+
+def local_kernel(x_ref, bc_ref, stepx_ref, prefix_ref, meta_ref, mixing_ref, skip_ref, y_ref):
     inner = y_ref.shape[1]
     state_width = bc_ref.shape[1] // 2
     head_dim = LANES // 2
     tok = y_ref.shape[0]
+    half = BLOCK // 2
     lane = lax.broadcasted_iota(jnp.int32, (BLOCK, LANES), 1)
-    half = BLOCK // 2
     for b in range(tok // BLOCK):
         own_rows = slice(b * BLOCK, (b + 1) * BLOCK)
-        b_blk = bc_ref[own_rows, 0:state_width]
         c_blk = bc_ref[own_rows, state_width:]
-        scores = dot32(c_blk, b_blk, 1, 1)
-        pen = pen_ref[b]
-        prefix = prefix_ref[own_rows, :]
-        across = prefix.T
         if b > 0:
-            carried = jnp.exp(prefix - prefix_ref[b * BLOCK - 1 : b * BLOCK, :])
-            carried = carried * meta_ref[own_rows, 4:5]
             before_rows = slice((b - 1) * BLOCK, b * BLOCK)
             before = prefix_ref[before_rows, :]
+            carried = jnp.exp(prefix_ref[own_rows, :] - before[BLOCK - 1 : BLOCK, :])
+            carried = carried * meta_ref[own_rows, 4:5]
             fade = jnp.exp(before[BLOCK - 1 : BLOCK, :] - before)
             b_before = bc_ref[before_rows, 0:state_width].astype(jnp.float32)
             b_before = (b_before * meta_ref[before_rows, 5:6]).astype(jnp.bfloat16)
@@ -671,31 +676,28 @@
             for rows, seen in ((slice(0, half), half), (slice(half, BLOCK), BLOCK)):
                 part = out[rows]
                 for side in range(2):
-                    h = 2 * q + side
-                    gaps = prefix[rows, h : h + 1] - across[h : h + 1, 0:seen] + pen[rows, 0:seen]
-                    mixing = (scores[rows, 0:seen] * jnp.exp(gaps)).astype(jnp.bfloat16)
+                    mixing = mixing_ref[b, 2 * q + side, rows, 0:seen]
                     part = part + dot32(mixing, sides[side][0:seen])
                 y_ref[b * BLOCK + rows.start : b * BLOCK + rows.stop, own] = part
 
 
-def z_most_kernel(normed_ref, own_ref, near_ref, far_ref, most_ref):
-    position = lax.axis_index("dp")
-    rows = own_ref.shape[0]
-    total = 0.0
-    for j, w_ref in enumerate((own_ref, near_ref, far_ref)):
-        at = pl.multiple_of(jnp.bitwise_xor(position, j) * rows, LANES)
-        total = total + dot32(normed_ref[:, pl.ds(at, rows)], w_ref[...])
-    most_ref[...] = total
+def z_most_kernel(
+    normed_ref, own_ref, near_ref, far_ref, part_ref, most_ref, first_ref, second_ref
+):
+    half = first_ref.shape[0]
+    first_ref[...] = part_ref[0:half, :]
+    second_ref[...] = part_ref[half:, :]
+    most_ref[...] = sum(
+        shard_product(normed_ref, j, w_ref) for j, w_ref in enumerate((own_ref, near_ref, far_ref))
+    )
 
 
 def z_last_kernel(normed_ref, last_ref, most_ref, gate_ref):
-    rows = last_ref.shape[0]
-    at = pl.multiple_of(jnp.bitwise_xor(lax.axis_index("dp"), 3) * rows, LANES)
-    gate_ref[...] = silu_tanh(most_ref[...] + dot32(normed_ref[:, pl.ds(at, rows)], last_ref[...]))
-
-
-def gate_kernel(enter_ref, bc_ref, prefix_ref, meta_ref, y_ref, z_ref, arrived_ref, *outs):
-    scratch = outs[-1]
+    gate_ref[...] = silu_tanh(most_ref[...] + shard_product(normed_ref, 3, last_ref))
+
+
+def gate_kernel(enter_ref, bc_ref, prefix_ref, meta_ref, y_ref, z_ref, *outs):
+    scratch, outs = outs[-1], outs[:-1]
     inner = y_ref.shape[1]
     state_width = enter_ref.shape[1]
     head_dim = LANES // 2
@@ -757,7 +759,9 @@
     return high + ref[:, model + 1 : model + 2].astype(jnp.float32)
 
 
-def out_kernel(kept_ref, got_ref, own_ref, part_ref, near_ref, wide_out, bf16_out, sums_ref):
+def out_kernel(kept_ref, got_ref, own_ref, part_ref, first_ref, second_ref, wide_out, *refs):
+    outs, sums_ref = refs[:-1], refs[-1]
+    near = jnp.concatenate([first_ref[...], second_ref[...]], axis=0)
     core = lax.axis_index("dp") % 2
     width = part_ref.shape[1]
     rows, model = sums_ref.shape
@@ -767,17 +771,20 @@
     for value in (kept, got):
         wide = value.astype(jnp.float32)
         squares = squares + jnp.sum(wide * wide, axis=1, keepdims=True)
-    for j, other_ref in enumerate((part_ref, near_ref)):
+    for j, other in enumerate((part_ref[...], near)):
         at = pl.multiple_of(jnp.bitwise_xor(core, j) * width, LANES)
         own = dot32(kept, own_ref[:, pl.ds(at, width)])
-        sums_ref[:, pl.ds(at, width)] = own + dot32(got, other_ref[...])
+        sums_ref[:, pl.ds(at, width)] = own + dot32(got, other)
     wide_out[:, 0:model] = sums_ref[0:part, :]
     wide_out[:, model:] = jnp.broadcast_to(squares[0:part], (part, LANES))
-    bf16_out[:, 0:model] = sums_ref[part:, :].astype(jnp.bfloat16)
-    bf16_out[:, model:] = split_squares(squares[part:])
-
-
-def pass_kernel(pass_ref, cross_ref, out_ref):
+    size = part // len(outs)
+    for k, out in enumerate(outs):
+        own = slice(part + k * size, part + (k + 1) * size)
+        out[:, 0:model] = sums_ref[own, :].astype(jnp.bfloat16)
+        out[:, model:] = split_squares(squares[own])
+
+
+def pass_kernel(pass_ref, cross_ref, arrived_ref, out_ref):
     model = out_ref.shape[1] - LANES
     total = pass_ref[:, 0:model] + cross_ref[:, 0:model].astype(jnp.float32)
     out_ref[:, 0:model] = total.astype(jnp.bfloat16)
@@ -785,16 +792,19 @@
     out_ref[:, model:] = split_squares(squares)
 
 
-def finish_kernel(inner_total, hidden_ref, joined_ref, keep_ref, *refs):
-    got, out_ref = refs[:-1], refs[-1]
+def finish_kernel(inner_total, hidden_ref, joined_ref, keep_ref, passed_ref, *refs):
+    nears, out_ref = refs[:-1], refs[-1]
     model = hidden_ref.shape[1]
-    squares = keep_ref[:, model : model + 1]
-    total = keep_ref[:, 0:model]
-    for ref in got:
-        squares = squares + joined_squares(ref, model)
-        total = total + ref[:, 0:model].astype(jnp.float32)
-    scale = lax.rsqrt(squares / inner_total + EPSILON)
-    out_ref[...] = (hidden_ref[...].astype(jnp.float32) + scale * total).astype(jnp.bfloat16)
+    size = nears[0].shape[0]
+    for k, near_ref in enumerate(nears):
+        own = slice(k * size, (k + 1) * size)
+        squares = keep_ref[own, model : model + 1] + joined_squares(near_ref, model)
+        squares = squares + joined_squares(passed_ref.at[own], model)
+        scale = lax.rsqrt(squares / inner_total + EPSILON)
+        total = keep_ref[own, 0:model] + near_ref[:, 0:model].astype(jnp.float32)
+        total = total + passed_ref[own, 0:model].astype(jnp.float32)
+        hidden = hidden_ref[own, :].astype(jnp.float32)
+        out_ref[own, :] = (hidden + scale * total).astype(jnp.bfloat16)
 
 
 def join_kernel(keep_ref, *refs):
@@ -898,7 +908,6 @@
         cost_estimate=LITTLE,
     )(w_out, out_gain[None, :])
     out_part = exchange(half_out, "head", Z_NEAR)
-    out_near = exchange(out_part, "dp", 1)
 
     x_far = exchange(x_own, "dp", 2)
     first_most, first_raw = pl.pallas_call(
@@ -911,10 +920,10 @@
         compiler_params=kernel_params(8),
         cost_estimate=LITTLE,
     )(normed, first_own, first_near)
-    first_far, first_most, first_raw, meta, order, pen, x_own, gate_own = lax.optimization_barrier(
-        (first_far, first_most, first_raw, meta, order, pen, x_own, gate_own)
-    )
     x_near = exchange(x_own, "dp", 1)
+    first_far, first_most, first_raw, meta, order, pen, gate_own = lax.optimization_barrier(
+        (first_far, first_most, first_raw, meta, order, pen, gate_own)
+    )
     gate_near = exchange(gate_own, "dp", 1)
     first_last = exchange(first_far, "dp", 1)
     bc, step, prefix, fade, halo = pl.pallas_call(
@@ -951,10 +960,37 @@
         dt_bias,
         a_log,
     )
-    x_far, gate_own, bc, step, prefix, fade, halo = lax.optimization_barrier(
-        (x_far, gate_own, bc, step, prefix, fade, halo)
-    )
-    x_last = exchange(x_far, "dp", 1)
+    x_most = pl.pallas_call(
+        inner_most_kernel,
+        name="project_x_of_chip",
+        out_shape=shape((tok, inner), f32),
+        in_specs=in_vmem(3),
+        out_specs=in_vmem(1)[0],
+        compiler_params=kernel_params(8),
+        cost_estimate=LITTLE,
+    )(normed, x_own, x_near)
+    mixing = pl.pallas_call(
+        mixing_kernel,
+        name="mixing_weights",
+        out_shape=shape((blocks, heads, BLOCK, BLOCK), bf16),
+        in_specs=in_vmem(3),
+        out_specs=in_vmem(1)[0],
+        compiler_params=kernel_params(8),
+        cost_estimate=LITTLE,
+    )(bc, prefix, pen)
+    x_far, x_most, bc, step, prefix, fade, halo, mixing = lax.optimization_barrier(
+        (x_far, x_most, bc, step, prefix, fade, halo, mixing)
+    )
+    x_most, *x_halves = pl.pallas_call(
+        inner_far_kernel,
+        name="project_x_of_far_device",
+        out_shape=(shape((tok, inner), f32),) + (shape((rows // 2, inner), bf16),) * 2,
+        in_specs=in_vmem(3),
+        out_specs=tuple(in_vmem(3)),
+        compiler_params=kernel_params(8),
+        cost_estimate=LITTLE,
+    )(normed, x_most, x_far)
+    x_last = [exchange(part, "dp", 1) for part in x_halves]
     gate_far = exchange(gate_own, "dp", 2)
     x, stepx, faded, leaving = pl.pallas_call(
         inner_kernel,
@@ -965,21 +1001,18 @@
             shape((inner, tok), bf16),
             shape((inner, state_width), bf16),
         ),
-        in_specs=in_vmem(1) + [anywhere] * 4 + in_vmem(6),
+        in_specs=in_vmem(13),
         out_specs=tuple(in_vmem(4)),
-        scratch_shapes=[
-            pltpu.VMEM((model, inner), bf16),
-            pltpu.VMEM((TILE_ROWS + tok, inner), f32),
-            pltpu.SemaphoreType.DMA((peers,)),
-        ],
+        scratch_shapes=[pltpu.VMEM((TILE_ROWS + tok, inner), f32)],
         compiler_params=kernel_params(14),
         cost_estimate=LITTLE,
     )(
         normed,
+        x_most,
         x_own,
         x_near,
         x_far,
-        x_last,
+        *x_last,
         halo,
         conv_x,
         meta,
@@ -998,31 +1031,32 @@
         out_specs=in_vmem(1)[0],
         compiler_params=kernel_params(14),
         cost_estimate=LITTLE,
-    )(x, bc, stepx, prefix, meta, pen, skip_gain)
+    )(x, bc, stepx, prefix, meta, mixing, skip_gain)
     gate_far, gate_near, entering, y_local = lax.optimization_barrier(
         (gate_far, gate_near, entering, y_local)
     )
     gate_last = exchange(gate_far, "dp", 1)
+    gate_most, *out_halves = pl.pallas_call(
+        z_most_kernel,
+        name="project_gate_most",
+        out_shape=(shape((tok, inner), f32),) + (shape((inner // 2, model // 2), bf16),) * 2,
+        in_specs=in_vmem(5),
+        out_specs=tuple(in_vmem(3)),
+        compiler_params=kernel_params(8),
+        cost_estimate=LITTLE,
+    )(normed, gate_own, gate_near, gate_far, out_part)
+    out_near = [exchange(part, "dp", 1) for part in out_halves]
     tables = pl.pallas_call(
         table_kernel,
         name="sum_ended_states",
         out_shape=(shape((PROMPTS, inner // 4, state_width), bf16),) * 4,
-        in_specs=[smem] + in_vmem(5),
+        in_specs=[smem] + in_vmem(5) + [anywhere] * 2,
         out_specs=tuple(in_vmem(4)),
         compiler_params=kernel_params(8),
         cost_estimate=LITTLE,
-    )(token_prompt, bc, faded, meta, prefix, entering)
+    )(token_prompt, bc, faded, meta, prefix, entering, *out_near)
     tables_near = [exchange(table, "dp", 1) for table in tables]
 
-    gate_most = pl.pallas_call(
-        z_most_kernel,
-        name="project_gate_most",
-        out_shape=shape((tok, inner), f32),
-        in_specs=in_vmem(4),
-        out_specs=in_vmem(1)[0],
-        compiler_params=kernel_params(8),
-        cost_estimate=LITTLE,
-    )(normed, gate_own, gate_near, gate_far)
     gate = pl.pallas_call(
         z_last_kernel,
         name="project_gate_last",
@@ -1038,12 +1072,12 @@
         gate_kernel,
         name="add_entering_and_gate",
         out_shape=(shape((2 * out_rows, inner), bf16),) * 4,
-        in_specs=in_vmem(6) + [anywhere],
+        in_specs=in_vmem(6),
         out_specs=tuple(in_vmem(4)),
         scratch_shapes=[pltpu.VMEM((tok, inner), bf16)],
         compiler_params=kernel_params(8),
         cost_estimate=LITTLE,
-    )(entering, bc, prefix, meta, y_local, gate, out_near)
+    )(entering, bc, prefix, meta, y_local, gate)
     got_first = exchange(sent_first, "head", Z_NEAR)
     got_rest = exchange(sent_rest, "head", Z_NEAR)
 
@@ -1064,31 +1098,35 @@
     fars = [exchange(send, "dp", 2) for send in sends]
 
     sums_shape = (out_rows, model + LANES)
-    project = pl.pallas_call(
-        out_kernel,
-        name="project_out",
-        out_shape=(shape(sums_shape, f32), shape(sums_shape, bf16)),
-        in_specs=in_vmem(5),
-        out_specs=tuple(in_vmem(2)),
-        scratch_shapes=[pltpu.VMEM((2 * out_rows, model), f32)],
-        compiler_params=kernel_params(8),
-        cost_estimate=LITTLE,
-    )
-    sums_pass, sums_cross = project(kept_first, got_first, scaled_out, out_part, out_near)
-    sums_keep, sums_near = project(kept_rest, got_rest, scaled_out, out_part, out_near)
+
+    def project(kept, got, pieces):
+        piece = (out_rows // pieces, model + LANES)
+        return pl.pallas_call(
+            out_kernel,
+            name="project_out",
+            out_shape=(shape(sums_shape, f32),) + (shape(piece, bf16),) * pieces,
+            in_specs=in_vmem(6),
+            out_specs=tuple(in_vmem(1 + pieces)),
+            scratch_shapes=[pltpu.VMEM((2 * out_rows, model), f32)],
+            compiler_params=kernel_params(8),
+            cost_estimate=LITTLE,
+        )(kept, got, scaled_out, out_part, *out_near)
+
+    sums_pass, sums_cross = project(kept_first, got_first, 1)
     cross = exchange(sums_cross, "head", Y_NEAR)
-    cross, sums_near = lax.optimization_barrier((cross, sums_near))
-    sums_near = exchange(sums_near, "head", Y_NEAR)
     passed = pl.pallas_call(
         pass_kernel,
         name="add_sums_to_pass_on",
         out_shape=shape(sums_shape, bf16),
-        in_specs=in_vmem(2),
+        in_specs=in_vmem(2) + [anywhere],
         out_specs=in_vmem(1)[0],
         compiler_params=kernel_params(4),
         cost_estimate=LITTLE,
-    )(sums_pass, cross)
+    )(sums_pass, cross, got_rest)
+    got_rest, passed = lax.optimization_barrier((got_rest, passed))
     passed = exchange(passed, "head", Z_FAR)
+    sums_keep, *sums_near = project(kept_rest, got_rest, 2)
+    sums_near = [exchange(part, "head", Y_NEAR) for part in sums_near]
     request_states, joined = pl.pallas_call(
         join_kernel,
         name="join_request_states",
@@ -1102,11 +1140,11 @@
         functools.partial(finish_kernel, inner * head_count),
         name="scale_and_add_hidden",
         out_shape=shape((out_rows, model), bf16),
-        in_specs=in_vmem(1) + [anywhere] + in_vmem(3),
+        in_specs=in_vmem(1) + [anywhere] + in_vmem(4),
         out_specs=in_vmem(1)[0],
         compiler_params=kernel_params(4),
         cost_estimate=LITTLE,
-    )(own_hidden, joined, sums_keep, sums_near, passed)
+    )(own_hidden, joined, sums_keep, passed, *sums_near)
     return (
         layer_out,
         request_states.reshape(requests, heads, inner // heads, state_width),

time: 56.4 us -> 56.7 us (level)
  waiting for transfers between devices: 11.2 us -> 6.51 us
  starting transfers between devices: 24.6 us -> 28.9 us
  Pallas kernels: 19.4 us -> 20 us
    ppermute x22 -> x25, waiting for transfers between devices: 11.2 us -> 6.51 us  [exchange(): lax.ppermute(values, axis, [(i, i ^ bits) for i in range(lax.axis_size(ax...]
    ppermute x22 -> x25, starting transfers between devices: 22.2 us -> 26.5 us  [exchange(): lax.ppermute(values, axis, [(i, i ^ bits) for i in range(lax.axis_size(ax...]
    pallas_call x3 -> x6, Pallas kernels: 2.14 us -> 3.88 us  [the longest x2 1.25 us: project(): pl.pallas_call(out_kernel, name='project_out', out_shape=(shape(sums_shap...]
  transfers between devices with their start and end apart: 23 -> 26, of which waited for: 9 -> 6; matrix products, arithmetic and copies ran while one was open for 0% -> 0% of each run, Pallas kernels for 28% -> 30%
where the time goes in v6:
time: 56.7 us; the launch traced here: 56.6 us
  starting transfers between devices  28.9 us (51%)
  Pallas kernels  20 us (35%)
  waiting for transfers between devices  6.51 us (11%)
  between operations  1.02 us (2%)
    ppermute x25, starting transfers between devices, exchange(): lax.ppermute(values, axis, [(i, i ^ bits) for i in range(lax.axis_size(ax...  26.5 us
    ppermute x25, waiting for transfers between devices, exchange(): lax.ppermute(values, axis, [(i, i ^ bits) for i in range(lax.axis_size(ax...  6.51 us
    ppermute x1, starting transfers between devices, fused_on_device(): lax.ppermute(leaving, 'dp', [(i, i + 1) for i in range(peers - 1)])  2.39 us
    pallas_call x1, Pallas kernels, fused_on_device(): pl.pallas_call(first_kernel, name='project_b_c_and_steps', out_shape=(sha...  2.3 us
    pallas_call x1, Pallas kernels, fused_on_device(): pl.pallas_call(inner_kernel, name='project_and_convolve_x', out_shape=(sh...  2.11 us
    pallas_call x1, Pallas kernels, fused_on_device(): pl.pallas_call(pack_first_kernel, name='pack_first_weights', out_shape=sh...  1.95 us
    pallas_call x1, Pallas kernels, fused_on_device(): pl.pallas_call(local_kernel, name='mix_within_blocks', out_shape=shape((t...  1.61 us
    pallas_call x1, Pallas kernels, fused_on_device(): pl.pallas_call(table_kernel, name='sum_ended_states', out_shape=(shape((P...  1.39 us
  transfers between devices with their start and end apart: 26, of which 6 were waited for; matrix products, arithmetic and copies ran while one was open for 0% of the time, Pallas kernels for 30%

profile of v6, /device:TPU:0, one launch (start us, length us, event | category | flops | bytes accessed | tf_op | source)
XLA Modules:
  0.0 56.6 jit_solution(7080795449957544543)
XLA Ops:
  0.7 2.0 %pack_first_weights.1.own_ref = bf16[480,256]{1,0:T(8,128)(2,1)} custom-call(s32[1,4]{1,0:T(1,128)} %bitcast.5, f32[384,256]{1,0:T(8,128)} %wbc_ref.1, f32[6,384]{1,0:T(8,128)} %bitcast.6, bf16[512,1536]{1,0:T(8,128)(2,1)} %hidden_ref.1), custom_call_target="tpu_custom_call" | custom-call | flops 1000 | bytes 1000 | tf_op jit(solution)/shard_map/pack_first_weights/pallas_call | solution.py:851
  3.2 2.6 %collective-permute-start = (bf16[480,256]{1,0:T(8,128)(2,1)}, bf16[480,256]{1,0:T(8,128)(2,1)S(1)}, u32[]{:S(2)}, u32[]{:S(2)}) collective-permute-start(bf16[480,256]{1,0:T(8,128)(2,1)} %pack_first_weights.1.own_ref), channel_id=1, source_target_pairs={{0,16},{8,24},{16,0},{24,8},{1,17},{9,25},{17,1},{25,9},{2,18},{10... | collective-permute-start | bytes 737288 | tf_op jit(solution)/shard_map/ppermute | solution.py:275
  7.0 1.6 %collective-permute-start.10 = (bf16[384,768]{1,0:T(8,128)(2,1)S(1)}, bf16[384,768]{1,0:T(8,128)(2,1)S(1)}, u32[]{:S(2)}, u32[]{:S(2)}) collective-permute-start(bf16[384,768]{1,0:T(8,128)(2,1)S(1)} %get-tuple-element.106), channel_id=1, source_target_pairs={{0,2},{1,3},{2,0},{3,1},{4,6},{5,7},{6,4},{7,5},{8,10},{9,11},{10,... | collective-permute-start | bytes 1769480 | tf_op jit(solution)/shard_map/ppermute | solution.py:275
  9.2 1.2 %norm_and_token_facts.1 = (bf16[512,1536]{1,0:T(8,128)(2,1)S(1)}, f32[512,128]{1,0:T(8,128)S(1)}, bf16[1024,512]{1,0:T(8,128)(2,1)S(1)}, f32[2,256,256]{2,1,0:T(8,128)S(1)}, bf16[64,1536]{1,0:T(8,128)(2,1)S(1)}) custom-call(s32[1,2048]{1,0:T(1,128)S(1)} %bitcast.4, bf16[512,1536]{1,0:T(8,128)(2,1)S(1)} %copy-done, f32[1,1536]{1,0:T(1,128)S(1)} %broadcast_in_dim.14.gain_ref), custom_call_target="tpu_custom_call" | custom-call | flops 1000 | bytes 1000 | tf_op jit(solution)/shard_map/norm_and_token_facts/pallas_call | solution.py:885
  10.5 0.6 %project_b_c_and_steps_of_chip.1 = (f32[512,256]{1,0:T(8,128)S(1)}, f32[512,128]{1,0:T(8,128)S(1)}) custom-call(bf16[512,1536]{1,0:T(8,128)(2,1)S(1)} %get-tuple-element.68.normed_ref, bf16[480,256]{1,0:T(8,128)(2,1)S(1)} %copy-done.1, bf16[480,256]{1,0:T(8,128)(2,1)S(1)} %collective-permute-done.1.near_ref), custom_call_target="tpu_custom_call" | custom-call | flops 1000 | bytes 1000 | tf_op jit(solution)/shard_map/project_b_c_and_steps_of_chip/pallas_call | solution.py:913
  11.2 1.6 %collective-permute-done.far_ref = bf16[480,256]{1,0:T(8,128)(2,1)S(1)} collective-permute-done((bf16[480,256]{1,0:T(8,128)(2,1)}, bf16[480,256]{1,0:T(8,128)(2,1)S(1)}, u32[]{:S(2)}, u32[]{:S(2)}) %collective-permute-start) | collective-permute-done | bytes 245792 | tf_op jit(solution)/shard_map/ppermute | solution.py:275
  12.8 1.9 %collective-permute-start.7 = (bf16[384,384]{1,0:T(8,128)(2,1)S(1)}, bf16[384,384]{1,0:T(8,128)(2,1)S(1)}, u32[]{:S(2)}, u32[]{:S(2)}) collective-permute-start(bf16[384,384]{1,0:T(8,128)(2,1)S(1)} %get-tuple-element.98.own_ref), channel_id=1, source_target_pairs={{0,16},{8,24},{16,0},{24,8},{1,17},{9,25},{17,1},{25,9},{2,18},{10... | collective-permute-start | bytes 884744 | tf_op jit(solution)/shard_map/ppermute | solution.py:275
  14.9 0.6 %project_x_of_chip.1.most_ref = f32[512,384]{1,0:T(8,128)S(1)} custom-call(bf16[512,1536]{1,0:T(8,128)(2,1)S(1)} %get-tuple-element.68.normed_ref, bf16[384,384]{1,0:T(8,128)(2,1)S(1)} %get-tuple-element.76.own_ref, bf16[384,384]{1,0:T(8,128)(2,1)S(1)} %collective-permute-done.3.near_ref), custom_call_target="tpu_custom_call" | custom-call | flops 1000 | bytes 1000 | tf_op jit(solution)/shard_map/project_x_of_chip/pallas_call | solution.py:963
  15.6 2.3 %project_b_c_and_steps.1 = (bf16[512,256]{1,0:T(8,128)(2,1)S(1)}, f32[512,128]{1,0:T(8,128)S(1)}, f32[512,128]{1,0:T(8,128)S(1)}, f32[512,128]{1,0:T(8,128)S(1)}, bf16[16,1536]{1,0:T(8,128)(2,1)S(1)}) custom-call(bf16[512,1536]{1,0:T(8,128)(2,1)S(1)} %get-tuple-element.68.normed_ref, f32[512,256]{1,0:T(8,128)S(1)} %get-tuple-element.77.most_ref, ...), custom_call_target="tpu_custom_call" | custom-call | flops 1000 | bytes 1000 | tf_op jit(solution)/shard_map/project_b_c_and_steps/pallas_call | solution.py:929
  17.9 0.7 %mixing_weights.1.mixing_ref = bf16[2,6,256,256]{3,2,1,0:T(8,128)(2,1)S(1)} custom-call(bf16[512,256]{1,0:T(8,128)(2,1)S(1)} %get-tuple-element.87.bc_ref, f32[512,128]{1,0:T(8,128)S(1)} %get-tuple-element.97.prefix_ref, f32[2,256,256]{2,1,0:T(8,128)S(1)} %get-tuple-element.86.pen_ref), custom_call_target="tpu_custom_call" | custom-call | flops 1000 | bytes 1000 | tf_op jit(solution)/shard_map/mixing_weights/pallas_call | solution.py:972
  20.1 0.9 %collective-permute-done.5.last_first_ref = bf16[192,384]{1,0:T(8,128)(2,1)S(1)} collective-permute-done((bf16[192,384]{1,0:T(8,128)(2,1)S(1)}, bf16[192,384]{1,0:T(8,128)(2,1)S(1)}, u32[]{:S(2)}, u32[]{:S(2)}) %collective-permute-start.5) | collective-permute-done | bytes 147488 | tf_op jit(solution)/shard_map/ppermute | solution.py:275
  21.2 2.1 %project_and_convolve_x.1 = (bf16[512,384]{1,0:T(8,128)(2,1)S(1)}, bf16[512,384]{1,0:T(8,128)(2,1)S(1)}, bf16[384,512]{1,0:T(8,128)(2,1)S(1)}, bf16[384,128]{1,0:T(8,128)(2,1)S(1)}) custom-call(bf16[512,1536]{1,0:T(8,128)(2,1)S(1)} %get-tuple-element.68.normed_ref, f32[512,384]{1,0:T(8,128)S(1)} %get-tuple-element.90.most_ref, ...), custom_call_target="tpu_custom_call" | custom-call | flops 1000 | bytes 1000 | tf_op jit(solution)/shard_map/project_and_convolve_x/pallas_call | solution.py:995
  23.3 2.4 %collective-permute-start.9 = (bf16[384,128]{1,0:T(8,128)(2,1)S(1)}, bf16[384,128]{1,0:T(8,128)(2,1)S(1)}, u32[]{:S(2)}, u32[]{:S(2)}) collective-permute-start(bf16[384,128]{1,0:T(8,128)(2,1)S(1)} %get-tuple-element.99), channel_id=1, source_target_pairs={{0,8},{8,16},{16,24},{1,9},{9,17},{17,25},{2,10},{10,18},{18,26},{... | collective-permute-start | bytes 294920 | tf_op jit(solution)/shard_map/ppermute | solution.py:1024
  25.7 1.6 %mix_within_blocks.1.y_ref = f32[512,384]{1,0:T(8,128)S(1)} custom-call(bf16[512,384]{1,0:T(8,128)(2,1)S(1)} %get-tuple-element.100.x_ref, bf16[512,256]{1,0:T(8,128)(2,1)S(1)} %get-tuple-element.87.bc_ref, bf16[512,384]{1,0:T(8,128)(2,1)S(1)} %get-tuple-element.101.stepx_ref, f32[512,128]{1,0:T(8,128)S(1)} %get-tuple-element.97.prefix_ref, ...), custom_call_target="tpu_custom_call" | custom-call | flops 1000 | bytes 1000 | tf_op jit(solution)/shard_map/mix_within_blocks/pallas_call | solution.py:1026
  27.3 1.8 %collective-permute-start.19 = (bf16[384,384]{1,0:T(8,128)(2,1)S(1)}, bf16[384,384]{1,0:T(8,128)(2,1)S(1)}, u32[]{:S(2)}, u32[]{:S(2)}) collective-permute-start(bf16[384,384]{1,0:T(8,128)(2,1)S(1)} %collective-permute-done.7.far_ref), channel_id=1, source_target_pairs={{0,8},{8,0},{16,24},{24,16},{1,9},{9,1},{17,25},{25,17},{2,10},{10... | collective-permute-start | bytes 884744 | tf_op jit(solution)/shard_map/ppermute | solution.py:275
  29.2 0.9 %project_gate_most.1 = (f32[512,384]{1,0:T(8,128)S(1)}, bf16[192,768]{1,0:T(8,128)(2,1)S(1)}, bf16[192,768]{1,0:T(8,128)(2,1)S(1)}) custom-call(bf16[512,1536]{1,0:T(8,128)(2,1)S(1)} %get-tuple-element.68.normed_ref, bf16[384,384]{1,0:T(8,128)(2,1)S(1)} %get-tuple-element.98.own_ref, bf16[384,384]{1,0:T(8,128)(2,1)S(1)} %collective-permute-done.8.near_ref, ...), custom_call_target="tpu_custom_call" | custom-call | flops 1000 | bytes 1000 | tf_op jit(solution)/shard_map/project_gate_most/pallas_call | solution.py:1039
  31.1 0.6 %add_entering_and_gate.1 = (bf16[128,384]{1,0:T(8,128)(2,1)S(1)}, bf16[128,384]{1,0:T(8,128)(2,1)S(1)}, bf16[128,384]{1,0:T(8,128)(2,1)S(1)}, bf16[128,384]{1,0:T(8,128)(2,1)S(1)}) custom-call(bf16[384,128]{1,0:T(8,128)(2,1)S(1)} %collective-permute-done.9.enter_ref, bf16[512,256]{1,0:T(8,128)(2,1)S(1)} %get-tuple-element.87.bc_ref, ...), custom_call_target="tpu_custom_call" | custom-call | flops 1000 | bytes 1000 | tf_op jit(solution)/shard_map/add_entering_and_gate/pallas_call | solution.py:1071
  31.7 1.6 %collective-permute-start.21 = (bf16[128,384]{1,0:T(8,128)(2,1)S(1)}, bf16[128,384]{1,0:T(8,128)(2,1)S(1)}, u32[]{:S(2)}, u32[]{:S(2)}) collective-permute-start(bf16[128,384]{1,0:T(8,128)(2,1)S(1)} %get-tuple-element.122), channel_id=1, source_target_pairs={{0,2},{1,3},{2,0},{3,1},{4,6},{5,7},{6,4},{7,5},{8,10},{9,11},{10,... | collective-permute-start | bytes 294920 | tf_op jit(solution)/shard_map/ppermute | solution.py:275
  33.4 1.4 %sum_ended_states.1 = (bf16[8,96,128]{2,1,0:T(8,128)(2,1)S(1)}, bf16[8,96,128]{2,1,0:T(8,128)(2,1)S(1)}, bf16[8,96,128]{2,1,0:T(8,128)(2,1)S(1)}, bf16[8,96,128]{2,1,0:T(8,128)(2,1)S(1)}) custom-call(s32[2048]{0:T(1024)S(1)} %copy-done.4, bf16[512,256]{1,0:T(8,128)(2,1)S(1)} %get-tuple-element.87.bc_ref, bf16[384,512]{1,0:T(8,128)(2,1)S(1)} %get-tuple-element.96.faded_ref, ...), custom_call_target="tpu_custom_call" | custom-call | flops 1000 | bytes 1000 | tf_op jit(solution)/shard_map/sum_ended_states/pallas_call | solution.py:1049
  35.9 0.7 %collective-permute-done.21.got_ref = bf16[128,384]{1,0:T(8,128)(2,1)S(1)} collective-permute-done((bf16[128,384]{1,0:T(8,128)(2,1)S(1)}, bf16[128,384]{1,0:T(8,128)(2,1)S(1)}, u32[]{:S(2)}, u32[]{:S(2)}) %collective-permute-start.21) | collective-permute-done | bytes 98336 | tf_op jit(solution)/shard_map/ppermute | solution.py:275
  36.6 0.6 %project_out.2 = (f32[64,1664]{1,0:T(8,128)S(1)}, bf16[64,1664]{1,0:T(8,128)(2,1)S(1)}) custom-call(bf16[128,384]{1,0:T(8,128)(2,1)S(1)} %get-tuple-element.121.kept_ref, bf16[128,384]{1,0:T(8,128)(2,1)S(1)} %collective-permute-done.21.got_ref, bf16[384,1536]{1,0:T(8,128)(2,1)S(1)} %get-tuple-element.123.own_ref, ...), custom_call_target="tpu_custom_call" | custom-call | flops 1000 | bytes 1000 | tf_op jit(solution)/shard_map/project_out/pallas_call | solution.py:1104
  37.2 1.6 %collective-permute-start.22 = (bf16[64,1664]{1,0:T(8,128)(2,1)S(1)}, bf16[64,1664]{1,0:T(8,128)(2,1)S(1)}, u32[]{:S(2)}, u32[]{:S(2)}) collective-permute-start(bf16[64,1664]{1,0:T(8,128)(2,1)S(1)} %get-tuple-element.125), channel_id=1, source_target_pairs={{0,1},{1,0},{2,3},{3,2},{4,5},{5,4},{6,7},{7,6},{8,9},{9,8},{10,11... | collective-permute-start | bytes 638984 | tf_op jit(solution)/shard_map/ppermute | solution.py:275
  38.8 1.6 %collective-permute-start.20 = (bf16[128,384]{1,0:T(8,128)(2,1)S(1)}, bf16[128,384]{1,0:T(8,128)(2,1)S(1)}, u32[]{:S(2)}, u32[]{:S(2)}) collective-permute-start(bf16[128,384]{1,0:T(8,128)(2,1)S(1)} %get-tuple-element.120), channel_id=1, source_target_pairs={{0,2},{1,3},{2,0},{3,1},{4,6},{5,7},{6,4},{7,5},{8,10},{9,11},{10,... | collective-permute-start | bytes 294920 | tf_op jit(solution)/shard_map/ppermute | solution.py:275
  40.4 0.9 %pick_request_states.1 = (bf16[4,384,128]{2,1,0:T(8,128)(2,1)S(1)}, bf16[4,288,128]{2,1,0:T(8,128)(2,1)S(1)}, bf16[4,96,128]{2,1,0:T(8,128)(2,1)S(1)}) custom-call(s32[4]{0:T(128)S(1)} %copy-done.7, bf16[480,256]{1,0:T(8,128)(2,1)S(1)} %collective-permute-done.far_ref, bf16[8,96,128]{2,1,0:T(8,128)(2,1)S(1)} %get-tuple-element.109.refs_0_, ...), custom_call_target="tpu_custom_call" | custom-call | flops 1000 | bytes 1000 | tf_op jit(solution)/shard_map/pick_request_states/pallas_call | solution.py:1086
  41.3 2.5 %collective-permute-start.17 = (bf16[4,288,128]{2,1,0:T(8,128)(2,1)S(1)}, bf16[4,288,128]{2,1,0:T(8,128)(2,1)S(1)}, u32[]{:S(2)}, u32[]{:S(2)}) collective-permute-start(bf16[4,288,128]{2,1,0:T(8,128)(2,1)S(1)} %get-tuple-element.114), channel_id=1, source_target_pairs={{0,16},{8,24},{16,0},{24,8},{1,17},{9,25},{17,1},{25,9},{2,18},{10... | collective-permute-start | bytes 884744 | tf_op jit(solution)/shard_map/ppermute | solution.py:275
  44.0 2.7 %collective-permute-start.23 = (bf16[64,1664]{1,0:T(8,128)(2,1)S(1)}, bf16[64,1664]{1,0:T(8,128)(2,1)S(1)}, u32[]{:S(2)}, u32[]{:S(2)}) collective-permute-start(bf16[64,1664]{1,0:T(8,128)(2,1)S(1)} %add_sums_to_pass_on.1), channel_id=1, source_target_pairs={{0,4},{1,5},{2,6},{3,7},{4,0},{5,1},{6,2},{7,3},{8,12},{9,13},{10,... | collective-permute-start | bytes 638984 | tf_op jit(solution)/shard_map/ppermute | solution.py:275
  46.6 0.6 %project_out.3 = (f32[64,1664]{1,0:T(8,128)S(1)}, bf16[32,1664]{1,0:T(8,128)(2,1)S(1)}, bf16[32,1664]{1,0:T(8,128)(2,1)S(1)}) custom-call(bf16[128,384]{1,0:T(8,128)(2,1)S(1)} %get-tuple-element.119.kept_ref, bf16[128,384]{1,0:T(8,128)(2,1)S(1)} %collective-permute-done.20.arrived_ref.got_ref, bf16[384,1536]{1,0:T(8,128)(2,1)S(1)} %get-tuple-element.123.own_ref, ...), custom_call_target="tpu_custom_call" | custom-call | flops 1000 | bytes 1000 | tf_op jit(solution)/shard_map/project_out/pallas_call | solution.py:1104
  47.3 1.6 %collective-permute-start.24 = (bf16[32,1664]{1,0:T(8,128)(2,1)S(1)}, bf16[32,1664]{1,0:T(8,128)(2,1)S(1)}, u32[]{:S(2)}, u32[]{:S(2)}) collective-permute-start(bf16[32,1664]{1,0:T(8,128)(2,1)S(1)} %get-tuple-element.129), channel_id=1, source_target_pairs={{0,1},{1,0},{2,3},{3,2},{4,5},{5,4},{6,7},{7,6},{8,9},{9,8},{10,11... | collective-permute-start | bytes 319496 | tf_op jit(solution)/shard_map/ppermute | solution.py:275
  49.4 2.7 %collective-permute-start.18 = (bf16[4,96,128]{2,1,0:T(8,128)(2,1)S(1)}, bf16[4,96,128]{2,1,0:T(8,128)(2,1)S(1)}, u32[]{:S(2)}, u32[]{:S(2)}) collective-permute-start(bf16[4,96,128]{2,1,0:T(8,128)(2,1)S(1)} %get-tuple-element.115), channel_id=1, source_target_pairs={{0,16},{8,24},{16,0},{24,8},{1,17},{9,25},{17,1},{25,9},{2,18},{10... | collective-permute-start | bytes 294920 | tf_op jit(solution)/shard_map/ppermute | solution.py:275
  52.1 2.6 %collective-permute-done.18.refs_1_ = bf16[4,96,128]{2,1,0:T(8,128)(2,1)S(1)} collective-permute-done((bf16[4,96,128]{2,1,0:T(8,128)(2,1)S(1)}, bf16[4,96,128]{2,1,0:T(8,128)(2,1)S(1)}, u32[]{:S(2)}, u32[]{:S(2)}) %collective-permute-start.18) | collective-permute-done | bytes 98336 | tf_op jit(solution)/shard_map/ppermute | solution.py:275
  54.7 1.0 %join_request_states.1 = (f32[4,384,128]{2,1,0:T(8,128)}, f32[8,128]{1,0:T(8,128)S(1)}) custom-call(bf16[4,384,128]{2,1,0:T(8,128)(2,1)S(1)} %get-tuple-element.113.keep_ref, bf16[4,288,128]{2,1,0:T(8,128)(2,1)S(1)} %collective-permute-done.17.refs_0_, bf16[4,96,128]{2,1,0:T(8,128)(2,1)S(1)} %collective-permute-done.18.refs_1_), custom_call_target="tpu_custom_call" | custom-call | flops 1000 | bytes 1000 | tf_op jit(solution)/shard_map/join_request_states/pallas_call | solution.py:1130
  55.7 0.9 %scale_and_add_hidden.1 = bf16[64,1536]{1,0:T(8,128)(2,1)} custom-call(bf16[64,1536]{1,0:T(8,128)(2,1)S(1)} %get-tuple-element.67.hidden_ref, f32[8,128]{1,0:T(8,128)S(1)} %get-tuple-element.116.joined_ref, f32[64,1664]{1,0:T(8,128)S(1)} %get-tuple-element.127.keep_ref, bf16[64,1664]{1,0:T(8,128)(2,1)S(1)} %collective-permute-done.23.passed_ref, ...), custom_call_target="tpu_custom_call" | custom-call | flops 1000 | bytes 1000 | tf_op jit(solution)/shard_map/scale_and_add_hidden/pallas_call | solution.py:1139
  (69 shorter events, 7.1 us)
Async XLA Ops:
  0.6 5.9 %copy-start.12 = (f32[384]{0:T(512)S(1)}, f32[384]{0:T(512)}, u32[]{:S(2)}) copy-start(f32[384]{0:T(512)} %param.26) | copy-start | bytes 4612
  0.7 5.9 %copy-start.3 = (bf16[384,1536]{1,0:T(8,128)(2,1)S(1)}, bf16[384,1536]{1,0:T(8,128)(2,1)}, u32[]{:S(2)}) copy-start(bf16[384,1536]{1,0:T(8,128)(2,1)} %w_ref.1) | copy-start | bytes 3538948
  2.6 6.6 %copy-start.11 = (f32[1536]{0:T(1024)S(1)}, f32[1536]{0:T(1024)}, u32[]{:S(2)}) copy-start(f32[1536]{0:T(1024)} %param.17) | copy-start | bytes 18436
  2.6 6.6 %copy-start = (bf16[512,1536]{1,0:T(8,128)(2,1)S(1)}, bf16[512,1536]{1,0:T(8,128)(2,1)}, u32[]{:S(2)}) copy-start(bf16[512,1536]{1,0:T(8,128)(2,1)} %hidden_ref.1) | copy-start | bytes 4718596
  2.6 6.6 %copy-start.4 = (s32[2048]{0:T(1024)S(1)}, s32[2048]{0:T(1024)}, u32[]{:S(2)}) copy-start(s32[2048]{0:T(1024)} %ids_ref.1) | copy-start | bytes 24580
  2.7 7.8 %collective-permute-start.1 = (bf16[480,256]{1,0:T(8,128)(2,1)}, bf16[480,256]{1,0:T(8,128)(2,1)S(1)}, u32[]{:S(2)}, u32[]{:S(2)}) collective-permute-start(bf16[480,256]{1,0:T(8,128)(2,1)} %pack_first_weights.1.own_ref), channel_id=1, source_target_pairs={{0,8},{8,0},{16,24},{24,16},{1,9},{9,1},{17,25},{25,17},{2,10},{10... | collective-permute-start | bytes 737288 | tf_op jit(solution)/shard_map/ppermute | solution.py:275
  3.2 9.6 %collective-permute-start = (bf16[480,256]{1,0:T(8,128)(2,1)}, bf16[480,256]{1,0:T(8,128)(2,1)S(1)}, u32[]{:S(2)}, u32[]{:S(2)}) collective-permute-start(bf16[480,256]{1,0:T(8,128)(2,1)} %pack_first_weights.1.own_ref), channel_id=1, source_target_pairs={{0,16},{8,24},{16,0},{24,8},{1,17},{9,25},{17,1},{25,9},{2,18},{10... | collective-permute-start | bytes 737288 | tf_op jit(solution)/shard_map/ppermute | solution.py:275
  6.3 8.4 %collective-permute-start.3 = (bf16[384,384]{1,0:T(8,128)(2,1)S(1)}, bf16[384,384]{1,0:T(8,128)(2,1)S(1)}, u32[]{:S(2)}, u32[]{:S(2)}) collective-permute-start(bf16[384,384]{1,0:T(8,128)(2,1)S(1)} %get-tuple-element.76.own_ref), channel_id=1, source_target_pairs={{0,8},{8,0},{16,24},{24,16},{1,9},{9,1},{17,25},{25,17},{2,10},{10... | collective-permute-start | bytes 884744 | tf_op jit(solution)/shard_map/ppermute | solution.py:275
  7.0 22.1 %collective-permute-start.10 = (bf16[384,768]{1,0:T(8,128)(2,1)S(1)}, bf16[384,768]{1,0:T(8,128)(2,1)S(1)}, u32[]{:S(2)}, u32[]{:S(2)}) collective-permute-start(bf16[384,768]{1,0:T(8,128)(2,1)S(1)} %get-tuple-element.106), channel_id=1, source_target_pairs={{0,2},{1,3},{2,0},{3,1},{4,6},{5,7},{6,4},{7,5},{8,10},{9,11},{10,... | collective-permute-start | bytes 1769480 | tf_op jit(solution)/shard_map/ppermute | solution.py:275
  8.6 10.4 %collective-permute-start.2 = (bf16[384,384]{1,0:T(8,128)(2,1)S(1)}, bf16[384,384]{1,0:T(8,128)(2,1)S(1)}, u32[]{:S(2)}, u32[]{:S(2)}) collective-permute-start(bf16[384,384]{1,0:T(8,128)(2,1)S(1)} %get-tuple-element.76.own_ref), channel_id=1, source_target_pairs={{0,16},{8,24},{16,0},{24,8},{1,17},{9,25},{17,1},{25,9},{2,18},{10... | collective-permute-start | bytes 884744 | tf_op jit(solution)/shard_map/ppermute | solution.py:275
  12.8 2.8 %collective-permute-start.4 = (bf16[480,256]{1,0:T(8,128)(2,1)S(1)}, bf16[480,256]{1,0:T(8,128)(2,1)S(1)}, u32[]{:S(2)}, u32[]{:S(2)}) collective-permute-start(bf16[480,256]{1,0:T(8,128)(2,1)S(1)} %collective-permute-done.far_ref), channel_id=1, source_target_pairs={{0,8},{8,0},{16,24},{24,16},{1,9},{9,1},{17,25},{25,17},{2,10},{10... | collective-permute-start | bytes 737288 | tf_op jit(solution)/shard_map/ppermute | solution.py:275
  12.8 14.5 %collective-permute-start.7 = (bf16[384,384]{1,0:T(8,128)(2,1)S(1)}, bf16[384,384]{1,0:T(8,128)(2,1)S(1)}, u32[]{:S(2)}, u32[]{:S(2)}) collective-permute-start(bf16[384,384]{1,0:T(8,128)(2,1)S(1)} %get-tuple-element.98.own_ref), channel_id=1, source_target_pairs={{0,16},{8,24},{16,0},{24,8},{1,17},{9,25},{17,1},{25,9},{2,18},{10... | collective-permute-start | bytes 884744 | tf_op jit(solution)/shard_map/ppermute | solution.py:275
  14.7 12.6 %collective-permute-start.8 = (bf16[384,384]{1,0:T(8,128)(2,1)S(1)}, bf16[384,384]{1,0:T(8,128)(2,1)S(1)}, u32[]{:S(2)}, u32[]{:S(2)}) collective-permute-start(bf16[384,384]{1,0:T(8,128)(2,1)S(1)} %get-tuple-element.98.own_ref), channel_id=1, source_target_pairs={{0,8},{8,0},{16,24},{24,16},{1,9},{9,1},{17,25},{25,17},{2,10},{10... | collective-permute-start | bytes 884744 | tf_op jit(solution)/shard_map/ppermute | solution.py:275
  19.5 1.4 %collective-permute-start.5 = (bf16[192,384]{1,0:T(8,128)(2,1)S(1)}, bf16[192,384]{1,0:T(8,128)(2,1)S(1)}, u32[]{:S(2)}, u32[]{:S(2)}) collective-permute-start(bf16[192,384]{1,0:T(8,128)(2,1)S(1)} %get-tuple-element.91), channel_id=1, source_target_pairs={{0,8},{8,0},{16,24},{24,16},{1,9},{9,1},{17,25},{25,17},{2,10},{10... | collective-permute-start | bytes 442376 | tf_op jit(solution)/shard_map/ppermute | solution.py:275
  19.6 1.6 %collective-permute-start.6 = (bf16[192,384]{1,0:T(8,128)(2,1)S(1)}, bf16[192,384]{1,0:T(8,128)(2,1)S(1)}, u32[]{:S(2)}, u32[]{:S(2)}) collective-permute-start(bf16[192,384]{1,0:T(8,128)(2,1)S(1)} %get-tuple-element.92), channel_id=1, source_target_pairs={{0,8},{8,0},{16,24},{24,16},{1,9},{9,1},{17,25},{25,17},{2,10},{10... | collective-permute-start | bytes 442376 | tf_op jit(solution)/shard_map/ppermute | solution.py:275
  23.3 4.0 %collective-permute-start.9 = (bf16[384,128]{1,0:T(8,128)(2,1)S(1)}, bf16[384,128]{1,0:T(8,128)(2,1)S(1)}, u32[]{:S(2)}, u32[]{:S(2)}) collective-permute-start(bf16[384,128]{1,0:T(8,128)(2,1)S(1)} %get-tuple-element.99), channel_id=1, source_target_pairs={{0,8},{8,16},{16,24},{1,9},{9,17},{17,25},{2,10},{10,18},{18,26},{... | collective-permute-start | bytes 294920 | tf_op jit(solution)/shard_map/ppermute | solution.py:1024
  27.3 3.3 %collective-permute-start.19 = (bf16[384,384]{1,0:T(8,128)(2,1)S(1)}, bf16[384,384]{1,0:T(8,128)(2,1)S(1)}, u32[]{:S(2)}, u32[]{:S(2)}) collective-permute-start(bf16[384,384]{1,0:T(8,128)(2,1)S(1)} %collective-permute-done.7.far_ref), channel_id=1, source_target_pairs={{0,8},{8,0},{16,24},{24,16},{1,9},{9,1},{17,25},{25,17},{2,10},{10... | collective-permute-start | bytes 884744 | tf_op jit(solution)/shard_map/ppermute | solution.py:275
  30.1 3.3 %collective-permute-start.11 = (bf16[192,768]{1,0:T(8,128)(2,1)S(1)}, bf16[192,768]{1,0:T(8,128)(2,1)S(1)}, u32[]{:S(2)}, u32[]{:S(2)}) collective-permute-start(bf16[192,768]{1,0:T(8,128)(2,1)S(1)} %get-tuple-element.107), channel_id=1, source_target_pairs={{0,8},{8,0},{16,24},{24,16},{1,9},{9,1},{17,25},{25,17},{2,10},{10... | collective-permute-start | bytes 884744 | tf_op jit(solution)/shard_map/ppermute | solution.py:275
  30.2 3.2 %collective-permute-start.12 = (bf16[192,768]{1,0:T(8,128)(2,1)S(1)}, bf16[192,768]{1,0:T(8,128)(2,1)S(1)}, u32[]{:S(2)}, u32[]{:S(2)}) collective-permute-start(bf16[192,768]{1,0:T(8,128)(2,1)S(1)} %get-tuple-element.108), channel_id=1, source_target_pairs={{0,8},{8,0},{16,24},{24,16},{1,9},{9,1},{17,25},{25,17},{2,10},{10... | collective-permute-start | bytes 884744 | tf_op jit(solution)/shard_map/ppermute | solution.py:275
  31.7 4.8 %collective-permute-start.21 = (bf16[128,384]{1,0:T(8,128)(2,1)S(1)}, bf16[128,384]{1,0:T(8,128)(2,1)S(1)}, u32[]{:S(2)}, u32[]{:S(2)}) collective-permute-start(bf16[128,384]{1,0:T(8,128)(2,1)S(1)} %get-tuple-element.122), channel_id=1, source_target_pairs={{0,2},{1,3},{2,0},{3,1},{4,6},{5,7},{6,4},{7,5},{8,10},{9,11},{10,... | collective-permute-start | bytes 294920 | tf_op jit(solution)/shard_map/ppermute | solution.py:275
  34.8 5.6 %copy-start.7 = (s32[4]{0:T(128)S(1)}, s32[4]{0:T(128)}, u32[]{:S(2)}) copy-start(s32[4]{0:T(128)} %own_ref.1) | copy-start | bytes 52
  34.8 4.0 %collective-permute-start.13 = (bf16[8,96,128]{2,1,0:T(8,128)(2,1)S(1)}, bf16[8,96,128]{2,1,0:T(8,128)(2,1)S(1)}, u32[]{:S(2)}, u32[]{:S(2)}) collective-permute-start(bf16[8,96,128]{2,1,0:T(8,128)(2,1)S(1)} %get-tuple-element.109.refs_0_), channel_id=1, source_target_pairs={{0,8},{8,0},{16,24},{24,16},{1,9},{9,1},{17,25},{25,17},{2,10},{10... | collective-permute-start | bytes 589832 | tf_op jit(solution)/shard_map/ppermute | solution.py:275
  34.9 5.5 %collective-permute-start.14 = (bf16[8,96,128]{2,1,0:T(8,128)(2,1)S(1)}, bf16[8,96,128]{2,1,0:T(8,128)(2,1)S(1)}, u32[]{:S(2)}, u32[]{:S(2)}) collective-permute-start(bf16[8,96,128]{2,1,0:T(8,128)(2,1)S(1)} %get-tuple-element.110.refs_1_), channel_id=1, source_target_pairs={{0,8},{8,0},{16,24},{24,16},{1,9},{9,1},{17,25},{25,17},{2,10},{10... | collective-permute-start | bytes 589832 | tf_op jit(solution)/shard_map/ppermute | solution.py:275
  35.4 5.0 %collective-permute-start.15 = (bf16[8,96,128]{2,1,0:T(8,128)(2,1)S(1)}, bf16[8,96,128]{2,1,0:T(8,128)(2,1)S(1)}, u32[]{:S(2)}, u32[]{:S(2)}) collective-permute-start(bf16[8,96,128]{2,1,0:T(8,128)(2,1)S(1)} %get-tuple-element.111.refs_2_), channel_id=1, source_target_pairs={{0,8},{8,0},{16,24},{24,16},{1,9},{9,1},{17,25},{25,17},{2,10},{10... | collective-permute-start | bytes 589832 | tf_op jit(solution)/shard_map/ppermute | solution.py:275
  35.5 4.9 %collective-permute-start.16 = (bf16[8,96,128]{2,1,0:T(8,128)(2,1)S(1)}, bf16[8,96,128]{2,1,0:T(8,128)(2,1)S(1)}, u32[]{:S(2)}, u32[]{:S(2)}) collective-permute-start(bf16[8,96,128]{2,1,0:T(8,128)(2,1)S(1)} %get-tuple-element.112.refs_3_), channel_id=1, source_target_pairs={{0,8},{8,0},{16,24},{24,16},{1,9},{9,1},{17,25},{25,17},{2,10},{10... | collective-permute-start | bytes 589832 | tf_op jit(solution)/shard_map/ppermute | solution.py:275
  37.2 6.6 %collective-permute-start.22 = (bf16[64,1664]{1,0:T(8,128)(2,1)S(1)}, bf16[64,1664]{1,0:T(8,128)(2,1)S(1)}, u32[]{:S(2)}, u32[]{:S(2)}) collective-permute-start(bf16[64,1664]{1,0:T(8,128)(2,1)S(1)} %get-tuple-element.125), channel_id=1, source_target_pairs={{0,1},{1,0},{2,3},{3,2},{4,5},{5,4},{6,7},{7,6},{8,9},{9,8},{10,11... | collective-permute-start | bytes 638984 | tf_op jit(solution)/shard_map/ppermute | solution.py:275
  38.8 5.0 %collective-permute-start.20 = (bf16[128,384]{1,0:T(8,128)(2,1)S(1)}, bf16[128,384]{1,0:T(8,128)(2,1)S(1)}, u32[]{:S(2)}, u32[]{:S(2)}) collective-permute-start(bf16[128,384]{1,0:T(8,128)(2,1)S(1)} %get-tuple-element.120), channel_id=1, source_target_pairs={{0,2},{1,3},{2,0},{3,1},{4,6},{5,7},{6,4},{7,5},{8,10},{9,11},{10,... | collective-permute-start | bytes 294920 | tf_op jit(solution)/shard_map/ppermute | solution.py:275
  41.3 13.4 %collective-permute-start.17 = (bf16[4,288,128]{2,1,0:T(8,128)(2,1)S(1)}, bf16[4,288,128]{2,1,0:T(8,128)(2,1)S(1)}, u32[]{:S(2)}, u32[]{:S(2)}) collective-permute-start(bf16[4,288,128]{2,1,0:T(8,128)(2,1)S(1)} %get-tuple-element.114), channel_id=1, source_target_pairs={{0,16},{8,24},{16,0},{24,8},{1,17},{9,25},{17,1},{25,9},{2,18},{10... | collective-permute-start | bytes 884744 | tf_op jit(solution)/shard_map/ppermute | solution.py:275
  44.0 11.7 %collective-permute-start.23 = (bf16[64,1664]{1,0:T(8,128)(2,1)S(1)}, bf16[64,1664]{1,0:T(8,128)(2,1)S(1)}, u32[]{:S(2)}, u32[]{:S(2)}) collective-permute-start(bf16[64,1664]{1,0:T(8,128)(2,1)S(1)} %add_sums_to_pass_on.1), channel_id=1, source_target_pairs={{0,4},{1,5},{2,6},{3,7},{4,0},{5,1},{6,2},{7,3},{8,12},{9,13},{10,... | collective-permute-start | bytes 638984 | tf_op jit(solution)/shard_map/ppermute | solution.py:275
  47.3 8.4 %collective-permute-start.24 = (bf16[32,1664]{1,0:T(8,128)(2,1)S(1)}, bf16[32,1664]{1,0:T(8,128)(2,1)S(1)}, u32[]{:S(2)}, u32[]{:S(2)}) collective-permute-start(bf16[32,1664]{1,0:T(8,128)(2,1)S(1)} %get-tuple-element.129), channel_id=1, source_target_pairs={{0,1},{1,0},{2,3},{3,2},{4,5},{5,4},{6,7},{7,6},{8,9},{9,8},{10,11... | collective-permute-start | bytes 319496 | tf_op jit(solution)/shard_map/ppermute | solution.py:275
  48.9 6.8 %collective-permute-start.25 = (bf16[32,1664]{1,0:T(8,128)(2,1)S(1)}, bf16[32,1664]{1,0:T(8,128)(2,1)S(1)}, u32[]{:S(2)}, u32[]{:S(2)}) collective-permute-start(bf16[32,1664]{1,0:T(8,128)(2,1)S(1)} %get-tuple-element.130), channel_id=1, source_target_pairs={{0,1},{1,0},{2,3},{3,2},{4,5},{5,4},{6,7},{7,6},{8,9},{9,8},{10,11... | collective-permute-start | bytes 319496 | tf_op jit(solution)/shard_map/ppermute | solution.py:275
  49.4 5.3 %collective-permute-start.18 = (bf16[4,96,128]{2,1,0:T(8,128)(2,1)S(1)}, bf16[4,96,128]{2,1,0:T(8,128)(2,1)S(1)}, u32[]{:S(2)}, u32[]{:S(2)}) collective-permute-start(bf16[4,96,128]{2,1,0:T(8,128)(2,1)S(1)} %get-tuple-element.115), channel_id=1, source_target_pairs={{0,16},{8,24},{16,0},{24,8},{1,17},{9,25},{17,1},{25,9},{2,18},{10... | collective-permute-start | bytes 294920 | tf_op jit(solution)/shard_map/ppermute | solution.py:275
  (7 other events, 29.8 us)

commit v7 on v6

--- a/solution.py
+++ b/solution.py
@@ -532,21 +532,13 @@
     most_ref[...] = shard_product(normed_ref, 0, own_ref) + shard_product(normed_ref, 1, near_ref)
 
 
-def inner_far_kernel(normed_ref, most_ref, far_ref, sum_ref, first_ref, second_ref):
-    half = first_ref.shape[0]
-    first_ref[...] = far_ref[0:half, :]
-    second_ref[...] = far_ref[half:, :]
-    sum_ref[...] = most_ref[...] + shard_product(normed_ref, 2, far_ref)
-
-
 def inner_kernel(
     normed_ref,
     most_ref,
     own_ref,
     near_ref,
     far_ref,
-    last_first_ref,
-    last_second_ref,
+    last_ref,
     halo_ref,
     taps_ref,
     meta_ref,
@@ -562,13 +554,13 @@
     tok = normed_ref.shape[0]
     inner = x_ref.shape[1]
     head_dim = LANES // 2
-    rows = far_ref.shape[0]
-    at = pl.multiple_of(jnp.bitwise_xor(lax.axis_index("dp"), 3) * rows, LANES)
-    last = jnp.concatenate([last_first_ref[...], last_second_ref[...]], axis=0)
     ext_ref[0:TILE_ROWS, :] = sum(
-        shard_product(halo_ref, j, w_ref) for j, w_ref in enumerate((own_ref, near_ref, far_ref))
-    ) + dot32(halo_ref[:, pl.ds(at, rows)], last)
-    ext_ref[TILE_ROWS:, :] = most_ref[...] + dot32(normed_ref[:, pl.ds(at, rows)], last)
+        shard_product(halo_ref, j, w_ref)
+        for j, w_ref in enumerate((own_ref, near_ref, far_ref, last_ref))
+    )
+    ext_ref[TILE_ROWS:, :] = (
+        most_ref[...] + shard_product(normed_ref, 2, far_ref) + shard_product(normed_ref, 3, last_ref)
+    )
     state_width = leaving_ref.shape[1]
     step = step_ref[...]
     fade = fade_ref[...]
@@ -590,8 +582,7 @@
     return jnp.where(position > 0, ids_ref[jnp.maximum(position * tok - 1, 0)], -1)
 
 
-def table_kernel(ids_ref, bc_ref, faded_ref, meta_ref, prefix_ref, enter_ref, *refs):
-    table_refs = refs[2:]
+def table_kernel(ids_ref, bc_ref, faded_ref, meta_ref, prefix_ref, enter_ref, *table_refs):
     rows, state_width = table_refs[0].shape[1:]
     head_dim = LANES // 2
     tok = bc_ref.shape[0]
@@ -627,38 +618,35 @@
             table_ref[before, own, :] = (old + gain[:, h : h + 1] * entering).astype(jnp.bfloat16)
 
 
-def mixing_kernel(bc_ref, prefix_ref, pen_ref, mixing_ref):
-    blocks, heads = mixing_ref.shape[0:2]
-    state_width = bc_ref.shape[1] // 2
-    half = BLOCK // 2
-    for b in range(blocks):
-        own_rows = slice(b * BLOCK, (b + 1) * BLOCK)
-        scores = dot32(bc_ref[own_rows, state_width:], bc_ref[own_rows, 0:state_width], 1, 1)
-        prefix = prefix_ref[own_rows, :]
-        across = prefix.T
-        for h in range(heads):
-            for rows, seen in ((slice(0, half), half), (slice(half, BLOCK), BLOCK)):
-                gaps = prefix[rows, h : h + 1] - across[h : h + 1, 0:seen] + pen_ref[b, rows, 0:seen]
-                mixing_ref[b, h, rows, 0:seen] = (scores[rows, 0:seen] * jnp.exp(gaps)).astype(
-                    jnp.bfloat16
-                )
-
-
-def local_kernel(x_ref, bc_ref, stepx_ref, prefix_ref, meta_ref, mixing_ref, skip_ref, y_ref):
+def local_kernel(
+    x_ref,
+    bc_ref,
+    stepx_ref,
+    prefix_ref,
+    meta_ref,
+    pen_ref,
+    skip_ref,
+    y_ref,
+):
     inner = y_ref.shape[1]
     state_width = bc_ref.shape[1] // 2
     head_dim = LANES // 2
     tok = y_ref.shape[0]
+    lane = lax.broadcasted_iota(jnp.int32, (BLOCK, LANES), 1)
     half = BLOCK // 2
-    lane = lax.broadcasted_iota(jnp.int32, (BLOCK, LANES), 1)
     for b in range(tok // BLOCK):
         own_rows = slice(b * BLOCK, (b + 1) * BLOCK)
+        b_blk = bc_ref[own_rows, 0:state_width]
         c_blk = bc_ref[own_rows, state_width:]
+        scores = dot32(c_blk, b_blk, 1, 1)
+        pen = pen_ref[b]
+        prefix = prefix_ref[own_rows, :]
+        across = prefix.T
         if b > 0:
+            carried = jnp.exp(prefix - prefix_ref[b * BLOCK - 1 : b * BLOCK, :])
+            carried = carried * meta_ref[own_rows, 4:5]
             before_rows = slice((b - 1) * BLOCK, b * BLOCK)
             before = prefix_ref[before_rows, :]
-            carried = jnp.exp(prefix_ref[own_rows, :] - before[BLOCK - 1 : BLOCK, :])
-            carried = carried * meta_ref[own_rows, 4:5]
             fade = jnp.exp(before[BLOCK - 1 : BLOCK, :] - before)
             b_before = bc_ref[before_rows, 0:state_width].astype(jnp.float32)
             b_before = (b_before * meta_ref[before_rows, 5:6]).astype(jnp.bfloat16)
@@ -676,17 +664,14 @@
             for rows, seen in ((slice(0, half), half), (slice(half, BLOCK), BLOCK)):
                 part = out[rows]
                 for side in range(2):
-                    mixing = mixing_ref[b, 2 * q + side, rows, 0:seen]
+                    h = 2 * q + side
+                    gaps = prefix[rows, h : h + 1] - across[h : h + 1, 0:seen] + pen[rows, 0:seen]
+                    mixing = (scores[rows, 0:seen] * jnp.exp(gaps)).astype(jnp.bfloat16)
                     part = part + dot32(mixing, sides[side][0:seen])
                 y_ref[b * BLOCK + rows.start : b * BLOCK + rows.stop, own] = part
 
 
-def z_most_kernel(
-    normed_ref, own_ref, near_ref, far_ref, part_ref, most_ref, first_ref, second_ref
-):
-    half = first_ref.shape[0]
-    first_ref[...] = part_ref[0:half, :]
-    second_ref[...] = part_ref[half:, :]
+def z_most_kernel(normed_ref, own_ref, near_ref, far_ref, most_ref):
     most_ref[...] = sum(
         shard_product(normed_ref, j, w_ref) for j, w_ref in enumerate((own_ref, near_ref, far_ref))
     )
@@ -696,8 +681,8 @@
     gate_ref[...] = silu_tanh(most_ref[...] + shard_product(normed_ref, 3, last_ref))
 
 
-def gate_kernel(enter_ref, bc_ref, prefix_ref, meta_ref, y_ref, z_ref, *outs):
-    scratch, outs = outs[-1], outs[:-1]
+def gate_kernel(enter_ref, bc_ref, prefix_ref, meta_ref, y_ref, z_ref, arrived_ref, *outs):
+    scratch = outs[-1]
     inner = y_ref.shape[1]
     state_width = enter_ref.shape[1]
     head_dim = LANES // 2
@@ -759,9 +744,8 @@
     return high + ref[:, model + 1 : model + 2].astype(jnp.float32)
 
 
-def out_kernel(kept_ref, got_ref, own_ref, part_ref, first_ref, second_ref, wide_out, *refs):
+def out_kernel(kept_ref, got_ref, own_ref, part_ref, near_ref, wide_out, *refs):
     outs, sums_ref = refs[:-1], refs[-1]
-    near = jnp.concatenate([first_ref[...], second_ref[...]], axis=0)
     core = lax.axis_index("dp") % 2
     width = part_ref.shape[1]
     rows, model = sums_ref.shape
@@ -771,10 +755,10 @@
     for value in (kept, got):
         wide = value.astype(jnp.float32)
         squares = squares + jnp.sum(wide * wide, axis=1, keepdims=True)
-    for j, other in enumerate((part_ref[...], near)):
+    for j, other_ref in enumerate((part_ref, near_ref)):
         at = pl.multiple_of(jnp.bitwise_xor(core, j) * width, LANES)
         own = dot32(kept, own_ref[:, pl.ds(at, width)])
-        sums_ref[:, pl.ds(at, width)] = own + dot32(got, other)
+        sums_ref[:, pl.ds(at, width)] = own + dot32(got, other_ref[...])
     wide_out[:, 0:model] = sums_ref[0:part, :]
     wide_out[:, model:] = jnp.broadcast_to(squares[0:part], (part, LANES))
     size = part // len(outs)
@@ -908,6 +892,7 @@
         cost_estimate=LITTLE,
     )(w_out, out_gain[None, :])
     out_part = exchange(half_out, "head", Z_NEAR)
+    out_near = exchange(out_part, "dp", 1)
 
     x_far = exchange(x_own, "dp", 2)
     first_most, first_raw = pl.pallas_call(
@@ -969,28 +954,10 @@
         compiler_params=kernel_params(8),
         cost_estimate=LITTLE,
     )(normed, x_own, x_near)
-    mixing = pl.pallas_call(
-        mixing_kernel,
-        name="mixing_weights",
-        out_shape=shape((blocks, heads, BLOCK, BLOCK), bf16),
-        in_specs=in_vmem(3),
-        out_specs=in_vmem(1)[0],
-        compiler_params=kernel_params(8),
-        cost_estimate=LITTLE,
-    )(bc, prefix, pen)
-    x_far, x_most, bc, step, prefix, fade, halo, mixing = lax.optimization_barrier(
-        (x_far, x_most, bc, step, prefix, fade, halo, mixing)
-    )
-    x_most, *x_halves = pl.pallas_call(
-        inner_far_kernel,
-        name="project_x_of_far_device",
-        out_shape=(shape((tok, inner), f32),) + (shape((rows // 2, inner), bf16),) * 2,
-        in_specs=in_vmem(3),
-        out_specs=tuple(in_vmem(3)),
-        compiler_params=kernel_params(8),
-        cost_estimate=LITTLE,
-    )(normed, x_most, x_far)
-    x_last = [exchange(part, "dp", 1) for part in x_halves]
+    x_far, x_most, gate_own, bc, step, prefix, fade, halo = lax.optimization_barrier(
+        (x_far, x_most, gate_own, bc, step, prefix, fade, halo)
+    )
+    x_last = exchange(x_far, "dp", 1)
     gate_far = exchange(gate_own, "dp", 2)
     x, stepx, faded, leaving = pl.pallas_call(
         inner_kernel,
@@ -1001,7 +968,7 @@
             shape((inner, tok), bf16),
             shape((inner, state_width), bf16),
         ),
-        in_specs=in_vmem(13),
+        in_specs=in_vmem(12),
         out_specs=tuple(in_vmem(4)),
         scratch_shapes=[pltpu.VMEM((TILE_ROWS + tok, inner), f32)],
         compiler_params=kernel_params(14),
@@ -1012,7 +979,7 @@
         x_own,
         x_near,
         x_far,
-        *x_last,
+        x_last,
         halo,
         conv_x,
         meta,
@@ -1031,32 +998,31 @@
         out_specs=in_vmem(1)[0],
         compiler_params=kernel_params(14),
         cost_estimate=LITTLE,
-    )(x, bc, stepx, prefix, meta, mixing, skip_gain)
+    )(x, bc, stepx, prefix, meta, pen, skip_gain)
     gate_far, gate_near, entering, y_local = lax.optimization_barrier(
         (gate_far, gate_near, entering, y_local)
     )
     gate_last = exchange(gate_far, "dp", 1)
-    gate_most, *out_halves = pl.pallas_call(
-        z_most_kernel,
-        name="project_gate_most",
-        out_shape=(shape((tok, inner), f32),) + (shape((inner // 2, model // 2), bf16),) * 2,
-        in_specs=in_vmem(5),
-        out_specs=tuple(in_vmem(3)),
-        compiler_params=kernel_params(8),
-        cost_estimate=LITTLE,
-    )(normed, gate_own, gate_near, gate_far, out_part)
-    out_near = [exchange(part, "dp", 1) for part in out_halves]
     tables = pl.pallas_call(
         table_kernel,
         name="sum_ended_states",
         out_shape=(shape((PROMPTS, inner // 4, state_width), bf16),) * 4,
-        in_specs=[smem] + in_vmem(5) + [anywhere] * 2,
+        in_specs=[smem] + in_vmem(5),
         out_specs=tuple(in_vmem(4)),
         compiler_params=kernel_params(8),
         cost_estimate=LITTLE,
-    )(token_prompt, bc, faded, meta, prefix, entering, *out_near)
+    )(token_prompt, bc, faded, meta, prefix, entering)
     tables_near = [exchange(table, "dp", 1) for table in tables]
 
+    gate_most = pl.pallas_call(
+        z_most_kernel,
+        name="project_gate_most",
+        out_shape=shape((tok, inner), f32),
+        in_specs=in_vmem(4),
+        out_specs=in_vmem(1)[0],
+        compiler_params=kernel_params(8),
+        cost_estimate=LITTLE,
+    )(normed, gate_own, gate_near, gate_far)
     gate = pl.pallas_call(
         z_last_kernel,
         name="project_gate_last",
@@ -1072,12 +1038,12 @@
         gate_kernel,
         name="add_entering_and_gate",
         out_shape=(shape((2 * out_rows, inner), bf16),) * 4,
-        in_specs=in_vmem(6),
+        in_specs=in_vmem(6) + [anywhere],
         out_specs=tuple(in_vmem(4)),
         scratch_shapes=[pltpu.VMEM((tok, inner), bf16)],
         compiler_params=kernel_params(8),
         cost_estimate=LITTLE,
-    )(entering, bc, prefix, meta, y_local, gate)
+    )(entering, bc, prefix, meta, y_local, gate, out_near)
     got_first = exchange(sent_first, "head", Z_NEAR)
     got_rest = exchange(sent_rest, "head", Z_NEAR)
 
@@ -1105,12 +1071,12 @@
             out_kernel,
             name="project_out",
             out_shape=(shape(sums_shape, f32),) + (shape(piece, bf16),) * pieces,
-            in_specs=in_vmem(6),
+            in_specs=in_vmem(5),
             out_specs=tuple(in_vmem(1 + pieces)),
             scratch_shapes=[pltpu.VMEM((2 * out_rows, model), f32)],
             compiler_params=kernel_params(8),
             cost_estimate=LITTLE,
-        )(kept, got, scaled_out, out_part, *out_near)
+        )(kept, got, scaled_out, out_part, out_near)
 
     sums_pass, sums_cross = project(kept_first, got_first, 1)
     cross = exchange(sums_cross, "head", Y_NEAR)

time: 56.7 us -> 56.3 us (level)
  waiting for transfers between devices: 6.51 us -> 9.51 us
  starting transfers between devices: 28.9 us -> 26.2 us
    ppermute x25 -> x23, waiting for transfers between devices: 6.51 us -> 9.51 us  [exchange(): lax.ppermute(values, axis, [(i, i ^ bits) for i in range(lax.axis_size(ax...]
    ppermute x25 -> x23, starting transfers between devices: 26.5 us -> 23.8 us  [exchange(): lax.ppermute(values, axis, [(i, i ^ bits) for i in range(lax.axis_size(ax...]
    pallas_call x3 -> x1, Pallas kernels: 2.01 us -> 0.89 us  [fused_on_device(): pl.pallas_call(z_most_kernel, name='project_gate_most', out_shape=shape((...]
  transfers between devices with their start and end apart: 26 -> 24, of which waited for: 6 -> 9; matrix products, arithmetic and copies ran while one was open for 0% -> 0% of each run, Pallas kernels for 30% -> 29%
where the time goes in v7:
time: 56.3 us; the launch traced here: 56.2 us
  starting transfers between devices  26.2 us (47%)
  Pallas kernels  19.5 us (35%)
  waiting for transfers between devices  9.51 us (17%)
  between operations  0.96 us (2%)
    ppermute x23, starting transfers between devices, exchange(): lax.ppermute(values, axis, [(i, i ^ bits) for i in range(lax.axis_size(ax...  23.8 us
    ppermute x23, waiting for transfers between devices, exchange(): lax.ppermute(values, axis, [(i, i ^ bits) for i in range(lax.axis_size(ax...  9.51 us
    ppermute x1, starting transfers between devices, fused_on_device(): lax.ppermute(leaving, 'dp', [(i, i + 1) for i in range(peers - 1)])  2.41 us
    pallas_call x1, Pallas kernels, fused_on_device(): pl.pallas_call(first_kernel, name='project_b_c_and_steps', out_shape=(sha...  2.29 us
    pallas_call x1, Pallas kernels, fused_on_device(): pl.pallas_call(local_kernel, name='mix_within_blocks', out_shape=shape((t...  2.16 us
    pallas_call x1, Pallas kernels, fused_on_device(): pl.pallas_call(pack_first_kernel, name='pack_first_weights', out_shape=sh...  1.95 us
    pallas_call x1, Pallas kernels, fused_on_device(): pl.pallas_call(inner_kernel, name='project_and_convolve_x', out_shape=(sh...  1.94 us
    pallas_call x1, Pallas kernels, fused_on_device(): pl.pallas_call(table_kernel, name='sum_ended_states', out_shape=(shape((P...  1.57 us
  transfers between devices with their start and end apart: 24, of which 9 were waited for; matrix products, arithmetic and copies ran while one was open for 0% of the time, Pallas kernels for 29%

profile of v7, /device:TPU:0, one launch (start us, length us, event | category | flops | bytes accessed | tf_op | source)
XLA Modules:
  0.0 56.2 jit_solution(12494645347612786255)
XLA Ops:
  0.7 2.0 %pack_first_weights.1.own_ref = bf16[480,256]{1,0:T(8,128)(2,1)} custom-call(s32[1,4]{1,0:T(1,128)} %bitcast.5, f32[384,256]{1,0:T(8,128)} %wbc_ref.1, f32[6,384]{1,0:T(8,128)} %bitcast.6, bf16[512,1536]{1,0:T(8,128)(2,1)} %hidden_ref.1), custom_call_target="tpu_custom_call" | custom-call | flops 1000 | bytes 1000 | tf_op jit(solution)/shard_map/pack_first_weights/pallas_call | solution.py:835
  3.1 2.6 %collective-permute-start = (bf16[480,256]{1,0:T(8,128)(2,1)}, bf16[480,256]{1,0:T(8,128)(2,1)S(1)}, u32[]{:S(2)}, u32[]{:S(2)}) collective-permute-start(bf16[480,256]{1,0:T(8,128)(2,1)} %pack_first_weights.1.own_ref), channel_id=1, source_target_pairs={{0,16},{8,24},{16,0},{24,8},{1,17},{9,25},{17,1},{25,9},{2,18},{10... | collective-permute-start | bytes 737288 | tf_op jit(solution)/shard_map/ppermute | solution.py:275
  6.2 1.6 %collective-permute-start.16 = (bf16[384,768]{1,0:T(8,128)(2,1)S(1)}, bf16[384,768]{1,0:T(8,128)(2,1)S(1)}, u32[]{:S(2)}, u32[]{:S(2)}) collective-permute-start(bf16[384,768]{1,0:T(8,128)(2,1)S(1)} %get-tuple-element.106), channel_id=1, source_target_pairs={{0,2},{1,3},{2,0},{3,1},{4,6},{5,7},{6,4},{7,5},{8,10},{9,11},{10,... | collective-permute-start | bytes 1769480 | tf_op jit(solution)/shard_map/ppermute | solution.py:275
  9.1 1.2 %norm_and_token_facts.1 = (bf16[512,1536]{1,0:T(8,128)(2,1)S(1)}, f32[512,128]{1,0:T(8,128)S(1)}, bf16[1024,512]{1,0:T(8,128)(2,1)S(1)}, f32[2,256,256]{2,1,0:T(8,128)S(1)}, bf16[64,1536]{1,0:T(8,128)(2,1)S(1)}) custom-call(s32[1,2048]{1,0:T(1,128)S(1)} %bitcast.4, bf16[512,1536]{1,0:T(8,128)(2,1)S(1)} %copy-done, f32[1,1536]{1,0:T(1,128)S(1)} %broadcast_in_dim.14.gain_ref), custom_call_target="tpu_custom_call" | custom-call | flops 1000 | bytes 1000 | tf_op jit(solution)/shard_map/norm_and_token_facts/pallas_call | solution.py:869
  10.4 0.6 %project_b_c_and_steps_of_chip.1 = (f32[512,256]{1,0:T(8,128)S(1)}, f32[512,128]{1,0:T(8,128)S(1)}) custom-call(bf16[512,1536]{1,0:T(8,128)(2,1)S(1)} %get-tuple-element.62.normed_ref, bf16[480,256]{1,0:T(8,128)(2,1)S(1)} %copy-done.1, bf16[480,256]{1,0:T(8,128)(2,1)S(1)} %collective-permute-done.1.near_ref), custom_call_target="tpu_custom_call" | custom-call | flops 1000 | bytes 1000 | tf_op jit(solution)/shard_map/project_b_c_and_steps_of_chip/pallas_call | solution.py:898
  11.0 1.7 %collective-permute-done.far_ref = bf16[480,256]{1,0:T(8,128)(2,1)S(1)} collective-permute-done((bf16[480,256]{1,0:T(8,128)(2,1)}, bf16[480,256]{1,0:T(8,128)(2,1)S(1)}, u32[]{:S(2)}, u32[]{:S(2)}) %collective-permute-start) | collective-permute-done | bytes 245792 | tf_op jit(solution)/shard_map/ppermute | solution.py:275
  12.7 0.6 %project_x_of_chip.1.most_ref = f32[512,384]{1,0:T(8,128)S(1)} custom-call(bf16[512,1536]{1,0:T(8,128)(2,1)S(1)} %get-tuple-element.62.normed_ref, bf16[384,384]{1,0:T(8,128)(2,1)S(1)} %get-tuple-element.70.own_ref, bf16[384,384]{1,0:T(8,128)(2,1)S(1)} %collective-permute-done.3.near_ref), custom_call_target="tpu_custom_call" | custom-call | flops 1000 | bytes 1000 | tf_op jit(solution)/shard_map/project_x_of_chip/pallas_call | solution.py:948
  13.4 0.8 %collective-permute-done.4.last_ref = bf16[480,256]{1,0:T(8,128)(2,1)S(1)} collective-permute-done((bf16[480,256]{1,0:T(8,128)(2,1)S(1)}, bf16[480,256]{1,0:T(8,128)(2,1)S(1)}, u32[]{:S(2)}, u32[]{:S(2)}) %collective-permute-start.4) | collective-permute-done | bytes 245792 | tf_op jit(solution)/shard_map/ppermute | solution.py:275
  14.2 2.3 %project_b_c_and_steps.1 = (bf16[512,256]{1,0:T(8,128)(2,1)S(1)}, f32[512,128]{1,0:T(8,128)S(1)}, f32[512,128]{1,0:T(8,128)S(1)}, f32[512,128]{1,0:T(8,128)S(1)}, bf16[16,1536]{1,0:T(8,128)(2,1)S(1)}) custom-call(bf16[512,1536]{1,0:T(8,128)(2,1)S(1)} %get-tuple-element.62.normed_ref, f32[512,256]{1,0:T(8,128)S(1)} %get-tuple-element.72.most_ref, ...), custom_call_target="tpu_custom_call" | custom-call | flops 1000 | bytes 1000 | tf_op jit(solution)/shard_map/project_b_c_and_steps/pallas_call | solution.py:914
  16.5 2.2 %collective-permute-done.2.far_ref = bf16[384,384]{1,0:T(8,128)(2,1)S(1)} collective-permute-done((bf16[384,384]{1,0:T(8,128)(2,1)S(1)}, bf16[384,384]{1,0:T(8,128)(2,1)S(1)}, u32[]{:S(2)}, u32[]{:S(2)}) %collective-permute-start.2) | collective-permute-done | bytes 294944 | tf_op jit(solution)/shard_map/ppermute | solution.py:275
  19.3 1.8 %collective-permute-start.6 = (bf16[384,384]{1,0:T(8,128)(2,1)S(1)}, bf16[384,384]{1,0:T(8,128)(2,1)S(1)}, u32[]{:S(2)}, u32[]{:S(2)}) collective-permute-start(bf16[384,384]{1,0:T(8,128)(2,1)S(1)} %get-tuple-element.89.own_ref), channel_id=1, source_target_pairs={{0,16},{8,24},{16,0},{24,8},{1,17},{9,25},{17,1},{25,9},{2,18},{10... | collective-permute-start | bytes 884744 | tf_op jit(solution)/shard_map/ppermute | solution.py:275
  21.1 0.6 %collective-permute-done.16.part_ref = bf16[384,768]{1,0:T(8,128)(2,1)S(1)} collective-permute-done((bf16[384,768]{1,0:T(8,128)(2,1)S(1)}, bf16[384,768]{1,0:T(8,128)(2,1)S(1)}, u32[]{:S(2)}, u32[]{:S(2)}) %collective-permute-start.16) | collective-permute-done | bytes 589856 | tf_op jit(solution)/shard_map/ppermute | solution.py:275
  21.7 1.9 %project_and_convolve_x.1 = (bf16[512,384]{1,0:T(8,128)(2,1)S(1)}, bf16[512,384]{1,0:T(8,128)(2,1)S(1)}, bf16[384,512]{1,0:T(8,128)(2,1)S(1)}, bf16[384,128]{1,0:T(8,128)(2,1)S(1)}) custom-call(bf16[512,1536]{1,0:T(8,128)(2,1)S(1)} %get-tuple-element.62.normed_ref, f32[512,384]{1,0:T(8,128)S(1)} %project_x_of_chip.1.most_ref, ...), custom_call_target="tpu_custom_call" | custom-call | flops 1000 | bytes 1000 | tf_op jit(solution)/shard_map/project_and_convolve_x/pallas_call | solution.py:962
  23.6 2.4 %collective-permute-start.8 = (bf16[384,128]{1,0:T(8,128)(2,1)S(1)}, bf16[384,128]{1,0:T(8,128)(2,1)S(1)}, u32[]{:S(2)}, u32[]{:S(2)}) collective-permute-start(bf16[384,128]{1,0:T(8,128)(2,1)S(1)} %get-tuple-element.90), channel_id=1, source_target_pairs={{0,8},{8,16},{16,24},{1,9},{9,17},{17,25},{2,10},{10,18},{18,26},{... | collective-permute-start | bytes 294920 | tf_op jit(solution)/shard_map/ppermute | solution.py:991
  26.1 2.2 %mix_within_blocks.1.y_ref = f32[512,384]{1,0:T(8,128)S(1)} custom-call(bf16[512,384]{1,0:T(8,128)(2,1)S(1)} %get-tuple-element.91.x_ref, bf16[512,256]{1,0:T(8,128)(2,1)S(1)} %get-tuple-element.81.bc_ref, bf16[512,384]{1,0:T(8,128)(2,1)S(1)} %get-tuple-element.92.stepx_ref, f32[512,128]{1,0:T(8,128)S(1)} %get-tuple-element.88.prefix_ref, ...), custom_call_target="tpu_custom_call" | custom-call | flops 1000 | bytes 1000 | tf_op jit(solution)/shard_map/mix_within_blocks/pallas_call | solution.py:993
  28.7 0.9 %project_gate_most.1.most_ref = f32[512,384]{1,0:T(8,128)S(1)} custom-call(bf16[512,1536]{1,0:T(8,128)(2,1)S(1)} %get-tuple-element.62.normed_ref, bf16[384,384]{1,0:T(8,128)(2,1)S(1)} %get-tuple-element.89.own_ref, bf16[384,384]{1,0:T(8,128)(2,1)S(1)} %collective-permute-done.7.near_ref, bf16[384,384]{1,0:T(8,128)(2,1)S(1)} %collective-permute-done.6.far_ref), custom_call_target="tpu_custom_call" | custom-call | flops 1000 | bytes 1000 | tf_op jit(solution)/shard_map/project_gate_most/pallas_call | solution.py:1017
  30.5 0.6 %add_entering_and_gate.1 = (bf16[128,384]{1,0:T(8,128)(2,1)S(1)}, bf16[128,384]{1,0:T(8,128)(2,1)S(1)}, bf16[128,384]{1,0:T(8,128)(2,1)S(1)}, bf16[128,384]{1,0:T(8,128)(2,1)S(1)}) custom-call(bf16[384,128]{1,0:T(8,128)(2,1)S(1)} %collective-permute-done.8.enter_ref, bf16[512,256]{1,0:T(8,128)(2,1)S(1)} %get-tuple-element.81.bc_ref, ...), custom_call_target="tpu_custom_call" | custom-call | flops 1000 | bytes 1000 | tf_op jit(solution)/shard_map/add_entering_and_gate/pallas_call | solution.py:1037
  31.1 1.7 %collective-permute-start.19 = (bf16[128,384]{1,0:T(8,128)(2,1)S(1)}, bf16[128,384]{1,0:T(8,128)(2,1)S(1)}, u32[]{:S(2)}, u32[]{:S(2)}) collective-permute-start(bf16[128,384]{1,0:T(8,128)(2,1)S(1)} %get-tuple-element.110), channel_id=1, source_target_pairs={{0,2},{1,3},{2,0},{3,1},{4,6},{5,7},{6,4},{7,5},{8,10},{9,11},{10,... | collective-permute-start | bytes 294920 | tf_op jit(solution)/shard_map/ppermute | solution.py:275
  32.8 1.6 %sum_ended_states.1 = (bf16[8,96,128]{2,1,0:T(8,128)(2,1)S(1)}, bf16[8,96,128]{2,1,0:T(8,128)(2,1)S(1)}, bf16[8,96,128]{2,1,0:T(8,128)(2,1)S(1)}, bf16[8,96,128]{2,1,0:T(8,128)(2,1)S(1)}) custom-call(s32[2048]{0:T(1024)S(1)} %copy-done.4, bf16[512,256]{1,0:T(8,128)(2,1)S(1)} %get-tuple-element.81.bc_ref, bf16[384,512]{1,0:T(8,128)(2,1)S(1)} %get-tuple-element.87.faded_ref, ...), custom_call_target="tpu_custom_call" | custom-call | flops 1000 | bytes 1000 | tf_op jit(solution)/shard_map/sum_ended_states/pallas_call | solution.py:1006
  35.5 0.7 %collective-permute-done.19.got_ref = bf16[128,384]{1,0:T(8,128)(2,1)S(1)} collective-permute-done((bf16[128,384]{1,0:T(8,128)(2,1)S(1)}, bf16[128,384]{1,0:T(8,128)(2,1)S(1)}, u32[]{:S(2)}, u32[]{:S(2)}) %collective-permute-start.19) | collective-permute-done | bytes 98336 | tf_op jit(solution)/shard_map/ppermute | solution.py:275
  36.2 0.6 %project_out.2 = (f32[64,1664]{1,0:T(8,128)S(1)}, bf16[64,1664]{1,0:T(8,128)(2,1)S(1)}) custom-call(bf16[128,384]{1,0:T(8,128)(2,1)S(1)} %get-tuple-element.109.kept_ref, bf16[128,384]{1,0:T(8,128)(2,1)S(1)} %collective-permute-done.19.got_ref, bf16[384,1536]{1,0:T(8,128)(2,1)S(1)} %get-tuple-element.111.own_ref, ...), custom_call_target="tpu_custom_call" | custom-call | flops 1000 | bytes 1000 | tf_op jit(solution)/shard_map/project_out/pallas_call | solution.py:1070
  36.8 1.5 %collective-permute-start.20 = (bf16[64,1664]{1,0:T(8,128)(2,1)S(1)}, bf16[64,1664]{1,0:T(8,128)(2,1)S(1)}, u32[]{:S(2)}, u32[]{:S(2)}) collective-permute-start(bf16[64,1664]{1,0:T(8,128)(2,1)S(1)} %get-tuple-element.113), channel_id=1, source_target_pairs={{0,1},{1,0},{2,3},{3,2},{4,5},{5,4},{6,7},{7,6},{8,9},{9,8},{10,11... | collective-permute-start | bytes 638984 | tf_op jit(solution)/shard_map/ppermute | solution.py:275
  38.3 1.6 %collective-permute-start.18 = (bf16[128,384]{1,0:T(8,128)(2,1)S(1)}, bf16[128,384]{1,0:T(8,128)(2,1)S(1)}, u32[]{:S(2)}, u32[]{:S(2)}) collective-permute-start(bf16[128,384]{1,0:T(8,128)(2,1)S(1)} %get-tuple-element.108), channel_id=1, source_target_pairs={{0,2},{1,3},{2,0},{3,1},{4,6},{5,7},{6,4},{7,5},{8,10},{9,11},{10,... | collective-permute-start | bytes 294920 | tf_op jit(solution)/shard_map/ppermute | solution.py:275
  39.9 0.9 %pick_request_states.1 = (bf16[4,384,128]{2,1,0:T(8,128)(2,1)S(1)}, bf16[4,288,128]{2,1,0:T(8,128)(2,1)S(1)}, bf16[4,96,128]{2,1,0:T(8,128)(2,1)S(1)}) custom-call(s32[4]{0:T(128)S(1)} %copy-done.7, bf16[480,256]{1,0:T(8,128)(2,1)S(1)} %collective-permute-done.far_ref, bf16[8,96,128]{2,1,0:T(8,128)(2,1)S(1)} %get-tuple-element.95.refs_0_, ...), custom_call_target="tpu_custom_call" | custom-call | flops 1000 | bytes 1000 | tf_op jit(solution)/shard_map/pick_request_states/pallas_call | solution.py:1052
  40.8 2.6 %collective-permute-start.13 = (bf16[4,288,128]{2,1,0:T(8,128)(2,1)S(1)}, bf16[4,288,128]{2,1,0:T(8,128)(2,1)S(1)}, u32[]{:S(2)}, u32[]{:S(2)}) collective-permute-start(bf16[4,288,128]{2,1,0:T(8,128)(2,1)S(1)} %get-tuple-element.100), channel_id=1, source_target_pairs={{0,16},{8,24},{16,0},{24,8},{1,17},{9,25},{17,1},{25,9},{2,18},{10... | collective-permute-start | bytes 884744 | tf_op jit(solution)/shard_map/ppermute | solution.py:275
  43.7 2.5 %collective-permute-start.21 = (bf16[64,1664]{1,0:T(8,128)(2,1)S(1)}, bf16[64,1664]{1,0:T(8,128)(2,1)S(1)}, u32[]{:S(2)}, u32[]{:S(2)}) collective-permute-start(bf16[64,1664]{1,0:T(8,128)(2,1)S(1)} %add_sums_to_pass_on.1), channel_id=1, source_target_pairs={{0,4},{1,5},{2,6},{3,7},{4,0},{5,1},{6,2},{7,3},{8,12},{9,13},{10,... | collective-permute-start | bytes 638984 | tf_op jit(solution)/shard_map/ppermute | solution.py:275
  46.2 0.6 %project_out.3 = (f32[64,1664]{1,0:T(8,128)S(1)}, bf16[32,1664]{1,0:T(8,128)(2,1)S(1)}, bf16[32,1664]{1,0:T(8,128)(2,1)S(1)}) custom-call(bf16[128,384]{1,0:T(8,128)(2,1)S(1)} %get-tuple-element.107.kept_ref, bf16[128,384]{1,0:T(8,128)(2,1)S(1)} %collective-permute-done.18.arrived_ref.got_ref, bf16[384,1536]{1,0:T(8,128)(2,1)S(1)} %get-tuple-element.111.own_ref, ...), custom_call_target="tpu_custom_call" | custom-call | flops 1000 | bytes 1000 | tf_op jit(solution)/shard_map/project_out/pallas_call | solution.py:1070
  46.8 1.6 %collective-permute-start.22 = (bf16[32,1664]{1,0:T(8,128)(2,1)S(1)}, bf16[32,1664]{1,0:T(8,128)(2,1)S(1)}, u32[]{:S(2)}, u32[]{:S(2)}) collective-permute-start(bf16[32,1664]{1,0:T(8,128)(2,1)S(1)} %get-tuple-element.117), channel_id=1, source_target_pairs={{0,1},{1,0},{2,3},{3,2},{4,5},{5,4},{6,7},{7,6},{8,9},{9,8},{10,11... | collective-permute-start | bytes 319496 | tf_op jit(solution)/shard_map/ppermute | solution.py:275
  48.9 2.8 %collective-permute-start.14 = (bf16[4,96,128]{2,1,0:T(8,128)(2,1)S(1)}, bf16[4,96,128]{2,1,0:T(8,128)(2,1)S(1)}, u32[]{:S(2)}, u32[]{:S(2)}) collective-permute-start(bf16[4,96,128]{2,1,0:T(8,128)(2,1)S(1)} %get-tuple-element.101), channel_id=1, source_target_pairs={{0,16},{8,24},{16,0},{24,8},{1,17},{9,25},{17,1},{25,9},{2,18},{10... | collective-permute-start | bytes 294920 | tf_op jit(solution)/shard_map/ppermute | solution.py:275
  51.7 2.6 %collective-permute-done.14.refs_1_ = bf16[4,96,128]{2,1,0:T(8,128)(2,1)S(1)} collective-permute-done((bf16[4,96,128]{2,1,0:T(8,128)(2,1)S(1)}, bf16[4,96,128]{2,1,0:T(8,128)(2,1)S(1)}, u32[]{:S(2)}, u32[]{:S(2)}) %collective-permute-start.14) | collective-permute-done | bytes 98336 | tf_op jit(solution)/shard_map/ppermute | solution.py:275
  54.3 1.0 %join_request_states.1 = (f32[4,384,128]{2,1,0:T(8,128)}, f32[8,128]{1,0:T(8,128)S(1)}) custom-call(bf16[4,384,128]{2,1,0:T(8,128)(2,1)S(1)} %get-tuple-element.99.keep_ref, bf16[4,288,128]{2,1,0:T(8,128)(2,1)S(1)} %collective-permute-done.13.refs_0_, bf16[4,96,128]{2,1,0:T(8,128)(2,1)S(1)} %collective-permute-done.14.refs_1_), custom_call_target="tpu_custom_call" | custom-call | flops 1000 | bytes 1000 | tf_op jit(solution)/shard_map/join_request_states/pallas_call | solution.py:1096
  55.3 0.9 %scale_and_add_hidden.1 = bf16[64,1536]{1,0:T(8,128)(2,1)} custom-call(bf16[64,1536]{1,0:T(8,128)(2,1)S(1)} %get-tuple-element.61.hidden_ref, f32[8,128]{1,0:T(8,128)S(1)} %get-tuple-element.102.joined_ref, f32[64,1664]{1,0:T(8,128)S(1)} %get-tuple-element.115.keep_ref, bf16[64,1664]{1,0:T(8,128)(2,1)S(1)} %collective-permute-done.21.passed_ref, ...), custom_call_target="tpu_custom_call" | custom-call | flops 1000 | bytes 1000 | tf_op jit(solution)/shard_map/scale_and_add_hidden/pallas_call | solution.py:1105
  (63 shorter events, 6.1 us)
Async XLA Ops:
  0.6 5.1 %copy-start.12 = (f32[384]{0:T(512)S(1)}, f32[384]{0:T(512)}, u32[]{:S(2)}) copy-start(f32[384]{0:T(512)} %param.26) | copy-start | bytes 4612
  0.6 5.1 %copy-start.2 = (bf16[384,1536]{1,0:T(8,128)(2,1)S(1)}, bf16[384,1536]{1,0:T(8,128)(2,1)}, u32[]{:S(2)}) copy-start(bf16[384,1536]{1,0:T(8,128)(2,1)} %w_ref.1) | copy-start | bytes 3538948
  0.7 7.2 %copy-start.3 = (f32[384,2,384]{2,1,0:T(2,128)S(1)}, f32[384,2,384]{2,1,0:T(2,128)}, u32[]{:S(2)}) copy-start(f32[384,2,384]{2,1,0:T(2,128)} %wzx_ref.1) | copy-start | bytes 3538948
  2.6 7.8 %collective-permute-start.1 = (bf16[480,256]{1,0:T(8,128)(2,1)}, bf16[480,256]{1,0:T(8,128)(2,1)S(1)}, u32[]{:S(2)}, u32[]{:S(2)}) collective-permute-start(bf16[480,256]{1,0:T(8,128)(2,1)} %pack_first_weights.1.own_ref), channel_id=1, source_target_pairs={{0,8},{8,0},{16,24},{24,16},{1,9},{9,1},{17,25},{25,17},{2,10},{10... | collective-permute-start | bytes 737288 | tf_op jit(solution)/shard_map/ppermute | solution.py:275
  3.1 9.6 %collective-permute-start = (bf16[480,256]{1,0:T(8,128)(2,1)}, bf16[480,256]{1,0:T(8,128)(2,1)S(1)}, u32[]{:S(2)}, u32[]{:S(2)}) collective-permute-start(bf16[480,256]{1,0:T(8,128)(2,1)} %pack_first_weights.1.own_ref), channel_id=1, source_target_pairs={{0,16},{8,24},{16,0},{24,8},{1,17},{9,25},{17,1},{25,9},{2,18},{10... | collective-permute-start | bytes 737288 | tf_op jit(solution)/shard_map/ppermute | solution.py:275
  5.7 3.4 %copy-start = (bf16[512,1536]{1,0:T(8,128)(2,1)S(1)}, bf16[512,1536]{1,0:T(8,128)(2,1)}, u32[]{:S(2)}) copy-start(bf16[512,1536]{1,0:T(8,128)(2,1)} %hidden_ref.1) | copy-start | bytes 4718596
  6.2 4.2 %copy-start.1 = (bf16[480,256]{1,0:T(8,128)(2,1)S(1)}, bf16[480,256]{1,0:T(8,128)(2,1)}, u32[]{:S(2)}) copy-start(bf16[480,256]{1,0:T(8,128)(2,1)} %pack_first_weights.1.own_ref) | copy-start | bytes 737284
  6.2 15.5 %collective-permute-start.16 = (bf16[384,768]{1,0:T(8,128)(2,1)S(1)}, bf16[384,768]{1,0:T(8,128)(2,1)S(1)}, u32[]{:S(2)}, u32[]{:S(2)}) collective-permute-start(bf16[384,768]{1,0:T(8,128)(2,1)S(1)} %get-tuple-element.106), channel_id=1, source_target_pairs={{0,2},{1,3},{2,0},{3,1},{4,6},{5,7},{6,4},{7,5},{8,10},{9,11},{10,... | collective-permute-start | bytes 1769480 | tf_op jit(solution)/shard_map/ppermute | solution.py:275
  8.4 4.3 %collective-permute-start.3 = (bf16[384,384]{1,0:T(8,128)(2,1)S(1)}, bf16[384,384]{1,0:T(8,128)(2,1)S(1)}, u32[]{:S(2)}, u32[]{:S(2)}) collective-permute-start(bf16[384,384]{1,0:T(8,128)(2,1)S(1)} %get-tuple-element.70.own_ref), channel_id=1, source_target_pairs={{0,8},{8,0},{16,24},{24,16},{1,9},{9,1},{17,25},{25,17},{2,10},{10... | collective-permute-start | bytes 884744 | tf_op jit(solution)/shard_map/ppermute | solution.py:275
  8.5 10.3 %collective-permute-start.2 = (bf16[384,384]{1,0:T(8,128)(2,1)S(1)}, bf16[384,384]{1,0:T(8,128)(2,1)S(1)}, u32[]{:S(2)}, u32[]{:S(2)}) collective-permute-start(bf16[384,384]{1,0:T(8,128)(2,1)S(1)} %get-tuple-element.70.own_ref), channel_id=1, source_target_pairs={{0,16},{8,24},{16,0},{24,8},{1,17},{9,25},{17,1},{25,9},{2,18},{10... | collective-permute-start | bytes 884744 | tf_op jit(solution)/shard_map/ppermute | solution.py:275
  12.7 1.5 %collective-permute-start.4 = (bf16[480,256]{1,0:T(8,128)(2,1)S(1)}, bf16[480,256]{1,0:T(8,128)(2,1)S(1)}, u32[]{:S(2)}, u32[]{:S(2)}) collective-permute-start(bf16[480,256]{1,0:T(8,128)(2,1)S(1)} %collective-permute-done.far_ref), channel_id=1, source_target_pairs={{0,8},{8,0},{16,24},{24,16},{1,9},{9,1},{17,25},{25,17},{2,10},{10... | collective-permute-start | bytes 737288 | tf_op jit(solution)/shard_map/ppermute | solution.py:275
  13.4 8.3 %copy-start.5 = (f32[4,384]{1,0:T(4,128)S(1)}, f32[4,384]{1,0:T(4,128)}, u32[]{:S(2)}) copy-start(f32[4,384]{1,0:T(4,128)} %taps_ref.3) | copy-start | bytes 18436
  18.8 7.3 %copy-start.10 = (f32[6]{0:T(128)S(1)}, f32[6]{0:T(128)}, u32[]{:S(2)}) copy-start(f32[6]{0:T(128)} %skip_ref.1) | copy-start | bytes 76
  18.8 2.9 %collective-permute-start.5 = (bf16[384,384]{1,0:T(8,128)(2,1)S(1)}, bf16[384,384]{1,0:T(8,128)(2,1)S(1)}, u32[]{:S(2)}, u32[]{:S(2)}) collective-permute-start(bf16[384,384]{1,0:T(8,128)(2,1)S(1)} %collective-permute-done.2.far_ref), channel_id=1, source_target_pairs={{0,8},{8,0},{16,24},{24,16},{1,9},{9,1},{17,25},{25,17},{2,10},{10... | collective-permute-start | bytes 884744 | tf_op jit(solution)/shard_map/ppermute | solution.py:275
  18.8 9.4 %collective-permute-start.7 = (bf16[384,384]{1,0:T(8,128)(2,1)S(1)}, bf16[384,384]{1,0:T(8,128)(2,1)S(1)}, u32[]{:S(2)}, u32[]{:S(2)}) collective-permute-start(bf16[384,384]{1,0:T(8,128)(2,1)S(1)} %get-tuple-element.89.own_ref), channel_id=1, source_target_pairs={{0,8},{8,0},{16,24},{24,16},{1,9},{9,1},{17,25},{25,17},{2,10},{10... | collective-permute-start | bytes 884744 | tf_op jit(solution)/shard_map/ppermute | solution.py:275
  19.3 9.2 %collective-permute-start.6 = (bf16[384,384]{1,0:T(8,128)(2,1)S(1)}, bf16[384,384]{1,0:T(8,128)(2,1)S(1)}, u32[]{:S(2)}, u32[]{:S(2)}) collective-permute-start(bf16[384,384]{1,0:T(8,128)(2,1)S(1)} %get-tuple-element.89.own_ref), channel_id=1, source_target_pairs={{0,16},{8,24},{16,0},{24,8},{1,17},{9,25},{17,1},{25,9},{2,18},{10... | collective-permute-start | bytes 884744 | tf_op jit(solution)/shard_map/ppermute | solution.py:275
  21.7 8.8 %collective-permute-start.17 = (bf16[384,768]{1,0:T(8,128)(2,1)S(1)}, bf16[384,768]{1,0:T(8,128)(2,1)S(1)}, u32[]{:S(2)}, u32[]{:S(2)}) collective-permute-start(bf16[384,768]{1,0:T(8,128)(2,1)S(1)} %collective-permute-done.16.part_ref), channel_id=1, source_target_pairs={{0,8},{8,0},{16,24},{24,16},{1,9},{9,1},{17,25},{25,17},{2,10},{10... | collective-permute-start | bytes 1769480 | tf_op jit(solution)/shard_map/ppermute | solution.py:275
  23.6 4.8 %collective-permute-start.8 = (bf16[384,128]{1,0:T(8,128)(2,1)S(1)}, bf16[384,128]{1,0:T(8,128)(2,1)S(1)}, u32[]{:S(2)}, u32[]{:S(2)}) collective-permute-start(bf16[384,128]{1,0:T(8,128)(2,1)S(1)} %get-tuple-element.90), channel_id=1, source_target_pairs={{0,8},{8,16},{16,24},{1,9},{9,17},{17,25},{2,10},{10,18},{18,26},{... | collective-permute-start | bytes 294920 | tf_op jit(solution)/shard_map/ppermute | solution.py:991
  28.5 1.6 %collective-permute-start.15 = (bf16[384,384]{1,0:T(8,128)(2,1)S(1)}, bf16[384,384]{1,0:T(8,128)(2,1)S(1)}, u32[]{:S(2)}, u32[]{:S(2)}) collective-permute-start(bf16[384,384]{1,0:T(8,128)(2,1)S(1)} %collective-permute-done.6.far_ref), channel_id=1, source_target_pairs={{0,8},{8,0},{16,24},{24,16},{1,9},{9,1},{17,25},{25,17},{2,10},{10... | collective-permute-start | bytes 884744 | tf_op jit(solution)/shard_map/ppermute | solution.py:275
  31.1 5.1 %collective-permute-start.19 = (bf16[128,384]{1,0:T(8,128)(2,1)S(1)}, bf16[128,384]{1,0:T(8,128)(2,1)S(1)}, u32[]{:S(2)}, u32[]{:S(2)}) collective-permute-start(bf16[128,384]{1,0:T(8,128)(2,1)S(1)} %get-tuple-element.110), channel_id=1, source_target_pairs={{0,2},{1,3},{2,0},{3,1},{4,6},{5,7},{6,4},{7,5},{8,10},{9,11},{10,... | collective-permute-start | bytes 294920 | tf_op jit(solution)/shard_map/ppermute | solution.py:275
  34.4 4.0 %collective-permute-start.10 = (bf16[8,96,128]{2,1,0:T(8,128)(2,1)S(1)}, bf16[8,96,128]{2,1,0:T(8,128)(2,1)S(1)}, u32[]{:S(2)}, u32[]{:S(2)}) collective-permute-start(bf16[8,96,128]{2,1,0:T(8,128)(2,1)S(1)} %get-tuple-element.96.refs_1_), channel_id=1, source_target_pairs={{0,8},{8,0},{16,24},{24,16},{1,9},{9,1},{17,25},{25,17},{2,10},{10... | collective-permute-start | bytes 589832 | tf_op jit(solution)/shard_map/ppermute | solution.py:275
  34.4 5.5 %collective-permute-start.11 = (bf16[8,96,128]{2,1,0:T(8,128)(2,1)S(1)}, bf16[8,96,128]{2,1,0:T(8,128)(2,1)S(1)}, u32[]{:S(2)}, u32[]{:S(2)}) collective-permute-start(bf16[8,96,128]{2,1,0:T(8,128)(2,1)S(1)} %get-tuple-element.97.refs_2_), channel_id=1, source_target_pairs={{0,8},{8,0},{16,24},{24,16},{1,9},{9,1},{17,25},{25,17},{2,10},{10... | collective-permute-start | bytes 589832 | tf_op jit(solution)/shard_map/ppermute | solution.py:275
  34.9 5.0 %collective-permute-start.12 = (bf16[8,96,128]{2,1,0:T(8,128)(2,1)S(1)}, bf16[8,96,128]{2,1,0:T(8,128)(2,1)S(1)}, u32[]{:S(2)}, u32[]{:S(2)}) collective-permute-start(bf16[8,96,128]{2,1,0:T(8,128)(2,1)S(1)} %get-tuple-element.98.refs_3_), channel_id=1, source_target_pairs={{0,8},{8,0},{16,24},{24,16},{1,9},{9,1},{17,25},{25,17},{2,10},{10... | collective-permute-start | bytes 589832 | tf_op jit(solution)/shard_map/ppermute | solution.py:275
  35.0 4.9 %collective-permute-start.9 = (bf16[8,96,128]{2,1,0:T(8,128)(2,1)S(1)}, bf16[8,96,128]{2,1,0:T(8,128)(2,1)S(1)}, u32[]{:S(2)}, u32[]{:S(2)}) collective-permute-start(bf16[8,96,128]{2,1,0:T(8,128)(2,1)S(1)} %get-tuple-element.95.refs_0_), channel_id=1, source_target_pairs={{0,8},{8,0},{16,24},{24,16},{1,9},{9,1},{17,25},{25,17},{2,10},{10... | collective-permute-start | bytes 589832 | tf_op jit(solution)/shard_map/ppermute | solution.py:275
  36.2 3.7 %copy-start.7 = (s32[4]{0:T(128)S(1)}, s32[4]{0:T(128)}, u32[]{:S(2)}) copy-start(s32[4]{0:T(128)} %own_ref.1) | copy-start | bytes 52
  36.8 6.7 %collective-permute-start.20 = (bf16[64,1664]{1,0:T(8,128)(2,1)S(1)}, bf16[64,1664]{1,0:T(8,128)(2,1)S(1)}, u32[]{:S(2)}, u32[]{:S(2)}) collective-permute-start(bf16[64,1664]{1,0:T(8,128)(2,1)S(1)} %get-tuple-element.113), channel_id=1, source_target_pairs={{0,1},{1,0},{2,3},{3,2},{4,5},{5,4},{6,7},{7,6},{8,9},{9,8},{10,11... | collective-permute-start | bytes 638984 | tf_op jit(solution)/shard_map/ppermute | solution.py:275
  38.3 5.0 %collective-permute-start.18 = (bf16[128,384]{1,0:T(8,128)(2,1)S(1)}, bf16[128,384]{1,0:T(8,128)(2,1)S(1)}, u32[]{:S(2)}, u32[]{:S(2)}) collective-permute-start(bf16[128,384]{1,0:T(8,128)(2,1)S(1)} %get-tuple-element.108), channel_id=1, source_target_pairs={{0,2},{1,3},{2,0},{3,1},{4,6},{5,7},{6,4},{7,5},{8,10},{9,11},{10,... | collective-permute-start | bytes 294920 | tf_op jit(solution)/shard_map/ppermute | solution.py:275
  40.8 13.5 %collective-permute-start.13 = (bf16[4,288,128]{2,1,0:T(8,128)(2,1)S(1)}, bf16[4,288,128]{2,1,0:T(8,128)(2,1)S(1)}, u32[]{:S(2)}, u32[]{:S(2)}) collective-permute-start(bf16[4,288,128]{2,1,0:T(8,128)(2,1)S(1)} %get-tuple-element.100), channel_id=1, source_target_pairs={{0,16},{8,24},{16,0},{24,8},{1,17},{9,25},{17,1},{25,9},{2,18},{10... | collective-permute-start | bytes 884744 | tf_op jit(solution)/shard_map/ppermute | solution.py:275
  43.7 11.6 %collective-permute-start.21 = (bf16[64,1664]{1,0:T(8,128)(2,1)S(1)}, bf16[64,1664]{1,0:T(8,128)(2,1)S(1)}, u32[]{:S(2)}, u32[]{:S(2)}) collective-permute-start(bf16[64,1664]{1,0:T(8,128)(2,1)S(1)} %add_sums_to_pass_on.1), channel_id=1, source_target_pairs={{0,4},{1,5},{2,6},{3,7},{4,0},{5,1},{6,2},{7,3},{8,12},{9,13},{10,... | collective-permute-start | bytes 638984 | tf_op jit(solution)/shard_map/ppermute | solution.py:275
  46.8 8.4 %collective-permute-start.22 = (bf16[32,1664]{1,0:T(8,128)(2,1)S(1)}, bf16[32,1664]{1,0:T(8,128)(2,1)S(1)}, u32[]{:S(2)}, u32[]{:S(2)}) collective-permute-start(bf16[32,1664]{1,0:T(8,128)(2,1)S(1)} %get-tuple-element.117), channel_id=1, source_target_pairs={{0,1},{1,0},{2,3},{3,2},{4,5},{5,4},{6,7},{7,6},{8,9},{9,8},{10,11... | collective-permute-start | bytes 319496 | tf_op jit(solution)/shard_map/ppermute | solution.py:275
  48.4 6.9 %collective-permute-start.23 = (bf16[32,1664]{1,0:T(8,128)(2,1)S(1)}, bf16[32,1664]{1,0:T(8,128)(2,1)S(1)}, u32[]{:S(2)}, u32[]{:S(2)}) collective-permute-start(bf16[32,1664]{1,0:T(8,128)(2,1)S(1)} %get-tuple-element.118), channel_id=1, source_target_pairs={{0,1},{1,0},{2,3},{3,2},{4,5},{5,4},{6,7},{7,6},{8,9},{9,8},{10,11... | collective-permute-start | bytes 319496 | tf_op jit(solution)/shard_map/ppermute | solution.py:275
  48.9 5.4 %collective-permute-start.14 = (bf16[4,96,128]{2,1,0:T(8,128)(2,1)S(1)}, bf16[4,96,128]{2,1,0:T(8,128)(2,1)S(1)}, u32[]{:S(2)}, u32[]{:S(2)}) collective-permute-start(bf16[4,96,128]{2,1,0:T(8,128)(2,1)S(1)} %get-tuple-element.101), channel_id=1, source_target_pairs={{0,16},{8,24},{16,0},{24,8},{1,17},{9,25},{17,1},{25,9},{2,18},{10... | collective-permute-start | bytes 294920 | tf_op jit(solution)/shard_map/ppermute | solution.py:275
  (5 other events, 11.3 us)

commit v8 on v5

--- a/solution.py
+++ b/solution.py
@@ -757,7 +757,8 @@
     return high + ref[:, model + 1 : model + 2].astype(jnp.float32)
 
 
-def out_kernel(kept_ref, got_ref, own_ref, part_ref, near_ref, wide_out, bf16_out, sums_ref):
+def out_kernel(kept_ref, got_ref, own_ref, part_ref, near_ref, wide_out, *refs):
+    outs, sums_ref = refs[:-1], refs[-1]
     core = lax.axis_index("dp") % 2
     width = part_ref.shape[1]
     rows, model = sums_ref.shape
@@ -773,11 +774,14 @@
         sums_ref[:, pl.ds(at, width)] = own + dot32(got, other_ref[...])
     wide_out[:, 0:model] = sums_ref[0:part, :]
     wide_out[:, model:] = jnp.broadcast_to(squares[0:part], (part, LANES))
-    bf16_out[:, 0:model] = sums_ref[part:, :].astype(jnp.bfloat16)
-    bf16_out[:, model:] = split_squares(squares[part:])
-
-
-def pass_kernel(pass_ref, cross_ref, out_ref):
+    size = part // len(outs)
+    for k, out in enumerate(outs):
+        own = slice(part + k * size, part + (k + 1) * size)
+        out[:, 0:model] = sums_ref[own, :].astype(jnp.bfloat16)
+        out[:, model:] = split_squares(squares[own])
+
+
+def pass_kernel(pass_ref, cross_ref, arrived_ref, out_ref):
     model = out_ref.shape[1] - LANES
     total = pass_ref[:, 0:model] + cross_ref[:, 0:model].astype(jnp.float32)
     out_ref[:, 0:model] = total.astype(jnp.bfloat16)
@@ -785,16 +789,19 @@
     out_ref[:, model:] = split_squares(squares)
 
 
-def finish_kernel(inner_total, hidden_ref, joined_ref, keep_ref, *refs):
-    got, out_ref = refs[:-1], refs[-1]
+def finish_kernel(inner_total, hidden_ref, joined_ref, keep_ref, passed_ref, *refs):
+    nears, out_ref = refs[:-1], refs[-1]
     model = hidden_ref.shape[1]
-    squares = keep_ref[:, model : model + 1]
-    total = keep_ref[:, 0:model]
-    for ref in got:
-        squares = squares + joined_squares(ref, model)
-        total = total + ref[:, 0:model].astype(jnp.float32)
-    scale = lax.rsqrt(squares / inner_total + EPSILON)
-    out_ref[...] = (hidden_ref[...].astype(jnp.float32) + scale * total).astype(jnp.bfloat16)
+    size = nears[0].shape[0]
+    for k, near_ref in enumerate(nears):
+        own = slice(k * size, (k + 1) * size)
+        squares = keep_ref[own, model : model + 1] + joined_squares(near_ref, model)
+        squares = squares + joined_squares(passed_ref.at[own], model)
+        scale = lax.rsqrt(squares / inner_total + EPSILON)
+        total = keep_ref[own, 0:model] + near_ref[:, 0:model].astype(jnp.float32)
+        total = total + passed_ref[own, 0:model].astype(jnp.float32)
+        hidden = hidden_ref[own, :].astype(jnp.float32)
+        out_ref[own, :] = (hidden + scale * total).astype(jnp.bfloat16)
 
 
 def join_kernel(keep_ref, *refs):
@@ -1064,31 +1071,35 @@
     fars = [exchange(send, "dp", 2) for send in sends]
 
     sums_shape = (out_rows, model + LANES)
-    project = pl.pallas_call(
-        out_kernel,
-        name="project_out",
-        out_shape=(shape(sums_shape, f32), shape(sums_shape, bf16)),
-        in_specs=in_vmem(5),
-        out_specs=tuple(in_vmem(2)),
-        scratch_shapes=[pltpu.VMEM((2 * out_rows, model), f32)],
-        compiler_params=kernel_params(8),
-        cost_estimate=LITTLE,
-    )
-    sums_pass, sums_cross = project(kept_first, got_first, scaled_out, out_part, out_near)
-    sums_keep, sums_near = project(kept_rest, got_rest, scaled_out, out_part, out_near)
+
+    def project(kept, got, pieces):
+        piece = (out_rows // pieces, model + LANES)
+        return pl.pallas_call(
+            out_kernel,
+            name="project_out",
+            out_shape=(shape(sums_shape, f32),) + (shape(piece, bf16),) * pieces,
+            in_specs=in_vmem(5),
+            out_specs=tuple(in_vmem(1 + pieces)),
+            scratch_shapes=[pltpu.VMEM((2 * out_rows, model), f32)],
+            compiler_params=kernel_params(8),
+            cost_estimate=LITTLE,
+        )(kept, got, scaled_out, out_part, out_near)
+
+    sums_pass, sums_cross = project(kept_first, got_first, 1)
     cross = exchange(sums_cross, "head", Y_NEAR)
-    cross, sums_near = lax.optimization_barrier((cross, sums_near))
-    sums_near = exchange(sums_near, "head", Y_NEAR)
     passed = pl.pallas_call(
         pass_kernel,
         name="add_sums_to_pass_on",
         out_shape=shape(sums_shape, bf16),
-        in_specs=in_vmem(2),
+        in_specs=in_vmem(2) + [anywhere],
         out_specs=in_vmem(1)[0],
         compiler_params=kernel_params(4),
         cost_estimate=LITTLE,
-    )(sums_pass, cross)
+    )(sums_pass, cross, got_rest)
+    got_rest, passed = lax.optimization_barrier((got_rest, passed))
     passed = exchange(passed, "head", Z_FAR)
+    sums_keep, *sums_near = project(kept_rest, got_rest, 2)
+    sums_near = [exchange(part, "head", Y_NEAR) for part in sums_near]
     request_states, joined = pl.pallas_call(
         join_kernel,
         name="join_request_states",
@@ -1102,11 +1113,11 @@
         functools.partial(finish_kernel, inner * head_count),
         name="scale_and_add_hidden",
         out_shape=shape((out_rows, model), bf16),
-        in_specs=in_vmem(1) + [anywhere] + in_vmem(3),
+        in_specs=in_vmem(1) + [anywhere] + in_vmem(4),
         out_specs=in_vmem(1)[0],
         compiler_params=kernel_params(4),
         cost_estimate=LITTLE,
-    )(own_hidden, joined, sums_keep, sums_near, passed)
+    )(own_hidden, joined, sums_keep, passed, *sums_near)
     return (
         layer_out,
         request_states.reshape(requests, heads, inner // heads, state_width),

time: 56.4 us -> 56.5 us (level)
  starting transfers between devices: 24.6 us -> 25.5 us
  waiting for transfers between devices: 11.2 us -> 10.3 us
    ppermute x22 -> x23, waiting for transfers between devices: 11.2 us -> 10.3 us  [exchange(): lax.ppermute(values, axis, [(i, i ^ bits) for i in range(lax.axis_size(ax...]
    ppermute x22 -> x23, starting transfers between devices: 22.2 us -> 23.1 us  [exchange(): lax.ppermute(values, axis, [(i, i ^ bits) for i in range(lax.axis_size(ax...]
  transfers between devices with their start and end apart: 23 -> 24, of which waited for: 9 -> 10; matrix products, arithmetic and copies ran while one was open for 0% -> 0% of each run, Pallas kernels for 28% -> 29%
where the time goes in v8:
time: 56.5 us; the launch traced here: 56.3 us
  starting transfers between devices  25.5 us (45%)
  Pallas kernels  19.5 us (35%)
  waiting for transfers between devices  10.3 us (18%)
  between operations  0.96 us (2%)
    ppermute x23, starting transfers between devices, exchange(): lax.ppermute(values, axis, [(i, i ^ bits) for i in range(lax.axis_size(ax...  23.1 us
    ppermute x23, waiting for transfers between devices, exchange(): lax.ppermute(values, axis, [(i, i ^ bits) for i in range(lax.axis_size(ax...  10.3 us
    pallas_call x1, Pallas kernels, fused_on_device(): pl.pallas_call(inner_kernel, name='project_and_convolve_x', out_shape=(sh...  2.64 us
    ppermute x1, starting transfers between devices, fused_on_device(): lax.ppermute(leaving, 'dp', [(i, i + 1) for i in range(peers - 1)])  2.41 us
    pallas_call x1, Pallas kernels, fused_on_device(): pl.pallas_call(first_kernel, name='project_b_c_and_steps', out_shape=(sha...  2.29 us
    pallas_call x1, Pallas kernels, fused_on_device(): pl.pallas_call(local_kernel, name='mix_within_blocks', out_shape=shape((t...  2.16 us
    pallas_call x1, Pallas kernels, fused_on_device(): pl.pallas_call(pack_first_kernel, name='pack_first_weights', out_shape=sh...  1.95 us
    pallas_call x1, Pallas kernels, fused_on_device(): pl.pallas_call(table_kernel, name='sum_ended_states', out_shape=(shape((P...  1.57 us
  transfers between devices with their start and end apart: 24, of which 10 were waited for; matrix products, arithmetic and copies ran while one was open for 0% of the time, Pallas kernels for 29%

profile of v8, /device:TPU:0, one launch (start us, length us, event | category | flops | bytes accessed | tf_op | source)
XLA Modules:
  0.0 56.3 jit_solution(14254199995274330095)
XLA Ops:
  0.7 2.0 %pack_first_weights.1.own_ref = bf16[480,256]{1,0:T(8,128)(2,1)} custom-call(s32[1,4]{1,0:T(1,128)} %bitcast.5, f32[384,256]{1,0:T(8,128)} %wbc_ref.1, f32[6,384]{1,0:T(8,128)} %bitcast.6, bf16[512,1536]{1,0:T(8,128)(2,1)} %hidden_ref.1), custom_call_target="tpu_custom_call" | custom-call | flops 1000 | bytes 1000 | tf_op jit(solution)/shard_map/pack_first_weights/pallas_call | solution.py:848
  3.1 2.6 %collective-permute-start = (bf16[480,256]{1,0:T(8,128)(2,1)}, bf16[480,256]{1,0:T(8,128)(2,1)S(1)}, u32[]{:S(2)}, u32[]{:S(2)}) collective-permute-start(bf16[480,256]{1,0:T(8,128)(2,1)} %pack_first_weights.1.own_ref), channel_id=1, source_target_pairs={{0,16},{8,24},{16,0},{24,8},{1,17},{9,25},{17,1},{25,9},{2,18},{10... | collective-permute-start | bytes 737288 | tf_op jit(solution)/shard_map/ppermute | solution.py:275
  6.2 1.6 %collective-permute-start.16 = (bf16[384,768]{1,0:T(8,128)(2,1)S(1)}, bf16[384,768]{1,0:T(8,128)(2,1)S(1)}, u32[]{:S(2)}, u32[]{:S(2)}) collective-permute-start(bf16[384,768]{1,0:T(8,128)(2,1)S(1)} %get-tuple-element.106), channel_id=1, source_target_pairs={{0,2},{1,3},{2,0},{3,1},{4,6},{5,7},{6,4},{7,5},{8,10},{9,11},{10,... | collective-permute-start | bytes 1769480 | tf_op jit(solution)/shard_map/ppermute | solution.py:275
  9.0 1.2 %norm_and_token_facts.1 = (bf16[512,1536]{1,0:T(8,128)(2,1)S(1)}, f32[512,128]{1,0:T(8,128)S(1)}, bf16[1024,512]{1,0:T(8,128)(2,1)S(1)}, f32[2,256,256]{2,1,0:T(8,128)S(1)}, bf16[64,1536]{1,0:T(8,128)(2,1)S(1)}) custom-call(s32[1,2048]{1,0:T(1,128)S(1)} %bitcast.4, bf16[512,1536]{1,0:T(8,128)(2,1)S(1)} %copy-done, f32[1,1536]{1,0:T(1,128)S(1)} %broadcast_in_dim.14.gain_ref), custom_call_target="tpu_custom_call" | custom-call | flops 1000 | bytes 1000 | tf_op jit(solution)/shard_map/norm_and_token_facts/pallas_call | solution.py:882
  10.3 0.6 %project_b_c_and_steps_of_chip.1 = (f32[512,256]{1,0:T(8,128)S(1)}, f32[512,128]{1,0:T(8,128)S(1)}) custom-call(bf16[512,1536]{1,0:T(8,128)(2,1)S(1)} %get-tuple-element.62.normed_ref, bf16[480,256]{1,0:T(8,128)(2,1)S(1)} %copy-done.1, bf16[480,256]{1,0:T(8,128)(2,1)S(1)} %collective-permute-done.1.near_ref), custom_call_target="tpu_custom_call" | custom-call | flops 1000 | bytes 1000 | tf_op jit(solution)/shard_map/project_b_c_and_steps_of_chip/pallas_call | solution.py:911
  11.0 1.7 %collective-permute-done.far_ref = bf16[480,256]{1,0:T(8,128)(2,1)S(1)} collective-permute-done((bf16[480,256]{1,0:T(8,128)(2,1)}, bf16[480,256]{1,0:T(8,128)(2,1)S(1)}, u32[]{:S(2)}, u32[]{:S(2)}) %collective-permute-start) | collective-permute-done | bytes 245792 | tf_op jit(solution)/shard_map/ppermute | solution.py:275
  13.2 1.0 %collective-permute-done.3.last_ref = bf16[480,256]{1,0:T(8,128)(2,1)S(1)} collective-permute-done((bf16[480,256]{1,0:T(8,128)(2,1)S(1)}, bf16[480,256]{1,0:T(8,128)(2,1)S(1)}, u32[]{:S(2)}, u32[]{:S(2)}) %collective-permute-start.3) | collective-permute-done | bytes 245792 | tf_op jit(solution)/shard_map/ppermute | solution.py:275
  14.2 2.3 %project_b_c_and_steps.1 = (bf16[512,256]{1,0:T(8,128)(2,1)S(1)}, f32[512,128]{1,0:T(8,128)S(1)}, f32[512,128]{1,0:T(8,128)S(1)}, f32[512,128]{1,0:T(8,128)S(1)}, bf16[16,1536]{1,0:T(8,128)(2,1)S(1)}) custom-call(bf16[512,1536]{1,0:T(8,128)(2,1)S(1)} %get-tuple-element.62.normed_ref, f32[512,256]{1,0:T(8,128)S(1)} %get-tuple-element.72.most_ref, ...), custom_call_target="tpu_custom_call" | custom-call | flops 1000 | bytes 1000 | tf_op jit(solution)/shard_map/project_b_c_and_steps/pallas_call | solution.py:927
  16.5 2.2 %collective-permute-done.2.far_ref = bf16[384,384]{1,0:T(8,128)(2,1)S(1)} collective-permute-done((bf16[384,384]{1,0:T(8,128)(2,1)S(1)}, bf16[384,384]{1,0:T(8,128)(2,1)S(1)}, u32[]{:S(2)}, u32[]{:S(2)}) %collective-permute-start.2) | collective-permute-done | bytes 294944 | tf_op jit(solution)/shard_map/ppermute | solution.py:275
  19.3 1.8 %collective-permute-start.6 = (bf16[384,384]{1,0:T(8,128)(2,1)S(1)}, bf16[384,384]{1,0:T(8,128)(2,1)S(1)}, u32[]{:S(2)}, u32[]{:S(2)}) collective-permute-start(bf16[384,384]{1,0:T(8,128)(2,1)S(1)} %get-tuple-element.89.own_ref), channel_id=1, source_target_pairs={{0,16},{8,24},{16,0},{24,8},{1,17},{9,25},{17,1},{25,9},{2,18},{10... | collective-permute-start | bytes 884744 | tf_op jit(solution)/shard_map/ppermute | solution.py:275
  21.1 0.6 %collective-permute-done.16.part_ref = bf16[384,768]{1,0:T(8,128)(2,1)S(1)} collective-permute-done((bf16[384,768]{1,0:T(8,128)(2,1)S(1)}, bf16[384,768]{1,0:T(8,128)(2,1)S(1)}, u32[]{:S(2)}, u32[]{:S(2)}) %collective-permute-start.16) | collective-permute-done | bytes 589856 | tf_op jit(solution)/shard_map/ppermute | solution.py:275
  21.7 2.6 %project_and_convolve_x.1 = (bf16[512,384]{1,0:T(8,128)(2,1)S(1)}, bf16[512,384]{1,0:T(8,128)(2,1)S(1)}, bf16[384,512]{1,0:T(8,128)(2,1)S(1)}, bf16[384,128]{1,0:T(8,128)(2,1)S(1)}) custom-call(bf16[512,1536]{1,0:T(8,128)(2,1)S(1)} %get-tuple-element.62.normed_ref, bf16[384,384]{1,0:T(8,128)(2,1)S(1)} %get-tuple-element.82.own_ref, ...), custom_call_target="tpu_custom_call" | custom-call | flops 1000 | bytes 1000 | tf_op jit(solution)/shard_map/project_and_convolve_x/pallas_call | solution.py:966
  24.3 2.4 %collective-permute-start.8 = (bf16[384,128]{1,0:T(8,128)(2,1)S(1)}, bf16[384,128]{1,0:T(8,128)(2,1)S(1)}, u32[]{:S(2)}, u32[]{:S(2)}) collective-permute-start(bf16[384,128]{1,0:T(8,128)(2,1)S(1)} %get-tuple-element.90), channel_id=1, source_target_pairs={{0,8},{8,16},{16,24},{1,9},{9,17},{17,25},{2,10},{10,18},{18,26},{... | collective-permute-start | bytes 294920 | tf_op jit(solution)/shard_map/ppermute | solution.py:998
  26.8 2.2 %mix_within_blocks.1.y_ref = f32[512,384]{1,0:T(8,128)S(1)} custom-call(bf16[512,384]{1,0:T(8,128)(2,1)S(1)} %get-tuple-element.91.x_ref, bf16[512,256]{1,0:T(8,128)(2,1)S(1)} %get-tuple-element.81.bc_ref, bf16[512,384]{1,0:T(8,128)(2,1)S(1)} %get-tuple-element.92.stepx_ref, f32[512,128]{1,0:T(8,128)S(1)} %get-tuple-element.88.prefix_ref, ...), custom_call_target="tpu_custom_call" | custom-call | flops 1000 | bytes 1000 | tf_op jit(solution)/shard_map/mix_within_blocks/pallas_call | solution.py:1000
  29.1 0.9 %project_gate_most.1.most_ref = f32[512,384]{1,0:T(8,128)S(1)} custom-call(bf16[512,1536]{1,0:T(8,128)(2,1)S(1)} %get-tuple-element.62.normed_ref, bf16[384,384]{1,0:T(8,128)(2,1)S(1)} %get-tuple-element.89.own_ref, bf16[384,384]{1,0:T(8,128)(2,1)S(1)} %collective-permute-done.7.near_ref, bf16[384,384]{1,0:T(8,128)(2,1)S(1)} %collective-permute-done.6.far_ref), custom_call_target="tpu_custom_call" | custom-call | flops 1000 | bytes 1000 | tf_op jit(solution)/shard_map/project_gate_most/pallas_call | solution.py:1024
  29.9 0.7 %collective-permute-done.15.last_ref = bf16[384,384]{1,0:T(8,128)(2,1)S(1)} collective-permute-done((bf16[384,384]{1,0:T(8,128)(2,1)S(1)}, bf16[384,384]{1,0:T(8,128)(2,1)S(1)}, u32[]{:S(2)}, u32[]{:S(2)}) %collective-permute-start.15) | collective-permute-done | bytes 294944 | tf_op jit(solution)/shard_map/ppermute | solution.py:275
  31.1 0.6 %add_entering_and_gate.1 = (bf16[128,384]{1,0:T(8,128)(2,1)S(1)}, bf16[128,384]{1,0:T(8,128)(2,1)S(1)}, bf16[128,384]{1,0:T(8,128)(2,1)S(1)}, bf16[128,384]{1,0:T(8,128)(2,1)S(1)}) custom-call(bf16[384,128]{1,0:T(8,128)(2,1)S(1)} %collective-permute-done.8.enter_ref, bf16[512,256]{1,0:T(8,128)(2,1)S(1)} %get-tuple-element.81.bc_ref, ...), custom_call_target="tpu_custom_call" | custom-call | flops 1000 | bytes 1000 | tf_op jit(solution)/shard_map/add_entering_and_gate/pallas_call | solution.py:1044
  31.7 1.6 %collective-permute-start.19 = (bf16[128,384]{1,0:T(8,128)(2,1)S(1)}, bf16[128,384]{1,0:T(8,128)(2,1)S(1)}, u32[]{:S(2)}, u32[]{:S(2)}) collective-permute-start(bf16[128,384]{1,0:T(8,128)(2,1)S(1)} %get-tuple-element.110), channel_id=1, source_target_pairs={{0,2},{1,3},{2,0},{3,1},{4,6},{5,7},{6,4},{7,5},{8,10},{9,11},{10,... | collective-permute-start | bytes 294920 | tf_op jit(solution)/shard_map/ppermute | solution.py:275
  33.3 1.6 %sum_ended_states.1 = (bf16[8,96,128]{2,1,0:T(8,128)(2,1)S(1)}, bf16[8,96,128]{2,1,0:T(8,128)(2,1)S(1)}, bf16[8,96,128]{2,1,0:T(8,128)(2,1)S(1)}, bf16[8,96,128]{2,1,0:T(8,128)(2,1)S(1)}) custom-call(s32[2048]{0:T(1024)S(1)} %copy-done.4, bf16[512,256]{1,0:T(8,128)(2,1)S(1)} %get-tuple-element.81.bc_ref, bf16[384,512]{1,0:T(8,128)(2,1)S(1)} %get-tuple-element.87.faded_ref, ...), custom_call_target="tpu_custom_call" | custom-call | flops 1000 | bytes 1000 | tf_op jit(solution)/shard_map/sum_ended_states/pallas_call | solution.py:1013
  36.0 0.6 %collective-permute-done.19.got_ref = bf16[128,384]{1,0:T(8,128)(2,1)S(1)} collective-permute-done((bf16[128,384]{1,0:T(8,128)(2,1)S(1)}, bf16[128,384]{1,0:T(8,128)(2,1)S(1)}, u32[]{:S(2)}, u32[]{:S(2)}) %collective-permute-start.19) | collective-permute-done | bytes 98336 | tf_op jit(solution)/shard_map/ppermute | solution.py:275
  36.6 0.6 %project_out.2 = (f32[64,1664]{1,0:T(8,128)S(1)}, bf16[64,1664]{1,0:T(8,128)(2,1)S(1)}) custom-call(bf16[128,384]{1,0:T(8,128)(2,1)S(1)} %get-tuple-element.109.kept_ref, bf16[128,384]{1,0:T(8,128)(2,1)S(1)} %collective-permute-done.19.got_ref, bf16[384,1536]{1,0:T(8,128)(2,1)S(1)} %get-tuple-element.111.own_ref, ...), custom_call_target="tpu_custom_call" | custom-call | flops 1000 | bytes 1000 | tf_op jit(solution)/shard_map/project_out/pallas_call | solution.py:1077
  37.2 1.6 %collective-permute-start.20 = (bf16[64,1664]{1,0:T(8,128)(2,1)S(1)}, bf16[64,1664]{1,0:T(8,128)(2,1)S(1)}, u32[]{:S(2)}, u32[]{:S(2)}) collective-permute-start(bf16[64,1664]{1,0:T(8,128)(2,1)S(1)} %get-tuple-element.113), channel_id=1, source_target_pairs={{0,1},{1,0},{2,3},{3,2},{4,5},{5,4},{6,7},{7,6},{8,9},{9,8},{10,11... | collective-permute-start | bytes 638984 | tf_op jit(solution)/shard_map/ppermute | solution.py:275
  38.8 1.6 %collective-permute-start.18 = (bf16[128,384]{1,0:T(8,128)(2,1)S(1)}, bf16[128,384]{1,0:T(8,128)(2,1)S(1)}, u32[]{:S(2)}, u32[]{:S(2)}) collective-permute-start(bf16[128,384]{1,0:T(8,128)(2,1)S(1)} %get-tuple-element.108), channel_id=1, source_target_pairs={{0,2},{1,3},{2,0},{3,1},{4,6},{5,7},{6,4},{7,5},{8,10},{9,11},{10,... | collective-permute-start | bytes 294920 | tf_op jit(solution)/shard_map/ppermute | solution.py:275
  40.4 0.9 %pick_request_states.1 = (bf16[4,384,128]{2,1,0:T(8,128)(2,1)S(1)}, bf16[4,288,128]{2,1,0:T(8,128)(2,1)S(1)}, bf16[4,96,128]{2,1,0:T(8,128)(2,1)S(1)}) custom-call(s32[4]{0:T(128)S(1)} %copy-done.7, bf16[480,256]{1,0:T(8,128)(2,1)S(1)} %collective-permute-done.far_ref, bf16[8,96,128]{2,1,0:T(8,128)(2,1)S(1)} %get-tuple-element.95.refs_0_, ...), custom_call_target="tpu_custom_call" | custom-call | flops 1000 | bytes 1000 | tf_op jit(solution)/shard_map/pick_request_states/pallas_call | solution.py:1059
  41.3 2.0 %collective-permute-start.13 = (bf16[4,288,128]{2,1,0:T(8,128)(2,1)S(1)}, bf16[4,288,128]{2,1,0:T(8,128)(2,1)S(1)}, u32[]{:S(2)}, u32[]{:S(2)}) collective-permute-start(bf16[4,288,128]{2,1,0:T(8,128)(2,1)S(1)} %get-tuple-element.100), channel_id=1, source_target_pairs={{0,16},{8,24},{16,0},{24,8},{1,17},{9,25},{17,1},{25,9},{2,18},{10... | collective-permute-start | bytes 884744 | tf_op jit(solution)/shard_map/ppermute | solution.py:275
  44.1 2.7 %collective-permute-start.21 = (bf16[64,1664]{1,0:T(8,128)(2,1)S(1)}, bf16[64,1664]{1,0:T(8,128)(2,1)S(1)}, u32[]{:S(2)}, u32[]{:S(2)}) collective-permute-start(bf16[64,1664]{1,0:T(8,128)(2,1)S(1)} %add_sums_to_pass_on.1), channel_id=1, source_target_pairs={{0,4},{1,5},{2,6},{3,7},{4,0},{5,1},{6,2},{7,3},{8,12},{9,13},{10,... | collective-permute-start | bytes 638984 | tf_op jit(solution)/shard_map/ppermute | solution.py:275
  46.8 0.6 %project_out.3 = (f32[64,1664]{1,0:T(8,128)S(1)}, bf16[32,1664]{1,0:T(8,128)(2,1)S(1)}, bf16[32,1664]{1,0:T(8,128)(2,1)S(1)}) custom-call(bf16[128,384]{1,0:T(8,128)(2,1)S(1)} %get-tuple-element.107.kept_ref, bf16[128,384]{1,0:T(8,128)(2,1)S(1)} %collective-permute-done.18.arrived_ref.got_ref, bf16[384,1536]{1,0:T(8,128)(2,1)S(1)} %get-tuple-element.111.own_ref, ...), custom_call_target="tpu_custom_call" | custom-call | flops 1000 | bytes 1000 | tf_op jit(solution)/shard_map/project_out/pallas_call | solution.py:1077
  47.4 1.6 %collective-permute-start.22 = (bf16[32,1664]{1,0:T(8,128)(2,1)S(1)}, bf16[32,1664]{1,0:T(8,128)(2,1)S(1)}, u32[]{:S(2)}, u32[]{:S(2)}) collective-permute-start(bf16[32,1664]{1,0:T(8,128)(2,1)S(1)} %get-tuple-element.117), channel_id=1, source_target_pairs={{0,1},{1,0},{2,3},{3,2},{4,5},{5,4},{6,7},{7,6},{8,9},{9,8},{10,11... | collective-permute-start | bytes 319496 | tf_op jit(solution)/shard_map/ppermute | solution.py:275
  49.5 2.2 %collective-permute-start.14 = (bf16[4,96,128]{2,1,0:T(8,128)(2,1)S(1)}, bf16[4,96,128]{2,1,0:T(8,128)(2,1)S(1)}, u32[]{:S(2)}, u32[]{:S(2)}) collective-permute-start(bf16[4,96,128]{2,1,0:T(8,128)(2,1)S(1)} %get-tuple-element.101), channel_id=1, source_target_pairs={{0,16},{8,24},{16,0},{24,8},{1,17},{9,25},{17,1},{25,9},{2,18},{10... | collective-permute-start | bytes 294920 | tf_op jit(solution)/shard_map/ppermute | solution.py:275
  51.7 2.6 %collective-permute-done.14.refs_1_ = bf16[4,96,128]{2,1,0:T(8,128)(2,1)S(1)} collective-permute-done((bf16[4,96,128]{2,1,0:T(8,128)(2,1)S(1)}, bf16[4,96,128]{2,1,0:T(8,128)(2,1)S(1)}, u32[]{:S(2)}, u32[]{:S(2)}) %collective-permute-start.14) | collective-permute-done | bytes 98336 | tf_op jit(solution)/shard_map/ppermute | solution.py:275
  54.3 1.0 %join_request_states.1 = (f32[4,384,128]{2,1,0:T(8,128)}, f32[8,128]{1,0:T(8,128)S(1)}) custom-call(bf16[4,384,128]{2,1,0:T(8,128)(2,1)S(1)} %get-tuple-element.99.keep_ref, bf16[4,288,128]{2,1,0:T(8,128)(2,1)S(1)} %collective-permute-done.13.refs_0_, bf16[4,96,128]{2,1,0:T(8,128)(2,1)S(1)} %collective-permute-done.14.refs_1_), custom_call_target="tpu_custom_call" | custom-call | flops 1000 | bytes 1000 | tf_op jit(solution)/shard_map/join_request_states/pallas_call | solution.py:1103
  55.4 0.9 %scale_and_add_hidden.1 = bf16[64,1536]{1,0:T(8,128)(2,1)} custom-call(bf16[64,1536]{1,0:T(8,128)(2,1)S(1)} %get-tuple-element.61.hidden_ref, f32[8,128]{1,0:T(8,128)S(1)} %get-tuple-element.102.joined_ref, f32[64,1664]{1,0:T(8,128)S(1)} %get-tuple-element.115.keep_ref, bf16[64,1664]{1,0:T(8,128)(2,1)S(1)} %collective-permute-done.21.passed_ref, ...), custom_call_target="tpu_custom_call" | custom-call | flops 1000 | bytes 1000 | tf_op jit(solution)/shard_map/scale_and_add_hidden/pallas_call | solution.py:1112
  (62 shorter events, 6.3 us)
Async XLA Ops:
  0.6 5.1 %copy-start.12 = (f32[384]{0:T(512)S(1)}, f32[384]{0:T(512)}, u32[]{:S(2)}) copy-start(f32[384]{0:T(512)} %param.26) | copy-start | bytes 4612
  0.6 5.1 %copy-start.2 = (bf16[384,1536]{1,0:T(8,128)(2,1)S(1)}, bf16[384,1536]{1,0:T(8,128)(2,1)}, u32[]{:S(2)}) copy-start(bf16[384,1536]{1,0:T(8,128)(2,1)} %w_ref.1) | copy-start | bytes 3538948
  0.7 7.2 %copy-start.3 = (f32[384,2,384]{2,1,0:T(2,128)S(1)}, f32[384,2,384]{2,1,0:T(2,128)}, u32[]{:S(2)}) copy-start(f32[384,2,384]{2,1,0:T(2,128)} %wzx_ref.1) | copy-start | bytes 3538948
  2.6 7.7 %collective-permute-start.1 = (bf16[480,256]{1,0:T(8,128)(2,1)}, bf16[480,256]{1,0:T(8,128)(2,1)S(1)}, u32[]{:S(2)}, u32[]{:S(2)}) collective-permute-start(bf16[480,256]{1,0:T(8,128)(2,1)} %pack_first_weights.1.own_ref), channel_id=1, source_target_pairs={{0,8},{8,0},{16,24},{24,16},{1,9},{9,1},{17,25},{25,17},{2,10},{10... | collective-permute-start | bytes 737288 | tf_op jit(solution)/shard_map/ppermute | solution.py:275
  3.1 9.6 %collective-permute-start = (bf16[480,256]{1,0:T(8,128)(2,1)}, bf16[480,256]{1,0:T(8,128)(2,1)S(1)}, u32[]{:S(2)}, u32[]{:S(2)}) collective-permute-start(bf16[480,256]{1,0:T(8,128)(2,1)} %pack_first_weights.1.own_ref), channel_id=1, source_target_pairs={{0,16},{8,24},{16,0},{24,8},{1,17},{9,25},{17,1},{25,9},{2,18},{10... | collective-permute-start | bytes 737288 | tf_op jit(solution)/shard_map/ppermute | solution.py:275
  6.2 4.1 %copy-start.1 = (bf16[480,256]{1,0:T(8,128)(2,1)S(1)}, bf16[480,256]{1,0:T(8,128)(2,1)}, u32[]{:S(2)}) copy-start(bf16[480,256]{1,0:T(8,128)(2,1)} %pack_first_weights.1.own_ref) | copy-start | bytes 737284
  6.2 15.5 %collective-permute-start.16 = (bf16[384,768]{1,0:T(8,128)(2,1)S(1)}, bf16[384,768]{1,0:T(8,128)(2,1)S(1)}, u32[]{:S(2)}, u32[]{:S(2)}) collective-permute-start(bf16[384,768]{1,0:T(8,128)(2,1)S(1)} %get-tuple-element.106), channel_id=1, source_target_pairs={{0,2},{1,3},{2,0},{3,1},{4,6},{5,7},{6,4},{7,5},{8,10},{9,11},{10,... | collective-permute-start | bytes 1769480 | tf_op jit(solution)/shard_map/ppermute | solution.py:275
  8.4 10.4 %collective-permute-start.2 = (bf16[384,384]{1,0:T(8,128)(2,1)S(1)}, bf16[384,384]{1,0:T(8,128)(2,1)S(1)}, u32[]{:S(2)}, u32[]{:S(2)}) collective-permute-start(bf16[384,384]{1,0:T(8,128)(2,1)S(1)} %get-tuple-element.82.own_ref), channel_id=1, source_target_pairs={{0,16},{8,24},{16,0},{24,8},{1,17},{9,25},{17,1},{25,9},{2,18},{10... | collective-permute-start | bytes 884744 | tf_op jit(solution)/shard_map/ppermute | solution.py:275
  10.3 4.0 %copy-start.6 = (f32[4,256]{1,0:T(4,128)S(1)}, f32[4,256]{1,0:T(4,128)}, u32[]{:S(2)}) copy-start(f32[4,256]{1,0:T(4,128)} %taps_ref.2) | copy-start | bytes 12292
  10.3 3.9 %copy-start.8 = (f32[6]{0:T(128)S(1)}, f32[6]{0:T(128)}, u32[]{:S(2)}) copy-start(f32[6]{0:T(128)} %bias_ref.1) | copy-start | bytes 76
  12.7 9.0 %copy-start.5 = (f32[4,384]{1,0:T(4,128)S(1)}, f32[4,384]{1,0:T(4,128)}, u32[]{:S(2)}) copy-start(f32[4,384]{1,0:T(4,128)} %taps_ref.3) | copy-start | bytes 18436
  12.7 1.5 %collective-permute-start.3 = (bf16[480,256]{1,0:T(8,128)(2,1)S(1)}, bf16[480,256]{1,0:T(8,128)(2,1)S(1)}, u32[]{:S(2)}, u32[]{:S(2)}) collective-permute-start(bf16[480,256]{1,0:T(8,128)(2,1)S(1)} %collective-permute-done.far_ref), channel_id=1, source_target_pairs={{0,8},{8,0},{16,24},{24,16},{1,9},{9,1},{17,25},{25,17},{2,10},{10... | collective-permute-start | bytes 737288 | tf_op jit(solution)/shard_map/ppermute | solution.py:275
  12.7 9.0 %collective-permute-start.4 = (bf16[384,384]{1,0:T(8,128)(2,1)S(1)}, bf16[384,384]{1,0:T(8,128)(2,1)S(1)}, u32[]{:S(2)}, u32[]{:S(2)}) collective-permute-start(bf16[384,384]{1,0:T(8,128)(2,1)S(1)} %get-tuple-element.82.own_ref), channel_id=1, source_target_pairs={{0,8},{8,0},{16,24},{24,16},{1,9},{9,1},{17,25},{25,17},{2,10},{10... | collective-permute-start | bytes 884744 | tf_op jit(solution)/shard_map/ppermute | solution.py:275
  18.8 8.0 %copy-start.10 = (f32[6]{0:T(128)S(1)}, f32[6]{0:T(128)}, u32[]{:S(2)}) copy-start(f32[6]{0:T(128)} %skip_ref.1) | copy-start | bytes 76
  18.8 2.9 %collective-permute-start.5 = (bf16[384,384]{1,0:T(8,128)(2,1)S(1)}, bf16[384,384]{1,0:T(8,128)(2,1)S(1)}, u32[]{:S(2)}, u32[]{:S(2)}) collective-permute-start(bf16[384,384]{1,0:T(8,128)(2,1)S(1)} %collective-permute-done.2.far_ref), channel_id=1, source_target_pairs={{0,8},{8,0},{16,24},{24,16},{1,9},{9,1},{17,25},{25,17},{2,10},{10... | collective-permute-start | bytes 884744 | tf_op jit(solution)/shard_map/ppermute | solution.py:275
  18.8 10.2 %collective-permute-start.7 = (bf16[384,384]{1,0:T(8,128)(2,1)S(1)}, bf16[384,384]{1,0:T(8,128)(2,1)S(1)}, u32[]{:S(2)}, u32[]{:S(2)}) collective-permute-start(bf16[384,384]{1,0:T(8,128)(2,1)S(1)} %get-tuple-element.89.own_ref), channel_id=1, source_target_pairs={{0,8},{8,0},{16,24},{24,16},{1,9},{9,1},{17,25},{25,17},{2,10},{10... | collective-permute-start | bytes 884744 | tf_op jit(solution)/shard_map/ppermute | solution.py:275
  19.3 9.7 %collective-permute-start.6 = (bf16[384,384]{1,0:T(8,128)(2,1)S(1)}, bf16[384,384]{1,0:T(8,128)(2,1)S(1)}, u32[]{:S(2)}, u32[]{:S(2)}) collective-permute-start(bf16[384,384]{1,0:T(8,128)(2,1)S(1)} %get-tuple-element.89.own_ref), channel_id=1, source_target_pairs={{0,16},{8,24},{16,0},{24,8},{1,17},{9,25},{17,1},{25,9},{2,18},{10... | collective-permute-start | bytes 884744 | tf_op jit(solution)/shard_map/ppermute | solution.py:275
  21.7 9.4 %collective-permute-start.17 = (bf16[384,768]{1,0:T(8,128)(2,1)S(1)}, bf16[384,768]{1,0:T(8,128)(2,1)S(1)}, u32[]{:S(2)}, u32[]{:S(2)}) collective-permute-start(bf16[384,768]{1,0:T(8,128)(2,1)S(1)} %collective-permute-done.16.part_ref), channel_id=1, source_target_pairs={{0,8},{8,0},{16,24},{24,16},{1,9},{9,1},{17,25},{25,17},{2,10},{10... | collective-permute-start | bytes 1769480 | tf_op jit(solution)/shard_map/ppermute | solution.py:275
  24.3 4.6 %collective-permute-start.8 = (bf16[384,128]{1,0:T(8,128)(2,1)S(1)}, bf16[384,128]{1,0:T(8,128)(2,1)S(1)}, u32[]{:S(2)}, u32[]{:S(2)}) collective-permute-start(bf16[384,128]{1,0:T(8,128)(2,1)S(1)} %get-tuple-element.90), channel_id=1, source_target_pairs={{0,8},{8,16},{16,24},{1,9},{9,17},{17,25},{2,10},{10,18},{18,26},{... | collective-permute-start | bytes 294920 | tf_op jit(solution)/shard_map/ppermute | solution.py:998
  29.0 1.6 %collective-permute-start.15 = (bf16[384,384]{1,0:T(8,128)(2,1)S(1)}, bf16[384,384]{1,0:T(8,128)(2,1)S(1)}, u32[]{:S(2)}, u32[]{:S(2)}) collective-permute-start(bf16[384,384]{1,0:T(8,128)(2,1)S(1)} %collective-permute-done.6.far_ref), channel_id=1, source_target_pairs={{0,8},{8,0},{16,24},{24,16},{1,9},{9,1},{17,25},{25,17},{2,10},{10... | collective-permute-start | bytes 884744 | tf_op jit(solution)/shard_map/ppermute | solution.py:275
  31.7 4.9 %collective-permute-start.19 = (bf16[128,384]{1,0:T(8,128)(2,1)S(1)}, bf16[128,384]{1,0:T(8,128)(2,1)S(1)}, u32[]{:S(2)}, u32[]{:S(2)}) collective-permute-start(bf16[128,384]{1,0:T(8,128)(2,1)S(1)} %get-tuple-element.110), channel_id=1, source_target_pairs={{0,2},{1,3},{2,0},{3,1},{4,6},{5,7},{6,4},{7,5},{8,10},{9,11},{10,... | collective-permute-start | bytes 294920 | tf_op jit(solution)/shard_map/ppermute | solution.py:275
  34.9 3.9 %collective-permute-start.10 = (bf16[8,96,128]{2,1,0:T(8,128)(2,1)S(1)}, bf16[8,96,128]{2,1,0:T(8,128)(2,1)S(1)}, u32[]{:S(2)}, u32[]{:S(2)}) collective-permute-start(bf16[8,96,128]{2,1,0:T(8,128)(2,1)S(1)} %get-tuple-element.96.refs_1_), channel_id=1, source_target_pairs={{0,8},{8,0},{16,24},{24,16},{1,9},{9,1},{17,25},{25,17},{2,10},{10... | collective-permute-start | bytes 589832 | tf_op jit(solution)/shard_map/ppermute | solution.py:275
  35.1 5.3 %collective-permute-start.11 = (bf16[8,96,128]{2,1,0:T(8,128)(2,1)S(1)}, bf16[8,96,128]{2,1,0:T(8,128)(2,1)S(1)}, u32[]{:S(2)}, u32[]{:S(2)}) collective-permute-start(bf16[8,96,128]{2,1,0:T(8,128)(2,1)S(1)} %get-tuple-element.97.refs_2_), channel_id=1, source_target_pairs={{0,8},{8,0},{16,24},{24,16},{1,9},{9,1},{17,25},{25,17},{2,10},{10... | collective-permute-start | bytes 589832 | tf_op jit(solution)/shard_map/ppermute | solution.py:275
  35.5 4.9 %collective-permute-start.12 = (bf16[8,96,128]{2,1,0:T(8,128)(2,1)S(1)}, bf16[8,96,128]{2,1,0:T(8,128)(2,1)S(1)}, u32[]{:S(2)}, u32[]{:S(2)}) collective-permute-start(bf16[8,96,128]{2,1,0:T(8,128)(2,1)S(1)} %get-tuple-element.98.refs_3_), channel_id=1, source_target_pairs={{0,8},{8,0},{16,24},{24,16},{1,9},{9,1},{17,25},{25,17},{2,10},{10... | collective-permute-start | bytes 589832 | tf_op jit(solution)/shard_map/ppermute | solution.py:275
  35.6 4.8 %collective-permute-start.9 = (bf16[8,96,128]{2,1,0:T(8,128)(2,1)S(1)}, bf16[8,96,128]{2,1,0:T(8,128)(2,1)S(1)}, u32[]{:S(2)}, u32[]{:S(2)}) collective-permute-start(bf16[8,96,128]{2,1,0:T(8,128)(2,1)S(1)} %get-tuple-element.95.refs_0_), channel_id=1, source_target_pairs={{0,8},{8,0},{16,24},{24,16},{1,9},{9,1},{17,25},{25,17},{2,10},{10... | collective-permute-start | bytes 589832 | tf_op jit(solution)/shard_map/ppermute | solution.py:275
  37.2 6.7 %collective-permute-start.20 = (bf16[64,1664]{1,0:T(8,128)(2,1)S(1)}, bf16[64,1664]{1,0:T(8,128)(2,1)S(1)}, u32[]{:S(2)}, u32[]{:S(2)}) collective-permute-start(bf16[64,1664]{1,0:T(8,128)(2,1)S(1)} %get-tuple-element.113), channel_id=1, source_target_pairs={{0,1},{1,0},{2,3},{3,2},{4,5},{5,4},{6,7},{7,6},{8,9},{9,8},{10,11... | collective-permute-start | bytes 638984 | tf_op jit(solution)/shard_map/ppermute | solution.py:275
  38.8 4.6 %collective-permute-start.18 = (bf16[128,384]{1,0:T(8,128)(2,1)S(1)}, bf16[128,384]{1,0:T(8,128)(2,1)S(1)}, u32[]{:S(2)}, u32[]{:S(2)}) collective-permute-start(bf16[128,384]{1,0:T(8,128)(2,1)S(1)} %get-tuple-element.108), channel_id=1, source_target_pairs={{0,2},{1,3},{2,0},{3,1},{4,6},{5,7},{6,4},{7,5},{8,10},{9,11},{10,... | collective-permute-start | bytes 294920 | tf_op jit(solution)/shard_map/ppermute | solution.py:275
  41.3 13.0 %collective-permute-start.13 = (bf16[4,288,128]{2,1,0:T(8,128)(2,1)S(1)}, bf16[4,288,128]{2,1,0:T(8,128)(2,1)S(1)}, u32[]{:S(2)}, u32[]{:S(2)}) collective-permute-start(bf16[4,288,128]{2,1,0:T(8,128)(2,1)S(1)} %get-tuple-element.100), channel_id=1, source_target_pairs={{0,16},{8,24},{16,0},{24,8},{1,17},{9,25},{17,1},{25,9},{2,18},{10... | collective-permute-start | bytes 884744 | tf_op jit(solution)/shard_map/ppermute | solution.py:275
  44.1 11.3 %collective-permute-start.21 = (bf16[64,1664]{1,0:T(8,128)(2,1)S(1)}, bf16[64,1664]{1,0:T(8,128)(2,1)S(1)}, u32[]{:S(2)}, u32[]{:S(2)}) collective-permute-start(bf16[64,1664]{1,0:T(8,128)(2,1)S(1)} %add_sums_to_pass_on.1), channel_id=1, source_target_pairs={{0,4},{1,5},{2,6},{3,7},{4,0},{5,1},{6,2},{7,3},{8,12},{9,13},{10,... | collective-permute-start | bytes 638984 | tf_op jit(solution)/shard_map/ppermute | solution.py:275
  47.4 7.9 %collective-permute-start.22 = (bf16[32,1664]{1,0:T(8,128)(2,1)S(1)}, bf16[32,1664]{1,0:T(8,128)(2,1)S(1)}, u32[]{:S(2)}, u32[]{:S(2)}) collective-permute-start(bf16[32,1664]{1,0:T(8,128)(2,1)S(1)} %get-tuple-element.117), channel_id=1, source_target_pairs={{0,1},{1,0},{2,3},{3,2},{4,5},{5,4},{6,7},{7,6},{8,9},{9,8},{10,11... | collective-permute-start | bytes 319496 | tf_op jit(solution)/shard_map/ppermute | solution.py:275
  49.0 6.3 %collective-permute-start.23 = (bf16[32,1664]{1,0:T(8,128)(2,1)S(1)}, bf16[32,1664]{1,0:T(8,128)(2,1)S(1)}, u32[]{:S(2)}, u32[]{:S(2)}) collective-permute-start(bf16[32,1664]{1,0:T(8,128)(2,1)S(1)} %get-tuple-element.118), channel_id=1, source_target_pairs={{0,1},{1,0},{2,3},{3,2},{4,5},{5,4},{6,7},{7,6},{8,9},{9,8},{10,11... | collective-permute-start | bytes 319496 | tf_op jit(solution)/shard_map/ppermute | solution.py:275
  49.5 4.8 %collective-permute-start.14 = (bf16[4,96,128]{2,1,0:T(8,128)(2,1)S(1)}, bf16[4,96,128]{2,1,0:T(8,128)(2,1)S(1)}, u32[]{:S(2)}, u32[]{:S(2)}) collective-permute-start(bf16[4,96,128]{2,1,0:T(8,128)(2,1)S(1)} %get-tuple-element.101), channel_id=1, source_target_pairs={{0,16},{8,24},{16,0},{24,8},{1,17},{9,25},{17,1},{25,9},{2,18},{10... | collective-permute-start | bytes 294920 | tf_op jit(solution)/shard_map/ppermute | solution.py:275
  (5 other events, 17.7 us)

commit v9 on v8

--- a/solution.py
+++ b/solution.py
@@ -625,35 +625,38 @@
             table_ref[before, own, :] = (old + gain[:, h : h + 1] * entering).astype(jnp.bfloat16)
 
 
-def local_kernel(
-    x_ref,
-    bc_ref,
-    stepx_ref,
-    prefix_ref,
-    meta_ref,
-    pen_ref,
-    skip_ref,
-    y_ref,
-):
+def mixing_kernel(bc_ref, prefix_ref, pen_ref, mixing_ref):
+    blocks, heads = mixing_ref.shape[0:2]
+    state_width = bc_ref.shape[1] // 2
+    half = BLOCK // 2
+    for b in range(blocks):
+        own_rows = slice(b * BLOCK, (b + 1) * BLOCK)
+        scores = dot32(bc_ref[own_rows, state_width:], bc_ref[own_rows, 0:state_width], 1, 1)
+        prefix = prefix_ref[own_rows, :]
+        across = prefix.T
+        for h in range(heads):
+            for rows, seen in ((slice(0, half), half), (slice(half, BLOCK), BLOCK)):
+                gaps = prefix[rows, h : h + 1] - across[h : h + 1, 0:seen] + pen_ref[b, rows, 0:seen]
+                mixing_ref[b, h, rows, 0:seen] = (scores[rows, 0:seen] * jnp.exp(gaps)).astype(
+                    jnp.bfloat16
+                )
+
+
+def local_kernel(x_ref, bc_ref, stepx_ref, prefix_ref, meta_ref, mixing_ref, skip_ref, y_ref):
     inner = y_ref.shape[1]
     state_width = bc_ref.shape[1] // 2
     head_dim = LANES // 2
     tok = y_ref.shape[0]
+    half = BLOCK // 2
     lane = lax.broadcasted_iota(jnp.int32, (BLOCK, LANES), 1)
-    half = BLOCK // 2
     for b in range(tok // BLOCK):
         own_rows = slice(b * BLOCK, (b + 1) * BLOCK)
-        b_blk = bc_ref[own_rows, 0:state_width]
         c_blk = bc_ref[own_rows, state_width:]
-        scores = dot32(c_blk, b_blk, 1, 1)
-        pen = pen_ref[b]
-        prefix = prefix_ref[own_rows, :]
-        across = prefix.T
         if b > 0:
-            carried = jnp.exp(prefix - prefix_ref[b * BLOCK - 1 : b * BLOCK, :])
-            carried = carried * meta_ref[own_rows, 4:5]
             before_rows = slice((b - 1) * BLOCK, b * BLOCK)
             before = prefix_ref[before_rows, :]
+            carried = jnp.exp(prefix_ref[own_rows, :] - before[BLOCK - 1 : BLOCK, :])
+            carried = carried * meta_ref[own_rows, 4:5]
             fade = jnp.exp(before[BLOCK - 1 : BLOCK, :] - before)
             b_before = bc_ref[before_rows, 0:state_width].astype(jnp.float32)
             b_before = (b_before * meta_ref[before_rows, 5:6]).astype(jnp.bfloat16)
@@ -671,9 +674,7 @@
             for rows, seen in ((slice(0, half), half), (slice(half, BLOCK), BLOCK)):
                 part = out[rows]
                 for side in range(2):
-                    h = 2 * q + side
-                    gaps = prefix[rows, h : h + 1] - across[h : h + 1, 0:seen] + pen[rows, 0:seen]
-                    mixing = (scores[rows, 0:seen] * jnp.exp(gaps)).astype(jnp.bfloat16)
+                    mixing = mixing_ref[b, 2 * q + side, rows, 0:seen]
                     part = part + dot32(mixing, sides[side][0:seen])
                 y_ref[b * BLOCK + rows.start : b * BLOCK + rows.stop, own] = part
 
@@ -958,8 +959,17 @@
         dt_bias,
         a_log,
     )
-    x_far, gate_own, bc, step, prefix, fade, halo = lax.optimization_barrier(
-        (x_far, gate_own, bc, step, prefix, fade, halo)
+    mixing = pl.pallas_call(
+        mixing_kernel,
+        name="mixing_weights",
+        out_shape=shape((blocks, heads, BLOCK, BLOCK), bf16),
+        in_specs=in_vmem(3),
+        out_specs=in_vmem(1)[0],
+        compiler_params=kernel_params(8),
+        cost_estimate=LITTLE,
+    )(bc, prefix, pen)
+    x_far, gate_own, bc, step, prefix, fade, halo, mixing = lax.optimization_barrier(
+        (x_far, gate_own, bc, step, prefix, fade, halo, mixing)
     )
     x_last = exchange(x_far, "dp", 1)
     gate_far = exchange(gate_own, "dp", 2)
@@ -1005,7 +1015,7 @@
         out_specs=in_vmem(1)[0],
         compiler_params=kernel_params(14),
         cost_estimate=LITTLE,
-    )(x, bc, stepx, prefix, meta, pen, skip_gain)
+    )(x, bc, stepx, prefix, meta, mixing, skip_gain)
     gate_far, gate_near, entering, y_local = lax.optimization_barrier(
         (gate_far, gate_near, entering, y_local)
     )

time: 56.5 us -> 56.4 us (level)
  waiting for transfers between devices: 10.3 us -> 8.81 us
  starting transfers between devices: 25.5 us -> 26.7 us
    ppermute x23, waiting for transfers between devices: 10.3 us -> 8.81 us  [exchange(): lax.ppermute(values, axis, [(i, i ^ bits) for i in range(lax.axis_size(ax...]
    ppermute x23, starting transfers between devices: 23.1 us -> 24.3 us  [exchange(): lax.ppermute(values, axis, [(i, i ^ bits) for i in range(lax.axis_size(ax...]
    pallas_call x0 -> x1, Pallas kernels: none -> 0.62 us  [fused_on_device(): pl.pallas_call(mixing_kernel, name='mixing_weights', out_shape=shape((blo...]
  transfers between devices with their start and end apart: 24 -> 24, of which waited for: 10 -> 8; matrix products, arithmetic and copies ran while one was open for 0% -> 0% of each run, Pallas kernels for 29% -> 29%
where the time goes in v9:
time: 56.4 us; the launch traced here: 56.2 us
  starting transfers between devices  26.7 us (47%)
  Pallas kernels  19.6 us (35%)
  waiting for transfers between devices  8.81 us (16%)
  between operations  0.98 us (2%)
    ppermute x23, starting transfers between devices, exchange(): lax.ppermute(values, axis, [(i, i ^ bits) for i in range(lax.axis_size(ax...  24.3 us
    ppermute x23, waiting for transfers between devices, exchange(): lax.ppermute(values, axis, [(i, i ^ bits) for i in range(lax.axis_size(ax...  8.81 us
    pallas_call x1, Pallas kernels, fused_on_device(): pl.pallas_call(inner_kernel, name='project_and_convolve_x', out_shape=(sh...  2.63 us
    ppermute x1, starting transfers between devices, fused_on_device(): lax.ppermute(leaving, 'dp', [(i, i + 1) for i in range(peers - 1)])  2.41 us
    pallas_call x1, Pallas kernels, fused_on_device(): pl.pallas_call(first_kernel, name='project_b_c_and_steps', out_shape=(sha...  2.29 us
    pallas_call x1, Pallas kernels, fused_on_device(): pl.pallas_call(pack_first_kernel, name='pack_first_weights', out_shape=sh...  1.95 us
    pallas_call x1, Pallas kernels, fused_on_device(): pl.pallas_call(local_kernel, name='mix_within_blocks', out_shape=shape((t...  1.61 us
    pallas_call x1, Pallas kernels, fused_on_device(): pl.pallas_call(table_kernel, name='sum_ended_states', out_shape=(shape((P...  1.57 us
  transfers between devices with their start and end apart: 24, of which 8 were waited for; matrix products, arithmetic and copies ran while one was open for 0% of the time, Pallas kernels for 29%

profile of v9, /device:TPU:0, one launch (start us, length us, event | category | flops | bytes accessed | tf_op | source)
XLA Modules:
  0.0 56.2 jit_solution(859307997539189710)
XLA Ops:
  0.7 2.0 %pack_first_weights.1.own_ref = bf16[480,256]{1,0:T(8,128)(2,1)} custom-call(s32[1,4]{1,0:T(1,128)} %bitcast.5, f32[384,256]{1,0:T(8,128)} %wbc_ref.1, f32[6,384]{1,0:T(8,128)} %bitcast.6, bf16[512,1536]{1,0:T(8,128)(2,1)} %hidden_ref.1), custom_call_target="tpu_custom_call" | custom-call | flops 1000 | bytes 1000 | tf_op jit(solution)/shard_map/pack_first_weights/pallas_call | solution.py:849
  3.2 2.6 %collective-permute-start = (bf16[480,256]{1,0:T(8,128)(2,1)}, bf16[480,256]{1,0:T(8,128)(2,1)S(1)}, u32[]{:S(2)}, u32[]{:S(2)}) collective-permute-start(bf16[480,256]{1,0:T(8,128)(2,1)} %pack_first_weights.1.own_ref), channel_id=1, source_target_pairs={{0,16},{8,24},{16,0},{24,8},{1,17},{9,25},{17,1},{25,9},{2,18},{10... | collective-permute-start | bytes 737288 | tf_op jit(solution)/shard_map/ppermute | solution.py:275
  6.2 1.6 %collective-permute-start.16 = (bf16[384,768]{1,0:T(8,128)(2,1)S(1)}, bf16[384,768]{1,0:T(8,128)(2,1)S(1)}, u32[]{:S(2)}, u32[]{:S(2)}) collective-permute-start(bf16[384,768]{1,0:T(8,128)(2,1)S(1)} %get-tuple-element.108), channel_id=1, source_target_pairs={{0,2},{1,3},{2,0},{3,1},{4,6},{5,7},{6,4},{7,5},{8,10},{9,11},{10,... | collective-permute-start | bytes 1769480 | tf_op jit(solution)/shard_map/ppermute | solution.py:275
  8.4 0.6 %collective-permute-start.2 = (bf16[384,384]{1,0:T(8,128)(2,1)S(1)}, bf16[384,384]{1,0:T(8,128)(2,1)S(1)}, u32[]{:S(2)}, u32[]{:S(2)}) collective-permute-start(bf16[384,384]{1,0:T(8,128)(2,1)S(1)} %get-tuple-element.84.own_ref), channel_id=1, source_target_pairs={{0,16},{8,24},{16,0},{24,8},{1,17},{9,25},{17,1},{25,9},{2,18},{10... | collective-permute-start | bytes 884744 | tf_op jit(solution)/shard_map/ppermute | solution.py:275
  9.1 1.2 %norm_and_token_facts.1 = (bf16[512,1536]{1,0:T(8,128)(2,1)S(1)}, f32[512,128]{1,0:T(8,128)S(1)}, bf16[1024,512]{1,0:T(8,128)(2,1)S(1)}, f32[2,256,256]{2,1,0:T(8,128)S(1)}, bf16[64,1536]{1,0:T(8,128)(2,1)S(1)}) custom-call(s32[1,2048]{1,0:T(1,128)S(1)} %bitcast.4, bf16[512,1536]{1,0:T(8,128)(2,1)S(1)} %copy-done, f32[1,1536]{1,0:T(1,128)S(1)} %broadcast_in_dim.14.gain_ref), custom_call_target="tpu_custom_call" | custom-call | flops 1000 | bytes 1000 | tf_op jit(solution)/shard_map/norm_and_token_facts/pallas_call | solution.py:883
  10.4 0.6 %project_b_c_and_steps_of_chip.1 = (f32[512,256]{1,0:T(8,128)S(1)}, f32[512,128]{1,0:T(8,128)S(1)}) custom-call(bf16[512,1536]{1,0:T(8,128)(2,1)S(1)} %get-tuple-element.63.normed_ref, bf16[480,256]{1,0:T(8,128)(2,1)S(1)} %copy-done.1, bf16[480,256]{1,0:T(8,128)(2,1)S(1)} %collective-permute-done.1.near_ref), custom_call_target="tpu_custom_call" | custom-call | flops 1000 | bytes 1000 | tf_op jit(solution)/shard_map/project_b_c_and_steps_of_chip/pallas_call | solution.py:912
  11.0 1.8 %collective-permute-done.far_ref = bf16[480,256]{1,0:T(8,128)(2,1)S(1)} collective-permute-done((bf16[480,256]{1,0:T(8,128)(2,1)}, bf16[480,256]{1,0:T(8,128)(2,1)S(1)}, u32[]{:S(2)}, u32[]{:S(2)}) %collective-permute-start) | collective-permute-done | bytes 245792 | tf_op jit(solution)/shard_map/ppermute | solution.py:275
  13.3 1.0 %collective-permute-done.3.last_ref = bf16[480,256]{1,0:T(8,128)(2,1)S(1)} collective-permute-done((bf16[480,256]{1,0:T(8,128)(2,1)S(1)}, bf16[480,256]{1,0:T(8,128)(2,1)S(1)}, u32[]{:S(2)}, u32[]{:S(2)}) %collective-permute-start.3) | collective-permute-done | bytes 245792 | tf_op jit(solution)/shard_map/ppermute | solution.py:275
  14.3 2.3 %project_b_c_and_steps.1 = (bf16[512,256]{1,0:T(8,128)(2,1)S(1)}, f32[512,128]{1,0:T(8,128)S(1)}, f32[512,128]{1,0:T(8,128)S(1)}, f32[512,128]{1,0:T(8,128)S(1)}, bf16[16,1536]{1,0:T(8,128)(2,1)S(1)}) custom-call(bf16[512,1536]{1,0:T(8,128)(2,1)S(1)} %get-tuple-element.63.normed_ref, f32[512,256]{1,0:T(8,128)S(1)} %get-tuple-element.73.most_ref, ...), custom_call_target="tpu_custom_call" | custom-call | flops 1000 | bytes 1000 | tf_op jit(solution)/shard_map/project_b_c_and_steps/pallas_call | solution.py:928
  16.6 0.6 %mixing_weights.1.mixing_ref = bf16[2,6,256,256]{3,2,1,0:T(8,128)(2,1)S(1)} custom-call(bf16[512,256]{1,0:T(8,128)(2,1)S(1)} %get-tuple-element.83.bc_ref, f32[512,128]{1,0:T(8,128)S(1)} %get-tuple-element.90.prefix_ref, f32[2,256,256]{2,1,0:T(8,128)S(1)} %get-tuple-element.82.pen_ref), custom_call_target="tpu_custom_call" | custom-call | flops 1000 | bytes 1000 | tf_op jit(solution)/shard_map/mixing_weights/pallas_call | solution.py:962
  17.2 1.6 %collective-permute-done.2.far_ref = bf16[384,384]{1,0:T(8,128)(2,1)S(1)} collective-permute-done((bf16[384,384]{1,0:T(8,128)(2,1)S(1)}, bf16[384,384]{1,0:T(8,128)(2,1)S(1)}, u32[]{:S(2)}, u32[]{:S(2)}) %collective-permute-start.2) | collective-permute-done | bytes 294944 | tf_op jit(solution)/shard_map/ppermute | solution.py:275
  19.3 1.8 %collective-permute-start.6 = (bf16[384,384]{1,0:T(8,128)(2,1)S(1)}, bf16[384,384]{1,0:T(8,128)(2,1)S(1)}, u32[]{:S(2)}, u32[]{:S(2)}) collective-permute-start(bf16[384,384]{1,0:T(8,128)(2,1)S(1)} %get-tuple-element.91.own_ref), channel_id=1, source_target_pairs={{0,16},{8,24},{16,0},{24,8},{1,17},{9,25},{17,1},{25,9},{2,18},{10... | collective-permute-start | bytes 884744 | tf_op jit(solution)/shard_map/ppermute | solution.py:275
  21.7 2.6 %project_and_convolve_x.1 = (bf16[512,384]{1,0:T(8,128)(2,1)S(1)}, bf16[512,384]{1,0:T(8,128)(2,1)S(1)}, bf16[384,512]{1,0:T(8,128)(2,1)S(1)}, bf16[384,128]{1,0:T(8,128)(2,1)S(1)}) custom-call(bf16[512,1536]{1,0:T(8,128)(2,1)S(1)} %get-tuple-element.63.normed_ref, bf16[384,384]{1,0:T(8,128)(2,1)S(1)} %get-tuple-element.84.own_ref, ...), custom_call_target="tpu_custom_call" | custom-call | flops 1000 | bytes 1000 | tf_op jit(solution)/shard_map/project_and_convolve_x/pallas_call | solution.py:976
  24.3 2.4 %collective-permute-start.8 = (bf16[384,128]{1,0:T(8,128)(2,1)S(1)}, bf16[384,128]{1,0:T(8,128)(2,1)S(1)}, u32[]{:S(2)}, u32[]{:S(2)}) collective-permute-start(bf16[384,128]{1,0:T(8,128)(2,1)S(1)} %get-tuple-element.92), channel_id=1, source_target_pairs={{0,8},{8,16},{16,24},{1,9},{9,17},{17,25},{2,10},{10,18},{18,26},{... | collective-permute-start | bytes 294920 | tf_op jit(solution)/shard_map/ppermute | solution.py:1008
  26.8 1.6 %mix_within_blocks.1.y_ref = f32[512,384]{1,0:T(8,128)S(1)} custom-call(bf16[512,384]{1,0:T(8,128)(2,1)S(1)} %get-tuple-element.93.x_ref, bf16[512,256]{1,0:T(8,128)(2,1)S(1)} %get-tuple-element.83.bc_ref, bf16[512,384]{1,0:T(8,128)(2,1)S(1)} %get-tuple-element.94.stepx_ref, f32[512,128]{1,0:T(8,128)S(1)} %get-tuple-element.90.prefix_ref, ...), custom_call_target="tpu_custom_call" | custom-call | flops 1000 | bytes 1000 | tf_op jit(solution)/shard_map/mix_within_blocks/pallas_call | solution.py:1010
  28.7 0.9 %project_gate_most.1.most_ref = f32[512,384]{1,0:T(8,128)S(1)} custom-call(bf16[512,1536]{1,0:T(8,128)(2,1)S(1)} %get-tuple-element.63.normed_ref, bf16[384,384]{1,0:T(8,128)(2,1)S(1)} %get-tuple-element.91.own_ref, bf16[384,384]{1,0:T(8,128)(2,1)S(1)} %collective-permute-done.7.near_ref, bf16[384,384]{1,0:T(8,128)(2,1)S(1)} %collective-permute-done.6.far_ref), custom_call_target="tpu_custom_call" | custom-call | flops 1000 | bytes 1000 | tf_op jit(solution)/shard_map/project_gate_most/pallas_call | solution.py:1034
  30.5 0.6 %add_entering_and_gate.1 = (bf16[128,384]{1,0:T(8,128)(2,1)S(1)}, bf16[128,384]{1,0:T(8,128)(2,1)S(1)}, bf16[128,384]{1,0:T(8,128)(2,1)S(1)}, bf16[128,384]{1,0:T(8,128)(2,1)S(1)}) custom-call(bf16[384,128]{1,0:T(8,128)(2,1)S(1)} %collective-permute-done.8.enter_ref, bf16[512,256]{1,0:T(8,128)(2,1)S(1)} %get-tuple-element.83.bc_ref, ...), custom_call_target="tpu_custom_call" | custom-call | flops 1000 | bytes 1000 | tf_op jit(solution)/shard_map/add_entering_and_gate/pallas_call | solution.py:1054
  31.1 1.7 %collective-permute-start.19 = (bf16[128,384]{1,0:T(8,128)(2,1)S(1)}, bf16[128,384]{1,0:T(8,128)(2,1)S(1)}, u32[]{:S(2)}, u32[]{:S(2)}) collective-permute-start(bf16[128,384]{1,0:T(8,128)(2,1)S(1)} %get-tuple-element.112), channel_id=1, source_target_pairs={{0,2},{1,3},{2,0},{3,1},{4,6},{5,7},{6,4},{7,5},{8,10},{9,11},{10,... | collective-permute-start | bytes 294920 | tf_op jit(solution)/shard_map/ppermute | solution.py:275
  32.8 1.6 %sum_ended_states.1 = (bf16[8,96,128]{2,1,0:T(8,128)(2,1)S(1)}, bf16[8,96,128]{2,1,0:T(8,128)(2,1)S(1)}, bf16[8,96,128]{2,1,0:T(8,128)(2,1)S(1)}, bf16[8,96,128]{2,1,0:T(8,128)(2,1)S(1)}) custom-call(s32[2048]{0:T(1024)S(1)} %copy-done.4, bf16[512,256]{1,0:T(8,128)(2,1)S(1)} %get-tuple-element.83.bc_ref, bf16[384,512]{1,0:T(8,128)(2,1)S(1)} %get-tuple-element.89.faded_ref, ...), custom_call_target="tpu_custom_call" | custom-call | flops 1000 | bytes 1000 | tf_op jit(solution)/shard_map/sum_ended_states/pallas_call | solution.py:1023
  35.5 0.6 %collective-permute-done.19.got_ref = bf16[128,384]{1,0:T(8,128)(2,1)S(1)} collective-permute-done((bf16[128,384]{1,0:T(8,128)(2,1)S(1)}, bf16[128,384]{1,0:T(8,128)(2,1)S(1)}, u32[]{:S(2)}, u32[]{:S(2)}) %collective-permute-start.19) | collective-permute-done | bytes 98336 | tf_op jit(solution)/shard_map/ppermute | solution.py:275
  36.1 0.6 %project_out.2 = (f32[64,1664]{1,0:T(8,128)S(1)}, bf16[64,1664]{1,0:T(8,128)(2,1)S(1)}) custom-call(bf16[128,384]{1,0:T(8,128)(2,1)S(1)} %get-tuple-element.111.kept_ref, bf16[128,384]{1,0:T(8,128)(2,1)S(1)} %collective-permute-done.19.got_ref, bf16[384,1536]{1,0:T(8,128)(2,1)S(1)} %get-tuple-element.113.own_ref, ...), custom_call_target="tpu_custom_call" | custom-call | flops 1000 | bytes 1000 | tf_op jit(solution)/shard_map/project_out/pallas_call | solution.py:1087
  36.8 1.6 %collective-permute-start.20 = (bf16[64,1664]{1,0:T(8,128)(2,1)S(1)}, bf16[64,1664]{1,0:T(8,128)(2,1)S(1)}, u32[]{:S(2)}, u32[]{:S(2)}) collective-permute-start(bf16[64,1664]{1,0:T(8,128)(2,1)S(1)} %get-tuple-element.115), channel_id=1, source_target_pairs={{0,1},{1,0},{2,3},{3,2},{4,5},{5,4},{6,7},{7,6},{8,9},{9,8},{10,11... | collective-permute-start | bytes 638984 | tf_op jit(solution)/shard_map/ppermute | solution.py:275
  38.3 1.6 %collective-permute-start.18 = (bf16[128,384]{1,0:T(8,128)(2,1)S(1)}, bf16[128,384]{1,0:T(8,128)(2,1)S(1)}, u32[]{:S(2)}, u32[]{:S(2)}) collective-permute-start(bf16[128,384]{1,0:T(8,128)(2,1)S(1)} %get-tuple-element.110), channel_id=1, source_target_pairs={{0,2},{1,3},{2,0},{3,1},{4,6},{5,7},{6,4},{7,5},{8,10},{9,11},{10,... | collective-permute-start | bytes 294920 | tf_op jit(solution)/shard_map/ppermute | solution.py:275
  40.0 0.9 %pick_request_states.1 = (bf16[4,384,128]{2,1,0:T(8,128)(2,1)S(1)}, bf16[4,288,128]{2,1,0:T(8,128)(2,1)S(1)}, bf16[4,96,128]{2,1,0:T(8,128)(2,1)S(1)}) custom-call(s32[4]{0:T(128)S(1)} %copy-done.7, bf16[480,256]{1,0:T(8,128)(2,1)S(1)} %collective-permute-done.far_ref, bf16[8,96,128]{2,1,0:T(8,128)(2,1)S(1)} %get-tuple-element.97.refs_0_, ...), custom_call_target="tpu_custom_call" | custom-call | flops 1000 | bytes 1000 | tf_op jit(solution)/shard_map/pick_request_states/pallas_call | solution.py:1069
  40.8 2.6 %collective-permute-start.13 = (bf16[4,288,128]{2,1,0:T(8,128)(2,1)S(1)}, bf16[4,288,128]{2,1,0:T(8,128)(2,1)S(1)}, u32[]{:S(2)}, u32[]{:S(2)}) collective-permute-start(bf16[4,288,128]{2,1,0:T(8,128)(2,1)S(1)} %get-tuple-element.102), channel_id=1, source_target_pairs={{0,16},{8,24},{16,0},{24,8},{1,17},{9,25},{17,1},{25,9},{2,18},{10... | collective-permute-start | bytes 884744 | tf_op jit(solution)/shard_map/ppermute | solution.py:275
  43.7 2.7 %collective-permute-start.21 = (bf16[64,1664]{1,0:T(8,128)(2,1)S(1)}, bf16[64,1664]{1,0:T(8,128)(2,1)S(1)}, u32[]{:S(2)}, u32[]{:S(2)}) collective-permute-start(bf16[64,1664]{1,0:T(8,128)(2,1)S(1)} %add_sums_to_pass_on.1), channel_id=1, source_target_pairs={{0,4},{1,5},{2,6},{3,7},{4,0},{5,1},{6,2},{7,3},{8,12},{9,13},{10,... | collective-permute-start | bytes 638984 | tf_op jit(solution)/shard_map/ppermute | solution.py:275
  46.3 0.6 %project_out.3 = (f32[64,1664]{1,0:T(8,128)S(1)}, bf16[32,1664]{1,0:T(8,128)(2,1)S(1)}, bf16[32,1664]{1,0:T(8,128)(2,1)S(1)}) custom-call(bf16[128,384]{1,0:T(8,128)(2,1)S(1)} %get-tuple-element.109.kept_ref, bf16[128,384]{1,0:T(8,128)(2,1)S(1)} %collective-permute-done.18.arrived_ref.got_ref, bf16[384,1536]{1,0:T(8,128)(2,1)S(1)} %get-tuple-element.113.own_ref, ...), custom_call_target="tpu_custom_call" | custom-call | flops 1000 | bytes 1000 | tf_op jit(solution)/shard_map/project_out/pallas_call | solution.py:1087
  47.0 1.6 %collective-permute-start.22 = (bf16[32,1664]{1,0:T(8,128)(2,1)S(1)}, bf16[32,1664]{1,0:T(8,128)(2,1)S(1)}, u32[]{:S(2)}, u32[]{:S(2)}) collective-permute-start(bf16[32,1664]{1,0:T(8,128)(2,1)S(1)} %get-tuple-element.119), channel_id=1, source_target_pairs={{0,1},{1,0},{2,3},{3,2},{4,5},{5,4},{6,7},{7,6},{8,9},{9,8},{10,11... | collective-permute-start | bytes 319496 | tf_op jit(solution)/shard_map/ppermute | solution.py:275
  49.1 2.7 %collective-permute-start.14 = (bf16[4,96,128]{2,1,0:T(8,128)(2,1)S(1)}, bf16[4,96,128]{2,1,0:T(8,128)(2,1)S(1)}, u32[]{:S(2)}, u32[]{:S(2)}) collective-permute-start(bf16[4,96,128]{2,1,0:T(8,128)(2,1)S(1)} %get-tuple-element.103), channel_id=1, source_target_pairs={{0,16},{8,24},{16,0},{24,8},{1,17},{9,25},{17,1},{25,9},{2,18},{10... | collective-permute-start | bytes 294920 | tf_op jit(solution)/shard_map/ppermute | solution.py:275
  51.8 2.6 %collective-permute-done.14.refs_1_ = bf16[4,96,128]{2,1,0:T(8,128)(2,1)S(1)} collective-permute-done((bf16[4,96,128]{2,1,0:T(8,128)(2,1)S(1)}, bf16[4,96,128]{2,1,0:T(8,128)(2,1)S(1)}, u32[]{:S(2)}, u32[]{:S(2)}) %collective-permute-start.14) | collective-permute-done | bytes 98336 | tf_op jit(solution)/shard_map/ppermute | solution.py:275
  54.4 1.0 %join_request_states.1 = (f32[4,384,128]{2,1,0:T(8,128)}, f32[8,128]{1,0:T(8,128)S(1)}) custom-call(bf16[4,384,128]{2,1,0:T(8,128)(2,1)S(1)} %get-tuple-element.101.keep_ref, bf16[4,288,128]{2,1,0:T(8,128)(2,1)S(1)} %collective-permute-done.13.refs_0_, bf16[4,96,128]{2,1,0:T(8,128)(2,1)S(1)} %collective-permute-done.14.refs_1_), custom_call_target="tpu_custom_call" | custom-call | flops 1000 | bytes 1000 | tf_op jit(solution)/shard_map/join_request_states/pallas_call | solution.py:1113
  55.3 0.9 %scale_and_add_hidden.1 = bf16[64,1536]{1,0:T(8,128)(2,1)} custom-call(bf16[64,1536]{1,0:T(8,128)(2,1)S(1)} %get-tuple-element.62.hidden_ref, f32[8,128]{1,0:T(8,128)S(1)} %get-tuple-element.104.joined_ref, f32[64,1664]{1,0:T(8,128)S(1)} %get-tuple-element.117.keep_ref, bf16[64,1664]{1,0:T(8,128)(2,1)S(1)} %collective-permute-done.21.passed_ref, ...), custom_call_target="tpu_custom_call" | custom-call | flops 1000 | bytes 1000 | tf_op jit(solution)/shard_map/scale_and_add_hidden/pallas_call | solution.py:1122
  (63 shorter events, 6.3 us)
Async XLA Ops:
  0.7 7.2 %copy-start.3 = (f32[384,2,384]{2,1,0:T(2,128)S(1)}, f32[384,2,384]{2,1,0:T(2,128)}, u32[]{:S(2)}) copy-start(f32[384,2,384]{2,1,0:T(2,128)} %wzx_ref.1) | copy-start | bytes 3538948
  2.6 6.4 %copy-start.11 = (f32[1536]{0:T(1024)S(1)}, f32[1536]{0:T(1024)}, u32[]{:S(2)}) copy-start(f32[1536]{0:T(1024)} %param.17) | copy-start | bytes 18436
  2.6 6.4 %copy-start = (bf16[512,1536]{1,0:T(8,128)(2,1)S(1)}, bf16[512,1536]{1,0:T(8,128)(2,1)}, u32[]{:S(2)}) copy-start(bf16[512,1536]{1,0:T(8,128)(2,1)} %hidden_ref.1) | copy-start | bytes 4718596
  2.6 6.4 %copy-start.4 = (s32[2048]{0:T(1024)S(1)}, s32[2048]{0:T(1024)}, u32[]{:S(2)}) copy-start(s32[2048]{0:T(1024)} %ids_ref.1) | copy-start | bytes 24580
  2.7 7.7 %collective-permute-start.1 = (bf16[480,256]{1,0:T(8,128)(2,1)}, bf16[480,256]{1,0:T(8,128)(2,1)S(1)}, u32[]{:S(2)}, u32[]{:S(2)}) collective-permute-start(bf16[480,256]{1,0:T(8,128)(2,1)} %pack_first_weights.1.own_ref), channel_id=1, source_target_pairs={{0,8},{8,0},{16,24},{24,16},{1,9},{9,1},{17,25},{25,17},{2,10},{10... | collective-permute-start | bytes 737288 | tf_op jit(solution)/shard_map/ppermute | solution.py:275
  3.2 9.6 %collective-permute-start = (bf16[480,256]{1,0:T(8,128)(2,1)}, bf16[480,256]{1,0:T(8,128)(2,1)S(1)}, u32[]{:S(2)}, u32[]{:S(2)}) collective-permute-start(bf16[480,256]{1,0:T(8,128)(2,1)} %pack_first_weights.1.own_ref), channel_id=1, source_target_pairs={{0,16},{8,24},{16,0},{24,8},{1,17},{9,25},{17,1},{25,9},{2,18},{10... | collective-permute-start | bytes 737288 | tf_op jit(solution)/shard_map/ppermute | solution.py:275
  6.2 15.5 %collective-permute-start.16 = (bf16[384,768]{1,0:T(8,128)(2,1)S(1)}, bf16[384,768]{1,0:T(8,128)(2,1)S(1)}, u32[]{:S(2)}, u32[]{:S(2)}) collective-permute-start(bf16[384,768]{1,0:T(8,128)(2,1)S(1)} %get-tuple-element.108), channel_id=1, source_target_pairs={{0,2},{1,3},{2,0},{3,1},{4,6},{5,7},{6,4},{7,5},{8,10},{9,11},{10,... | collective-permute-start | bytes 1769480 | tf_op jit(solution)/shard_map/ppermute | solution.py:275
  8.4 10.4 %collective-permute-start.2 = (bf16[384,384]{1,0:T(8,128)(2,1)S(1)}, bf16[384,384]{1,0:T(8,128)(2,1)S(1)}, u32[]{:S(2)}, u32[]{:S(2)}) collective-permute-start(bf16[384,384]{1,0:T(8,128)(2,1)S(1)} %get-tuple-element.84.own_ref), channel_id=1, source_target_pairs={{0,16},{8,24},{16,0},{24,8},{1,17},{9,25},{17,1},{25,9},{2,18},{10... | collective-permute-start | bytes 884744 | tf_op jit(solution)/shard_map/ppermute | solution.py:275
  9.0 5.2 %copy-start.6 = (f32[4,256]{1,0:T(4,128)S(1)}, f32[4,256]{1,0:T(4,128)}, u32[]{:S(2)}) copy-start(f32[4,256]{1,0:T(4,128)} %taps_ref.2) | copy-start | bytes 12292
  9.1 5.2 %copy-start.8 = (f32[6]{0:T(128)S(1)}, f32[6]{0:T(128)}, u32[]{:S(2)}) copy-start(f32[6]{0:T(128)} %bias_ref.1) | copy-start | bytes 76
  12.8 1.5 %collective-permute-start.3 = (bf16[480,256]{1,0:T(8,128)(2,1)S(1)}, bf16[480,256]{1,0:T(8,128)(2,1)S(1)}, u32[]{:S(2)}, u32[]{:S(2)}) collective-permute-start(bf16[480,256]{1,0:T(8,128)(2,1)S(1)} %collective-permute-done.far_ref), channel_id=1, source_target_pairs={{0,8},{8,0},{16,24},{24,16},{1,9},{9,1},{17,25},{25,17},{2,10},{10... | collective-permute-start | bytes 737288 | tf_op jit(solution)/shard_map/ppermute | solution.py:275
  12.8 8.9 %collective-permute-start.4 = (bf16[384,384]{1,0:T(8,128)(2,1)S(1)}, bf16[384,384]{1,0:T(8,128)(2,1)S(1)}, u32[]{:S(2)}, u32[]{:S(2)}) collective-permute-start(bf16[384,384]{1,0:T(8,128)(2,1)S(1)} %get-tuple-element.84.own_ref), channel_id=1, source_target_pairs={{0,8},{8,0},{16,24},{24,16},{1,9},{9,1},{17,25},{25,17},{2,10},{10... | collective-permute-start | bytes 884744 | tf_op jit(solution)/shard_map/ppermute | solution.py:275
  18.8 7.9 %copy-start.10 = (f32[6]{0:T(128)S(1)}, f32[6]{0:T(128)}, u32[]{:S(2)}) copy-start(f32[6]{0:T(128)} %skip_ref.1) | copy-start | bytes 76
  18.8 2.9 %collective-permute-start.5 = (bf16[384,384]{1,0:T(8,128)(2,1)S(1)}, bf16[384,384]{1,0:T(8,128)(2,1)S(1)}, u32[]{:S(2)}, u32[]{:S(2)}) collective-permute-start(bf16[384,384]{1,0:T(8,128)(2,1)S(1)} %collective-permute-done.2.far_ref), channel_id=1, source_target_pairs={{0,8},{8,0},{16,24},{24,16},{1,9},{9,1},{17,25},{25,17},{2,10},{10... | collective-permute-start | bytes 884744 | tf_op jit(solution)/shard_map/ppermute | solution.py:275
  18.8 9.6 %collective-permute-start.7 = (bf16[384,384]{1,0:T(8,128)(2,1)S(1)}, bf16[384,384]{1,0:T(8,128)(2,1)S(1)}, u32[]{:S(2)}, u32[]{:S(2)}) collective-permute-start(bf16[384,384]{1,0:T(8,128)(2,1)S(1)} %get-tuple-element.91.own_ref), channel_id=1, source_target_pairs={{0,8},{8,0},{16,24},{24,16},{1,9},{9,1},{17,25},{25,17},{2,10},{10... | collective-permute-start | bytes 884744 | tf_op jit(solution)/shard_map/ppermute | solution.py:275
  19.3 9.1 %collective-permute-start.6 = (bf16[384,384]{1,0:T(8,128)(2,1)S(1)}, bf16[384,384]{1,0:T(8,128)(2,1)S(1)}, u32[]{:S(2)}, u32[]{:S(2)}) collective-permute-start(bf16[384,384]{1,0:T(8,128)(2,1)S(1)} %get-tuple-element.91.own_ref), channel_id=1, source_target_pairs={{0,16},{8,24},{16,0},{24,8},{1,17},{9,25},{17,1},{25,9},{2,18},{10... | collective-permute-start | bytes 884744 | tf_op jit(solution)/shard_map/ppermute | solution.py:275
  21.7 8.8 %collective-permute-start.17 = (bf16[384,768]{1,0:T(8,128)(2,1)S(1)}, bf16[384,768]{1,0:T(8,128)(2,1)S(1)}, u32[]{:S(2)}, u32[]{:S(2)}) collective-permute-start(bf16[384,768]{1,0:T(8,128)(2,1)S(1)} %collective-permute-done.16.part_ref), channel_id=1, source_target_pairs={{0,8},{8,0},{16,24},{24,16},{1,9},{9,1},{17,25},{25,17},{2,10},{10... | collective-permute-start | bytes 1769480 | tf_op jit(solution)/shard_map/ppermute | solution.py:275
  24.3 4.1 %collective-permute-start.8 = (bf16[384,128]{1,0:T(8,128)(2,1)S(1)}, bf16[384,128]{1,0:T(8,128)(2,1)S(1)}, u32[]{:S(2)}, u32[]{:S(2)}) collective-permute-start(bf16[384,128]{1,0:T(8,128)(2,1)S(1)} %get-tuple-element.92), channel_id=1, source_target_pairs={{0,8},{8,16},{16,24},{1,9},{9,17},{17,25},{2,10},{10,18},{18,26},{... | collective-permute-start | bytes 294920 | tf_op jit(solution)/shard_map/ppermute | solution.py:1008
  28.4 1.6 %collective-permute-start.15 = (bf16[384,384]{1,0:T(8,128)(2,1)S(1)}, bf16[384,384]{1,0:T(8,128)(2,1)S(1)}, u32[]{:S(2)}, u32[]{:S(2)}) collective-permute-start(bf16[384,384]{1,0:T(8,128)(2,1)S(1)} %collective-permute-done.6.far_ref), channel_id=1, source_target_pairs={{0,8},{8,0},{16,24},{24,16},{1,9},{9,1},{17,25},{25,17},{2,10},{10... | collective-permute-start | bytes 884744 | tf_op jit(solution)/shard_map/ppermute | solution.py:275
  31.1 5.0 %collective-permute-start.19 = (bf16[128,384]{1,0:T(8,128)(2,1)S(1)}, bf16[128,384]{1,0:T(8,128)(2,1)S(1)}, u32[]{:S(2)}, u32[]{:S(2)}) collective-permute-start(bf16[128,384]{1,0:T(8,128)(2,1)S(1)} %get-tuple-element.112), channel_id=1, source_target_pairs={{0,2},{1,3},{2,0},{3,1},{4,6},{5,7},{6,4},{7,5},{8,10},{9,11},{10,... | collective-permute-start | bytes 294920 | tf_op jit(solution)/shard_map/ppermute | solution.py:275
  34.4 5.5 %copy-start.7 = (s32[4]{0:T(128)S(1)}, s32[4]{0:T(128)}, u32[]{:S(2)}) copy-start(s32[4]{0:T(128)} %own_ref.1) | copy-start | bytes 52
  34.4 3.9 %collective-permute-start.9 = (bf16[8,96,128]{2,1,0:T(8,128)(2,1)S(1)}, bf16[8,96,128]{2,1,0:T(8,128)(2,1)S(1)}, u32[]{:S(2)}, u32[]{:S(2)}) collective-permute-start(bf16[8,96,128]{2,1,0:T(8,128)(2,1)S(1)} %get-tuple-element.97.refs_0_), channel_id=1, source_target_pairs={{0,8},{8,0},{16,24},{24,16},{1,9},{9,1},{17,25},{25,17},{2,10},{10... | collective-permute-start | bytes 589832 | tf_op jit(solution)/shard_map/ppermute | solution.py:275
  34.6 5.3 %collective-permute-start.10 = (bf16[8,96,128]{2,1,0:T(8,128)(2,1)S(1)}, bf16[8,96,128]{2,1,0:T(8,128)(2,1)S(1)}, u32[]{:S(2)}, u32[]{:S(2)}) collective-permute-start(bf16[8,96,128]{2,1,0:T(8,128)(2,1)S(1)} %get-tuple-element.98.refs_1_), channel_id=1, source_target_pairs={{0,8},{8,0},{16,24},{24,16},{1,9},{9,1},{17,25},{25,17},{2,10},{10... | collective-permute-start | bytes 589832 | tf_op jit(solution)/shard_map/ppermute | solution.py:275
  35.0 4.9 %collective-permute-start.11 = (bf16[8,96,128]{2,1,0:T(8,128)(2,1)S(1)}, bf16[8,96,128]{2,1,0:T(8,128)(2,1)S(1)}, u32[]{:S(2)}, u32[]{:S(2)}) collective-permute-start(bf16[8,96,128]{2,1,0:T(8,128)(2,1)S(1)} %get-tuple-element.99.refs_2_), channel_id=1, source_target_pairs={{0,8},{8,0},{16,24},{24,16},{1,9},{9,1},{17,25},{25,17},{2,10},{10... | collective-permute-start | bytes 589832 | tf_op jit(solution)/shard_map/ppermute | solution.py:275
  35.1 4.8 %collective-permute-start.12 = (bf16[8,96,128]{2,1,0:T(8,128)(2,1)S(1)}, bf16[8,96,128]{2,1,0:T(8,128)(2,1)S(1)}, u32[]{:S(2)}, u32[]{:S(2)}) collective-permute-start(bf16[8,96,128]{2,1,0:T(8,128)(2,1)S(1)} %get-tuple-element.100.refs_3_), channel_id=1, source_target_pairs={{0,8},{8,0},{16,24},{24,16},{1,9},{9,1},{17,25},{25,17},{2,10},{10... | collective-permute-start | bytes 589832 | tf_op jit(solution)/shard_map/ppermute | solution.py:275
  36.8 6.7 %collective-permute-start.20 = (bf16[64,1664]{1,0:T(8,128)(2,1)S(1)}, bf16[64,1664]{1,0:T(8,128)(2,1)S(1)}, u32[]{:S(2)}, u32[]{:S(2)}) collective-permute-start(bf16[64,1664]{1,0:T(8,128)(2,1)S(1)} %get-tuple-element.115), channel_id=1, source_target_pairs={{0,1},{1,0},{2,3},{3,2},{4,5},{5,4},{6,7},{7,6},{8,9},{9,8},{10,11... | collective-permute-start | bytes 638984 | tf_op jit(solution)/shard_map/ppermute | solution.py:275
  38.3 5.0 %collective-permute-start.18 = (bf16[128,384]{1,0:T(8,128)(2,1)S(1)}, bf16[128,384]{1,0:T(8,128)(2,1)S(1)}, u32[]{:S(2)}, u32[]{:S(2)}) collective-permute-start(bf16[128,384]{1,0:T(8,128)(2,1)S(1)} %get-tuple-element.110), channel_id=1, source_target_pairs={{0,2},{1,3},{2,0},{3,1},{4,6},{5,7},{6,4},{7,5},{8,10},{9,11},{10,... | collective-permute-start | bytes 294920 | tf_op jit(solution)/shard_map/ppermute | solution.py:275
  40.8 13.5 %collective-permute-start.13 = (bf16[4,288,128]{2,1,0:T(8,128)(2,1)S(1)}, bf16[4,288,128]{2,1,0:T(8,128)(2,1)S(1)}, u32[]{:S(2)}, u32[]{:S(2)}) collective-permute-start(bf16[4,288,128]{2,1,0:T(8,128)(2,1)S(1)} %get-tuple-element.102), channel_id=1, source_target_pairs={{0,16},{8,24},{16,0},{24,8},{1,17},{9,25},{17,1},{25,9},{2,18},{10... | collective-permute-start | bytes 884744 | tf_op jit(solution)/shard_map/ppermute | solution.py:275
  43.7 11.7 %collective-permute-start.21 = (bf16[64,1664]{1,0:T(8,128)(2,1)S(1)}, bf16[64,1664]{1,0:T(8,128)(2,1)S(1)}, u32[]{:S(2)}, u32[]{:S(2)}) collective-permute-start(bf16[64,1664]{1,0:T(8,128)(2,1)S(1)} %add_sums_to_pass_on.1), channel_id=1, source_target_pairs={{0,4},{1,5},{2,6},{3,7},{4,0},{5,1},{6,2},{7,3},{8,12},{9,13},{10,... | collective-permute-start | bytes 638984 | tf_op jit(solution)/shard_map/ppermute | solution.py:275
  47.0 8.4 %collective-permute-start.22 = (bf16[32,1664]{1,0:T(8,128)(2,1)S(1)}, bf16[32,1664]{1,0:T(8,128)(2,1)S(1)}, u32[]{:S(2)}, u32[]{:S(2)}) collective-permute-start(bf16[32,1664]{1,0:T(8,128)(2,1)S(1)} %get-tuple-element.119), channel_id=1, source_target_pairs={{0,1},{1,0},{2,3},{3,2},{4,5},{5,4},{6,7},{7,6},{8,9},{9,8},{10,11... | collective-permute-start | bytes 319496 | tf_op jit(solution)/shard_map/ppermute | solution.py:275
  48.5 6.8 %collective-permute-start.23 = (bf16[32,1664]{1,0:T(8,128)(2,1)S(1)}, bf16[32,1664]{1,0:T(8,128)(2,1)S(1)}, u32[]{:S(2)}, u32[]{:S(2)}) collective-permute-start(bf16[32,1664]{1,0:T(8,128)(2,1)S(1)} %get-tuple-element.120), channel_id=1, source_target_pairs={{0,1},{1,0},{2,3},{3,2},{4,5},{5,4},{6,7},{7,6},{8,9},{9,8},{10,11... | collective-permute-start | bytes 319496 | tf_op jit(solution)/shard_map/ppermute | solution.py:275
  49.1 5.3 %collective-permute-start.14 = (bf16[4,96,128]{2,1,0:T(8,128)(2,1)S(1)}, bf16[4,96,128]{2,1,0:T(8,128)(2,1)S(1)}, u32[]{:S(2)}, u32[]{:S(2)}) collective-permute-start(bf16[4,96,128]{2,1,0:T(8,128)(2,1)S(1)} %get-tuple-element.103), channel_id=1, source_target_pairs={{0,16},{8,24},{16,0},{24,8},{1,17},{9,25},{17,1},{25,9},{2,18},{10... | collective-permute-start | bytes 294920 | tf_op jit(solution)/shard_map/ppermute | solution.py:275
  (5 other events, 24.7 us)
